TPU v7x, 32 devices: a whole 2x2x4 slice. The times are simulated.
32 devices in a mesh: row: 4 (over y, core), col: 8 (over z, x).
Axes of the slice: x: 2, y: 2, z: 4, core: 2. Of those that a mesh axis runs over, the one named last changes fastest.
Arguments:
- rhs_scen: bfloat16 [256, 32768], P(('row', 'col')), may hold values from -6 to 6
- factor_panels: bfloat16 [32768, 8192], P(('row', 'col')), as said below
Outputs:
- current: float32 [32768, 256], P(('row', 'col'))
Inputs may be any that keep to these rules, and one draw needn't show every extreme that they name: `factor_panels`: in the rows of block b (b < 4, blocks of 2048 rows), every entry in the columns of later blocks is zero, and so is every entry above the diagonal of block b's own columns.
All inputs are finite; a program needn't handle non-finite values.
Results may differ from a plain program's by a relative error of at most 0.0023.
Values may be sent and summed in bfloat16 or wider, within the bound.
No kernel may reach another device: no remote copies, remote signals or barrier semaphores. Data moves between devices by JAX's collectives and lax.ppermute only.
A program may use at most 128 MiB of HBM per device.

v0:
```python
import jax
import jax.numpy as jnp
from jax import lax
from jax.sharding import PartitionSpec as P

NB = 2048
STEPS = 4


def broadcast(value, axis, source):
    kept = jnp.where(lax.axis_index(axis) == source, value, 0).astype(value.dtype)
    return lax.psum(kept, axis)


def on_device(rhs_scen, factor_panels):
    rows_here = factor_panels.shape[0]
    per_block = NB // rows_here
    regrouped = lax.all_to_all(rhs_scen, ("row", "col"), split_axis=1, concat_axis=0, tiled=True)
    current = jnp.transpose(regrouped).astype(jnp.float32)
    my_block = lax.axis_index(("row", "col")) * rows_here // NB
    for block_step in range(STEPS):
        outgoing = current.astype(jnp.bfloat16)
        product = jnp.zeros(current.shape, jnp.float32)
        for member in range(per_block):
            received = broadcast(outgoing, ("row", "col"), block_step * per_block + member)
            first_col = block_step * NB + member * rows_here
            panel_cols = factor_panels[:, first_col : first_col + rows_here]
            product = product + jnp.dot(panel_cols, received, preferred_element_type=jnp.float32)
        current = jnp.where(my_block == block_step, product, current - product)
    return current


def solution(mesh):
    placed = (P(("row", "col"), None), P(("row", "col"), None))
    return jax.shard_map(
        on_device, mesh=mesh, in_specs=placed, out_specs=P(("row", "col"), None), check_vma=False
    )
```

profile of v0, /device:TPU:0, one launch (start us, length us, event | category | flops | bytes accessed | tf_op | source)
XLA Modules:
  0.0 578.9 jit_solution(13452215287559720164)
XLA Ops:
  6.5 7.3 %all-to-all-start = ((bf16[8,32,1024]{2,0,1:T(8,128)(2,1)}), bf16[8,32,1024]{2,0,1:T(8,128)(2,1)S(1)}, u32[]{:S(2)}, u32[]{:S(2)}) async-start(bf16[8,32,1024]{2,0,1:T(8,128)(2,1)} %bitcast.43), calls=%async_computation | async-start | bytes 1048576 | tf_op jit(solution)/shard_map/all_to_all | solution.py:18
  13.8 0.0 all-reduce.15.cloned.1.call-start
  13.9 16.3 %all-to-all-done = bf16[8,32,1024]{2,0,1:T(8,128)(2,1)S(1)} async-done(((bf16[8,32,1024]{2,0,1:T(8,128)(2,1)}), bf16[8,32,1024]{2,0,1:T(8,128)(2,1)S(1)}, u32[]{:S(2)}, u32[]{:S(2)}) %all-to-all-start) | async-done | bytes 524320 | tf_op jit(solution)/shard_map/all_to_all | solution.py:18
  30.2 1.1 select_bitcast_fusion.1
  31.3 0.0 all-reduce.15.cloned.1.call-update
  31.3 0.0 all-reduce.13.cloned.1.call-start
  31.4 128.0 %all-reduce.15.cloned.1.call-done = (bf16[1024,256]{0,1:T(8,128)(2,1)}, bf16[1024,256]{0,1:T(8,128)(2,1)}) async-done(((bf16[1024,256]{0,1:T(8,128)(2,1)}, bf16[1024,256]{0,1:T(8,128)(2,1)}), (bf16[1024,256]{0,1:T(8,128)(2,1)}, bf16[1024,256]{0,1:T(8,128)(2,1)})) %all-reduce.15.cloned.1.call-update) | async-done | bytes 1048592 | tf_op jit(solution)/shard_map/psum | solution.py:12
  159.4 2.5 fusion.12
  161.9 3.7 broadcast_select_fusion.3
  165.5 0.0 all-reduce.13.cloned.1.call-update
  165.6 0.0 all-reduce.11.cloned.1.call-start
  165.6 129.3 %all-reduce.13.cloned.1.call-done = (bf16[1024,256]{0,1:T(8,128)(2,1)}, bf16[1024,256]{0,1:T(8,128)(2,1)}) async-done(((bf16[1024,256]{0,1:T(8,128)(2,1)}, bf16[1024,256]{0,1:T(8,128)(2,1)}), (bf16[1024,256]{0,1:T(8,128)(2,1)}, bf16[1024,256]{0,1:T(8,128)(2,1)})) %all-reduce.13.cloned.1.call-update) | async-done | bytes 1048592 | tf_op jit(solution)/shard_map/psum | solution.py:12
  294.9 2.5 fusion.8
  297.4 3.6 broadcast_select_fusion.4
  301.0 0.0 all-reduce.11.cloned.1.call-update
  301.1 0.0 all-reduce.9.cloned.1.call-start
  301.1 129.3 %all-reduce.11.cloned.1.call-done = (bf16[1024,256]{0,1:T(8,128)(2,1)}, bf16[1024,256]{0,1:T(8,128)(2,1)}) async-done(((bf16[1024,256]{0,1:T(8,128)(2,1)}, bf16[1024,256]{0,1:T(8,128)(2,1)}), (bf16[1024,256]{0,1:T(8,128)(2,1)}, bf16[1024,256]{0,1:T(8,128)(2,1)})) %all-reduce.11.cloned.1.call-update) | async-done | bytes 1048592 | tf_op jit(solution)/shard_map/psum | solution.py:12
  430.4 2.5 fusion.4
  432.9 3.6 broadcast_select_fusion.5
  436.6 0.0 all-reduce.9.cloned.1.call-update
  436.6 129.4 %all-reduce.9.cloned.1.call-done = (bf16[1024,256]{0,1:T(8,128)(2,1)}, bf16[1024,256]{0,1:T(8,128)(2,1)}) async-done(((bf16[1024,256]{0,1:T(8,128)(2,1)}, bf16[1024,256]{0,1:T(8,128)(2,1)}), (bf16[1024,256]{0,1:T(8,128)(2,1)}, bf16[1024,256]{0,1:T(8,128)(2,1)})) %all-reduce.9.cloned.1.call-update) | async-done | bytes 1048592 | tf_op jit(solution)/shard_map/psum | solution.py:12
  566.0 2.5 fusion
  568.5 2.6 subtract_select_fusion
  571.1 1.3 copy.3
Async XLA Ops:
  6.5 23.7 %all-to-all-start = ((bf16[8,32,1024]{2,0,1:T(8,128)(2,1)}), bf16[8,32,1024]{2,0,1:T(8,128)(2,1)S(1)}, u32[]{:S(2)}, u32[]{:S(2)}) async-start(bf16[8,32,1024]{2,0,1:T(8,128)(2,1)} %bitcast.43), calls=%async_computation | async-start | bytes 1048576 | tf_op jit(solution)/shard_map/all_to_all | solution.py:18
  13.8 145.5 %all-reduce.15.cloned.1.call-start = ((), (), s32[]{:S(2)}) async-start(), calls=%async_computation.4 | async-start | bytes 2097152 | tf_op jit(solution)/shard_map/psum | solution.py:12
  31.3 263.6 %all-reduce.13.cloned.1.call-start = ((), (), s32[]{:S(2)}) async-start(), calls=%async_computation.3 | async-start | bytes 2097152 | tf_op jit(solution)/shard_map/psum | solution.py:12
  165.6 264.9 %all-reduce.11.cloned.1.call-start = ((), (), s32[]{:S(2)}) async-start(), calls=%async_computation.2 | async-start | bytes 2097152 | tf_op jit(solution)/shard_map/psum | solution.py:12
  301.1 264.9 %all-reduce.9.cloned.1.call-start = ((), (), s32[]{:S(2)}) async-start(), calls=%async_computation.1 | async-start | bytes 2097152 | tf_op jit(solution)/shard_map/psum | solution.py:12
Sparse Core Ops, SparseCore 0:
  31.4 127.9 all-reduce.14
  165.7 129.1 all-reduce.12
  301.2 129.1 all-reduce.10
  436.7 129.2 all-reduce.8
where the time goes:
time: 579 us
  waiting for transfers between devices  532 us (92%)
  matrix products  23.5 us (4%)
  between operations  13.2 us (2%)
  starting transfers between devices  7.46 us (1%)
    psum x4, waiting for transfers between devices, broadcast(): return lax.psum(kept, axis)  516 us
    dot_general x8, matrix products, on_device(): jnp.dot(panel_cols, received, preferred_element_type=jnp.float32)  23.5 us
    all_to_all x1, waiting for transfers between devices, on_device(): lax.all_to_all(rhs_scen, ('row', 'col'), split_axis=1, concat_axis=0, til...  16.3 us
  transfers between devices with their start and end apart: 5, of which 5 were waited for; matrix products, arithmetic and copies ran while one was open for 0% of the time, Pallas kernels for 0%

commit v1 on v0

v1 whole, which is shorter than its diff:
```python
import jax
import jax.numpy as jnp
from jax import lax
from jax.sharding import PartitionSpec as P

NB = 2048
STEPS = 4
AXES = ("row", "col")
CORES = 2


def make_on_device(n_row, n_col):
    def on_device(rhs_scen, factor_panels):
        rows_here = factor_panels.shape[0]
        lanes = NB // rows_here
        planes = n_col // lanes
        n_y = n_row // CORES
        row, col = lax.axis_index("row"), lax.axis_index("col")
        y, core = row // CORES, row % CORES
        plane, lane = col // lanes, col % lanes
        flat = row * n_col + col
        my_block = flat // lanes
        piece_rows = rows_here // n_y

        def device(y, core, plane, lane):
            return (y * CORES + core) * n_col + plane * lanes + lane

        def send(value, pairs):
            return lax.ppermute(value, AXES, pairs)

        def in_order(parts, me):
            n = len(parts)
            if n == 1:
                return parts[0]
            size = parts[0].shape[0]
            twice = jnp.concatenate(parts + parts[:-1], axis=0)
            start = ((n - me) % n) * size
            return lax.dynamic_slice_in_dim(twice, start, n * size, axis=0)

        def to_next_block(own, k):
            parts = []
            for d in range(lanes):
                pairs = [
                    (device(0, 0, k, (m + d) % lanes), device(0, 0, k + 1, m)) for m in range(lanes)
                ]
                parts.append(send(own, pairs))
            return in_order(parts, lane)

        def to_all(own, k):
            piece = own[:piece_rows]
            for t in range(1, n_y):
                cut = own[t * piece_rows : (t + 1) * piece_rows]
                pairs = [(device(0, 0, k, m), device(t, 0, k, m)) for m in range(lanes)]
                piece = jnp.where(y == t, send(cut, pairs), piece)
            held = piece
            for z in range(planes):
                if z != k:
                    pairs = [
                        (device(t, 0, k, m), device(t, 0, z, m)) for t in range(n_y) for m in range(lanes)
                    ]
                    held = jnp.where(plane == z, send(piece, pairs), held)
            members = lanes * n_y
            parts = [held]
            for d in range(1, members):
                pairs = []
                for z in range(planes):
                    for i in range(members):
                        j = (i + d) % members
                        pairs.append(
                            (device(j % n_y, 0, z, j // n_y), device(i % n_y, 0, z, i // n_y))
                        )
                parts.append(send(held, pairs))
            whole = in_order(parts, lane * n_y + y)
            pairs = [
                (device(t, 0, z, m), device(t, 1, z, m))
                for t in range(n_y) for z in range(planes) for m in range(lanes)
            ]
            return jnp.where(core == 0, whole, send(whole, pairs))

        def panel(k):
            return factor_panels[:, k * NB : (k + 1) * NB]

        first = lax.all_gather(rhs_scen[:, :NB], AXES, axis=0, tiled=True)
        regrouped = lax.all_to_all(rhs_scen, AXES, split_axis=1, concat_axis=0, tiled=True)
        rhs = jnp.transpose(regrouped).astype(jnp.float32)

        def product(k, outgoing):
            return jnp.dot(panel(k), outgoing, preferred_element_type=jnp.float32)

        products = [
            lax.dot_general(panel(0), first, (((1,), (1,)), ((), ())), preferred_element_type=jnp.float32)
        ]
        current = rhs - products[0]
        chain = current
        for k in range(1, STEPS):
            own = chain.astype(jnp.bfloat16)
            if k + 1 < STEPS:
                ahead = product(k, to_next_block(own, k))
            whole = to_all(own, k)
            products.append(product(k, whole))
            chain = current - ahead if k + 1 < STEPS else None
            current = current - products[k]
        out = current
        for k in range(STEPS):
            out = jnp.where(my_block == k, products[k], out)
        return out

    return on_device


def solution(mesh):
    placed = (P(AXES, None), P(AXES, None))
    on_device = make_on_device(mesh.shape["row"], mesh.shape["col"])
    return jax.shard_map(
        on_device, mesh=mesh, in_specs=placed, out_specs=P(AXES, None), check_vma=False
    )
```

time: 579 us -> 206 us (0.36)
  waiting for transfers between devices: 532 us -> 81.7 us
  starting transfers between devices: 7.46 us -> 48.5 us
  blocking collectives: 0 us -> 24.1 us
  local copies, waits for them, and re-layouts: 1.31 us -> 7.73 us
    psum x4 -> x0, waiting for transfers between devices: 516 us -> none  [broadcast(): return lax.psum(kept, axis)]
    ppermute x0 -> x28, starting transfers between devices: none -> 48.5 us  [send(): return lax.ppermute(value, AXES, pairs)]
    ppermute x0 -> x28, waiting for transfers between devices: none -> 46.7 us  [send(): return lax.ppermute(value, AXES, pairs)]
    all_gather x0 -> x1, waiting for transfers between devices: none -> 35 us  [on_device(): first = lax.all_gather(rhs_scen[:, :NB], AXES, axis=0, tiled=True)]
    all_to_all x0 -> x1, blocking collectives: none -> 24.1 us  [on_device(): lax.all_to_all(rhs_scen, AXES, split_axis=1, concat_axis=0, tiled=True)]
    all_to_all x1 -> x0, waiting for transfers between devices: 16.3 us -> none  [on_device(): lax.all_to_all(rhs_scen, ('row', 'col'), split_axis=1, concat_axis=0, til...]
    all_to_all x1 -> x0, starting transfers between devices: 7.3 us -> none  [on_device(): lax.all_to_all(rhs_scen, ('row', 'col'), split_axis=1, concat_axis=0, til...]
    dot_general x8 -> x6, matrix products: 23.5 us -> 26.9 us  [the longest x5 22.2 us: product(): return jnp.dot(panel(k), outgoing, preferred_element_type=jnp.float32)]
  transfers between devices with their start and end apart: 5 -> 29, of which waited for: 5 -> 9; matrix products, arithmetic and copies ran while one was open for 0% -> 12% of each run, Pallas kernels for 0% -> 0%
where the time goes in v1:
time: 206 us; the launch traced here: 205 us
  waiting for transfers between devices  81.7 us (40%)
  starting transfers between devices  48.5 us (24%)
  matrix products  26.9 us (13%)
  blocking collectives  24.1 us (12%)
  between operations  14.1 us (7%)
  local copies, waits for them, and re-layouts  7.73 us (4%)
  other arithmetic  2.26 us (1%)
    ppermute x28, starting transfers between devices, send(): return lax.ppermute(value, AXES, pairs)  48.5 us
    ppermute x28, waiting for transfers between devices, send(): return lax.ppermute(value, AXES, pairs)  46.7 us
    all_gather x1, waiting for transfers between devices, on_device(): first = lax.all_gather(rhs_scen[:, :NB], AXES, axis=0, tiled=True)  35 us
    all_to_all x1, blocking collectives, on_device(): lax.all_to_all(rhs_scen, AXES, split_axis=1, concat_axis=0, tiled=True)  24.1 us
    dot_general x5, matrix products, product(): return jnp.dot(panel(k), outgoing, preferred_element_type=jnp.float32)  22.2 us
    dot_general x1, matrix products, on_device(): lax.dot_general(panel(0), first, (((1,), (1,)), ((), ())), preferred_elem...  4.75 us
  transfers between devices with their start and end apart: 29, of which 9 were waited for; matrix products, arithmetic and copies ran while one was open for 12% of the time, Pallas kernels for 0%

profile of v1, /device:TPU:0, one launch (start us, length us, event | category | flops | bytes accessed | tf_op | source)
XLA Modules:
  0.0 205.4 jit_solution(14846453623767711878)
XLA Ops:
  7.9 24.1 %all_to_all.13 = bf16[8,32,1024]{2,0,1:T(8,128)(2,1)S(1)} all-to-all(bf16[8,32,1024]{2,0,1:T(8,128)(2,1)} %bitcast.36), channel_id=1, replica_groups=mesh['row'=4,'col'=8] {'row','col'}, dimensions={1} | all-to-all | bytes 1048576 | tf_op jit(solution)/shard_map/all_to_all | solution.py:84
  32.5 35.0 %all-gather.2.cloned.1.call-done = bf16[256,2048]{1,0:T(8,128)(2,1)} async-done(((bf16[8,2048]{1,0:T(8,128)(2,1)}), bf16[256,2048]{1,0:T(8,128)(2,1)}) %all-gather.2.cloned.1.call-update) | async-done | bytes 1048592 | tf_op jit(solution)/shard_map/all_gather | solution.py:83
  67.5 4.8 %fusion.59 = (bf16[1024,256]{1,0:T(8,128)(2,1)S(1)}, f32[1024,256]{1,0:T(8,128)}) fusion(f32[256,1024]{0,1:T(8,128)S(1)} %copy.9, bf16[256,2048]{1,0:T(8,128)(2,1)} %all-gather.2.cloned.1.call-done, bf16[1024,8192]{1,0:T(8,128)(2,1)} %param.3), kind=kOutput, calls=%fused_computation.74 | convolution fusion | flops 1074266112 | bytes 7864320 | tf_op jit(solution)/shard_map/dot_general | solution.py:91
  75.8 12.8 %collective-permute-done.3 = bf16[512,256]{1,0:T(8,128)(2,1)S(1)} collective-permute-done((bf16[512,256]{1,0:T(8,128)(2,1)S(1)}, bf16[512,256]{1,0:T(8,128)(2,1)S(1)}, u32[]{:S(2)}, u32[]{:S(2)}) %collective-permute-start.3) | collective-permute-done | bytes 262176 | tf_op jit(solution)/shard_map/ppermute | solution.py:29
  89.4 5.3 %collective-permute-start.4 = (bf16[512,256]{1,0:T(8,128)(2,1)S(1)}, bf16[512,256]{1,0:T(8,128)(2,1)S(1)}, u32[]{:S(2)}, u32[]{:S(2)}) collective-permute-start(bf16[512,256]{1,0:T(8,128)(2,1)S(1)} %get-tuple-element.8), channel_id=1, source_target_pairs={{16,0},{1,16},{17,1},{0,17},{18,2},{3,18},{19,3},{2,19},{20,4},{5,... | collective-permute-start | bytes 786440 | tf_op jit(solution)/shard_map/ppermute | solution.py:29
  94.7 2.5 %collective-permute-start.5 = (bf16[512,256]{1,0:T(8,128)(2,1)S(1)}, bf16[512,256]{1,0:T(8,128)(2,1)S(1)}, u32[]{:S(2)}, u32[]{:S(2)}) collective-permute-start(bf16[512,256]{1,0:T(8,128)(2,1)S(1)} %get-tuple-element.8), channel_id=1, source_target_pairs={{1,0},{17,16},{0,1},{16,17},{3,2},{19,18},{2,3},{18,19},{5,4},{21,... | collective-permute-start | bytes 786440 | tf_op jit(solution)/shard_map/ppermute | solution.py:29
  97.2 1.9 collective-permute-start.6
  103.7 2.7 %collective-permute-done.6 = bf16[512,256]{1,0:T(8,128)(2,1)S(1)} collective-permute-done((bf16[512,256]{1,0:T(8,128)(2,1)S(1)}, bf16[512,256]{1,0:T(8,128)(2,1)S(1)}, u32[]{:S(2)}, u32[]{:S(2)}) %collective-permute-start.6) | collective-permute-done | bytes 262176 | tf_op jit(solution)/shard_map/ppermute | solution.py:29
  110.5 2.3 %collective-permute-start.7 = (bf16[2048,256]{1,0:T(8,128)(2,1)S(1)}, bf16[2048,256]{1,0:T(8,128)(2,1)}, u32[]{:S(2)}, u32[]{:S(2)}) collective-permute-start(bf16[2048,256]{1,0:T(8,128)(2,1)S(1)} %constant_dynamic-slice_fusion.2), channel_id=1, source_target_pairs={{0,8},{1,9},{2,10},{3,11},{4,12},{5,13},{6,14},{7,15},{16,24},{17,... | collective-permute-start | bytes 3145736 | tf_op jit(solution)/shard_map/ppermute | solution.py:29
  112.8 5.1 %fusion.33 = bf16[1024,256]{1,0:T(8,128)(2,1)S(1)} fusion(bf16[1024,8192]{1,0:T(8,128)(2,1)} %param.3, s32[]{:T(128)S(6)} %select_n.165, bf16[1024,256]{1,0:T(8,128)(2,1)S(1)} %collective-permute-done.8, bf16[1024,256]{1,0:T(8,128)(2,1)S(1)} %collective-permute-done.9, f32[1024,256]{1,0:T(8,128)S(1)} %copy-done, f32[256,1024]{0,1:T(8,128)S(1)} %copy.9), kind=kOutput, calls=%fused_computation.25 | convolution fusion | flops 1077673984 | bytes 7864324 | tf_op jit(solution)/shard_map/dot_general | solution.py:88
  122.8 15.8 %collective-permute-done.23 = bf16[512,256]{1,0:T(8,128)(2,1)} collective-permute-done((bf16[512,256]{1,0:T(8,128)(2,1)S(1)}, bf16[512,256]{1,0:T(8,128)(2,1)}, u32[]{:S(2)}, u32[]{:S(2)}) %collective-permute-start.23) | collective-permute-done | bytes 262176 | tf_op jit(solution)/shard_map/ppermute | solution.py:29
  139.7 4.5 %collective-permute-start.24 = (bf16[512,256]{1,0:T(8,128)(2,1)S(1)}, bf16[512,256]{1,0:T(8,128)(2,1)S(1)}, u32[]{:S(2)}, u32[]{:S(2)}) collective-permute-start(bf16[512,256]{1,0:T(8,128)(2,1)S(1)} %get-tuple-element.10), channel_id=1, source_target_pairs={{16,0},{1,16},{17,1},{0,17},{18,2},{3,18},{19,3},{2,19},{20,4},{5,... | collective-permute-start | bytes 786440 | tf_op jit(solution)/shard_map/ppermute | solution.py:29
  144.2 3.4 %collective-permute-start.25 = (bf16[512,256]{1,0:T(8,128)(2,1)S(1)}, bf16[512,256]{1,0:T(8,128)(2,1)S(1)}, u32[]{:S(2)}, u32[]{:S(2)}) collective-permute-start(bf16[512,256]{1,0:T(8,128)(2,1)S(1)} %get-tuple-element.10), channel_id=1, source_target_pairs={{1,0},{17,16},{0,1},{16,17},{3,2},{19,18},{2,3},{18,19},{5,4},{21,... | collective-permute-start | bytes 786440 | tf_op jit(solution)/shard_map/ppermute | solution.py:29
  147.6 3.5 %fusion.15 = f32[1024,256]{1,0:T(8,128)S(1)} fusion(bf16[1024,8192]{1,0:T(8,128)(2,1)} %param.3, bf16[2048,256]{1,0:T(8,128)(2,1)S(1)} %constant_dynamic-slice_fusion.2, bf16[2048,256]{1,0:T(8,128)(2,1)} %collective-permute-done.7, pred[]{:T(512)S(6)} %eq.48), kind=kOutput, calls=%fused_computation.19 | convolution fusion | flops 1074266112 | bytes 7340033 | tf_op jit(solution)/shard_map/dot_general | solution.py:88
  151.1 5.4 %fusion.36 = bf16[1024,256]{1,0:T(8,128)(2,1)S(1)} fusion(bf16[1024,8192]{1,0:T(8,128)(2,1)} %param.3, s32[]{:T(128)S(6)} %select_n.165, bf16[1024,256]{1,0:T(8,128)(2,1)S(1)} %collective-permute-done.10, bf16[1024,256]{1,0:T(8,128)(2,1)S(1)} %collective-permute-done.11, f32[1024,256]{1,0:T(8,128)S(1)} %fusion.15, f32[1024,256]{1,0:T(8,128)S(1)} %copy-done.1, ...), kind=kOutput, calls=%fused_computation.26 | convolution fusion | flops 1077936128 | bytes 8912900 | tf_op jit(solution)/shard_map/dot_general | solution.py:88
  162.2 4.3 %collective-permute-done.26 = bf16[512,256]{1,0:T(8,128)(2,1)S(1)} collective-permute-done((bf16[512,256]{1,0:T(8,128)(2,1)S(1)}, bf16[512,256]{1,0:T(8,128)(2,1)S(1)}, u32[]{:S(2)}, u32[]{:S(2)}) %collective-permute-start.26) | collective-permute-done | bytes 262176 | tf_op jit(solution)/shard_map/ppermute | solution.py:29
  166.5 4.6 %collective-permute-done.15 = bf16[512,256]{1,0:T(8,128)(2,1)S(1)} collective-permute-done((bf16[512,256]{1,0:T(8,128)(2,1)S(1)}, bf16[512,256]{1,0:T(8,128)(2,1)S(1)}, u32[]{:S(2)}, u32[]{:S(2)}) %collective-permute-start.15) | collective-permute-done | bytes 262176 | tf_op jit(solution)/shard_map/ppermute | solution.py:29
  171.2 4.9 %collective-permute-start.16 = (bf16[512,256]{1,0:T(8,128)(2,1)S(1)}, bf16[512,256]{1,0:T(8,128)(2,1)S(1)}, u32[]{:S(2)}, u32[]{:S(2)}) collective-permute-start(bf16[512,256]{1,0:T(8,128)(2,1)S(1)} %get-tuple-element.6), channel_id=1, source_target_pairs={{16,0},{1,16},{17,1},{0,17},{18,2},{3,18},{19,3},{2,19},{20,4},{5,... | collective-permute-start | bytes 786440 | tf_op jit(solution)/shard_map/ppermute | solution.py:29
  176.2 2.5 %collective-permute-start.17 = (bf16[512,256]{1,0:T(8,128)(2,1)S(1)}, bf16[512,256]{1,0:T(8,128)(2,1)S(1)}, u32[]{:S(2)}, u32[]{:S(2)}) collective-permute-start(bf16[512,256]{1,0:T(8,128)(2,1)S(1)} %get-tuple-element.6), channel_id=1, source_target_pairs={{1,0},{17,16},{0,1},{16,17},{3,2},{19,18},{2,3},{18,19},{5,4},{21,... | collective-permute-start | bytes 786440 | tf_op jit(solution)/shard_map/ppermute | solution.py:29
  180.7 2.3 %collective-permute-start.27 = (bf16[2048,256]{1,0:T(8,128)(2,1)S(1)}, bf16[2048,256]{1,0:T(8,128)(2,1)}, u32[]{:S(2)}, u32[]{:S(2)}) collective-permute-start(bf16[2048,256]{1,0:T(8,128)(2,1)S(1)} %constant_dynamic-slice_fusion), channel_id=1, source_target_pairs={{0,8},{1,9},{2,10},{3,11},{4,12},{5,13},{6,14},{7,15},{16,24},{17,... | collective-permute-start | bytes 3145736 | tf_op jit(solution)/shard_map/ppermute | solution.py:29
  184.4 3.4 %collective-permute-done.18 = bf16[512,256]{1,0:T(8,128)(2,1)S(1)} collective-permute-done((bf16[512,256]{1,0:T(8,128)(2,1)S(1)}, bf16[512,256]{1,0:T(8,128)(2,1)S(1)}, u32[]{:S(2)}, u32[]{:S(2)}) %collective-permute-start.18) | collective-permute-done | bytes 262176 | tf_op jit(solution)/shard_map/ppermute | solution.py:29
  188.0 2.3 %collective-permute-start.19 = (bf16[2048,256]{1,0:T(8,128)(2,1)S(1)}, bf16[2048,256]{1,0:T(8,128)(2,1)}, u32[]{:S(2)}, u32[]{:S(2)}) collective-permute-start(bf16[2048,256]{1,0:T(8,128)(2,1)S(1)} %constant_dynamic-slice_fusion.1), channel_id=1, source_target_pairs={{0,8},{1,9},{2,10},{3,11},{4,12},{5,13},{6,14},{7,15},{16,24},{17,... | collective-permute-start | bytes 3145736 | tf_op jit(solution)/shard_map/ppermute | solution.py:29
  190.3 3.6 %fusion.18 = f32[1024,256]{1,0:T(8,128)S(1)} fusion(bf16[1024,8192]{1,0:T(8,128)(2,1)} %param.3, bf16[2048,256]{1,0:T(8,128)(2,1)S(1)} %constant_dynamic-slice_fusion, bf16[2048,256]{1,0:T(8,128)(2,1)} %collective-permute-done.27, pred[]{:T(512)S(6)} %eq.48), kind=kOutput, calls=%fused_computation.20 | convolution fusion | flops 1074266112 | bytes 7340033 | tf_op jit(solution)/shard_map/dot_general | solution.py:88
  193.9 4.6 %select_select_fusion = f32[1024,256]{1,0:T(8,128)} fusion(f32[1024,256]{1,0:T(8,128)S(1)} %fusion.18, f32[1024,256]{1,0:T(8,128)S(1)} %copy-done.4, f32[1024,256]{1,0:T(8,128)S(1)} %copy-done.2, bf16[2048,256]{1,0:T(8,128)(2,1)S(1)} %constant_dynamic-slice_fusion.1, bf16[2048,256]{1,0:T(8,128)(2,1)} %collective-permute-done.19, pred[]{:T(512)S(6)} %eq.48, ...), kind=kOutput, calls=%fused_computation.33 | convolution fusion | flops 1076363264 | bytes 11534341 | tf_op jit(solution)/shard_map/dot_general | solution.py:88
  (85 shorter events, 30.0 us)
Async XLA Ops:
  6.5 61.0 %all-gather.2.cloned.1.call-start = ((), (), s32[]{:S(2)}) async-start(), calls=%async_computation.1 | async-start | bytes 1081344 | tf_op jit(solution)/shard_map/all_gather | solution.py:83
  74.4 14.2 %collective-permute-start.3 = (bf16[512,256]{1,0:T(8,128)(2,1)S(1)}, bf16[512,256]{1,0:T(8,128)(2,1)S(1)}, u32[]{:S(2)}, u32[]{:S(2)}) collective-permute-start(bf16[512,256]{1,0:T(8,128)(2,1)S(1)} %slice_select_fusion.2), channel_id=1, source_target_pairs={{2,0},{3,1},{18,16},{19,17}} | collective-permute-start | bytes 786440 | tf_op jit(solution)/shard_map/ppermute | solution.py:29
  89.4 11.2 %collective-permute-start.4 = (bf16[512,256]{1,0:T(8,128)(2,1)S(1)}, bf16[512,256]{1,0:T(8,128)(2,1)S(1)}, u32[]{:S(2)}, u32[]{:S(2)}) collective-permute-start(bf16[512,256]{1,0:T(8,128)(2,1)S(1)} %get-tuple-element.8), channel_id=1, source_target_pairs={{16,0},{1,16},{17,1},{0,17},{18,2},{3,18},{19,3},{2,19},{20,4},{5,... | collective-permute-start | bytes 786440 | tf_op jit(solution)/shard_map/ppermute | solution.py:29
  94.7 8.3 %collective-permute-start.5 = (bf16[512,256]{1,0:T(8,128)(2,1)S(1)}, bf16[512,256]{1,0:T(8,128)(2,1)S(1)}, u32[]{:S(2)}, u32[]{:S(2)}) collective-permute-start(bf16[512,256]{1,0:T(8,128)(2,1)S(1)} %get-tuple-element.8), channel_id=1, source_target_pairs={{1,0},{17,16},{0,1},{16,17},{3,2},{19,18},{2,3},{18,19},{5,4},{21,... | collective-permute-start | bytes 786440 | tf_op jit(solution)/shard_map/ppermute | solution.py:29
  97.2 9.2 %collective-permute-start.6 = (bf16[512,256]{1,0:T(8,128)(2,1)S(1)}, bf16[512,256]{1,0:T(8,128)(2,1)S(1)}, u32[]{:S(2)}, u32[]{:S(2)}) collective-permute-start(bf16[512,256]{1,0:T(8,128)(2,1)S(1)} %get-tuple-element.8), channel_id=1, source_target_pairs={{17,0},{0,16},{16,1},{1,17},{19,2},{2,18},{18,3},{3,19},{21,4},{4,... | collective-permute-start | bytes 786440 | tf_op jit(solution)/shard_map/ppermute | solution.py:29
  99.2 13.6 %collective-permute-start.8 = (bf16[1024,256]{1,0:T(8,128)(2,1)S(1)}, bf16[1024,256]{1,0:T(8,128)(2,1)S(1)}, u32[]{:S(2)}, u32[]{:S(2)}) collective-permute-start(bf16[1024,256]{1,0:T(8,128)(2,1)S(1)} %get-tuple-element.11), channel_id=1, source_target_pairs={{2,4},{3,5}} | collective-permute-start | bytes 1572872 | tf_op jit(solution)/shard_map/ppermute | solution.py:29
  99.9 12.9 %collective-permute-start.9 = (bf16[1024,256]{1,0:T(8,128)(2,1)S(1)}, bf16[1024,256]{1,0:T(8,128)(2,1)S(1)}, u32[]{:S(2)}, u32[]{:S(2)}) collective-permute-start(bf16[1024,256]{1,0:T(8,128)(2,1)S(1)} %get-tuple-element.11), channel_id=1, source_target_pairs={{3,4},{2,5}} | collective-permute-start | bytes 1572872 | tf_op jit(solution)/shard_map/ppermute | solution.py:29
  110.5 37.1 %collective-permute-start.7 = (bf16[2048,256]{1,0:T(8,128)(2,1)S(1)}, bf16[2048,256]{1,0:T(8,128)(2,1)}, u32[]{:S(2)}, u32[]{:S(2)}) collective-permute-start(bf16[2048,256]{1,0:T(8,128)(2,1)S(1)} %constant_dynamic-slice_fusion.2), channel_id=1, source_target_pairs={{0,8},{1,9},{2,10},{3,11},{4,12},{5,13},{6,14},{7,15},{16,24},{17,... | collective-permute-start | bytes 3145736 | tf_op jit(solution)/shard_map/ppermute | solution.py:29
  118.6 3.4 %collective-permute-start.21 = (bf16[512,256]{1,0:T(8,128)(2,1)S(1)}, bf16[512,256]{1,0:T(8,128)(2,1)S(1)}, u32[]{:S(2)}, u32[]{:S(2)}) collective-permute-start(bf16[512,256]{1,0:T(8,128)(2,1)S(1)} %slice_select_fusion), channel_id=1, source_target_pairs={{4,6},{5,7},{20,22},{21,23}} | collective-permute-start | bytes 786440 | tf_op jit(solution)/shard_map/ppermute | solution.py:29
  119.3 3.4 %collective-permute-start.22 = (bf16[512,256]{1,0:T(8,128)(2,1)S(1)}, bf16[512,256]{1,0:T(8,128)(2,1)S(1)}, u32[]{:S(2)}, u32[]{:S(2)}) collective-permute-start(bf16[512,256]{1,0:T(8,128)(2,1)S(1)} %slice_select_fusion), channel_id=1, source_target_pairs={{4,2},{5,3},{20,18},{21,19}} | collective-permute-start | bytes 786440 | tf_op jit(solution)/shard_map/ppermute | solution.py:29
  120.0 18.6 %collective-permute-start.23 = (bf16[512,256]{1,0:T(8,128)(2,1)S(1)}, bf16[512,256]{1,0:T(8,128)(2,1)}, u32[]{:S(2)}, u32[]{:S(2)}) collective-permute-start(bf16[512,256]{1,0:T(8,128)(2,1)S(1)} %slice_select_fusion), channel_id=1, source_target_pairs={{4,0},{5,1},{20,16},{21,17}} | collective-permute-start | bytes 786440 | tf_op jit(solution)/shard_map/ppermute | solution.py:29
  121.3 29.7 %collective-permute-start.10 = (bf16[1024,256]{1,0:T(8,128)(2,1)S(1)}, bf16[1024,256]{1,0:T(8,128)(2,1)S(1)}, u32[]{:S(2)}, u32[]{:S(2)}) collective-permute-start(bf16[1024,256]{1,0:T(8,128)(2,1)S(1)} %fusion.33), channel_id=1, source_target_pairs={{4,6},{5,7}} | collective-permute-start | bytes 1572872 | tf_op jit(solution)/shard_map/ppermute | solution.py:29
  122.0 29.0 %collective-permute-start.11 = (bf16[1024,256]{1,0:T(8,128)(2,1)S(1)}, bf16[1024,256]{1,0:T(8,128)(2,1)S(1)}, u32[]{:S(2)}, u32[]{:S(2)}) collective-permute-start(bf16[1024,256]{1,0:T(8,128)(2,1)S(1)} %fusion.33), channel_id=1, source_target_pairs={{5,6},{4,7}} | collective-permute-start | bytes 1572872 | tf_op jit(solution)/shard_map/ppermute | solution.py:29
  139.7 19.5 %collective-permute-start.24 = (bf16[512,256]{1,0:T(8,128)(2,1)S(1)}, bf16[512,256]{1,0:T(8,128)(2,1)S(1)}, u32[]{:S(2)}, u32[]{:S(2)}) collective-permute-start(bf16[512,256]{1,0:T(8,128)(2,1)S(1)} %get-tuple-element.10), channel_id=1, source_target_pairs={{16,0},{1,16},{17,1},{0,17},{18,2},{3,18},{19,3},{2,19},{20,4},{5,... | collective-permute-start | bytes 786440 | tf_op jit(solution)/shard_map/ppermute | solution.py:29
  144.2 15.0 %collective-permute-start.25 = (bf16[512,256]{1,0:T(8,128)(2,1)S(1)}, bf16[512,256]{1,0:T(8,128)(2,1)S(1)}, u32[]{:S(2)}, u32[]{:S(2)}) collective-permute-start(bf16[512,256]{1,0:T(8,128)(2,1)S(1)} %get-tuple-element.10), channel_id=1, source_target_pairs={{1,0},{17,16},{0,1},{16,17},{3,2},{19,18},{2,3},{18,19},{5,4},{21,... | collective-permute-start | bytes 786440 | tf_op jit(solution)/shard_map/ppermute | solution.py:29
  157.2 9.2 %collective-permute-start.26 = (bf16[512,256]{1,0:T(8,128)(2,1)S(1)}, bf16[512,256]{1,0:T(8,128)(2,1)S(1)}, u32[]{:S(2)}, u32[]{:S(2)}) collective-permute-start(bf16[512,256]{1,0:T(8,128)(2,1)S(1)} %get-tuple-element.10), channel_id=1, source_target_pairs={{17,0},{0,16},{16,1},{1,17},{19,2},{2,18},{18,3},{3,19},{21,4},{4,... | collective-permute-start | bytes 786440 | tf_op jit(solution)/shard_map/ppermute | solution.py:29
  159.3 7.2 %collective-permute-start.13 = (bf16[512,256]{1,0:T(8,128)(2,1)S(1)}, bf16[512,256]{1,0:T(8,128)(2,1)S(1)}, u32[]{:S(2)}, u32[]{:S(2)}) collective-permute-start(bf16[512,256]{1,0:T(8,128)(2,1)S(1)} %slice_select_fusion.1), channel_id=1, source_target_pairs={{6,4},{7,5},{22,20},{23,21}} | collective-permute-start | bytes 786440 | tf_op jit(solution)/shard_map/ppermute | solution.py:29
  160.2 6.3 %collective-permute-start.14 = (bf16[512,256]{1,0:T(8,128)(2,1)S(1)}, bf16[512,256]{1,0:T(8,128)(2,1)S(1)}, u32[]{:S(2)}, u32[]{:S(2)}) collective-permute-start(bf16[512,256]{1,0:T(8,128)(2,1)S(1)} %slice_select_fusion.1), channel_id=1, source_target_pairs={{6,2},{7,3},{22,18},{23,19}} | collective-permute-start | bytes 786440 | tf_op jit(solution)/shard_map/ppermute | solution.py:29
  160.9 10.3 %collective-permute-start.15 = (bf16[512,256]{1,0:T(8,128)(2,1)S(1)}, bf16[512,256]{1,0:T(8,128)(2,1)S(1)}, u32[]{:S(2)}, u32[]{:S(2)}) collective-permute-start(bf16[512,256]{1,0:T(8,128)(2,1)S(1)} %slice_select_fusion.1), channel_id=1, source_target_pairs={{6,0},{7,1},{22,16},{23,17}} | collective-permute-start | bytes 786440 | tf_op jit(solution)/shard_map/ppermute | solution.py:29
  171.2 11.7 %collective-permute-start.16 = (bf16[512,256]{1,0:T(8,128)(2,1)S(1)}, bf16[512,256]{1,0:T(8,128)(2,1)S(1)}, u32[]{:S(2)}, u32[]{:S(2)}) collective-permute-start(bf16[512,256]{1,0:T(8,128)(2,1)S(1)} %get-tuple-element.6), channel_id=1, source_target_pairs={{16,0},{1,16},{17,1},{0,17},{18,2},{3,18},{19,3},{2,19},{20,4},{5,... | collective-permute-start | bytes 786440 | tf_op jit(solution)/shard_map/ppermute | solution.py:29
  176.2 8.3 %collective-permute-start.17 = (bf16[512,256]{1,0:T(8,128)(2,1)S(1)}, bf16[512,256]{1,0:T(8,128)(2,1)S(1)}, u32[]{:S(2)}, u32[]{:S(2)}) collective-permute-start(bf16[512,256]{1,0:T(8,128)(2,1)S(1)} %get-tuple-element.6), channel_id=1, source_target_pairs={{1,0},{17,16},{0,1},{16,17},{3,2},{19,18},{2,3},{18,19},{5,4},{21,... | collective-permute-start | bytes 786440 | tf_op jit(solution)/shard_map/ppermute | solution.py:29
  178.6 9.2 %collective-permute-start.18 = (bf16[512,256]{1,0:T(8,128)(2,1)S(1)}, bf16[512,256]{1,0:T(8,128)(2,1)S(1)}, u32[]{:S(2)}, u32[]{:S(2)}) collective-permute-start(bf16[512,256]{1,0:T(8,128)(2,1)S(1)} %get-tuple-element.6), channel_id=1, source_target_pairs={{17,0},{0,16},{16,1},{1,17},{19,2},{2,18},{18,3},{3,19},{21,4},{4,... | collective-permute-start | bytes 786440 | tf_op jit(solution)/shard_map/ppermute | solution.py:29
  180.7 9.6 %collective-permute-start.27 = (bf16[2048,256]{1,0:T(8,128)(2,1)S(1)}, bf16[2048,256]{1,0:T(8,128)(2,1)}, u32[]{:S(2)}, u32[]{:S(2)}) collective-permute-start(bf16[2048,256]{1,0:T(8,128)(2,1)S(1)} %constant_dynamic-slice_fusion), channel_id=1, source_target_pairs={{0,8},{1,9},{2,10},{3,11},{4,12},{5,13},{6,14},{7,15},{16,24},{17,... | collective-permute-start | bytes 3145736 | tf_op jit(solution)/shard_map/ppermute | solution.py:29
  188.0 5.9 %collective-permute-start.19 = (bf16[2048,256]{1,0:T(8,128)(2,1)S(1)}, bf16[2048,256]{1,0:T(8,128)(2,1)}, u32[]{:S(2)}, u32[]{:S(2)}) collective-permute-start(bf16[2048,256]{1,0:T(8,128)(2,1)S(1)} %constant_dynamic-slice_fusion.1), channel_id=1, source_target_pairs={{0,8},{1,9},{2,10},{3,11},{4,12},{5,13},{6,14},{7,15},{16,24},{17,... | collective-permute-start | bytes 3145736 | tf_op jit(solution)/shard_map/ppermute | solution.py:29
  (10 other events, 38.7 us)
Sparse Core Ops, SparseCore 0:
  10.4 57.1 all-gather.1

commit v2 on v0

v2 whole, which is shorter than its diff:
```python
import functools

import jax
import jax.numpy as jnp
from jax import lax
from jax.experimental import pallas as pl
from jax.experimental.pallas import tpu as pltpu
from jax.sharding import PartitionSpec as P

NB = 2048
STEPS = 4
AXES = ("row", "col")
CORES = 2
TILE = 256


def after(value, *others):
    return lax.optimization_barrier((value, *others))[0]


def step_kernel(counts, n_out, *refs):
    info, current = refs[0], refs[1]
    at = 2
    panels = refs[at : at + len(counts)]
    at += len(counts)
    pieces = []
    for n in counts:
        pieces.append(refs[at : at + n])
        at += n
    outs = refs[at : at + n_out]
    held = refs[at + n_out :]

    @pl.when(pl.program_id(0) == 0)
    def _():
        place = len(counts)
        for t, n in enumerate(counts):
            for piece in pieces[t]:
                size = piece.shape[0]
                start = pl.multiple_of(info[place] * size, size)
                held[t][pl.ds(start, size), :] = piece[...]
                place += 1

    value = current[...]
    for t in range(len(counts)):
        product = jnp.dot(panels[t][...], held[t][...], preferred_element_type=jnp.float32)
        value = jnp.where(info[t] == 1, product, value - product)
    for out in outs:
        out[...] = value.astype(out.dtype)


def steps(current, factor_panels, terms, my_block, out_types):
    rows, scenarios = current.shape
    tile = min(TILE, rows)
    counts = tuple(len(pieces) for _, pieces, _ in terms)
    info = [my_block == k for k, _, _ in terms]
    for _, _, places in terms:
        info.extend(places)
    info = jnp.stack([jnp.asarray(x, jnp.int32) for x in info])
    by_tile = pl.BlockSpec((tile, scenarios), lambda i, _: (i, 0))
    specs = [by_tile]
    operands = [current]
    for k, _, _ in terms:
        specs.append(pl.BlockSpec((tile, NB), functools.partial(lambda k, i, _: (i, k), k)))
        operands.append(factor_panels)
    for _, pieces, _ in terms:
        for piece in pieces:
            specs.append(pl.BlockSpec(piece.shape, lambda i, _: (0, 0)))
            operands.append(piece)
    result = pl.pallas_call(
        functools.partial(step_kernel, counts, len(out_types)),
        grid_spec=pltpu.PrefetchScalarGridSpec(
            num_scalar_prefetch=1,
            grid=(rows // tile,),
            in_specs=specs,
            out_specs=[by_tile] * len(out_types),
            scratch_shapes=[pltpu.VMEM((NB, scenarios), jnp.bfloat16)] * len(terms),
        ),
        out_shape=[jax.ShapeDtypeStruct((rows, scenarios), t) for t in out_types],
        compiler_params=pltpu.CompilerParams(vmem_limit_bytes=50 * 1024 * 1024),
        cost_estimate=pl.CostEstimate(
            flops=2 * rows * NB * scenarios * len(terms),
            bytes_accessed=2 * rows * NB * len(terms) + 8 * rows * scenarios,
            transcendentals=0,
        ),
    )(info, *operands)
    return result


def make_on_device(n_row, n_col):
    def on_device(rhs_scen, factor_panels):
        rows_here = factor_panels.shape[0]
        lanes = NB // rows_here
        planes = n_col // lanes
        n_y = n_row // CORES
        members = lanes * n_y * CORES
        row, col = lax.axis_index("row"), lax.axis_index("col")
        y, core = row // CORES, row % CORES
        plane, lane = col // lanes, col % lanes
        my_block = (row * n_col + col) // lanes

        def device(y, core, plane, lane):
            return (y * CORES + core) * n_col + plane * lanes + lane

        def send(value, pairs):
            return lax.ppermute(value, AXES, pairs)

        def lane_gather(value, cores, zs):
            out = [value]
            for d in range(1, lanes):
                pairs = [
                    (device(t, c, z, (m + d) % lanes), device(t, c, z, m))
                    for t in range(n_y) for c in cores for z in zs for m in range(lanes)
                ]
                out.append(send(value, pairs))
            return out

        def y_gather(value, cores):
            out = [value]
            for d in range(1, n_y):
                pairs = [
                    (device((t + d) % n_y, c, z, m), device(t, c, z, m))
                    for t in range(n_y) for c in cores for z in range(planes) for m in range(lanes)
                ]
                out.append(send(value, pairs))
            return out

        def ahead(own, k):
            return [
                send(own, [(device(0, 0, k, (m + d) % lanes), device(0, 0, k + 1, m)) for m in range(lanes)])
                for d in range(lanes)
            ]

        lane_places = [(lane + d) % lanes for d in range(lanes)]

        def scatter_y(own, k):
            size = rows_here // n_y
            piece = own[:size]
            for t in range(1, n_y):
                cut = own[t * size : (t + 1) * size]
                got = send(cut, [(device(0, 0, k, m), device(t, 0, k, m)) for m in range(lanes)])
                piece = jnp.where(y == t, got, piece)
            return piece

        def plane_rounds(k):
            left = sorted((z for z in range(planes) if z != k), key=lambda z: -abs(z - k))
            half = max(planes // 2, 1)
            holders, rounds = [k], []
            while half:
                pairs = []
                for h in list(holders):
                    for z in (h ^ half, *left):
                        if z in left:
                            pairs.append((h, z))
                            holders.append(z)
                            left.remove(z)
                            break
                if pairs:
                    rounds.append(pairs)
                half //= 2
            while left:
                pairs = [(h, z) for h, z in zip(list(holders), list(left))]
                for _, z in pairs:
                    left.remove(z)
                    holders.append(z)
                rounds.append(pairs)
            return rounds

        def plane_send(piece, zpairs):
            got = send(
                piece,
                [
                    (device(t, 0, a, m), device(t, 0, b, m))
                    for a, b in zpairs for t in range(n_y) for m in range(lanes)
                ],
            )
            new = functools.reduce(jnp.logical_or, [plane == b for _, b in zpairs])
            return jnp.where(new, got, piece)

        def core_send(value):
            got = send(
                value,
                [
                    (device(t, 0, z, m), device(t, 1, z, m))
                    for t in range(n_y) for z in range(planes) for m in range(lanes)
                ],
            )
            return jnp.where(core == 0, value, got)

        tree_places = [
            ((lane + dm) % lanes) * n_y + (y + dy) % n_y for dy in range(n_y) for dm in range(lanes)
        ]

        extra = NB // members
        start_places = [
            (((lane + dm) % lanes) * n_y + (y + dy) % n_y) * CORES + (core + dc) % CORES
            for dc in range(CORES) for dy in range(n_y) for dm in range(lanes)
        ]
        first = rhs_scen[:, :NB].reshape(-1, lanes, n_y, CORES, extra).transpose(0, 2, 3, 1, 4)
        first = jnp.broadcast_to(
            first[:, :, :, None], (first.shape[0], n_y, CORES, planes, lanes, extra)
        ).reshape(first.shape[0], n_row * n_col, extra)
        outgoing = jnp.concatenate(
            [rhs_scen.reshape(rhs_scen.shape[0], n_row * n_col, rows_here), first], axis=2
        )
        regrouped = lax.all_to_all(outgoing, AXES, split_axis=1, concat_axis=0, tiled=True)
        regrouped = regrouped.reshape(-1, rows_here + extra)
        current = jnp.transpose(regrouped[:, :rows_here]).astype(jnp.float32)
        piece = jnp.transpose(regrouped[:, rows_here:])
        both = range(CORES)
        whole = jnp.concatenate(lane_gather(piece, both, range(planes)), axis=0)
        whole = jnp.concatenate(y_gather(whole, both), axis=0)
        other = send(
            whole,
            [
                (device(t, 1 - c, z, m), device(t, c, z, m))
                for t in range(n_y) for c in both for z in range(planes) for m in range(lanes)
            ],
        )
        halves = [whole, other]
        pieces = [h[i * extra : (i + 1) * extra] for h in halves for i in range(members // CORES)]

        def run(current, terms, types):
            return steps(current, factor_panels, terms, my_block, types)

        current, own1 = run(current, [(0, pieces, start_places)], [jnp.float32, jnp.bfloat16])

        def tree_start(own, k):
            piece = scatter_y(own, k)
            rounds = plane_rounds(k)
            return piece, rounds

        def tree_end(piece):
            got = jnp.concatenate(lane_gather(piece, [0], range(planes)), axis=0)
            return jnp.concatenate(y_gather(got, [0]), axis=0)

        hop1 = ahead(own1, 1)
        piece1, rounds1 = tree_start(own1, 1)
        fwd = send(hop1[0], [(device(0, 0, 2, m), device(0, 0, 3, m)) for m in range(lanes)])
        (own2,) = run(current, [(1, hop1, lane_places)], [jnp.bfloat16])
        hop2 = ahead(own2, 2)
        piece1 = after(piece1, own2)
        fwd_all = [fwd] + [
            send(fwd, [(device(0, 0, 3, (m + d) % lanes), device(0, 0, 3, m)) for m in range(lanes)])
            for d in range(1, lanes)
        ]
        (current_c,) = run(current, [(1, fwd_all, lane_places)], [jnp.float32])
        for pairs in rounds1:
            piece1 = plane_send(piece1, pairs)
        piece2, rounds2 = tree_start(own2, 2)
        (own3,) = run(current_c, [(2, hop2, lane_places)], [jnp.bfloat16])
        piece3, rounds3 = tree_start(own3, 3)
        piece1 = after(piece1, own3)
        piece2 = after(piece2, own3)
        got1 = tree_end(piece1)
        for pairs in rounds2:
            piece2 = plane_send(piece2, pairs)
        all1 = core_send(got1)
        for pairs in rounds3:
            piece3 = plane_send(piece3, pairs)
        got2 = tree_end(piece2)
        all2 = core_send(got2)
        (current,) = run(
            current,
            [(1, split(all1, tree_places), tree_places), (2, split(all2, tree_places), tree_places)],
            [jnp.float32],
        )
        got3 = tree_end(piece3)
        all3 = core_send(got3)
        (out,) = run(current, [(3, split(all3, tree_places), tree_places)], [jnp.float32])
        return out

    def split(whole, places):
        size = whole.shape[0] // len(places)
        return [whole[i * size : (i + 1) * size] for i in range(len(places))]

    return on_device


def solution(mesh):
    placed = (P(AXES, None), P(AXES, None))
    on_device = make_on_device(mesh.shape["row"], mesh.shape["col"])
    return jax.shard_map(
        on_device, mesh=mesh, in_specs=placed, out_specs=P(AXES, None), check_vma=False
    )
```

time: 579 us -> 158 us (0.27)
  waiting for transfers between devices: 532 us -> 50.8 us
  starting transfers between devices: 7.46 us -> 39.8 us
  Pallas kernels: 0 us -> 30.8 us
  blocking collectives: 0 us -> 26.3 us
  matrix products: 23.5 us -> 0 us
  between operations: 13.2 us -> 0.69 us
    psum x4 -> x0, waiting for transfers between devices: 516 us -> none  [broadcast(): return lax.psum(kept, axis)]
    ppermute x0 -> x27, waiting for transfers between devices: none -> 50.8 us  [send(): return lax.ppermute(value, AXES, pairs)]
    ppermute x0 -> x27, starting transfers between devices: none -> 39.8 us  [send(): return lax.ppermute(value, AXES, pairs)]
    pallas_call x0 -> x6, Pallas kernels: none -> 30.8 us  [steps(): pl.pallas_call(functools.partial(step_kernel, counts, len(out_types)), gr...]
    all_to_all x0 -> x1, blocking collectives: none -> 26.3 us  [on_device(): lax.all_to_all(outgoing, AXES, split_axis=1, concat_axis=0, tiled=True)]
    dot_general x8 -> x0, matrix products: 23.5 us -> none  [on_device(): jnp.dot(panel_cols, received, preferred_element_type=jnp.float32)]
    all_to_all x1 -> x0, waiting for transfers between devices: 16.3 us -> none  [on_device(): lax.all_to_all(rhs_scen, ('row', 'col'), split_axis=1, concat_axis=0, til...]
    all_to_all x1 -> x0, starting transfers between devices: 7.3 us -> none  [on_device(): lax.all_to_all(rhs_scen, ('row', 'col'), split_axis=1, concat_axis=0, til...]
  transfers between devices with their start and end apart: 5 -> 27, of which waited for: 5 -> 11; matrix products, arithmetic and copies ran while one was open for 0% -> 4% of each run, Pallas kernels for 0% -> 13%
where the time goes in v2:
time: 158 us; the launch traced here: 157 us
  waiting for transfers between devices  50.8 us (32%)
  starting transfers between devices  39.8 us (25%)
  Pallas kernels  30.8 us (19%)
  blocking collectives  26.3 us (17%)
  other arithmetic  6.16 us (4%)
  local copies, waits for them, and re-layouts  2.76 us (2%)
    ppermute x27, waiting for transfers between devices, send(): return lax.ppermute(value, AXES, pairs)  50.8 us
    ppermute x27, starting transfers between devices, send(): return lax.ppermute(value, AXES, pairs)  39.8 us
    pallas_call x6, Pallas kernels, steps(): pl.pallas_call(functools.partial(step_kernel, counts, len(out_types)), gr...  30.8 us
    all_to_all x1, blocking collectives, on_device(): lax.all_to_all(outgoing, AXES, split_axis=1, concat_axis=0, tiled=True)  26.3 us
  transfers between devices with their start and end apart: 27, of which 11 were waited for; matrix products, arithmetic and copies ran while one was open for 4% of the time, Pallas kernels for 13%

profile of v2, /device:TPU:0, one launch (start us, length us, event | category | flops | bytes accessed | tf_op | source)
XLA Modules:
  0.0 157.3 jit_solution(8924950394949380461)
XLA Ops:
  1.9 26.3 %all_to_all.15 = bf16[8,32,1280]{2,0,1:T(8,128)(2,1)S(1)} all-to-all(bf16[8,32,1280]{2,0,1:T(8,128)(2,1)S(1)} %pad_maximum_fusion.2), channel_id=1, replica_groups=mesh['row'=4,'col'=8] {'row','col'}, dimensions={1} | all-to-all | bytes 1310720 | tf_op jit(solution)/shard_map/all_to_all | solution.py:205
  29.1 4.2 %collective-permute-done.refs_4_ = bf16[256,256]{1,0:T(8,128)(2,1)S(1)} collective-permute-done((bf16[256,256]{1,0:T(8,128)(2,1)S(1)}, bf16[256,256]{1,0:T(8,128)(2,1)S(1)}, u32[]{:S(2)}, u32[]{:S(2)}) %collective-permute-start) | collective-permute-done | bytes 131104 | tf_op jit(solution)/shard_map/ppermute | solution.py:105
  34.7 6.0 %collective-permute-done.1 = bf16[512,256]{1,0:T(8,128)(2,1)S(1)} collective-permute-done((bf16[512,256]{1,0:T(8,128)(2,1)S(1)}, bf16[512,256]{1,0:T(8,128)(2,1)S(1)}, u32[]{:S(2)}, u32[]{:S(2)}) %collective-permute-start.1) | collective-permute-done | bytes 262176 | tf_op jit(solution)/shard_map/ppermute | solution.py:105
  42.7 5.3 %shard_map.28 = (f32[1024,256]{1,0:T(8,128)S(1)}, bf16[1024,256]{1,0:T(8,128)(2,1)}) custom-call(s32[9]{0:T(128)S(1)} %stack.119.refs_0_, f32[1024,256]{1,0:T(8,128)S(1)} %convert_bitcast_fusion.refs_1_, bf16[1024,8192]{1,0:T(8,128)(2,1)} %refs_2_.11, bf16[256,256]{1,0:T(8,128)(2,1)S(1)} %bitcast.34, bf16[256,256]{1,0:T(8,128)(2,1)S(1)} %collective-permute-done.refs_4_, ...), custom_call_target="tpu_custom_call" | custom-call | flops 1073741824 | bytes 6291456 | tf_op jit(solution)/shard_map/pallas_call | solution.py:69
  52.9 4.5 %shard_map.29 = bf16[1024,256]{1,0:T(8,128)(2,1)S(1)} custom-call(s32[3]{0:T(128)S(1)} %add_add_fusion.refs_0_, f32[1024,256]{1,0:T(8,128)S(1)} %get-tuple-element.10.refs_1_, bf16[1024,8192]{1,0:T(8,128)(2,1)} %refs_2_.11, bf16[1024,256]{1,0:T(8,128)(2,1)S(1)} %collective-permute-done.4.refs_3_, bf16[1024,256]{1,0:T(8,128)(2,1)S(1)} %collective-permute-done.5.refs_4_), custom_call_target="tpu_custom_call" | custom-call | flops 1073741824 | bytes 6291456 | tf_op jit(solution)/shard_map/pallas_call | solution.py:69
  63.9 16.0 %collective-permute-done.7 = bf16[512,256]{1,0:T(8,128)(2,1)S(1)} collective-permute-done((bf16[512,256]{1,0:T(8,128)(2,1)}, bf16[512,256]{1,0:T(8,128)(2,1)S(1)}, u32[]{:S(2)}, u32[]{:S(2)}) %collective-permute-start.7) | collective-permute-done | bytes 262176 | tf_op jit(solution)/shard_map/ppermute | solution.py:105
  79.9 4.5 %shard_map.30.refs_1_ = f32[1024,256]{1,0:T(8,128)S(1)} custom-call(s32[3]{0:T(128)S(1)} %add_add_fusion.refs_0_, f32[1024,256]{1,0:T(8,128)S(1)} %get-tuple-element.10.refs_1_, bf16[1024,8192]{1,0:T(8,128)(2,1)} %refs_2_.11, bf16[1024,256]{1,0:T(8,128)(2,1)S(1)} %collective-permute-done.8.refs_3_, bf16[1024,256]{1,0:T(8,128)(2,1)S(1)} %collective-permute-done.9.refs_4_), custom_call_target="tpu_custom_call" | custom-call | flops 1073741824 | bytes 6291456 | tf_op jit(solution)/shard_map/pallas_call | solution.py:69
  84.4 4.7 %shard_map.31 = bf16[1024,256]{1,0:T(8,128)(2,1)S(1)} custom-call(s32[3]{0:T(128)S(1)} %add_add_fusion.1.refs_0_, f32[1024,256]{1,0:T(8,128)S(1)} %shard_map.30.refs_1_, bf16[1024,8192]{1,0:T(8,128)(2,1)} %refs_2_.11, bf16[1024,256]{1,0:T(8,128)(2,1)S(1)} %collective-permute-done.10.refs_3_, bf16[1024,256]{1,0:T(8,128)(2,1)} %collective-permute-done.11.refs_4_), custom_call_target="tpu_custom_call" | custom-call | flops 1073741824 | bytes 6291456 | tf_op jit(solution)/shard_map/pallas_call | solution.py:69
  89.1 3.3 %collective-permute-start.12 = (bf16[512,256]{1,0:T(8,128)(2,1)S(1)}, bf16[512,256]{1,0:T(8,128)(2,1)S(1)}, u32[]{:S(2)}, u32[]{:S(2)}) collective-permute-start(bf16[512,256]{1,0:T(8,128)(2,1)S(1)} %broadcast_select_fusion.8), channel_id=1, source_target_pairs={{1,0},{0,1},{3,2},{2,3},{5,4},{4,5},{7,6},{6,7},{17,16},{16,17},{1... | collective-permute-start | bytes 786440 | tf_op jit(solution)/shard_map/ppermute | solution.py:105
  94.5 2.9 %collective-permute-done.12 = bf16[512,256]{1,0:T(8,128)(2,1)S(1)} collective-permute-done((bf16[512,256]{1,0:T(8,128)(2,1)S(1)}, bf16[512,256]{1,0:T(8,128)(2,1)S(1)}, u32[]{:S(2)}, u32[]{:S(2)}) %collective-permute-start.12) | collective-permute-done | bytes 262176 | tf_op jit(solution)/shard_map/ppermute | solution.py:105
  97.4 1.9 %collective-permute-start.13 = (bf16[1024,256]{1,0:T(8,128)(2,1)S(1)}, bf16[1024,256]{1,0:T(8,128)(2,1)S(1)}, u32[]{:S(2)}, u32[]{:S(2)}) collective-permute-start(bf16[1024,256]{1,0:T(8,128)(2,1)S(1)} %pad_maximum_fusion.4), channel_id=1, source_target_pairs={{16,0},{17,1},{18,2},{19,3},{20,4},{21,5},{22,6},{23,7},{0,16},{1,... | collective-permute-start | bytes 1572872 | tf_op jit(solution)/shard_map/ppermute | solution.py:105
  100.1 7.2 %collective-permute-done.16 = bf16[512,256]{1,0:T(8,128)(2,1)S(1)} collective-permute-done((bf16[512,256]{1,0:T(8,128)(2,1)S(1)}, bf16[512,256]{1,0:T(8,128)(2,1)S(1)}, u32[]{:S(2)}, u32[]{:S(2)}) %collective-permute-start.16) | collective-permute-done | bytes 262176 | tf_op jit(solution)/shard_map/ppermute | solution.py:105
  110.0 2.5 %collective-permute-done.17 = bf16[512,256]{1,0:T(8,128)(2,1)S(1)} collective-permute-done((bf16[512,256]{1,0:T(8,128)(2,1)S(1)}, bf16[512,256]{1,0:T(8,128)(2,1)S(1)}, u32[]{:S(2)}, u32[]{:S(2)}) %collective-permute-start.17) | collective-permute-done | bytes 262176 | tf_op jit(solution)/shard_map/ppermute | solution.py:105
  112.5 2.5 %collective-permute-start.18 = (bf16[512,256]{1,0:T(8,128)(2,1)S(1)}, bf16[512,256]{1,0:T(8,128)(2,1)S(1)}, u32[]{:S(2)}, u32[]{:S(2)}) collective-permute-start(bf16[512,256]{1,0:T(8,128)(2,1)S(1)} %broadcast_select_fusion.5), channel_id=1, source_target_pairs={{1,0},{0,1},{3,2},{2,3},{5,4},{4,5},{7,6},{6,7},{17,16},{16,17},{1... | collective-permute-start | bytes 786440 | tf_op jit(solution)/shard_map/ppermute | solution.py:105
  115.1 2.3 %collective-permute-start.14 = (bf16[2048,256]{1,0:T(8,128)(2,1)S(1)}, bf16[2048,256]{1,0:T(8,128)(2,1)}, u32[]{:S(2)}, u32[]{:S(2)}) collective-permute-start(bf16[2048,256]{1,0:T(8,128)(2,1)S(1)} %constant_dynamic-update-slice_fusion), channel_id=1, source_target_pairs={{0,8},{1,9},{2,10},{3,11},{4,12},{5,13},{6,14},{7,15},{16,24},{17,... | collective-permute-start | bytes 3145736 | tf_op jit(solution)/shard_map/ppermute | solution.py:105
  117.4 5.2 %collective-permute-done.23 = bf16[512,256]{1,0:T(8,128)(2,1)S(1)} collective-permute-done((bf16[512,256]{1,0:T(8,128)(2,1)S(1)}, bf16[512,256]{1,0:T(8,128)(2,1)S(1)}, u32[]{:S(2)}, u32[]{:S(2)}) %collective-permute-start.23) | collective-permute-done | bytes 262176 | tf_op jit(solution)/shard_map/ppermute | solution.py:105
  122.6 2.5 %collective-permute-start.24 = (bf16[512,256]{1,0:T(8,128)(2,1)S(1)}, bf16[512,256]{1,0:T(8,128)(2,1)S(1)}, u32[]{:S(2)}, u32[]{:S(2)}) collective-permute-start(bf16[512,256]{1,0:T(8,128)(2,1)S(1)} %broadcast_select_fusion.7), channel_id=1, source_target_pairs={{1,0},{0,1},{3,2},{2,3},{5,4},{4,5},{7,6},{6,7},{17,16},{16,17},{1... | collective-permute-start | bytes 786440 | tf_op jit(solution)/shard_map/ppermute | solution.py:105
  125.2 3.9 %collective-permute-start.19 = (bf16[1024,256]{1,0:T(8,128)(2,1)S(1)}, bf16[1024,256]{1,0:T(8,128)(2,1)S(1)}, u32[]{:S(2)}, u32[]{:S(2)}) collective-permute-start(bf16[1024,256]{1,0:T(8,128)(2,1)S(1)} %pad_maximum_fusion.5), channel_id=1, source_target_pairs={{16,0},{17,1},{18,2},{19,3},{20,4},{21,5},{22,6},{23,7},{0,16},{1,... | collective-permute-start | bytes 1572872 | tf_op jit(solution)/shard_map/ppermute | solution.py:105
  129.2 1.8 %collective-permute-done.24 = bf16[512,256]{1,0:T(8,128)(2,1)S(1)} collective-permute-done((bf16[512,256]{1,0:T(8,128)(2,1)S(1)}, bf16[512,256]{1,0:T(8,128)(2,1)S(1)}, u32[]{:S(2)}, u32[]{:S(2)}) %collective-permute-start.24) | collective-permute-done | bytes 262176 | tf_op jit(solution)/shard_map/ppermute | solution.py:105
  131.7 3.9 %collective-permute-start.25 = (bf16[1024,256]{1,0:T(8,128)(2,1)}, bf16[1024,256]{1,0:T(8,128)(2,1)S(1)}, u32[]{:S(2)}, u32[]{:S(2)}) collective-permute-start(bf16[1024,256]{1,0:T(8,128)(2,1)} %pad_maximum_fusion.6), channel_id=1, source_target_pairs={{16,0},{17,1},{18,2},{19,3},{20,4},{21,5},{22,6},{23,7},{0,16},{1,... | collective-permute-start | bytes 1572872 | tf_op jit(solution)/shard_map/ppermute | solution.py:105
  137.3 2.3 %collective-permute-start.20 = (bf16[2048,256]{1,0:T(8,128)(2,1)}, bf16[2048,256]{1,0:T(8,128)(2,1)}, u32[]{:S(2)}, u32[]{:S(2)}) collective-permute-start(bf16[2048,256]{1,0:T(8,128)(2,1)} %pad_maximum_fusion), channel_id=1, source_target_pairs={{0,8},{1,9},{2,10},{3,11},{4,12},{5,13},{6,14},{7,15},{16,24},{17,... | collective-permute-start | bytes 3145736 | tf_op jit(solution)/shard_map/ppermute | solution.py:105
  139.8 3.2 %collective-permute-done.25 = bf16[1024,256]{1,0:T(8,128)(2,1)S(1)} collective-permute-done((bf16[1024,256]{1,0:T(8,128)(2,1)}, bf16[1024,256]{1,0:T(8,128)(2,1)S(1)}, u32[]{:S(2)}, u32[]{:S(2)}) %collective-permute-start.25) | collective-permute-done | bytes 524320 | tf_op jit(solution)/shard_map/ppermute | solution.py:105
  145.1 6.3 %shard_map.32.refs_1_ = f32[1024,256]{1,0:T(8,128)S(1)} custom-call(s32[10]{0:T(128)S(1)} %stack.108.refs_0_, f32[1024,256]{1,0:T(8,128)} %copy-done, bf16[1024,8192]{1,0:T(8,128)(2,1)} %refs_2_.11, bf16[1024,8192]{1,0:T(8,128)(2,1)} %refs_2_.11, bf16[512,256]{1,0:T(8,128)(2,1)S(1)} %get-tuple-element.26.refs_4_, ...), custom_call_target="tpu_custom_call" | custom-call | flops 2147483648 | bytes 10485760 | tf_op jit(solution)/shard_map/pallas_call | solution.py:69
  151.9 5.4 %shard_map.33 = f32[1024,256]{1,0:T(8,128)} custom-call(s32[5]{0:T(128)S(1)} %stack.103.refs_0_, f32[1024,256]{1,0:T(8,128)S(1)} %shard_map.32.refs_1_, bf16[1024,8192]{1,0:T(8,128)(2,1)} %refs_2_.11, bf16[512,256]{1,0:T(8,128)(2,1)S(1)} %get-tuple-element.18.refs_3_, bf16[512,256]{1,0:T(8,128)(2,1)S(1)} %get-tuple-element.17.refs_4_, ...), custom_call_target="tpu_custom_call" | custom-call | flops 1073741824 | bytes 6291456 | tf_op jit(solution)/shard_map/pallas_call | solution.py:69
  (83 shorter events, 28.0 us)
Async XLA Ops:
  28.3 5.0 %collective-permute-start = (bf16[256,256]{1,0:T(8,128)(2,1)S(1)}, bf16[256,256]{1,0:T(8,128)(2,1)S(1)}, u32[]{:S(2)}, u32[]{:S(2)}) collective-permute-start(bf16[256,256]{1,0:T(8,128)(2,1)S(1)} %bitcast.31), channel_id=1, source_target_pairs={{1,0},{0,1},{3,2},{2,3},{5,4},{4,5},{7,6},{6,7},{9,8},{8,9},{11,10... | collective-permute-start | bytes 393224 | tf_op jit(solution)/shard_map/ppermute | solution.py:105
  33.3 7.4 %collective-permute-start.1 = (bf16[512,256]{1,0:T(8,128)(2,1)S(1)}, bf16[512,256]{1,0:T(8,128)(2,1)S(1)}, u32[]{:S(2)}, u32[]{:S(2)}) collective-permute-start(bf16[512,256]{1,0:T(8,128)(2,1)S(1)} %pad_maximum_fusion.7), channel_id=1, source_target_pairs={{16,0},{17,1},{18,2},{19,3},{20,4},{21,5},{22,6},{23,7},{24,8},{25... | collective-permute-start | bytes 786440 | tf_op jit(solution)/shard_map/ppermute | solution.py:105
  48.1 3.1 %collective-permute-start.4 = (bf16[1024,256]{1,0:T(8,128)(2,1)}, bf16[1024,256]{1,0:T(8,128)(2,1)S(1)}, u32[]{:S(2)}, u32[]{:S(2)}) collective-permute-start(bf16[1024,256]{1,0:T(8,128)(2,1)} %get-tuple-element.11), channel_id=1, source_target_pairs={{2,4},{3,5}} | collective-permute-start | bytes 1572872 | tf_op jit(solution)/shard_map/ppermute | solution.py:105
  48.8 4.1 %collective-permute-start.5 = (bf16[1024,256]{1,0:T(8,128)(2,1)}, bf16[1024,256]{1,0:T(8,128)(2,1)S(1)}, u32[]{:S(2)}, u32[]{:S(2)}) collective-permute-start(bf16[1024,256]{1,0:T(8,128)(2,1)} %get-tuple-element.11), channel_id=1, source_target_pairs={{3,4},{2,5}} | collective-permute-start | bytes 1572872 | tf_op jit(solution)/shard_map/ppermute | solution.py:105
  51.2 6.9 %collective-permute-start.8 = (bf16[1024,256]{1,0:T(8,128)(2,1)S(1)}, bf16[1024,256]{1,0:T(8,128)(2,1)S(1)}, u32[]{:S(2)}, u32[]{:S(2)}) collective-permute-start(bf16[1024,256]{1,0:T(8,128)(2,1)S(1)} %collective-permute-done.4.refs_3_), channel_id=1, source_target_pairs={{4,6},{5,7}} | collective-permute-start | bytes 1572872 | tf_op jit(solution)/shard_map/ppermute | solution.py:105
  58.2 21.7 %collective-permute-start.9 = (bf16[1024,256]{1,0:T(8,128)(2,1)S(1)}, bf16[1024,256]{1,0:T(8,128)(2,1)S(1)}, u32[]{:S(2)}, u32[]{:S(2)}) collective-permute-start(bf16[1024,256]{1,0:T(8,128)(2,1)S(1)} %collective-permute-done.8.refs_3_), channel_id=1, source_target_pairs={{7,6},{6,7}} | collective-permute-start | bytes 1572872 | tf_op jit(solution)/shard_map/ppermute | solution.py:105
  59.6 20.2 %collective-permute-start.7 = (bf16[512,256]{1,0:T(8,128)(2,1)}, bf16[512,256]{1,0:T(8,128)(2,1)S(1)}, u32[]{:S(2)}, u32[]{:S(2)}) collective-permute-start(bf16[512,256]{1,0:T(8,128)(2,1)} %broadcast_select_fusion.6), channel_id=1, source_target_pairs={{2,0},{3,1},{18,16},{19,17},{6,4},{7,5},{22,20},{23,21}} | collective-permute-start | bytes 786440 | tf_op jit(solution)/shard_map/ppermute | solution.py:105
  60.9 23.5 %collective-permute-start.10 = (bf16[1024,256]{1,0:T(8,128)(2,1)S(1)}, bf16[1024,256]{1,0:T(8,128)(2,1)S(1)}, u32[]{:S(2)}, u32[]{:S(2)}) collective-permute-start(bf16[1024,256]{1,0:T(8,128)(2,1)S(1)} %shard_map.29), channel_id=1, source_target_pairs={{4,6},{5,7}} | collective-permute-start | bytes 1572872 | tf_op jit(solution)/shard_map/ppermute | solution.py:105
  61.6 22.8 %collective-permute-start.11 = (bf16[1024,256]{1,0:T(8,128)(2,1)S(1)}, bf16[1024,256]{1,0:T(8,128)(2,1)}, u32[]{:S(2)}, u32[]{:S(2)}) collective-permute-start(bf16[1024,256]{1,0:T(8,128)(2,1)S(1)} %shard_map.29), channel_id=1, source_target_pairs={{5,6},{4,7}} | collective-permute-start | bytes 1572872 | tf_op jit(solution)/shard_map/ppermute | solution.py:105
  63.2 30.0 %collective-permute-start.15 = (bf16[512,256]{1,0:T(8,128)(2,1)S(1)}, bf16[512,256]{1,0:T(8,128)(2,1)S(1)}, u32[]{:S(2)}, u32[]{:S(2)}) collective-permute-start(bf16[512,256]{1,0:T(8,128)(2,1)S(1)} %slice.120), channel_id=1, source_target_pairs={{4,20},{5,21}} | collective-permute-start | bytes 786440 | tf_op jit(solution)/shard_map/ppermute | solution.py:105
  89.1 8.3 %collective-permute-start.12 = (bf16[512,256]{1,0:T(8,128)(2,1)S(1)}, bf16[512,256]{1,0:T(8,128)(2,1)S(1)}, u32[]{:S(2)}, u32[]{:S(2)}) collective-permute-start(bf16[512,256]{1,0:T(8,128)(2,1)S(1)} %broadcast_select_fusion.8), channel_id=1, source_target_pairs={{1,0},{0,1},{3,2},{2,3},{5,4},{4,5},{7,6},{6,7},{17,16},{16,17},{1... | collective-permute-start | bytes 786440 | tf_op jit(solution)/shard_map/ppermute | solution.py:105
  92.5 6.9 %collective-permute-start.21 = (bf16[512,256]{1,0:T(8,128)(2,1)S(1)}, bf16[512,256]{1,0:T(8,128)(2,1)S(1)}, u32[]{:S(2)}, u32[]{:S(2)}) collective-permute-start(bf16[512,256]{1,0:T(8,128)(2,1)S(1)} %slice.126), channel_id=1, source_target_pairs={{6,22},{7,23}} | collective-permute-start | bytes 786440 | tf_op jit(solution)/shard_map/ppermute | solution.py:105
  93.2 14.1 %collective-permute-start.16 = (bf16[512,256]{1,0:T(8,128)(2,1)S(1)}, bf16[512,256]{1,0:T(8,128)(2,1)S(1)}, u32[]{:S(2)}, u32[]{:S(2)}) collective-permute-start(bf16[512,256]{1,0:T(8,128)(2,1)S(1)} %slice_select_fusion.1), channel_id=1, source_target_pairs={{4,0},{5,1},{20,16},{21,17}} | collective-permute-start | bytes 786440 | tf_op jit(solution)/shard_map/ppermute | solution.py:105
  97.4 17.6 %collective-permute-start.13 = (bf16[1024,256]{1,0:T(8,128)(2,1)S(1)}, bf16[1024,256]{1,0:T(8,128)(2,1)S(1)}, u32[]{:S(2)}, u32[]{:S(2)}) collective-permute-start(bf16[1024,256]{1,0:T(8,128)(2,1)S(1)} %pad_maximum_fusion.4), channel_id=1, source_target_pairs={{16,0},{17,1},{18,2},{19,3},{20,4},{21,5},{22,6},{23,7},{0,16},{1,... | collective-permute-start | bytes 1572872 | tf_op jit(solution)/shard_map/ppermute | solution.py:105
  99.4 9.2 %collective-permute-start.22 = (bf16[512,256]{1,0:T(8,128)(2,1)S(1)}, bf16[512,256]{1,0:T(8,128)(2,1)S(1)}, u32[]{:S(2)}, u32[]{:S(2)}) collective-permute-start(bf16[512,256]{1,0:T(8,128)(2,1)S(1)} %slice_select_fusion), channel_id=1, source_target_pairs={{6,2},{7,3},{22,18},{23,19}} | collective-permute-start | bytes 786440 | tf_op jit(solution)/shard_map/ppermute | solution.py:105
  107.3 5.2 %collective-permute-start.17 = (bf16[512,256]{1,0:T(8,128)(2,1)S(1)}, bf16[512,256]{1,0:T(8,128)(2,1)S(1)}, u32[]{:S(2)}, u32[]{:S(2)}) collective-permute-start(bf16[512,256]{1,0:T(8,128)(2,1)S(1)} %broadcast_select_fusion.4), channel_id=1, source_target_pairs={{4,6},{5,7},{20,22},{21,23},{0,2},{1,3},{16,18},{17,19}} | collective-permute-start | bytes 786440 | tf_op jit(solution)/shard_map/ppermute | solution.py:105
  108.7 13.9 %collective-permute-start.23 = (bf16[512,256]{1,0:T(8,128)(2,1)S(1)}, bf16[512,256]{1,0:T(8,128)(2,1)S(1)}, u32[]{:S(2)}, u32[]{:S(2)}) collective-permute-start(bf16[512,256]{1,0:T(8,128)(2,1)S(1)} %broadcast_select_fusion.3), channel_id=1, source_target_pairs={{6,4},{7,5},{22,20},{23,21},{2,0},{3,1},{18,16},{19,17}} | collective-permute-start | bytes 786440 | tf_op jit(solution)/shard_map/ppermute | solution.py:105
  112.5 12.7 %collective-permute-start.18 = (bf16[512,256]{1,0:T(8,128)(2,1)S(1)}, bf16[512,256]{1,0:T(8,128)(2,1)S(1)}, u32[]{:S(2)}, u32[]{:S(2)}) collective-permute-start(bf16[512,256]{1,0:T(8,128)(2,1)S(1)} %broadcast_select_fusion.5), channel_id=1, source_target_pairs={{1,0},{0,1},{3,2},{2,3},{5,4},{4,5},{7,6},{6,7},{17,16},{16,17},{1... | collective-permute-start | bytes 786440 | tf_op jit(solution)/shard_map/ppermute | solution.py:105
  115.1 29.3 %collective-permute-start.14 = (bf16[2048,256]{1,0:T(8,128)(2,1)S(1)}, bf16[2048,256]{1,0:T(8,128)(2,1)}, u32[]{:S(2)}, u32[]{:S(2)}) collective-permute-start(bf16[2048,256]{1,0:T(8,128)(2,1)S(1)} %constant_dynamic-update-slice_fusion), channel_id=1, source_target_pairs={{0,8},{1,9},{2,10},{3,11},{4,12},{5,13},{6,14},{7,15},{16,24},{17,... | collective-permute-start | bytes 3145736 | tf_op jit(solution)/shard_map/ppermute | solution.py:105
  122.6 8.3 %collective-permute-start.24 = (bf16[512,256]{1,0:T(8,128)(2,1)S(1)}, bf16[512,256]{1,0:T(8,128)(2,1)S(1)}, u32[]{:S(2)}, u32[]{:S(2)}) collective-permute-start(bf16[512,256]{1,0:T(8,128)(2,1)S(1)} %broadcast_select_fusion.7), channel_id=1, source_target_pairs={{1,0},{0,1},{3,2},{2,3},{5,4},{4,5},{7,6},{6,7},{17,16},{16,17},{1... | collective-permute-start | bytes 786440 | tf_op jit(solution)/shard_map/ppermute | solution.py:105
  125.2 11.1 %collective-permute-start.19 = (bf16[1024,256]{1,0:T(8,128)(2,1)S(1)}, bf16[1024,256]{1,0:T(8,128)(2,1)S(1)}, u32[]{:S(2)}, u32[]{:S(2)}) collective-permute-start(bf16[1024,256]{1,0:T(8,128)(2,1)S(1)} %pad_maximum_fusion.5), channel_id=1, source_target_pairs={{16,0},{17,1},{18,2},{19,3},{20,4},{21,5},{22,6},{23,7},{0,16},{1,... | collective-permute-start | bytes 1572872 | tf_op jit(solution)/shard_map/ppermute | solution.py:105
  131.7 11.3 %collective-permute-start.25 = (bf16[1024,256]{1,0:T(8,128)(2,1)}, bf16[1024,256]{1,0:T(8,128)(2,1)S(1)}, u32[]{:S(2)}, u32[]{:S(2)}) collective-permute-start(bf16[1024,256]{1,0:T(8,128)(2,1)} %pad_maximum_fusion.6), channel_id=1, source_target_pairs={{16,0},{17,1},{18,2},{19,3},{20,4},{21,5},{22,6},{23,7},{0,16},{1,... | collective-permute-start | bytes 1572872 | tf_op jit(solution)/shard_map/ppermute | solution.py:105
  137.3 7.4 %collective-permute-start.20 = (bf16[2048,256]{1,0:T(8,128)(2,1)}, bf16[2048,256]{1,0:T(8,128)(2,1)}, u32[]{:S(2)}, u32[]{:S(2)}) collective-permute-start(bf16[2048,256]{1,0:T(8,128)(2,1)} %pad_maximum_fusion), channel_id=1, source_target_pairs={{0,8},{1,9},{2,10},{3,11},{4,12},{5,13},{6,14},{7,15},{16,24},{17,... | collective-permute-start | bytes 3145736 | tf_op jit(solution)/shard_map/ppermute | solution.py:105
  143.1 8.4 %collective-permute-start.26 = (bf16[2048,256]{1,0:T(8,128)(2,1)S(1)}, bf16[2048,256]{1,0:T(8,128)(2,1)S(1)}, u32[]{:S(2)}, u32[]{:S(2)}) collective-permute-start(bf16[2048,256]{1,0:T(8,128)(2,1)S(1)} %pad_maximum_fusion.1), channel_id=1, source_target_pairs={{0,8},{1,9},{2,10},{3,11},{4,12},{5,13},{6,14},{7,15},{16,24},{17,... | collective-permute-start | bytes 3145736 | tf_op jit(solution)/shard_map/ppermute | solution.py:105
  (4 other events, 36.7 us)

commit v3 on v0

v3 whole, which is shorter than its diff:
```python
import functools

import jax
import jax.numpy as jnp
from jax import lax
from jax.experimental import pallas as pl
from jax.experimental.pallas import tpu as pltpu
from jax.sharding import PartitionSpec as P

NB = 2048
STEPS = 4
AXES = ("row", "col")
CORES = 2
TILE = 256
KERNEL_VMEM = 50 * 1024 * 1024


def after(value, *others):
    return lax.optimization_barrier((value, *others))[0]


def step_kernel(plan, tile, *refs):
    terms, n_arrays, outs = plan
    info, current, panels = refs[:3]
    arrays = refs[3 : 3 + n_arrays]
    results = refs[3 + n_arrays : 3 + n_arrays + len(outs)]
    current_here, result_here, panels_here, held, sems, piece_sems, out_sems = refs[3 + n_arrays + len(outs) :]
    rows = current.shape[0]
    tiles = rows // tile
    n_terms = len(terms)

    copies, started = [], 0
    for t, (_, _, pieces) in enumerate(terms):
        for array, twin, first, size, place in pieces:
            start = pl.multiple_of(info[place] * size, size)

            def copy(source):
                return pltpu.make_async_copy(
                    arrays[source].at[pl.ds(first, size), :],
                    held.at[t, pl.ds(start, size), :],
                    piece_sems.at[started],
                )

            if twin is None:
                copy(array).start()
            else:
                pl.when(info[0] == 0)(lambda: copy(array).start())
                pl.when(info[0] != 0)(lambda: copy(twin).start())
            copies.append(copy(array))
            started += 1

    def panel_copy(t, i):
        k = terms[t][0]
        return pltpu.make_async_copy(
            panels.at[pl.ds(i * tile, tile), pl.ds(k * NB, NB)],
            panels_here.at[t, pl.ds(i * tile, tile), :],
            sems.at[t, i],
        )

    def current_copy(i):
        at = pl.ds(i * tile, tile)
        return pltpu.make_async_copy(current.at[at, :], current_here.at[at, :], sems.at[n_terms, i])

    for i in range(tiles):
        for t in range(n_terms):
            panel_copy(t, i).start()
        current_copy(i).start()
    for copy in copies:
        copy.wait()
    sent = []
    for i in range(tiles):
        at = pl.ds(i * tile, tile)
        current_copy(i).wait()
        value = current_here[at, :]
        for t in range(n_terms):
            panel_copy(t, i).wait()
            product = jnp.dot(panels_here[t, at, :], held[t], preferred_element_type=jnp.float32)
            value = jnp.where(info[terms[t][1]] == 1, product, value - product)
        for o, (dtype, first, size, far) in enumerate(outs):
            low, high = max(first, i * tile), min(first + size, (i + 1) * tile)
            if low < high:
                part = value[low - i * tile : high - i * tile].astype(dtype)
                if far:
                    result_here[at, :] = part
                    out = pltpu.make_async_copy(result_here.at[at, :], results[o].at[at, :], out_sems.at[i])
                    out.start()
                    sent.append(out)
                else:
                    results[o][pl.ds(low - first, high - low), :] = part
    for out in sent:
        out.wait()


def steps(current, factor_panels, terms, my_block, core, outs):
    rows, scenarios = current.shape
    tile = min(TILE, rows)
    info, arrays, plan = [core], [], []

    def index(array):
        if array is None:
            return None
        for i, other in enumerate(arrays):
            if other is array:
                return i
        arrays.append(array)
        return len(arrays) - 1

    for k, pieces in terms:
        info.append(my_block == k)
        flag, listed = len(info) - 1, []
        for array, twin, first, size, place in pieces:
            info.append(place)
            listed.append((index(array), index(twin), first, size, len(info) - 1))
        plan.append((k, flag, tuple(listed)))
    info = jnp.stack([jnp.asarray(x, jnp.int32) for x in info])
    n_terms = len(terms)
    n_pieces = sum(len(pieces) for _, pieces in terms)
    far = any(out[3] for out in outs)
    anywhere = pl.BlockSpec(memory_space=pl.ANY)
    return pl.pallas_call(
        functools.partial(step_kernel, (tuple(plan), len(arrays), tuple(outs)), tile),
        in_specs=[pl.BlockSpec(memory_space=pltpu.SMEM), anywhere, pl.BlockSpec(memory_space=pltpu.HBM)]
        + [anywhere] * len(arrays),
        out_specs=[pl.BlockSpec(memory_space=pltpu.HBM if out[3] else pltpu.VMEM) for out in outs],
        out_shape=[jax.ShapeDtypeStruct((size, scenarios), dtype) for dtype, _, size, _ in outs],
        scratch_shapes=[
            pltpu.VMEM((rows, scenarios), jnp.float32),
            pltpu.VMEM((rows if far else 8, scenarios), jnp.float32),
            pltpu.VMEM((n_terms, rows, NB), jnp.bfloat16),
            pltpu.VMEM((n_terms, NB, scenarios), jnp.bfloat16),
            pltpu.SemaphoreType.DMA((n_terms + 1, rows // tile)),
            pltpu.SemaphoreType.DMA((n_pieces,)),
            pltpu.SemaphoreType.DMA((rows // tile,)),
        ],
        compiler_params=pltpu.CompilerParams(vmem_limit_bytes=KERNEL_VMEM),
        cost_estimate=pl.CostEstimate(
            flops=2 * rows * NB * scenarios * n_terms,
            bytes_accessed=2 * rows * NB * n_terms + 8 * rows * scenarios,
            transcendentals=0,
        ),
    )(info, current, factor_panels, *arrays)


def make_on_device(n_row, n_col):
    def on_device(rhs_scen, factor_panels):
        rows_here = factor_panels.shape[0]
        lanes = NB // rows_here
        planes = n_col // lanes
        n_y = n_row // CORES
        members = lanes * n_y * CORES
        row, col = lax.axis_index("row"), lax.axis_index("col")
        y, core = row // CORES, row % CORES
        plane, lane = col // lanes, col % lanes
        my_block = (row * n_col + col) // lanes

        def device(y, core, plane, lane):
            return (y * CORES + core) * n_col + plane * lanes + lane

        def send(value, pairs):
            return lax.ppermute(value, AXES, pairs)

        def lane_gather(value, cores, zs, ys=range(n_y)):
            out = [value]
            for d in range(1, lanes):
                pairs = [
                    (device(t, c, z, (m + d) % lanes), device(t, c, z, m))
                    for t in ys for c in cores for z in zs for m in range(lanes)
                ]
                out.append(send(value, pairs))
            return out

        def y_gather(value, cores):
            out = [value]
            for d in range(1, n_y):
                pairs = [
                    (device((t + d) % n_y, c, z, m), device(t, c, z, m))
                    for t in range(n_y) for c in cores for z in range(planes) for m in range(lanes)
                ]
                out.append(send(value, pairs))
            return out

        def ahead(own, k):
            return [
                send(own, [(device(0, 0, k, (m + d) % lanes), device(0, 0, k + 1, m)) for m in range(lanes)])
                for d in range(lanes)
            ]

        lane_places = [(lane + d) % lanes for d in range(lanes)]

        def scatter_y(cuts, sources):
            piece = cuts[0]
            for t in range(1, n_y):
                pairs = [(device(0, 0, k, m), device(t, 0, k, m)) for k in sources for m in range(lanes)]
                piece = jnp.where(y == t, send(cuts[t], pairs), piece)
            return piece

        def along_planes(piece, sources):
            got = []
            for d in range(1, planes):
                pairs = [
                    (device(t, 0, k, m), device(t, 0, (k + d) % planes, m))
                    for k in sources for t in range(n_y) for m in range(lanes)
                ]
                got.append(send(piece, pairs))
            out = []
            for k in sources:
                value = piece
                for d in range(1, planes):
                    value = jnp.where(plane == (k + d) % planes, got[d - 1], value)
                out.append(value)
            return out

        def core_send(value):
            return send(
                value,
                [
                    (device(t, 0, z, m), device(t, 1, z, m))
                    for t in range(n_y) for z in range(planes) for m in range(lanes)
                ],
            )

        tree_places = [
            ((lane + dm) % lanes) * n_y + (y + dy) % n_y for dy in range(n_y) for dm in range(lanes)
        ]

        extra = NB // members
        start_places = [
            (((lane + dm) % lanes) * n_y + (y + dy) % n_y) * CORES + (core + dc) % CORES
            for dc in range(CORES) for dy in range(n_y) for dm in range(lanes)
        ]
        first = rhs_scen[:, :NB].reshape(-1, lanes, n_y, CORES, extra).transpose(0, 2, 3, 1, 4)
        first = jnp.broadcast_to(
            first[:, :, :, None], (first.shape[0], n_y, CORES, planes, lanes, extra)
        ).reshape(first.shape[0], n_row * n_col, extra)
        outgoing = jnp.concatenate(
            [rhs_scen.reshape(rhs_scen.shape[0], n_row * n_col, rows_here), first], axis=2
        )
        regrouped = lax.all_to_all(outgoing, AXES, split_axis=1, concat_axis=0, tiled=True)
        regrouped = regrouped.reshape(-1, rows_here + extra)
        current = jnp.transpose(regrouped[:, :rows_here]).astype(jnp.float32)
        piece = jnp.transpose(regrouped[:, rows_here:])
        both = range(CORES)
        whole = jnp.concatenate(lane_gather(piece, both, range(planes)), axis=0)
        whole = jnp.concatenate(y_gather(whole, both), axis=0)
        other = send(
            whole,
            [
                (device(t, 1 - c, z, m), device(t, c, z, m))
                for t in range(n_y) for c in both for z in range(planes) for m in range(lanes)
            ],
        )
        per_core = members // CORES
        pieces = [
            (half, None, i * extra, extra, start_places[c * per_core + i])
            for c, half in enumerate([whole, other]) for i in range(per_core)
        ]

        def run(current, terms, outs):
            return steps(current, factor_panels, terms, my_block, core, outs)

        cut = rows_here // n_y
        f32_rows = (jnp.float32, 0, rows_here, False)
        own_rows = (jnp.bfloat16, 0, rows_here, False)
        own_cuts = [(jnp.bfloat16, t * cut, cut, False) for t in range(n_y)]

        def lane_pieces(parts):
            return [(part, None, 0, rows_here, lane_places[d]) for d, part in enumerate(parts)]

        def gather_plane(value):
            mine = jnp.concatenate(lane_gather(value, [0], range(planes)), axis=0)
            far = y_gather(mine, [0])
            return [(part, core_send(part)) for part in far]

        def tree_pieces(arrays, first, size, stride):
            return [
                (mine, other, m * stride + first, size, tree_places[i * lanes + m])
                for i, (mine, other) in enumerate(arrays) for m in range(lanes)
            ]

        current, own1, *cuts1 = run(current, [(0, pieces)], [f32_rows, own_rows, *own_cuts])

        hop1 = ahead(own1, 1)
        near = jnp.where(plane == 2, after(hop1[0], *hop1[1:]), own1)
        pairs = [(device(0, 0, a, m), device(0, 0, b, m)) for a, b in ((2, 3), (1, 0)) for m in range(lanes)]
        passed = send(near, pairs)
        own2, *cuts2 = run(current, [(1, lane_pieces(hop1))], [own_rows, *own_cuts])
        passed = after(passed, own2)
        near = jnp.where((plane == 1) | (plane == 2), near, passed)
        hop2 = ahead(own2, 2)
        served = STEPS
        while served < planes:
            pairs = [
                (device(0, 0, z, m), device(0, 0, z + served, m))
                for z in range(min(served, planes - served)) for m in range(lanes)
            ]
            near = jnp.where((plane >= served) & (plane < 2 * served), send(near, pairs), near)
            served *= 2
        across = lane_gather(near, [0], [z for z in range(planes) if z != 2], [0])
        (chained,) = run(current, [(1, lane_pieces([passed, *across[1:]]))], [f32_rows])
        cuts3 = run(chained, [(2, lane_pieces(hop2))], own_cuts)

        near1 = after(near, own2)
        low1 = [near1] + [jnp.where(plane == 2, a, b) for a, b in zip(hop1[1:], across[1:])]
        for t in range(1, n_y):
            pairs = [(device(0, 0, z, m), device(t, 0, z, m)) for z in range(planes) for m in range(lanes)]
            near1 = jnp.where(y == t, send(near1, pairs), near1)
        high1 = lane_gather(near1, [0], range(planes), range(1, n_y))
        all1 = jnp.concatenate([jnp.where(y == 0, a, b) for a, b in zip(low1, high1)], axis=0)
        other1 = core_send(all1)

        cuts23 = [jnp.where(plane == 2, a, b) for a, b in zip(cuts2, cuts3)]
        piece23 = scatter_y(cuts23, [2, 3])
        piece23 = jnp.concatenate(along_planes(piece23, [2, 3]), axis=0)
        all23 = gather_plane(piece23)
        pieces1 = [(all1, other1, d * rows_here, rows_here, lane_places[d]) for d in range(lanes)]
        (current,) = run(current, [(1, pieces1)], [f32_rows])
        (out,) = run(
            current,
            [(2, tree_pieces(all23, 0, cut, 2 * cut)), (3, tree_pieces(all23, cut, cut, 2 * cut))],
            [(jnp.float32, 0, rows_here, True)],
        )
        return out

    return on_device


def solution(mesh):
    placed = (P(AXES, None), P(AXES, None))
    on_device = make_on_device(mesh.shape["row"], mesh.shape["col"])
    return jax.shard_map(
        on_device, mesh=mesh, in_specs=placed, out_specs=P(AXES, None), check_vma=False
    )
```

time: 579 us -> 169 us (0.29)
  waiting for transfers between devices: 532 us -> 64.6 us
  Pallas kernels: 0 us -> 35.8 us
  blocking collectives: 0 us -> 26.3 us
  starting transfers between devices: 7.46 us -> 31.7 us
  matrix products: 23.5 us -> 0 us
  between operations: 13.2 us -> 0.7 us
  other arithmetic: 1.08 us -> 7.6 us
    psum x4 -> x0, waiting for transfers between devices: 516 us -> none  [broadcast(): return lax.psum(kept, axis)]
    ppermute x0 -> x20, waiting for transfers between devices: none -> 64.6 us  [send(): return lax.ppermute(value, AXES, pairs)]
    pallas_call x0 -> x6, Pallas kernels: none -> 35.8 us  [steps(): pl.pallas_call(functools.partial(step_kernel, (tuple(plan), len(arrays),...]
    ppermute x0 -> x20, starting transfers between devices: none -> 31.7 us  [send(): return lax.ppermute(value, AXES, pairs)]
    all_to_all x0 -> x1, blocking collectives: none -> 26.3 us  [on_device(): lax.all_to_all(outgoing, AXES, split_axis=1, concat_axis=0, tiled=True)]
    dot_general x8 -> x0, matrix products: 23.5 us -> none  [on_device(): jnp.dot(panel_cols, received, preferred_element_type=jnp.float32)]
    all_to_all x1 -> x0, waiting for transfers between devices: 16.3 us -> none  [on_device(): lax.all_to_all(rhs_scen, ('row', 'col'), split_axis=1, concat_axis=0, til...]
    all_to_all x1 -> x0, starting transfers between devices: 7.3 us -> none  [on_device(): lax.all_to_all(rhs_scen, ('row', 'col'), split_axis=1, concat_axis=0, til...]
  transfers between devices with their start and end apart: 5 -> 20, of which waited for: 5 -> 8; matrix products, arithmetic and copies ran while one was open for 0% -> 3% of each run, Pallas kernels for 0% -> 9%
where the time goes in v3:
time: 169 us
  waiting for transfers between devices  64.6 us (38%)
  Pallas kernels  35.8 us (21%)
  starting transfers between devices  31.7 us (19%)
  blocking collectives  26.3 us (16%)
  other arithmetic  7.6 us (4%)
  local copies, waits for them, and re-layouts  2.02 us (1%)
    ppermute x20, waiting for transfers between devices, send(): return lax.ppermute(value, AXES, pairs)  64.6 us
    pallas_call x6, Pallas kernels, steps(): pl.pallas_call(functools.partial(step_kernel, (tuple(plan), len(arrays),...  35.8 us
    ppermute x20, starting transfers between devices, send(): return lax.ppermute(value, AXES, pairs)  31.7 us
    all_to_all x1, blocking collectives, on_device(): lax.all_to_all(outgoing, AXES, split_axis=1, concat_axis=0, tiled=True)  26.3 us
  transfers between devices with their start and end apart: 20, of which 8 were waited for; matrix products, arithmetic and copies ran while one was open for 3% of the time, Pallas kernels for 9%

profile of v3, /device:TPU:0, one launch (start us, length us, event | category | flops | bytes accessed | tf_op | source)
XLA Modules:
  0.0 168.6 jit_solution(3974882826968862375)
XLA Ops:
  1.9 26.3 %all_to_all.15 = bf16[8,32,1280]{2,0,1:T(8,128)(2,1)S(1)} all-to-all(bf16[8,32,1280]{2,0,1:T(8,128)(2,1)S(1)} %pad_maximum_fusion.2), channel_id=1, replica_groups=mesh['row'=4,'col'=8] {'row','col'}, dimensions={1} | all-to-all | bytes 1310720 | tf_op jit(solution)/shard_map/all_to_all | solution.py:238
  29.1 4.2 %collective-permute-done = bf16[256,256]{1,0:T(8,128)(2,1)S(1)} collective-permute-done((bf16[256,256]{1,0:T(8,128)(2,1)S(1)}, bf16[256,256]{1,0:T(8,128)(2,1)S(1)}, u32[]{:S(2)}, u32[]{:S(2)}) %collective-permute-start) | collective-permute-done | bytes 131104 | tf_op jit(solution)/shard_map/ppermute | solution.py:160
  33.3 1.4 collective-permute-start.1
  34.7 6.0 %collective-permute-done.1 = bf16[512,256]{1,0:T(8,128)(2,1)S(1)} collective-permute-done((bf16[512,256]{1,0:T(8,128)(2,1)S(1)}, bf16[512,256]{1,0:T(8,128)(2,1)S(1)}, u32[]{:S(2)}, u32[]{:S(2)}) %collective-permute-start.1) | collective-permute-done | bytes 262176 | tf_op jit(solution)/shard_map/ppermute | solution.py:160
  42.7 6.9 %shard_map.28 = (f32[1024,256]{1,0:T(8,128)S(1)}, bf16[1024,256]{1,0:T(8,128)(2,1)S(1)}, bf16[512,256]{1,0:T(8,128)(2,1)}, bf16[512,256]{1,0:T(8,128)(2,1)}) custom-call(s32[10]{0:T(128)S(1)} %stack.126.refs_0_, f32[1024,256]{1,0:T(8,128)} %convert_bitcast_fusion.refs_1_, bf16[1024,8192]{1,0:T(8,128)(2,1)} %refs_2_.11, ...), custom_call_target="tpu_custom_call" | custom-call | flops 1073741824 | bytes 6291456 | tf_op jit(solution)/shard_map/pallas_call | solution.py:120
  53.3 5.6 %shard_map.29 = (bf16[1024,256]{1,0:T(8,128)(2,1)}, bf16[512,256]{1,0:T(8,128)(2,1)S(1)}, bf16[512,256]{1,0:T(8,128)(2,1)S(1)}) custom-call(s32[4]{0:T(128)S(1)} %add_add_fusion.refs_0_, f32[1024,256]{1,0:T(8,128)S(1)} %get-tuple-element.15.refs_1_, bf16[1024,8192]{1,0:T(8,128)(2,1)} %refs_2_.11, bf16[1024,256]{1,0:T(8,128)(2,1)S(1)} %collective-permute-done.3.refs_3_, ...), custom_call_target="tpu_custom_call" | custom-call | flops 1073741824 | bytes 6291456 | tf_op jit(solution)/shard_map/pallas_call | solution.py:120
  59.5 14.7 %collective-permute-done.5.refs_3_ = bf16[1024,256]{1,0:T(8,128)(2,1)S(1)} collective-permute-done((bf16[1024,256]{1,0:T(8,128)(2,1)}, bf16[1024,256]{1,0:T(8,128)(2,1)S(1)}, u32[]{:S(2)}, u32[]{:S(2)}) %collective-permute-start.5) | collective-permute-done | bytes 524320 | tf_op jit(solution)/shard_map/ppermute | solution.py:160
  75.1 3.3 %collective-permute-start.7 = (bf16[1024,256]{1,0:T(8,128)(2,1)}, bf16[1024,256]{1,0:T(8,128)(2,1)S(1)}, u32[]{:S(2)}, u32[]{:S(2)}) collective-permute-start(bf16[1024,256]{1,0:T(8,128)(2,1)} %broadcast_select_fusion.2), channel_id=1, source_target_pairs={{1,0},{0,1},{3,2},{2,3},{7,6},{6,7}} | collective-permute-start | bytes 1572872 | tf_op jit(solution)/shard_map/ppermute | solution.py:160
  79.1 1.5 collective-permute-start.11
  80.6 5.7 %collective-permute-done.7.refs_4_ = bf16[1024,256]{1,0:T(8,128)(2,1)S(1)} collective-permute-done((bf16[1024,256]{1,0:T(8,128)(2,1)}, bf16[1024,256]{1,0:T(8,128)(2,1)S(1)}, u32[]{:S(2)}, u32[]{:S(2)}) %collective-permute-start.7) | collective-permute-done | bytes 524320 | tf_op jit(solution)/shard_map/ppermute | solution.py:160
  86.3 4.8 %shard_map.31.refs_1_ = f32[1024,256]{1,0:T(8,128)S(1)} custom-call(s32[4]{0:T(128)S(1)} %add_add_fusion.refs_0_, f32[1024,256]{1,0:T(8,128)S(1)} %get-tuple-element.15.refs_1_, bf16[1024,8192]{1,0:T(8,128)(2,1)} %refs_2_.11, bf16[1024,256]{1,0:T(8,128)(2,1)S(1)} %collective-permute-done.5.refs_3_, bf16[1024,256]{1,0:T(8,128)(2,1)S(1)} %collective-permute-done.7.refs_4_), custom_call_target="tpu_custom_call" | custom-call | flops 1073741824 | bytes 6291456 | tf_op jit(solution)/shard_map/pallas_call | solution.py:120
  91.2 4.9 %shard_map.32 = (bf16[512,256]{1,0:T(8,128)(2,1)S(1)}, bf16[512,256]{1,0:T(8,128)(2,1)S(1)}) custom-call(s32[4]{0:T(128)S(1)} %add_add_fusion.1.refs_0_, f32[1024,256]{1,0:T(8,128)S(1)} %shard_map.31.refs_1_, bf16[1024,8192]{1,0:T(8,128)(2,1)} %refs_2_.11, bf16[1024,256]{1,0:T(8,128)(2,1)S(1)} %collective-permute-done.10.refs_3_, ...), custom_call_target="tpu_custom_call" | custom-call | flops 1073741824 | bytes 6291456 | tf_op jit(solution)/shard_map/pallas_call | solution.py:120
  97.5 1.3 collective-permute-start.14
  100.2 2.1 %collective-permute-start.6 = (bf16[1024,256]{1,0:T(8,128)(2,1)}, bf16[1024,256]{1,0:T(8,128)(2,1)}, u32[]{:S(2)}, u32[]{:S(2)}) collective-permute-start(bf16[1024,256]{1,0:T(8,128)(2,1)} %broadcast_select_fusion.2), channel_id=1, source_target_pairs={{0,16},{1,17},{2,18},{3,19},{4,20},{5,21},{6,22},{7,23}} | collective-permute-start | bytes 1572872 | tf_op jit(solution)/shard_map/ppermute | solution.py:160
  102.3 19.5 %collective-permute-done.14 = bf16[512,256]{1,0:T(8,128)(2,1)S(1)} collective-permute-done((bf16[512,256]{1,0:T(8,128)(2,1)S(1)}, bf16[512,256]{1,0:T(8,128)(2,1)S(1)}, u32[]{:S(2)}, u32[]{:S(2)}) %collective-permute-start.14) | collective-permute-done | bytes 262176 | tf_op jit(solution)/shard_map/ppermute | solution.py:160
  122.8 3.3 %collective-permute-start.16 = (bf16[1024,256]{1,0:T(8,128)(2,1)S(1)}, bf16[1024,256]{1,0:T(8,128)(2,1)}, u32[]{:S(2)}, u32[]{:S(2)}) collective-permute-start(bf16[1024,256]{1,0:T(8,128)(2,1)S(1)} %pad_maximum_fusion.4), channel_id=1, source_target_pairs={{1,0},{0,1},{3,2},{2,3},{5,4},{4,5},{7,6},{6,7},{17,16},{16,17},{1... | collective-permute-start | bytes 1572872 | tf_op jit(solution)/shard_map/ppermute | solution.py:160
  128.0 6.0 %collective-permute-done.16 = bf16[1024,256]{1,0:T(8,128)(2,1)} collective-permute-done((bf16[1024,256]{1,0:T(8,128)(2,1)S(1)}, bf16[1024,256]{1,0:T(8,128)(2,1)}, u32[]{:S(2)}, u32[]{:S(2)}) %collective-permute-start.16) | collective-permute-done | bytes 524320 | tf_op jit(solution)/shard_map/ppermute | solution.py:160
  135.2 4.4 %collective-permute-start.18 = (bf16[2048,256]{1,0:T(8,128)(2,1)S(1)}, bf16[2048,256]{1,0:T(8,128)(2,1)}, u32[]{:S(2)}, u32[]{:S(2)}) collective-permute-start(bf16[2048,256]{1,0:T(8,128)(2,1)S(1)} %pad_maximum_fusion.1.refs_3_), channel_id=1, source_target_pairs={{16,0},{17,1},{18,2},{19,3},{20,4},{21,5},{22,6},{23,7},{0,16},{1,... | collective-permute-start | bytes 3145736 | tf_op jit(solution)/shard_map/ppermute | solution.py:160
  139.7 2.3 %collective-permute-start.9 = (bf16[2048,256]{1,0:T(8,128)(2,1)S(1)}, bf16[2048,256]{1,0:T(8,128)(2,1)}, u32[]{:S(2)}, u32[]{:S(2)}) collective-permute-start(bf16[2048,256]{1,0:T(8,128)(2,1)S(1)} %pad_maximum_fusion.refs_3_), channel_id=1, source_target_pairs={{0,8},{1,9},{2,10},{3,11},{4,12},{5,13},{6,14},{7,15},{16,24},{17,... | collective-permute-start | bytes 3145736 | tf_op jit(solution)/shard_map/ppermute | solution.py:160
  142.0 2.2 %collective-permute-start.17 = (bf16[2048,256]{1,0:T(8,128)(2,1)S(1)}, bf16[2048,256]{1,0:T(8,128)(2,1)}, u32[]{:S(2)}, u32[]{:S(2)}) collective-permute-start(bf16[2048,256]{1,0:T(8,128)(2,1)S(1)} %pad_maximum_fusion.1.refs_3_), channel_id=1, source_target_pairs={{0,8},{1,9},{2,10},{3,11},{4,12},{5,13},{6,14},{7,15},{16,24},{17,... | collective-permute-start | bytes 3145736 | tf_op jit(solution)/shard_map/ppermute | solution.py:160
  144.2 8.2 %collective-permute-done.18.refs_5_ = bf16[2048,256]{1,0:T(8,128)(2,1)} collective-permute-done((bf16[2048,256]{1,0:T(8,128)(2,1)S(1)}, bf16[2048,256]{1,0:T(8,128)(2,1)}, u32[]{:S(2)}, u32[]{:S(2)}) %collective-permute-start.18) | collective-permute-done | bytes 1048608 | tf_op jit(solution)/shard_map/ppermute | solution.py:160
  152.4 2.3 %collective-permute-start.19 = (bf16[2048,256]{1,0:T(8,128)(2,1)}, bf16[2048,256]{1,0:T(8,128)(2,1)}, u32[]{:S(2)}, u32[]{:S(2)}) collective-permute-start(bf16[2048,256]{1,0:T(8,128)(2,1)} %collective-permute-done.18.refs_5_), channel_id=1, source_target_pairs={{0,8},{1,9},{2,10},{3,11},{4,12},{5,13},{6,14},{7,15},{16,24},{17,... | collective-permute-start | bytes 3145736 | tf_op jit(solution)/shard_map/ppermute | solution.py:160
  154.8 5.0 %shard_map.30.refs_1_ = f32[1024,256]{1,0:T(8,128)S(1)} custom-call(s32[4]{0:T(128)S(1)} %add_add_fusion.refs_0_, f32[1024,256]{1,0:T(8,128)S(1)} %get-tuple-element.15.refs_1_, bf16[1024,8192]{1,0:T(8,128)(2,1)} %refs_2_.11, bf16[2048,256]{1,0:T(8,128)(2,1)S(1)} %pad_maximum_fusion.refs_3_, bf16[2048,256]{1,0:T(8,128)(2,1)} %collective-permute-done.9.refs_4_), custom_call_target="tpu_custom_call" | custom-call | flops 1073741824 | bytes 6291456 | tf_op jit(solution)/shard_map/pallas_call | solution.py:120
  159.8 8.6 %shard_map.33 = f32[1024,256]{1,0:T(8,128)} custom-call(s32[11]{0:T(128)S(1)} %stack.110.refs_0_, f32[1024,256]{1,0:T(8,128)S(1)} %shard_map.30.refs_1_, bf16[1024,8192]{1,0:T(8,128)(2,1)} %refs_2_.11, bf16[2048,256]{1,0:T(8,128)(2,1)S(1)} %pad_maximum_fusion.1.refs_3_, bf16[2048,256]{1,0:T(8,128)(2,1)} %collective-permute-done.17.refs_4_, ...), custom_call_target="tpu_custom_call" | custom-call | flops 2147483648 | bytes 10485760 | tf_op jit(solution)/shard_map/pallas_call | solution.py:120
  (54 shorter events, 17.6 us)
Async XLA Ops:
  28.3 5.0 %collective-permute-start = (bf16[256,256]{1,0:T(8,128)(2,1)S(1)}, bf16[256,256]{1,0:T(8,128)(2,1)S(1)}, u32[]{:S(2)}, u32[]{:S(2)}) collective-permute-start(bf16[256,256]{1,0:T(8,128)(2,1)S(1)} %bitcast.34), channel_id=1, source_target_pairs={{1,0},{0,1},{3,2},{2,3},{5,4},{4,5},{7,6},{6,7},{9,8},{8,9},{11,10... | collective-permute-start | bytes 393224 | tf_op jit(solution)/shard_map/ppermute | solution.py:160
  33.3 7.4 %collective-permute-start.1 = (bf16[512,256]{1,0:T(8,128)(2,1)S(1)}, bf16[512,256]{1,0:T(8,128)(2,1)S(1)}, u32[]{:S(2)}, u32[]{:S(2)}) collective-permute-start(bf16[512,256]{1,0:T(8,128)(2,1)S(1)} %pad_maximum_fusion.5), channel_id=1, source_target_pairs={{16,0},{17,1},{18,2},{19,3},{20,4},{21,5},{22,6},{23,7},{24,8},{25... | collective-permute-start | bytes 786440 | tf_op jit(solution)/shard_map/ppermute | solution.py:160
  40.7 2.0 %collective-permute-start.2 = (bf16[1024,256]{1,0:T(8,128)(2,1)S(1)}, bf16[1024,256]{1,0:T(8,128)(2,1)S(1)}, u32[]{:S(2)}, u32[]{:S(2)}) collective-permute-start(bf16[1024,256]{1,0:T(8,128)(2,1)S(1)} %pad_maximum_fusion.3.refs_3_), channel_id=1, source_target_pairs={{8,0},{9,1},{10,2},{11,3},{12,4},{13,5},{14,6},{15,7},{0,8},{1,9},... | collective-permute-start | bytes 1572872 | tf_op jit(solution)/shard_map/ppermute | solution.py:160
  49.6 1.4 collective-permute-start.3
  50.3 0.7 collective-permute-start.4
  51.9 22.3 %collective-permute-start.5 = (bf16[1024,256]{1,0:T(8,128)(2,1)}, bf16[1024,256]{1,0:T(8,128)(2,1)S(1)}, u32[]{:S(2)}, u32[]{:S(2)}) collective-permute-start(bf16[1024,256]{1,0:T(8,128)(2,1)} %broadcast_select_fusion.1), channel_id=1, source_target_pairs={{4,6},{5,7},{2,0},{3,1}} | collective-permute-start | bytes 1572872 | tf_op jit(solution)/shard_map/ppermute | solution.py:160
  58.9 0.7 copy-start
  75.1 11.3 %collective-permute-start.7 = (bf16[1024,256]{1,0:T(8,128)(2,1)}, bf16[1024,256]{1,0:T(8,128)(2,1)S(1)}, u32[]{:S(2)}, u32[]{:S(2)}) collective-permute-start(bf16[1024,256]{1,0:T(8,128)(2,1)} %broadcast_select_fusion.2), channel_id=1, source_target_pairs={{1,0},{0,1},{3,2},{2,3},{7,6},{6,7}} | collective-permute-start | bytes 1572872 | tf_op jit(solution)/shard_map/ppermute | solution.py:160
  78.4 12.8 %collective-permute-start.10 = (bf16[1024,256]{1,0:T(8,128)(2,1)}, bf16[1024,256]{1,0:T(8,128)(2,1)S(1)}, u32[]{:S(2)}, u32[]{:S(2)}) collective-permute-start(bf16[1024,256]{1,0:T(8,128)(2,1)} %get-tuple-element.18), channel_id=1, source_target_pairs={{4,6},{5,7}} | collective-permute-start | bytes 1572872 | tf_op jit(solution)/shard_map/ppermute | solution.py:160
  79.1 12.1 %collective-permute-start.11 = (bf16[1024,256]{1,0:T(8,128)(2,1)}, bf16[1024,256]{1,0:T(8,128)(2,1)}, u32[]{:S(2)}, u32[]{:S(2)}) collective-permute-start(bf16[1024,256]{1,0:T(8,128)(2,1)} %get-tuple-element.18), channel_id=1, source_target_pairs={{5,6},{4,7}} | collective-permute-start | bytes 1572872 | tf_op jit(solution)/shard_map/ppermute | solution.py:160
  91.1 4.9 %copy-start.1 = (bf16[512,256]{1,0:T(8,128)(2,1)S(1)}, bf16[512,256]{1,0:T(8,128)(2,1)}, u32[]{:S(2)}) copy-start(bf16[512,256]{1,0:T(8,128)(2,1)} %copy-done) | copy-start | bytes 786436
  96.1 0.7 collective-permute-start.12
  96.9 5.4 %collective-permute-start.13 = (bf16[512,256]{1,0:T(8,128)(2,1)S(1)}, bf16[512,256]{1,0:T(8,128)(2,1)S(1)}, u32[]{:S(2)}, u32[]{:S(2)}) collective-permute-start(bf16[512,256]{1,0:T(8,128)(2,1)S(1)} %select_select_fusion.3), channel_id=1, source_target_pairs={{4,2},{5,3},{20,18},{21,19},{6,4},{7,5},{22,20},{23,21}} | collective-permute-start | bytes 786440 | tf_op jit(solution)/shard_map/ppermute | solution.py:160
  97.5 24.2 %collective-permute-start.14 = (bf16[512,256]{1,0:T(8,128)(2,1)S(1)}, bf16[512,256]{1,0:T(8,128)(2,1)S(1)}, u32[]{:S(2)}, u32[]{:S(2)}) collective-permute-start(bf16[512,256]{1,0:T(8,128)(2,1)S(1)} %select_select_fusion.3), channel_id=1, source_target_pairs={{4,0},{5,1},{20,16},{21,17},{6,2},{7,3},{22,18},{23,19}} | collective-permute-start | bytes 786440 | tf_op jit(solution)/shard_map/ppermute | solution.py:160
  98.8 22.9 %collective-permute-start.15 = (bf16[512,256]{1,0:T(8,128)(2,1)S(1)}, bf16[512,256]{1,0:T(8,128)(2,1)}, u32[]{:S(2)}, u32[]{:S(2)}) collective-permute-start(bf16[512,256]{1,0:T(8,128)(2,1)S(1)} %select_select_fusion.3), channel_id=1, source_target_pairs={{4,6},{5,7},{20,22},{21,23},{6,0},{7,1},{22,16},{23,17}} | collective-permute-start | bytes 786440 | tf_op jit(solution)/shard_map/ppermute | solution.py:160
  100.2 26.0 %collective-permute-start.6 = (bf16[1024,256]{1,0:T(8,128)(2,1)}, bf16[1024,256]{1,0:T(8,128)(2,1)}, u32[]{:S(2)}, u32[]{:S(2)}) collective-permute-start(bf16[1024,256]{1,0:T(8,128)(2,1)} %broadcast_select_fusion.2), channel_id=1, source_target_pairs={{0,16},{1,17},{2,18},{3,19},{4,20},{5,21},{6,22},{7,23}} | collective-permute-start | bytes 1572872 | tf_op jit(solution)/shard_map/ppermute | solution.py:160
  122.8 5.2 %copy-start.2 = (bf16[512,256]{1,0:T(8,128)(2,1)}, bf16[512,256]{1,0:T(8,128)(2,1)S(1)}, u32[]{:S(2)}) copy-start(bf16[512,256]{1,0:T(8,128)(2,1)S(1)} %get-tuple-element.28) | copy-start | bytes 786436
  122.8 11.2 %collective-permute-start.16 = (bf16[1024,256]{1,0:T(8,128)(2,1)S(1)}, bf16[1024,256]{1,0:T(8,128)(2,1)}, u32[]{:S(2)}, u32[]{:S(2)}) collective-permute-start(bf16[1024,256]{1,0:T(8,128)(2,1)S(1)} %pad_maximum_fusion.4), channel_id=1, source_target_pairs={{1,0},{0,1},{3,2},{2,3},{5,4},{4,5},{7,6},{6,7},{17,16},{16,17},{1... | collective-permute-start | bytes 1572872 | tf_op jit(solution)/shard_map/ppermute | solution.py:160
  127.3 12.3 %collective-permute-start.8 = (bf16[1024,256]{1,0:T(8,128)(2,1)S(1)}, bf16[1024,256]{1,0:T(8,128)(2,1)S(1)}, u32[]{:S(2)}, u32[]{:S(2)}) collective-permute-start(bf16[1024,256]{1,0:T(8,128)(2,1)S(1)} %get-tuple-element.26), channel_id=1, source_target_pairs={{17,16},{16,17},{19,18},{18,19},{21,20},{20,21},{23,22},{22,23}} | collective-permute-start | bytes 1572872 | tf_op jit(solution)/shard_map/ppermute | solution.py:160
  135.2 17.3 %collective-permute-start.18 = (bf16[2048,256]{1,0:T(8,128)(2,1)S(1)}, bf16[2048,256]{1,0:T(8,128)(2,1)}, u32[]{:S(2)}, u32[]{:S(2)}) collective-permute-start(bf16[2048,256]{1,0:T(8,128)(2,1)S(1)} %pad_maximum_fusion.1.refs_3_), channel_id=1, source_target_pairs={{16,0},{17,1},{18,2},{19,3},{20,4},{21,5},{22,6},{23,7},{0,16},{1,... | collective-permute-start | bytes 3145736 | tf_op jit(solution)/shard_map/ppermute | solution.py:160
  139.7 15.1 %collective-permute-start.9 = (bf16[2048,256]{1,0:T(8,128)(2,1)S(1)}, bf16[2048,256]{1,0:T(8,128)(2,1)}, u32[]{:S(2)}, u32[]{:S(2)}) collective-permute-start(bf16[2048,256]{1,0:T(8,128)(2,1)S(1)} %pad_maximum_fusion.refs_3_), channel_id=1, source_target_pairs={{0,8},{1,9},{2,10},{3,11},{4,12},{5,13},{6,14},{7,15},{16,24},{17,... | collective-permute-start | bytes 3145736 | tf_op jit(solution)/shard_map/ppermute | solution.py:160
  142.0 17.8 %collective-permute-start.17 = (bf16[2048,256]{1,0:T(8,128)(2,1)S(1)}, bf16[2048,256]{1,0:T(8,128)(2,1)}, u32[]{:S(2)}, u32[]{:S(2)}) collective-permute-start(bf16[2048,256]{1,0:T(8,128)(2,1)S(1)} %pad_maximum_fusion.1.refs_3_), channel_id=1, source_target_pairs={{0,8},{1,9},{2,10},{3,11},{4,12},{5,13},{6,14},{7,15},{16,24},{17,... | collective-permute-start | bytes 3145736 | tf_op jit(solution)/shard_map/ppermute | solution.py:160
  152.4 7.4 %collective-permute-start.19 = (bf16[2048,256]{1,0:T(8,128)(2,1)}, bf16[2048,256]{1,0:T(8,128)(2,1)}, u32[]{:S(2)}, u32[]{:S(2)}) collective-permute-start(bf16[2048,256]{1,0:T(8,128)(2,1)} %collective-permute-done.18.refs_5_), channel_id=1, source_target_pairs={{0,8},{1,9},{2,10},{3,11},{4,12},{5,13},{6,14},{7,15},{16,24},{17,... | collective-permute-start | bytes 3145736 | tf_op jit(solution)/shard_map/ppermute | solution.py:160

commit v4 on v3

v4 whole, which is shorter than its diff:
```python
import functools

import jax
import jax.numpy as jnp
from jax import lax
from jax.experimental import pallas as pl
from jax.experimental.pallas import tpu as pltpu
from jax.sharding import PartitionSpec as P

NB = 2048
STEPS = 4
AXES = ("row", "col")
CORES = 2
TILE = 256
DEPTH = 512
KERNEL_VMEM = 40 * 1024 * 1024


def after(value, *others):
    return lax.optimization_barrier((value, *others))[0]


def step_kernel(terms, n_arrays, outs, where_am_i, *refs):
    current, panels = refs[:2]
    arrays = refs[2 : 2 + n_arrays]
    results = refs[2 + n_arrays : 2 + n_arrays + len(outs)]
    current_here, totals, panels_here, held, sems, piece_sems, current_sem, out_sems = refs[2 + n_arrays + len(outs) :]
    rows = current.shape[0]
    depth = min(DEPTH, NB)
    chunks = NB // depth
    here = where_am_i()

    copies = []
    for t, (_, pieces) in enumerate(terms):
        for array, twin, first, size, place in pieces:
            start = pl.multiple_of(place(here) * size, size)

            def copy(source):
                return pltpu.make_async_copy(
                    arrays[source].at[pl.ds(first, size), :],
                    held.at[t, pl.ds(start, size), :],
                    piece_sems.at[len(copies)],
                )

            if twin is None:
                copy(array).start()
            else:
                pl.when(here.core == 0)(lambda: copy(array).start())
                pl.when(here.core != 0)(lambda: copy(twin).start())
            copies.append(copy(array))

    def panel_copy(t, i):
        k = terms[t][0]
        return pltpu.make_async_copy(
            panels.at[:, pl.ds(k * NB + i * depth, depth)], panels_here.at[t, i], sems.at[t, i]
        )

    for t in range(len(terms)):
        for i in range(chunks):
            panel_copy(t, i).start()
    current_copy = pltpu.make_async_copy(current, current_here, current_sem)
    current_copy.start()
    for copy in copies:
        copy.wait()
    for t in range(len(terms)):
        for i in range(chunks):
            panel_copy(t, i).wait()
            part = jnp.dot(
                panels_here[t, i], held[t, pl.ds(i * depth, depth), :], preferred_element_type=jnp.float32
            )
            totals[t] = part if i == 0 else totals[t] + part
    current_copy.wait()
    sent = []
    tile = min(TILE, rows)
    for i in range(rows // tile):
        at = pl.ds(i * tile, tile)
        value = current_here[at, :]
        for t, (k, _) in enumerate(terms):
            product = totals[t, at, :]
            value = jnp.where(here.block == k, product, value - product)
        for o, (dtype, first, size, far) in enumerate(outs):
            low, high = max(first, i * tile), min(first + size, (i + 1) * tile)
            if low < high:
                part = value[low - i * tile : high - i * tile].astype(dtype)
                if far:
                    current_here[at, :] = part
                    out = pltpu.make_async_copy(current_here.at[at, :], results[o].at[at, :], out_sems.at[i])
                    out.start()
                    sent.append(out)
                else:
                    results[o][pl.ds(low - first, high - low), :] = part
    for out in sent:
        out.wait()


def steps(current, factor_panels, terms, outs, where_am_i):
    rows, scenarios = current.shape
    arrays, plan = [], []

    def index(array):
        if array is None:
            return None
        for i, other in enumerate(arrays):
            if other is array:
                return i
        arrays.append(array)
        return len(arrays) - 1

    for k, pieces in terms:
        plan.append((k, tuple((index(a), index(b), first, size, place) for a, b, first, size, place in pieces)))
    n_terms = len(terms)
    depth = min(DEPTH, NB)
    n_pieces = sum(len(pieces) for _, pieces in terms)
    anywhere = pl.BlockSpec(memory_space=pl.ANY)
    return pl.pallas_call(
        functools.partial(step_kernel, tuple(plan), len(arrays), tuple(outs), where_am_i),
        in_specs=[anywhere] * (2 + len(arrays)),
        out_specs=[anywhere if out[3] else pl.BlockSpec(memory_space=pltpu.VMEM) for out in outs],
        out_shape=[jax.ShapeDtypeStruct((size, scenarios), dtype) for dtype, _, size, _ in outs],
        scratch_shapes=[
            pltpu.VMEM((rows, scenarios), jnp.float32),
            pltpu.VMEM((n_terms, rows, scenarios), jnp.float32),
            pltpu.VMEM((n_terms, NB // depth, rows, depth), jnp.bfloat16),
            pltpu.VMEM((n_terms, NB, scenarios), jnp.bfloat16),
            pltpu.SemaphoreType.DMA((n_terms, NB // depth)),
            pltpu.SemaphoreType.DMA((n_pieces,)),
            pltpu.SemaphoreType.DMA,
            pltpu.SemaphoreType.DMA((rows // min(TILE, rows),)),
        ],
        compiler_params=pltpu.CompilerParams(vmem_limit_bytes=KERNEL_VMEM),
        cost_estimate=pl.CostEstimate(
            flops=2 * rows * NB * scenarios * n_terms,
            bytes_accessed=8 * rows * scenarios,
            transcendentals=0,
        ),
    )(current, factor_panels, *arrays)


class Place:
    def __init__(self, n_col, lanes):
        row, col = lax.axis_index("row"), lax.axis_index("col")
        self.y, self.core = row // CORES, row % CORES
        self.plane, self.lane = col // lanes, col % lanes
        self.block = (row * n_col + col) // lanes


def make_on_device(n_row, n_col):
    def on_device(rhs_scen, factor_panels):
        rows_here = factor_panels.shape[0]
        lanes = NB // rows_here
        planes = n_col // lanes
        n_y = n_row // CORES
        members = lanes * n_y * CORES
        where_am_i = functools.partial(Place, n_col, lanes)
        here = where_am_i()
        y, core, plane = here.y, here.core, here.plane

        def device(y, core, plane, lane):
            return (y * CORES + core) * n_col + plane * lanes + lane

        def send(value, pairs):
            return lax.ppermute(value, AXES, pairs)

        def lane_gather(value, cores, zs, ys=range(n_y)):
            out = [value]
            for d in range(1, lanes):
                pairs = [
                    (device(t, c, z, (m + d) % lanes), device(t, c, z, m))
                    for t in ys for c in cores for z in zs for m in range(lanes)
                ]
                out.append(send(value, pairs))
            return out

        def y_gather(value, cores):
            out = [value]
            for d in range(1, n_y):
                pairs = [
                    (device((t + d) % n_y, c, z, m), device(t, c, z, m))
                    for t in range(n_y) for c in cores for z in range(planes) for m in range(lanes)
                ]
                out.append(send(value, pairs))
            return out

        def ahead(own, k):
            return [
                send(own, [(device(0, 0, k, (m + d) % lanes), device(0, 0, k + 1, m)) for m in range(lanes)])
                for d in range(lanes)
            ]

        lane_places = [functools.partial(lambda d, at: (at.lane + d) % lanes, d) for d in range(lanes)]

        def scatter_y(cuts, sources):
            piece = cuts[0]
            for t in range(1, n_y):
                pairs = [(device(0, 0, k, m), device(t, 0, k, m)) for k in sources for m in range(lanes)]
                piece = jnp.where(y == t, send(cuts[t], pairs), piece)
            return piece

        def along_planes(piece, sources):
            got = []
            for d in range(1, planes):
                pairs = [
                    (device(t, 0, k, m), device(t, 0, (k + d) % planes, m))
                    for k in sources for t in range(n_y) for m in range(lanes)
                ]
                got.append(send(piece, pairs))
            out = []
            for k in sources:
                value = piece
                for d in range(1, planes):
                    value = jnp.where(plane == (k + d) % planes, got[d - 1], value)
                out.append(value)
            return out

        def core_send(value):
            return send(
                value,
                [
                    (device(t, 0, z, m), device(t, 1, z, m))
                    for t in range(n_y) for z in range(planes) for m in range(lanes)
                ],
            )

        tree_places = [
            functools.partial(lambda dy, dm, at: ((at.lane + dm) % lanes) * n_y + (at.y + dy) % n_y, dy, dm)
            for dy in range(n_y) for dm in range(lanes)
        ]

        extra = NB // members
        start_places = [
            functools.partial(lambda dc, q, at: q(at) * CORES + (at.core + dc) % CORES, dc, q)
            for dc in range(CORES) for q in tree_places
        ]
        first = rhs_scen[:, :NB].reshape(-1, lanes, n_y, CORES, extra).transpose(0, 2, 3, 1, 4)
        first = jnp.broadcast_to(
            first[:, :, :, None], (first.shape[0], n_y, CORES, planes, lanes, extra)
        ).reshape(first.shape[0], n_row * n_col, extra)
        outgoing = jnp.concatenate(
            [rhs_scen.reshape(rhs_scen.shape[0], n_row * n_col, rows_here), first], axis=2
        )
        regrouped = lax.all_to_all(outgoing, AXES, split_axis=1, concat_axis=0, tiled=True)
        regrouped = regrouped.reshape(-1, rows_here + extra)
        current = jnp.transpose(regrouped[:, :rows_here]).astype(jnp.float32)
        piece = jnp.transpose(regrouped[:, rows_here:])
        both = range(CORES)
        whole = jnp.concatenate(lane_gather(piece, both, range(planes)), axis=0)
        whole = jnp.concatenate(y_gather(whole, both), axis=0)
        other = send(
            whole,
            [
                (device(t, 1 - c, z, m), device(t, c, z, m))
                for t in range(n_y) for c in both for z in range(planes) for m in range(lanes)
            ],
        )
        per_core = members // CORES
        pieces = [
            (half, None, i * extra, extra, start_places[c * per_core + i])
            for c, half in enumerate([whole, other]) for i in range(per_core)
        ]

        def run(current, terms, outs):
            return steps(current, factor_panels, terms, outs, where_am_i)

        cut = rows_here // n_y
        f32_rows = (jnp.float32, 0, rows_here, False)
        own_rows = (jnp.bfloat16, 0, rows_here, False)
        own_cuts = [(jnp.bfloat16, t * cut, cut, False) for t in range(n_y)]

        def lane_pieces(parts):
            return [(part, None, 0, rows_here, lane_places[d]) for d, part in enumerate(parts)]

        def gather_plane(value):
            mine = jnp.concatenate(lane_gather(value, [0], range(planes)), axis=0)
            far = y_gather(mine, [0])
            return [(part, core_send(part)) for part in far]

        def tree_pieces(arrays, first, size, stride):
            return [
                (mine, other, m * stride + first, size, tree_places[i * lanes + m])
                for i, (mine, other) in enumerate(arrays) for m in range(lanes)
            ]

        def to_rows(parts, order):
            whole = jnp.concatenate(parts, axis=0)
            kept = jnp.where((y == 0) & (core == 0), whole, 0).astype(whole.dtype)
            return kept, lax.psum(kept, "row", axis_index_groups=[order])

        current, own1 = run(current, [(0, pieces)], [f32_rows, own_rows])

        hop1 = ahead(own1, 1)
        near = jnp.where(plane == 2, after(hop1[0], *hop1[1:]), own1)
        pairs = [(device(0, 0, a, m), device(0, 0, b, m)) for a, b in ((2, 3), (1, 0)) for m in range(lanes)]
        passed = send(near, pairs)
        (own2,) = run(current, [(1, lane_pieces(hop1))], [own_rows])
        passed = after(passed, own2)
        near = jnp.where((plane == 1) | (plane == 2), near, passed)
        hop2 = ahead(own2, 2)
        served = STEPS
        while served < planes:
            pairs = [
                (device(0, 0, z, m), device(0, 0, z + served, m))
                for z in range(min(served, planes - served)) for m in range(lanes)
            ]
            near = jnp.where((plane >= served) & (plane < 2 * served), send(near, pairs), near)
            served *= 2
        across = lane_gather(near, [0], [z for z in range(planes) if z != 2], [0])
        (chained,) = run(current, [(1, lane_pieces([passed, *across[1:]]))], [f32_rows])

        start2 = after(own2, *across[1:])
        near2 = start2
        for d in range(1, planes):
            if d != 1:
                pairs = [(device(0, 0, 2, m), device(0, 0, (2 + d) % planes, m)) for m in range(lanes)]
                near2 = jnp.where(plane == (2 + d) % planes, send(start2, pairs), near2)
        order = list(range(n_row))
        parts1 = [near] + [jnp.where(plane == 2, a, b) for a, b in zip(hop1[1:], across[1:])]
        kept1, whole1 = to_rows(parts1, order)
        chained = after(chained, kept1, near2)
        cuts3 = run(chained, [(2, lane_pieces(hop2))], own_cuts)
        across2 = lane_gather(near2, [0], [z for z in range(planes) if z != 3], [0])
        near2 = jnp.where(plane == 3, hop2[0], near2)
        parts2 = [near2] + [jnp.where(plane == 3, a, b) for a, b in zip(hop2[1:], across2[1:])]
        kept2, whole2 = to_rows(parts2, order[::-1])

        (piece3,) = along_planes(scatter_y(cuts3, [3]), [3])
        piece3 = after(piece3, kept2)
        all3 = gather_plane(piece3)

        def whole_pieces(whole):
            return [(whole, None, d * rows_here, rows_here, lane_places[d]) for d in range(lanes)]

        (current,) = run(current, [(1, whole_pieces(whole1)), (2, whole_pieces(whole2))], [f32_rows])
        (out,) = run(current, [(3, tree_pieces(all3, 0, cut, cut))], [(jnp.float32, 0, rows_here, True)])
        return out

    return on_device


def solution(mesh):
    placed = (P(AXES, None), P(AXES, None))
    on_device = make_on_device(mesh.shape["row"], mesh.shape["col"])
    return jax.shard_map(
        on_device, mesh=mesh, in_specs=placed, out_specs=P(AXES, None), check_vma=False
    )
```

time: 169 us -> 234 us (1.38)
  waiting for transfers between devices: 64.6 us -> 117 us
  between operations: 0.7 us -> 13.9 us
  Pallas kernels: 35.8 us -> 30 us
  local copies, waits for them, and re-layouts: 2.02 us -> 6.54 us
  starting transfers between devices: 31.7 us -> 29.3 us
    psum x0 -> x2, waiting for transfers between devices: none -> 55.3 us  [to_rows(): return (kept, lax.psum(kept, 'row', axis_index_groups=[order]))]
    pallas_call x6, Pallas kernels: 35.8 us -> 30 us  [steps(): pl.pallas_call(functools.partial(step_kernel, tuple(plan), len(arrays), t...]
    select_n x3 -> x5, other arithmetic: 1.22 us -> 6.74 us  [the longest x2 3.41 us: to_rows(): kept = jnp.where((y == 0) & (core == 0), whole, 0).astype(whole.dtype)]
    unnamed x8 -> x21, local copies, waits for them, and re-layouts: 1 us -> 5.68 us
    ppermute x20, waiting for transfers between devices: 64.6 us -> 61.7 us  [send(): return lax.ppermute(value, AXES, pairs)]
    ppermute x20, starting transfers between devices: 31.7 us -> 29.3 us  [send(): return lax.ppermute(value, AXES, pairs)]
  transfers between devices with their start and end apart: 20 -> 22, of which waited for: 8 -> 11; matrix products, arithmetic and copies ran while one was open for 3% -> 3% of each run, Pallas kernels for 9% -> 8%
where the time goes in v4:
time: 234 us; the launch traced here: 233 us
  waiting for transfers between devices  117 us (50%)
  Pallas kernels  30 us (13%)
  starting transfers between devices  29.3 us (13%)
  blocking collectives  26.3 us (11%)
  between operations  13.9 us (6%)
  other arithmetic  9.89 us (4%)
  local copies, waits for them, and re-layouts  6.54 us (3%)
    ppermute x20, waiting for transfers between devices, send(): return lax.ppermute(value, AXES, pairs)  61.7 us
    psum x2, waiting for transfers between devices, to_rows(): return (kept, lax.psum(kept, 'row', axis_index_groups=[order]))  55.3 us
    pallas_call x6, Pallas kernels, steps(): pl.pallas_call(functools.partial(step_kernel, tuple(plan), len(arrays), t...  30 us
    ppermute x20, starting transfers between devices, send(): return lax.ppermute(value, AXES, pairs)  29.3 us
    all_to_all x1, blocking collectives, on_device(): lax.all_to_all(outgoing, AXES, split_axis=1, concat_axis=0, tiled=True)  26.3 us
    unnamed x21, local copies, waits for them, and re-layouts  5.68 us
  transfers between devices with their start and end apart: 22, of which 11 were waited for; matrix products, arithmetic and copies ran while one was open for 3% of the time, Pallas kernels for 8%

profile of v4, /device:TPU:0, one launch (start us, length us, event | category | flops | bytes accessed | tf_op | source)
XLA Modules:
  0.0 232.9 jit_solution(1761191092068814554)
XLA Ops:
  8.4 26.3 %all_to_all.15 = bf16[8,32,1280]{2,0,1:T(8,128)(2,1)S(1)} all-to-all(bf16[8,32,1280]{2,0,1:T(8,128)(2,1)S(1)} %pad_maximum_fusion), channel_id=1, replica_groups=mesh['row'=4,'col'=8] {'row','col'}, dimensions={1} | all-to-all | bytes 1310720 | tf_op jit(solution)/shard_map/all_to_all | solution.py:241
  35.7 4.2 %collective-permute-done = bf16[256,256]{1,0:T(8,128)(2,1)S(1)} collective-permute-done((bf16[256,256]{1,0:T(8,128)(2,1)S(1)}, bf16[256,256]{1,0:T(8,128)(2,1)S(1)}, u32[]{:S(2)}, u32[]{:S(2)}) %collective-permute-start) | collective-permute-done | bytes 131104 | tf_op jit(solution)/shard_map/ppermute | solution.py:162
  41.2 6.0 %collective-permute-done.1 = bf16[512,256]{1,0:T(8,128)(2,1)S(1)} collective-permute-done((bf16[512,256]{1,0:T(8,128)(2,1)S(1)}, bf16[512,256]{1,0:T(8,128)(2,1)S(1)}, u32[]{:S(2)}, u32[]{:S(2)}) %collective-permute-start.1) | collective-permute-done | bytes 262176 | tf_op jit(solution)/shard_map/ppermute | solution.py:162
  47.7 1.5 collective-permute-done.2.refs_3_
  49.2 5.4 %shard_map.28 = (f32[1024,256]{1,0:T(8,128)S(1)}, bf16[1024,256]{1,0:T(8,128)(2,1)S(1)}) custom-call(f32[1024,256]{1,0:T(8,128)S(1)} %convert_bitcast_fusion.refs_0_, bf16[1024,8192]{1,0:T(8,128)(2,1)} %refs_1_.11, bf16[1024,256]{1,0:T(8,128)(2,1)S(1)} %pad_maximum_fusion.1.refs_2_, bf16[1024,256]{1,0:T(8,128)(2,1)S(1)} %collective-permute-done.2.refs_3_), custom_call_target="tpu_custom_call" | custom-call | flops 1073741824 | bytes 2097152 | tf_op jit(solution)/shard_map/pallas_call | solution.py:115
  58.3 4.0 %shard_map.29 = bf16[1024,256]{1,0:T(8,128)(2,1)S(1)} custom-call(f32[1024,256]{1,0:T(8,128)S(1)} %get-tuple-element.14.refs_0_, bf16[1024,8192]{1,0:T(8,128)(2,1)} %refs_1_.11, bf16[1024,256]{1,0:T(8,128)(2,1)S(1)} %collective-permute-done.3.refs_2_, bf16[1024,256]{1,0:T(8,128)(2,1)S(1)} %collective-permute-done.4.refs_3_), custom_call_target="tpu_custom_call" | custom-call | flops 1073741824 | bytes 2097152 | tf_op jit(solution)/shard_map/pallas_call | solution.py:115
  62.4 17.0 %collective-permute-done.5.refs_2_ = bf16[1024,256]{1,0:T(8,128)(2,1)S(1)} collective-permute-done((bf16[1024,256]{1,0:T(8,128)(2,1)}, bf16[1024,256]{1,0:T(8,128)(2,1)S(1)}, u32[]{:S(2)}, u32[]{:S(2)}) %collective-permute-start.5) | collective-permute-done | bytes 524320 | tf_op jit(solution)/shard_map/ppermute | solution.py:162
  80.3 3.3 %collective-permute-start.6 = (bf16[1024,256]{1,0:T(8,128)(2,1)}, bf16[1024,256]{1,0:T(8,128)(2,1)S(1)}, u32[]{:S(2)}, u32[]{:S(2)}) collective-permute-start(bf16[1024,256]{1,0:T(8,128)(2,1)} %broadcast_select_fusion.4), channel_id=1, source_target_pairs={{1,0},{0,1},{3,2},{2,3},{7,6},{6,7}} | collective-permute-start | bytes 1572872 | tf_op jit(solution)/shard_map/ppermute | solution.py:162
  85.9 5.6 %collective-permute-done.6.refs_3_ = bf16[1024,256]{1,0:T(8,128)(2,1)S(1)} collective-permute-done((bf16[1024,256]{1,0:T(8,128)(2,1)}, bf16[1024,256]{1,0:T(8,128)(2,1)S(1)}, u32[]{:S(2)}, u32[]{:S(2)}) %collective-permute-start.6) | collective-permute-done | bytes 524320 | tf_op jit(solution)/shard_map/ppermute | solution.py:162
  97.2 4.0 %shard_map.31.refs_0_ = f32[1024,256]{1,0:T(8,128)S(1)} custom-call(f32[1024,256]{1,0:T(8,128)S(1)} %get-tuple-element.14.refs_0_, bf16[1024,8192]{1,0:T(8,128)(2,1)} %refs_1_.11, bf16[1024,256]{1,0:T(8,128)(2,1)S(1)} %copy-done.3, bf16[1024,256]{1,0:T(8,128)(2,1)S(1)} %copy-done.5), custom_call_target="tpu_custom_call" | custom-call | flops 1073741824 | bytes 2097152 | tf_op jit(solution)/shard_map/pallas_call | solution.py:115
  101.3 2.2 maximum_select_fusion
  103.5 5.9 %collective-permute-done.9 = bf16[1024,256]{1,0:T(8,128)(2,1)} collective-permute-done((bf16[1024,256]{1,0:T(8,128)(2,1)S(1)}, bf16[1024,256]{1,0:T(8,128)(2,1)}, u32[]{:S(2)}, u32[]{:S(2)}) %collective-permute-start.9) | collective-permute-done | bytes 524320 | tf_op jit(solution)/shard_map/ppermute | solution.py:162
  109.4 2.2 broadcast_select_fusion.1
  111.5 3.3 %collective-permute-start.11 = (bf16[1024,256]{1,0:T(8,128)(2,1)}, bf16[1024,256]{1,0:T(8,128)(2,1)}, u32[]{:S(2)}, u32[]{:S(2)}) collective-permute-start(bf16[1024,256]{1,0:T(8,128)(2,1)} %get-tuple-element.24), channel_id=1, source_target_pairs={{1,0},{0,1},{3,2},{2,3},{5,4},{4,5}} | collective-permute-start | bytes 1572872 | tf_op jit(solution)/shard_map/ppermute | solution.py:162
  114.9 5.1 %shard_map.32 = (bf16[512,256]{1,0:T(8,128)(2,1)S(1)}, bf16[512,256]{1,0:T(8,128)(2,1)S(1)}) custom-call(f32[1024,256]{1,0:T(8,128)S(1)} %shard_map.31.refs_0_, bf16[1024,8192]{1,0:T(8,128)(2,1)} %refs_1_.11, bf16[1024,256]{1,0:T(8,128)(2,1)S(1)} %collective-permute-done.7.refs_2_, bf16[1024,256]{1,0:T(8,128)(2,1)} %collective-permute-done.10.refs_3_), custom_call_target="tpu_custom_call" | custom-call | flops 1073741824 | bytes 2097152 | tf_op jit(solution)/shard_map/pallas_call | solution.py:115
  125.9 6.7 %collective-permute-done.15 = bf16[512,256]{1,0:T(8,128)(2,1)S(1)} collective-permute-done((bf16[512,256]{1,0:T(8,128)(2,1)S(1)}, bf16[512,256]{1,0:T(8,128)(2,1)S(1)}, u32[]{:S(2)}, u32[]{:S(2)}) %collective-permute-start.15) | collective-permute-done | bytes 262176 | tf_op jit(solution)/shard_map/ppermute | solution.py:162
  132.6 2.5 %collective-permute-start.16 = (bf16[512,256]{1,0:T(8,128)(2,1)S(1)}, bf16[512,256]{1,0:T(8,128)(2,1)S(1)}, u32[]{:S(2)}, u32[]{:S(2)}) collective-permute-start(bf16[512,256]{1,0:T(8,128)(2,1)S(1)} %select_select_fusion.1), channel_id=1, source_target_pairs={{1,0},{0,1},{3,2},{2,3},{5,4},{4,5},{7,6},{6,7},{17,16},{16,17},{1... | collective-permute-start | bytes 786440 | tf_op jit(solution)/shard_map/ppermute | solution.py:162
  135.3 5.6 %collective-permute-done.16 = bf16[512,256]{1,0:T(8,128)(2,1)S(1)} collective-permute-done((bf16[512,256]{1,0:T(8,128)(2,1)S(1)}, bf16[512,256]{1,0:T(8,128)(2,1)S(1)}, u32[]{:S(2)}, u32[]{:S(2)}) %collective-permute-start.16) | collective-permute-done | bytes 262176 | tf_op jit(solution)/shard_map/ppermute | solution.py:162
  140.9 4.0 %collective-permute-start.18 = (bf16[1024,256]{1,0:T(8,128)(2,1)S(1)}, bf16[1024,256]{1,0:T(8,128)(2,1)S(1)}, u32[]{:S(2)}, u32[]{:S(2)}) collective-permute-start(bf16[1024,256]{1,0:T(8,128)(2,1)S(1)} %constant_dynamic-update-slice_fusion.refs_2_), channel_id=1, source_target_pairs={{16,0},{17,1},{18,2},{19,3},{20,4},{21,5},{22,6},{23,7},{0,16},{1,... | collective-permute-start | bytes 1572872 | tf_op jit(solution)/shard_map/ppermute | solution.py:162
  146.3 9.2 %collective-permute-done.18.refs_4_ = bf16[1024,256]{1,0:T(8,128)(2,1)S(1)} collective-permute-done((bf16[1024,256]{1,0:T(8,128)(2,1)S(1)}, bf16[1024,256]{1,0:T(8,128)(2,1)S(1)}, u32[]{:S(2)}, u32[]{:S(2)}) %collective-permute-start.18) | collective-permute-done | bytes 524320 | tf_op jit(solution)/shard_map/ppermute | solution.py:162
  156.8 16.3 %all-reduce.3.cloned.1.call-done.refs_2_ = bf16[2048,256]{1,0:T(8,128)(2,1)} async-done(((bf16[2048,256]{1,0:T(8,128)(2,1)}), bf16[2048,256]{1,0:T(8,128)(2,1)}) %all-reduce.3.cloned.1.call-update) | async-done | bytes 1048592 | tf_op jit(solution)/shard_map/psum | solution.py:286
  173.1 39.0 %all-reduce.5.cloned.1.call-done.refs_3_ = bf16[2048,256]{1,0:T(8,128)(2,1)} async-done(((bf16[2048,256]{1,0:T(8,128)(2,1)}), bf16[2048,256]{1,0:T(8,128)(2,1)}) %all-reduce.5.cloned.1.call-update) | async-done | bytes 1048592 | tf_op jit(solution)/shard_map/psum | solution.py:286
  214.6 6.5 %shard_map.30.refs_0_ = f32[1024,256]{1,0:T(8,128)S(1)} custom-call(f32[1024,256]{1,0:T(8,128)S(1)} %get-tuple-element.14.refs_0_, bf16[1024,8192]{1,0:T(8,128)(2,1)} %refs_1_.11, bf16[2048,256]{1,0:T(8,128)(2,1)S(1)} %copy-done.6, bf16[2048,256]{1,0:T(8,128)(2,1)S(1)} %copy-done.7), custom_call_target="tpu_custom_call" | custom-call | flops 2147483648 | bytes 2097152 | tf_op jit(solution)/shard_map/pallas_call | solution.py:115
  221.1 5.0 %shard_map.33 = f32[1024,256]{1,0:T(8,128)} custom-call(f32[1024,256]{1,0:T(8,128)S(1)} %shard_map.30.refs_0_, bf16[1024,8192]{1,0:T(8,128)(2,1)} %refs_1_.11, bf16[1024,256]{1,0:T(8,128)(2,1)S(1)} %constant_dynamic-update-slice_fusion.refs_2_, bf16[1024,256]{1,0:T(8,128)(2,1)S(1)} %collective-permute-done.17.refs_3_, ...), custom_call_target="tpu_custom_call" | custom-call | flops 1073741824 | bytes 2097152 | tf_op jit(solution)/shard_map/pallas_call | solution.py:115
  (69 shorter events, 28.3 us)
Async XLA Ops:
  6.5 166.6 %all-reduce.3.cloned.1.call-start = ((), (), s32[]{:S(2)}) async-start(), calls=%async_computation.1 | async-start | bytes 2097152 | tf_op jit(solution)/shard_map/psum | solution.py:286
  34.8 5.0 %collective-permute-start = (bf16[256,256]{1,0:T(8,128)(2,1)S(1)}, bf16[256,256]{1,0:T(8,128)(2,1)S(1)}, u32[]{:S(2)}, u32[]{:S(2)}) collective-permute-start(bf16[256,256]{1,0:T(8,128)(2,1)S(1)} %bitcast.15), channel_id=1, source_target_pairs={{1,0},{0,1},{3,2},{2,3},{5,4},{4,5},{7,6},{6,7},{9,8},{8,9},{11,10... | collective-permute-start | bytes 393224 | tf_op jit(solution)/shard_map/ppermute | solution.py:162
  39.8 7.4 %collective-permute-start.1 = (bf16[512,256]{1,0:T(8,128)(2,1)S(1)}, bf16[512,256]{1,0:T(8,128)(2,1)S(1)}, u32[]{:S(2)}, u32[]{:S(2)}) collective-permute-start(bf16[512,256]{1,0:T(8,128)(2,1)S(1)} %pad_maximum_fusion.2), channel_id=1, source_target_pairs={{16,0},{17,1},{18,2},{19,3},{20,4},{21,5},{22,6},{23,7},{24,8},{25... | collective-permute-start | bytes 786440 | tf_op jit(solution)/shard_map/ppermute | solution.py:162
  47.2 2.0 collective-permute-start.2
  54.6 1.4 collective-permute-start.3
  55.3 0.7 collective-permute-start.4
  57.0 22.3 %collective-permute-start.5 = (bf16[1024,256]{1,0:T(8,128)(2,1)}, bf16[1024,256]{1,0:T(8,128)(2,1)S(1)}, u32[]{:S(2)}, u32[]{:S(2)}) collective-permute-start(bf16[1024,256]{1,0:T(8,128)(2,1)} %broadcast_select_fusion.3), channel_id=1, source_target_pairs={{4,6},{5,7},{2,0},{3,1}} | collective-permute-start | bytes 1572872 | tf_op jit(solution)/shard_map/ppermute | solution.py:162
  79.3 14.5 %copy-start.2 = (bf16[1024,256]{1,0:T(8,128)(2,1)}, bf16[1024,256]{1,0:T(8,128)(2,1)S(1)}, u32[]{:S(2)}) copy-start(bf16[1024,256]{1,0:T(8,128)(2,1)S(1)} %collective-permute-done.5.refs_2_) | copy-start | bytes 1572868
  80.3 11.3 %collective-permute-start.6 = (bf16[1024,256]{1,0:T(8,128)(2,1)}, bf16[1024,256]{1,0:T(8,128)(2,1)S(1)}, u32[]{:S(2)}, u32[]{:S(2)}) collective-permute-start(bf16[1024,256]{1,0:T(8,128)(2,1)} %broadcast_select_fusion.4), channel_id=1, source_target_pairs={{1,0},{0,1},{3,2},{2,3},{7,6},{6,7}} | collective-permute-start | bytes 1572872 | tf_op jit(solution)/shard_map/ppermute | solution.py:162
  83.6 17.6 %copy-start.1 = (bf16[1024,256]{1,0:T(8,128)(2,1)S(1)}, bf16[1024,256]{1,0:T(8,128)(2,1)}, u32[]{:S(2)}) copy-start(bf16[1024,256]{1,0:T(8,128)(2,1)} %copy-done) | copy-start | bytes 1572868
  83.6 19.9 %collective-permute-start.7 = (bf16[1024,256]{1,0:T(8,128)(2,1)S(1)}, bf16[1024,256]{1,0:T(8,128)(2,1)S(1)}, u32[]{:S(2)}, u32[]{:S(2)}) collective-permute-start(bf16[1024,256]{1,0:T(8,128)(2,1)S(1)} %shard_map.29), channel_id=1, source_target_pairs={{4,6},{5,7}} | collective-permute-start | bytes 1572872 | tf_op jit(solution)/shard_map/ppermute | solution.py:162
  84.4 30.4 %collective-permute-start.10 = (bf16[1024,256]{1,0:T(8,128)(2,1)S(1)}, bf16[1024,256]{1,0:T(8,128)(2,1)}, u32[]{:S(2)}, u32[]{:S(2)}) collective-permute-start(bf16[1024,256]{1,0:T(8,128)(2,1)S(1)} %shard_map.29), channel_id=1, source_target_pairs={{5,6},{4,7}} | collective-permute-start | bytes 1572872 | tf_op jit(solution)/shard_map/ppermute | solution.py:162
  92.3 11.2 %collective-permute-start.8 = (bf16[1024,256]{1,0:T(8,128)(2,1)S(1)}, bf16[1024,256]{1,0:T(8,128)(2,1)}, u32[]{:S(2)}, u32[]{:S(2)}) collective-permute-start(bf16[1024,256]{1,0:T(8,128)(2,1)S(1)} %shard_map.29), channel_id=1, source_target_pairs={{4,2},{5,3}} | collective-permute-start | bytes 1572872 | tf_op jit(solution)/shard_map/ppermute | solution.py:162
  93.8 15.6 %collective-permute-start.9 = (bf16[1024,256]{1,0:T(8,128)(2,1)S(1)}, bf16[1024,256]{1,0:T(8,128)(2,1)}, u32[]{:S(2)}, u32[]{:S(2)}) collective-permute-start(bf16[1024,256]{1,0:T(8,128)(2,1)S(1)} %shard_map.29), channel_id=1, source_target_pairs={{4,0},{5,1}} | collective-permute-start | bytes 1572872 | tf_op jit(solution)/shard_map/ppermute | solution.py:162
  111.5 12.0 %collective-permute-start.11 = (bf16[1024,256]{1,0:T(8,128)(2,1)}, bf16[1024,256]{1,0:T(8,128)(2,1)}, u32[]{:S(2)}, u32[]{:S(2)}) collective-permute-start(bf16[1024,256]{1,0:T(8,128)(2,1)} %get-tuple-element.24), channel_id=1, source_target_pairs={{1,0},{0,1},{3,2},{2,3},{5,4},{4,5}} | collective-permute-start | bytes 1572872 | tf_op jit(solution)/shard_map/ppermute | solution.py:162
  120.0 0.8 collective-permute-start.12
  120.9 5.0 %collective-permute-start.13 = (bf16[512,256]{1,0:T(8,128)(2,1)S(1)}, bf16[512,256]{1,0:T(8,128)(2,1)S(1)}, u32[]{:S(2)}, u32[]{:S(2)}) collective-permute-start(bf16[512,256]{1,0:T(8,128)(2,1)S(1)} %broadcast_select_fusion.5), channel_id=1, source_target_pairs={{6,4},{7,5},{22,20},{23,21}} | collective-permute-start | bytes 786440 | tf_op jit(solution)/shard_map/ppermute | solution.py:162
  121.5 4.3 %collective-permute-start.14 = (bf16[512,256]{1,0:T(8,128)(2,1)S(1)}, bf16[512,256]{1,0:T(8,128)(2,1)S(1)}, u32[]{:S(2)}, u32[]{:S(2)}) collective-permute-start(bf16[512,256]{1,0:T(8,128)(2,1)S(1)} %broadcast_select_fusion.5), channel_id=1, source_target_pairs={{6,2},{7,3},{22,18},{23,19}} | collective-permute-start | bytes 786440 | tf_op jit(solution)/shard_map/ppermute | solution.py:162
  122.2 10.4 %collective-permute-start.15 = (bf16[512,256]{1,0:T(8,128)(2,1)S(1)}, bf16[512,256]{1,0:T(8,128)(2,1)S(1)}, u32[]{:S(2)}, u32[]{:S(2)}) collective-permute-start(bf16[512,256]{1,0:T(8,128)(2,1)S(1)} %broadcast_select_fusion.5), channel_id=1, source_target_pairs={{6,0},{7,1},{22,16},{23,17}} | collective-permute-start | bytes 786440 | tf_op jit(solution)/shard_map/ppermute | solution.py:162
  132.6 8.3 %collective-permute-start.16 = (bf16[512,256]{1,0:T(8,128)(2,1)S(1)}, bf16[512,256]{1,0:T(8,128)(2,1)S(1)}, u32[]{:S(2)}, u32[]{:S(2)}) collective-permute-start(bf16[512,256]{1,0:T(8,128)(2,1)S(1)} %select_select_fusion.1), channel_id=1, source_target_pairs={{1,0},{0,1},{3,2},{2,3},{5,4},{4,5},{7,6},{6,7},{17,16},{16,17},{1... | collective-permute-start | bytes 786440 | tf_op jit(solution)/shard_map/ppermute | solution.py:162
  135.2 76.9 %all-reduce.5.cloned.1.call-start = ((), (), s32[]{:S(2)}) async-start(), calls=%async_computation.2 | async-start | bytes 2097152 | tf_op jit(solution)/shard_map/psum | solution.py:286
  140.9 14.6 %collective-permute-start.18 = (bf16[1024,256]{1,0:T(8,128)(2,1)S(1)}, bf16[1024,256]{1,0:T(8,128)(2,1)S(1)}, u32[]{:S(2)}, u32[]{:S(2)}) collective-permute-start(bf16[1024,256]{1,0:T(8,128)(2,1)S(1)} %constant_dynamic-update-slice_fusion.refs_2_), channel_id=1, source_target_pairs={{16,0},{17,1},{18,2},{19,3},{20,4},{21,5},{22,6},{23,7},{0,16},{1,... | collective-permute-start | bytes 1572872 | tf_op jit(solution)/shard_map/ppermute | solution.py:162
  145.0 76.1 %collective-permute-start.17 = (bf16[1024,256]{1,0:T(8,128)(2,1)S(1)}, bf16[1024,256]{1,0:T(8,128)(2,1)S(1)}, u32[]{:S(2)}, u32[]{:S(2)}) collective-permute-start(bf16[1024,256]{1,0:T(8,128)(2,1)S(1)} %constant_dynamic-update-slice_fusion.refs_2_), channel_id=1, source_target_pairs={{0,8},{1,9},{2,10},{3,11},{4,12},{5,13},{6,14},{7,15},{16,24},{17,... | collective-permute-start | bytes 1572872 | tf_op jit(solution)/shard_map/ppermute | solution.py:162
  155.5 65.6 %collective-permute-start.19 = (bf16[1024,256]{1,0:T(8,128)(2,1)S(1)}, bf16[1024,256]{1,0:T(8,128)(2,1)S(1)}, u32[]{:S(2)}, u32[]{:S(2)}) collective-permute-start(bf16[1024,256]{1,0:T(8,128)(2,1)S(1)} %collective-permute-done.18.refs_4_), channel_id=1, source_target_pairs={{0,8},{1,9},{2,10},{3,11},{4,12},{5,13},{6,14},{7,15},{16,24},{17,... | collective-permute-start | bytes 1572872 | tf_op jit(solution)/shard_map/ppermute | solution.py:162
  (7 other events, 16.3 us)
Sparse Core Ops, SparseCore 0:
  135.3 37.7 all-reduce.2
  175.6 36.4 all-reduce.4

commit v5 on v4

v5 whole, which is shorter than its diff:
```python
import functools

import jax
import jax.numpy as jnp
from jax import lax
from jax.experimental import pallas as pl
from jax.experimental.pallas import tpu as pltpu
from jax.sharding import PartitionSpec as P

NB = 2048
STEPS = 4
AXES = ("row", "col")
CORES = 2
TILE = 256
DEPTH = 512
KERNEL_VMEM = 40 * 1024 * 1024


def after(value, *others):
    return lax.optimization_barrier((value, *others))[0]


def step_kernel(terms, n_arrays, outs, where_am_i, active, *refs):
    current, panels = refs[:2]
    arrays = refs[2 : 2 + n_arrays]
    results = refs[2 + n_arrays : 2 + n_arrays + len(outs)]
    current_here, totals, panels_here, held, sems, piece_sems, current_sem, out_sems = refs[2 + n_arrays + len(outs) :]
    rows = current.shape[0]
    depth = min(DEPTH, NB)
    chunks = NB // depth
    here = where_am_i()

    def work():
        copies = []
        for t, (_, pieces) in enumerate(terms):
            for array, twin, first, size, place in pieces:
                start = pl.multiple_of(place(here) * size, size)

                def copy(source):
                    return pltpu.make_async_copy(
                        arrays[source].at[pl.ds(first, size), :],
                        held.at[t, pl.ds(start, size), :],
                        piece_sems.at[len(copies)],
                    )

                if twin is None:
                    copy(array).start()
                else:
                    pl.when(here.core == 0)(lambda: copy(array).start())
                    pl.when(here.core != 0)(lambda: copy(twin).start())
                copies.append(copy(array))

        def panel_copy(t, i):
            k = terms[t][0]
            return pltpu.make_async_copy(
                panels.at[:, pl.ds(k * NB + i * depth, depth)], panels_here.at[t, i], sems.at[t, i]
            )

        for t in range(len(terms)):
            for i in range(chunks):
                panel_copy(t, i).start()
        current_copy = pltpu.make_async_copy(current, current_here, current_sem)
        current_copy.start()
        for copy in copies:
            copy.wait()
        for t in range(len(terms)):
            for i in range(chunks):
                panel_copy(t, i).wait()
                part = jnp.dot(
                    panels_here[t, i], held[t, pl.ds(i * depth, depth), :], preferred_element_type=jnp.float32
                )
                totals[t] = part if i == 0 else totals[t] + part
        current_copy.wait()
        sent = []
        tile = min(TILE, rows)
        for i in range(rows // tile):
            at = pl.ds(i * tile, tile)
            value = current_here[at, :]
            for t, (k, _) in enumerate(terms):
                product = totals[t, at, :]
                value = jnp.where(here.block == k, product, value - product)
            for o, (dtype, first, size, far) in enumerate(outs):
                low, high = max(first, i * tile), min(first + size, (i + 1) * tile)
                if low < high:
                    part = value[low - i * tile : high - i * tile].astype(dtype)
                    if far:
                        current_here[at, :] = part
                        out = pltpu.make_async_copy(current_here.at[at, :], results[o].at[at, :], out_sems.at[i])
                        out.start()
                        sent.append(out)
                    else:
                        results[o][pl.ds(low - first, high - low), :] = part
        for out in sent:
            out.wait()

    if active is None:
        work()
    else:
        pl.when(active(here))(work)


def steps(current, factor_panels, terms, outs, where_am_i, active):
    rows, scenarios = current.shape
    arrays, plan = [], []

    def index(array):
        if array is None:
            return None
        for i, other in enumerate(arrays):
            if other is array:
                return i
        arrays.append(array)
        return len(arrays) - 1

    for k, pieces in terms:
        plan.append((k, tuple((index(a), index(b), first, size, place) for a, b, first, size, place in pieces)))
    n_terms = len(terms)
    depth = min(DEPTH, NB)
    n_pieces = sum(len(pieces) for _, pieces in terms)
    anywhere = pl.BlockSpec(memory_space=pl.ANY)
    return pl.pallas_call(
        functools.partial(step_kernel, tuple(plan), len(arrays), tuple(outs), where_am_i, active),
        in_specs=[anywhere] * (2 + len(arrays)),
        out_specs=[anywhere if out[3] else pl.BlockSpec(memory_space=pltpu.VMEM) for out in outs],
        out_shape=[jax.ShapeDtypeStruct((size, scenarios), dtype) for dtype, _, size, _ in outs],
        scratch_shapes=[
            pltpu.VMEM((rows, scenarios), jnp.float32),
            pltpu.VMEM((n_terms, rows, scenarios), jnp.float32),
            pltpu.VMEM((n_terms, NB // depth, rows, depth), jnp.bfloat16),
            pltpu.VMEM((n_terms, NB, scenarios), jnp.bfloat16),
            pltpu.SemaphoreType.DMA((n_terms, NB // depth)),
            pltpu.SemaphoreType.DMA((n_pieces,)),
            pltpu.SemaphoreType.DMA,
            pltpu.SemaphoreType.DMA((rows // min(TILE, rows),)),
        ],
        compiler_params=pltpu.CompilerParams(vmem_limit_bytes=KERNEL_VMEM),
        cost_estimate=pl.CostEstimate(
            flops=2 * rows * NB * scenarios * n_terms,
            bytes_accessed=8 * rows * scenarios,
            transcendentals=0,
        ),
    )(current, factor_panels, *arrays)


class Place:
    def __init__(self, n_col, lanes):
        row, col = lax.axis_index("row"), lax.axis_index("col")
        self.y, self.core = row // CORES, row % CORES
        self.plane, self.lane = col // lanes, col % lanes
        self.block = (row * n_col + col) // lanes


def make_on_device(n_row, n_col):
    def on_device(rhs_scen, factor_panels):
        rows_here = factor_panels.shape[0]
        lanes = NB // rows_here
        planes = n_col // lanes
        n_y = n_row // CORES
        members = lanes * n_y * CORES
        where_am_i = functools.partial(Place, n_col, lanes)
        here = where_am_i()
        y, core, plane = here.y, here.core, here.plane

        def device(y, core, plane, lane):
            return (y * CORES + core) * n_col + plane * lanes + lane

        def send(value, pairs):
            return lax.ppermute(value, AXES, pairs)

        def lane_gather(value, cores, zs, ys=range(n_y)):
            out = [value]
            for d in range(1, lanes):
                pairs = [
                    (device(t, c, z, (m + d) % lanes), device(t, c, z, m))
                    for t in ys for c in cores for z in zs for m in range(lanes)
                ]
                out.append(send(value, pairs))
            return out

        def y_gather(value, cores):
            out = [value]
            for d in range(1, n_y):
                pairs = [
                    (device((t + d) % n_y, c, z, m), device(t, c, z, m))
                    for t in range(n_y) for c in cores for z in range(planes) for m in range(lanes)
                ]
                out.append(send(value, pairs))
            return out

        def plane_gather(value, cores):
            first = lane_gather(value, cores, range(planes))
            far = y_gather(value, cores)[1:]
            return first + [part for got in far for part in lane_gather(got, cores, range(planes))]

        def ahead(own, k):
            return [
                send(own, [(device(0, 0, k, (m + d) % lanes), device(0, 0, k + 1, m)) for m in range(lanes)])
                for d in range(lanes)
            ]

        lane_places = [functools.partial(lambda d, at: (at.lane + d) % lanes, d) for d in range(lanes)]

        def scatter_y(cuts, sources):
            piece = cuts[0]
            for t in range(1, n_y):
                pairs = [(device(0, 0, k, m), device(t, 0, k, m)) for k in sources for m in range(lanes)]
                piece = jnp.where(y == t, send(cuts[t], pairs), piece)
            return piece

        def along_planes(piece, sources):
            got = []
            for d in range(1, planes):
                pairs = [
                    (device(t, 0, k, m), device(t, 0, (k + d) % planes, m))
                    for k in sources for t in range(n_y) for m in range(lanes)
                ]
                got.append(send(piece, pairs))
            out = []
            for k in sources:
                value = piece
                for d in range(1, planes):
                    value = jnp.where(plane == (k + d) % planes, got[d - 1], value)
                out.append(value)
            return out

        def core_send(value):
            return send(
                value,
                [
                    (device(t, 0, z, m), device(t, 1, z, m))
                    for t in range(n_y) for z in range(planes) for m in range(lanes)
                ],
            )

        tree_places = [
            functools.partial(lambda dy, dm, at: ((at.lane + dm) % lanes) * n_y + (at.y + dy) % n_y, dy, dm)
            for dy in range(n_y) for dm in range(lanes)
        ]

        extra = NB // members
        start_places = [
            functools.partial(lambda dc, q, at: q(at) * CORES + (at.core + dc) % CORES, dc, q)
            for dc in range(CORES) for q in tree_places
        ]
        first = rhs_scen[:, :NB].reshape(-1, lanes, n_y, CORES, extra).transpose(0, 2, 3, 1, 4)
        first = jnp.broadcast_to(
            first[:, :, :, None], (first.shape[0], n_y, CORES, planes, lanes, extra)
        ).reshape(first.shape[0], n_row * n_col, extra)
        outgoing = jnp.concatenate(
            [rhs_scen.reshape(rhs_scen.shape[0], n_row * n_col, rows_here), first], axis=2
        )
        regrouped = lax.all_to_all(outgoing, AXES, split_axis=1, concat_axis=0, tiled=True)
        regrouped = regrouped.reshape(-1, rows_here + extra)
        current = jnp.transpose(regrouped[:, :rows_here]).astype(jnp.float32)
        piece = jnp.transpose(regrouped[:, rows_here:])
        both = range(CORES)
        whole = jnp.concatenate(plane_gather(piece, both), axis=0)
        other = send(
            whole,
            [
                (device(t, 1 - c, z, m), device(t, c, z, m))
                for t in range(n_y) for c in both for z in range(planes) for m in range(lanes)
            ],
        )
        per_core = members // CORES
        pieces = [
            (half, None, i * extra, extra, start_places[c * per_core + i])
            for c, half in enumerate([whole, other]) for i in range(per_core)
        ]

        def run(current, terms, outs, only=None):
            active = None if only is None else lambda at: at.block == only
            return steps(current, factor_panels, terms, outs, where_am_i, active)

        cut = rows_here // n_y
        f32_rows = (jnp.float32, 0, rows_here, False)
        own_rows = (jnp.bfloat16, 0, rows_here, False)
        own_cuts = [(jnp.bfloat16, t * cut, cut, False) for t in range(n_y)]

        def lane_pieces(parts):
            return [(part, None, 0, rows_here, lane_places[d]) for d, part in enumerate(parts)]

        current, own1 = run(current, [(0, pieces)], [f32_rows, own_rows])

        def to_y(own, k):
            value = own
            for t in range(1, n_y):
                pairs = [(device(0, 0, k, m), device(t, 0, k, m)) for m in range(lanes)]
                value = jnp.where(y == t, send(own, pairs), value)
            return value

        def pairs_to(k, z, ys):
            return [(device(t, 0, k, m), device(t, 0, z, m)) for t in ys for m in range(lanes)]

        every_y = range(n_y)

        hop1 = ahead(own1, 1)
        near1 = after(to_y(own1, 1), hop1[0])
        crossed = [
            send(
                near1,
                [(device(0, 0, 1, (m + d) % lanes), device(0, 0, 3, m)) for m in range(lanes)]
                + (pairs_to(1, 2, every_y[1:]) if d == 1 else []),
            )
            for d in range(1, lanes)
        ]
        got1 = {z: send(near1, pairs_to(1, z, every_y)) for z in range(planes) if z not in (1, 2)}
        got1[2] = jnp.where(y == 0, hop1[0], crossed[0])
        (own2,) = run(current, [(1, lane_pieces(hop1))], [own_rows], 2)
        hop2 = ahead(own2, 2)
        (chained,) = run(current, [(1, lane_pieces([got1[3], *crossed]))], [f32_rows], 3)
        cuts3 = run(chained, [(2, lane_pieces(hop2))], own_cuts, 3)
        start2 = after(own2, chained)
        got2 = {z: send(start2, pairs_to(2, z, [0])) for z in range(planes) if z not in (2, 3)}
        got2[3] = hop2[0]

        piece3 = scatter_y(cuts3, [3])
        halves = []
        for value, got in ((near1, got1), (own2, got2)):
            for z, part in got.items():
                value = jnp.where(plane == z, part, value)
            halves.append(value)
        near2 = after(halves[1], cuts3[0])
        for t in every_y[1:]:
            pairs = [(device(0, 0, z, m), device(t, 0, z, m)) for z in range(planes) for m in range(lanes)]
            near2 = jnp.where(y == t, send(near2, pairs), near2)
        near12 = after(jnp.concatenate([halves[0], near2], axis=0), piece3)
        all12 = lane_gather(near12, [0], range(planes))
        (piece3,) = along_planes(piece3, [3])
        all12 = [near12] + [after(part, piece3) for part in all12[1:]]
        other12 = [core_send(part) for part in all12]
        *most3, last3 = plane_gather(piece3, [0])
        most3 = jnp.concatenate(most3, axis=0)
        other3 = core_send(most3)

        def whole_pieces(first):
            return [
                (mine, other, first * rows_here, rows_here, lane_places[d])
                for d, (mine, other) in enumerate(zip(all12, other12))
            ]

        (current,) = run(current, [(1, whole_pieces(0)), (2, whole_pieces(1))], [f32_rows])
        other_last3 = core_send(after(last3, current))
        pieces3 = [(most3, other3, i * cut, cut, place) for i, place in enumerate(tree_places[:-1])]
        pieces3.append((last3, other_last3, 0, cut, tree_places[-1]))
        (out,) = run(current, [(3, pieces3)], [(jnp.float32, 0, rows_here, True)])
        return out

    return on_device


def solution(mesh):
    placed = (P(AXES, None), P(AXES, None))
    on_device = make_on_device(mesh.shape["row"], mesh.shape["col"])
    return jax.shard_map(
        on_device, mesh=mesh, in_specs=placed, out_specs=P(AXES, None), check_vma=False
    )
```

time: 234 us -> 153 us (0.65)
  waiting for transfers between devices: 117 us -> 65.9 us
  between operations: 13.9 us -> 0.46 us
  Pallas kernels: 30 us -> 18.8 us
  local copies, waits for them, and re-layouts: 6.54 us -> 1.83 us
  starting transfers between devices: 29.3 us -> 33.6 us
  other arithmetic: 9.89 us -> 5.69 us
    psum x2 -> x0, waiting for transfers between devices: 55.3 us -> none  [to_rows(): return (kept, lax.psum(kept, 'row', axis_index_groups=[order]))]
    pallas_call x6, Pallas kernels: 30 us -> 18.8 us  [steps(): pl.pallas_call(functools.partial(step_kernel, tuple(plan), len(arrays), t...]
    unnamed x21 -> x6, local copies, waits for them, and re-layouts: 5.68 us -> 0.99 us
    ppermute x20 -> x27, starting transfers between devices: 29.3 us -> 33.6 us  [send(): return lax.ppermute(value, AXES, pairs)]
    select_n x7 -> x4, other arithmetic: 8.6 us -> 4.3 us  [the longest x2 2.31 us: on_device(): value = jnp.where(plane == z, part, value)]
    ppermute x20 -> x27, waiting for transfers between devices: 61.7 us -> 65.9 us  [send(): return lax.ppermute(value, AXES, pairs)]
  transfers between devices with their start and end apart: 22 -> 27, of which waited for: 11 -> 9; matrix products, arithmetic and copies ran while one was open for 3% -> 3% of each run, Pallas kernels for 8% -> 5%
where the time goes in v5:
time: 153 us
  waiting for transfers between devices  65.9 us (43%)
  starting transfers between devices  33.6 us (22%)
  blocking collectives  26.3 us (17%)
  Pallas kernels  18.8 us (12%)
  other arithmetic  5.69 us (4%)
  local copies, waits for them, and re-layouts  1.83 us (1%)
    ppermute x27, waiting for transfers between devices, send(): return lax.ppermute(value, AXES, pairs)  65.9 us
    ppermute x27, starting transfers between devices, send(): return lax.ppermute(value, AXES, pairs)  33.6 us
    all_to_all x1, blocking collectives, on_device(): lax.all_to_all(outgoing, AXES, split_axis=1, concat_axis=0, tiled=True)  26.3 us
    pallas_call x6, Pallas kernels, steps(): pl.pallas_call(functools.partial(step_kernel, tuple(plan), len(arrays), t...  18.8 us
  transfers between devices with their start and end apart: 27, of which 9 were waited for; matrix products, arithmetic and copies ran while one was open for 3% of the time, Pallas kernels for 5%

profile of v5, /device:TPU:0, one launch (start us, length us, event | category | flops | bytes accessed | tf_op | source)
XLA Modules:
  0.0 152.6 jit_solution(676764353805795365)
XLA Ops:
  1.9 26.3 %all_to_all.15 = bf16[8,32,1280]{2,0,1:T(8,128)(2,1)S(1)} all-to-all(bf16[8,32,1280]{2,0,1:T(8,128)(2,1)S(1)} %pad_maximum_fusion.2), channel_id=1, replica_groups=mesh['row'=4,'col'=8] {'row','col'}, dimensions={1} | all-to-all | bytes 1310720 | tf_op jit(solution)/shard_map/all_to_all | solution.py:252
  29.7 3.6 %collective-permute-done.1 = bf16[256,256]{1,0:T(8,128)(2,1)S(1)} collective-permute-done((bf16[256,256]{1,0:T(8,128)(2,1)S(1)}, bf16[256,256]{1,0:T(8,128)(2,1)S(1)}, u32[]{:S(2)}, u32[]{:S(2)}) %collective-permute-start.1) | collective-permute-done | bytes 131104 | tf_op jit(solution)/shard_map/ppermute | solution.py:168
  33.3 1.4 collective-permute-start.2
  34.6 3.6 %collective-permute-done.2 = bf16[256,256]{1,0:T(8,128)(2,1)S(1)} collective-permute-done((bf16[256,256]{1,0:T(8,128)(2,1)S(1)}, bf16[256,256]{1,0:T(8,128)(2,1)S(1)}, u32[]{:S(2)}, u32[]{:S(2)}) %collective-permute-start.2) | collective-permute-done | bytes 131104 | tf_op jit(solution)/shard_map/ppermute | solution.py:168
  38.7 1.5 %collective-permute-done.3.refs_3_ = bf16[1024,256]{1,0:T(8,128)(2,1)S(1)} collective-permute-done((bf16[1024,256]{1,0:T(8,128)(2,1)S(1)}, bf16[1024,256]{1,0:T(8,128)(2,1)S(1)}, u32[]{:S(2)}, u32[]{:S(2)}) %collective-permute-start.3) | collective-permute-done | bytes 524320 | tf_op jit(solution)/shard_map/ppermute | solution.py:168
  40.3 6.2 %shard_map.28 = (f32[1024,256]{1,0:T(8,128)S(1)}, bf16[1024,256]{1,0:T(8,128)(2,1)}) custom-call(f32[1024,256]{1,0:T(8,128)S(1)} %convert_bitcast_fusion.refs_0_, bf16[1024,8192]{1,0:T(8,128)(2,1)} %refs_1_.11, bf16[1024,256]{1,0:T(8,128)(2,1)S(1)} %pad_maximum_fusion.3.refs_2_, bf16[1024,256]{1,0:T(8,128)(2,1)S(1)} %collective-permute-done.3.refs_3_), custom_call_target="tpu_custom_call" | custom-call | flops 1073741824 | bytes 2097152 | tf_op jit(solution)/shard_map/pallas_call | solution.py:121
  48.6 1.9 %broadcast_select_fusion.1 = bf16[1024,256]{1,0:T(8,128)(2,1)} fusion(bf16[1024,256]{1,0:T(8,128)(2,1)S(1)} %collective-permute-done.5, bf16[1024,256]{1,0:T(8,128)(2,1)} %get-tuple-element.16, pred[]{:T(512)S(6)} %eq.27), kind=kLoop, calls=%fused_computation.8 | loop fusion | flops 262144 | bytes 1572865 | tf_op jit(solution)/shard_map/jit(_where)/select_n | solution.py:289
  52.8 1.5 collective-permute-start.10
  54.3 1.5 collective-permute-start.13
  56.6 1.5 collective-permute-start.11
  61.7 30.9 %collective-permute-done.12 = bf16[1024,256]{1,0:T(8,128)(2,1)} collective-permute-done((bf16[1024,256]{1,0:T(8,128)(2,1)}, bf16[1024,256]{1,0:T(8,128)(2,1)}, u32[]{:S(2)}, u32[]{:S(2)}) %collective-permute-start.12) | collective-permute-done | bytes 524320 | tf_op jit(solution)/shard_map/ppermute | solution.py:168
  96.3 5.4 %collective-permute-done.14 = bf16[1024,256]{1,0:T(8,128)(2,1)S(1)} collective-permute-done((bf16[1024,256]{1,0:T(8,128)(2,1)S(1)}, bf16[1024,256]{1,0:T(8,128)(2,1)S(1)}, u32[]{:S(2)}, u32[]{:S(2)}) %collective-permute-start.14) | collective-permute-done | bytes 524320 | tf_op jit(solution)/shard_map/ppermute | solution.py:168
  101.9 1.9 %collective-permute-start.17 = (bf16[2048,256]{1,0:T(8,128)(2,1)S(1)}, bf16[2048,256]{1,0:T(8,128)(2,1)S(1)}, u32[]{:S(2)}, u32[]{:S(2)}) collective-permute-start(bf16[2048,256]{1,0:T(8,128)(2,1)S(1)} %pad_maximum_fusion.refs_2_), channel_id=1, source_target_pairs={{1,0},{0,1},{3,2},{2,3},{5,4},{4,5},{7,6},{6,7},{17,16},{16,17},{1... | collective-permute-start | bytes 3145736 | tf_op jit(solution)/shard_map/ppermute | solution.py:168
  106.5 13.4 %collective-permute-done.20 = bf16[512,256]{1,0:T(8,128)(2,1)S(1)} collective-permute-done((bf16[512,256]{1,0:T(8,128)(2,1)S(1)}, bf16[512,256]{1,0:T(8,128)(2,1)S(1)}, u32[]{:S(2)}, u32[]{:S(2)}) %collective-permute-start.20) | collective-permute-done | bytes 262176 | tf_op jit(solution)/shard_map/ppermute | solution.py:168
  119.9 1.4 collective-permute-start.16
  121.3 1.4 collective-permute-start.21
  122.6 4.4 %collective-permute-start.23 = (bf16[512,256]{1,0:T(8,128)(2,1)S(1)}, bf16[512,256]{1,0:T(8,128)(2,1)S(1)}, u32[]{:S(2)}, u32[]{:S(2)}) collective-permute-start(bf16[512,256]{1,0:T(8,128)(2,1)S(1)} %select_select_fusion.2), channel_id=1, source_target_pairs={{16,0},{17,1},{18,2},{19,3},{20,4},{21,5},{22,6},{23,7},{0,16},{1,... | collective-permute-start | bytes 786440 | tf_op jit(solution)/shard_map/ppermute | solution.py:168
  127.0 1.9 %collective-permute-start.22 = (bf16[512,256]{1,0:T(8,128)(2,1)S(1)}, bf16[512,256]{1,0:T(8,128)(2,1)S(1)}, u32[]{:S(2)}, u32[]{:S(2)}) collective-permute-start(bf16[512,256]{1,0:T(8,128)(2,1)S(1)} %select_select_fusion.2), channel_id=1, source_target_pairs={{1,0},{0,1},{3,2},{2,3},{5,4},{4,5},{7,6},{6,7},{17,16},{16,17},{1... | collective-permute-start | bytes 786440 | tf_op jit(solution)/shard_map/ppermute | solution.py:168
  129.0 2.4 %collective-permute-done.23 = bf16[512,256]{1,0:T(8,128)(2,1)S(1)} collective-permute-done((bf16[512,256]{1,0:T(8,128)(2,1)S(1)}, bf16[512,256]{1,0:T(8,128)(2,1)S(1)}, u32[]{:S(2)}, u32[]{:S(2)}) %collective-permute-start.23) | collective-permute-done | bytes 262176 | tf_op jit(solution)/shard_map/ppermute | solution.py:168
  131.4 3.9 %collective-permute-done.22 = bf16[512,256]{1,0:T(8,128)(2,1)S(1)} collective-permute-done((bf16[512,256]{1,0:T(8,128)(2,1)S(1)}, bf16[512,256]{1,0:T(8,128)(2,1)S(1)}, u32[]{:S(2)}, u32[]{:S(2)}) %collective-permute-start.22) | collective-permute-done | bytes 262176 | tf_op jit(solution)/shard_map/ppermute | solution.py:168
  135.4 1.3 collective-permute-start.24
  136.7 1.9 %collective-permute-start.25 = (bf16[512,256]{1,0:T(8,128)(2,1)S(1)}, bf16[512,256]{1,0:T(8,128)(2,1)S(1)}, u32[]{:S(2)}, u32[]{:S(2)}) collective-permute-start(bf16[512,256]{1,0:T(8,128)(2,1)S(1)} %collective-permute-done.23), channel_id=1, source_target_pairs={{1,0},{0,1},{3,2},{2,3},{5,4},{4,5},{7,6},{6,7},{17,16},{16,17},{1... | collective-permute-start | bytes 786440 | tf_op jit(solution)/shard_map/ppermute | solution.py:168
  138.7 6.5 %shard_map.32.refs_0_ = f32[1024,256]{1,0:T(8,128)S(1)} custom-call(f32[1024,256]{1,0:T(8,128)S(1)} %get-tuple-element.15.refs_0_, bf16[1024,8192]{1,0:T(8,128)(2,1)} %refs_1_.11, bf16[2048,256]{1,0:T(8,128)(2,1)S(1)} %pad_maximum_fusion.refs_2_, bf16[2048,256]{1,0:T(8,128)(2,1)S(1)} %collective-permute-done.16.refs_3_, ...), custom_call_target="tpu_custom_call" | custom-call | flops 2147483648 | bytes 2097152 | tf_op jit(solution)/shard_map/pallas_call | solution.py:121
  147.7 5.0 %shard_map.33 = f32[1024,256]{1,0:T(8,128)} custom-call(f32[1024,256]{1,0:T(8,128)S(1)} %shard_map.32.refs_0_, bf16[1024,8192]{1,0:T(8,128)(2,1)} %refs_1_.11, bf16[1536,256]{1,0:T(8,128)(2,1)S(1)} %pad_maximum_fusion.1.refs_2_, bf16[1536,256]{1,0:T(8,128)(2,1)S(1)} %collective-permute-done.24.refs_3_, bf16[512,256]{1,0:T(8,128)(2,1)S(1)} %collective-permute-done.25.refs_4_, ...), custom_call_target="tpu_custom_call" | custom-call | flops 1073741824 | bytes 2097152 | tf_op jit(solution)/shard_map/pallas_call | solution.py:121
  (59 shorter events, 21.5 us)
Async XLA Ops:
  28.3 5.0 %collective-permute-start.1 = (bf16[256,256]{1,0:T(8,128)(2,1)S(1)}, bf16[256,256]{1,0:T(8,128)(2,1)S(1)}, u32[]{:S(2)}, u32[]{:S(2)}) collective-permute-start(bf16[256,256]{1,0:T(8,128)(2,1)S(1)} %bitcast.17), channel_id=1, source_target_pairs={{16,0},{17,1},{18,2},{19,3},{20,4},{21,5},{22,6},{23,7},{24,8},{25... | collective-permute-start | bytes 393224 | tf_op jit(solution)/shard_map/ppermute | solution.py:168
  28.9 5.8 %collective-permute-start = (bf16[256,256]{1,0:T(8,128)(2,1)S(1)}, bf16[256,256]{1,0:T(8,128)(2,1)S(1)}, u32[]{:S(2)}, u32[]{:S(2)}) collective-permute-start(bf16[256,256]{1,0:T(8,128)(2,1)S(1)} %bitcast.18), channel_id=1, source_target_pairs={{1,0},{0,1},{3,2},{2,3},{5,4},{4,5},{7,6},{6,7},{9,8},{8,9},{11,10... | collective-permute-start | bytes 393224 | tf_op jit(solution)/shard_map/ppermute | solution.py:168
  33.3 5.0 %collective-permute-start.2 = (bf16[256,256]{1,0:T(8,128)(2,1)S(1)}, bf16[256,256]{1,0:T(8,128)(2,1)S(1)}, u32[]{:S(2)}, u32[]{:S(2)}) collective-permute-start(bf16[256,256]{1,0:T(8,128)(2,1)S(1)} %collective-permute-done.1), channel_id=1, source_target_pairs={{1,0},{0,1},{3,2},{2,3},{5,4},{4,5},{7,6},{6,7},{9,8},{8,9},{11,10... | collective-permute-start | bytes 393224 | tf_op jit(solution)/shard_map/ppermute | solution.py:168
  47.1 3.4 %collective-permute-start.4 = (bf16[1024,256]{1,0:T(8,128)(2,1)}, bf16[1024,256]{1,0:T(8,128)(2,1)S(1)}, u32[]{:S(2)}, u32[]{:S(2)}) collective-permute-start(bf16[1024,256]{1,0:T(8,128)(2,1)} %get-tuple-element.16), channel_id=1, source_target_pairs={{2,4},{3,5}} | collective-permute-start | bytes 1572872 | tf_op jit(solution)/shard_map/ppermute | solution.py:168
  47.9 4.0 %collective-permute-start.9 = (bf16[1024,256]{1,0:T(8,128)(2,1)}, bf16[1024,256]{1,0:T(8,128)(2,1)S(1)}, u32[]{:S(2)}, u32[]{:S(2)}) collective-permute-start(bf16[1024,256]{1,0:T(8,128)(2,1)} %get-tuple-element.16), channel_id=1, source_target_pairs={{3,4},{2,5}} | collective-permute-start | bytes 1572872 | tf_op jit(solution)/shard_map/ppermute | solution.py:168
  50.5 5.3 %collective-permute-start.7 = (bf16[1024,256]{1,0:T(8,128)(2,1)}, bf16[1024,256]{1,0:T(8,128)(2,1)S(1)}, u32[]{:S(2)}, u32[]{:S(2)}) collective-permute-start(bf16[1024,256]{1,0:T(8,128)(2,1)} %broadcast_select_fusion.1), channel_id=1, source_target_pairs={{2,6},{3,7},{18,22},{19,23}} | collective-permute-start | bytes 1572872 | tf_op jit(solution)/shard_map/ppermute | solution.py:168
  51.2 4.6 %collective-permute-start.6 = (bf16[1024,256]{1,0:T(8,128)(2,1)}, bf16[1024,256]{1,0:T(8,128)(2,1)S(1)}, u32[]{:S(2)}, u32[]{:S(2)}) collective-permute-start(bf16[1024,256]{1,0:T(8,128)(2,1)} %broadcast_select_fusion.1), channel_id=1, source_target_pairs={{3,6},{2,7},{18,20},{19,21}} | collective-permute-start | bytes 1572872 | tf_op jit(solution)/shard_map/ppermute | solution.py:168
  52.8 7.9 %collective-permute-start.10 = (bf16[1024,256]{1,0:T(8,128)(2,1)}, bf16[1024,256]{1,0:T(8,128)(2,1)}, u32[]{:S(2)}, u32[]{:S(2)}) collective-permute-start(bf16[1024,256]{1,0:T(8,128)(2,1)} %shard_map.29), channel_id=1, source_target_pairs={{4,6},{5,7}} | collective-permute-start | bytes 1572872 | tf_op jit(solution)/shard_map/ppermute | solution.py:168
  54.3 6.4 %collective-permute-start.13 = (bf16[1024,256]{1,0:T(8,128)(2,1)}, bf16[1024,256]{1,0:T(8,128)(2,1)}, u32[]{:S(2)}, u32[]{:S(2)}) collective-permute-start(bf16[1024,256]{1,0:T(8,128)(2,1)} %shard_map.29), channel_id=1, source_target_pairs={{5,6},{4,7}} | collective-permute-start | bytes 1572872 | tf_op jit(solution)/shard_map/ppermute | solution.py:168
  56.6 5.1 %collective-permute-start.11 = (bf16[1024,256]{1,0:T(8,128)(2,1)}, bf16[1024,256]{1,0:T(8,128)(2,1)}, u32[]{:S(2)}, u32[]{:S(2)}) collective-permute-start(bf16[1024,256]{1,0:T(8,128)(2,1)} %shard_map.29), channel_id=1, source_target_pairs={{4,2},{5,3}} | collective-permute-start | bytes 1572872 | tf_op jit(solution)/shard_map/ppermute | solution.py:168
  58.1 34.5 %collective-permute-start.12 = (bf16[1024,256]{1,0:T(8,128)(2,1)}, bf16[1024,256]{1,0:T(8,128)(2,1)}, u32[]{:S(2)}, u32[]{:S(2)}) collective-permute-start(bf16[1024,256]{1,0:T(8,128)(2,1)} %shard_map.29), channel_id=1, source_target_pairs={{4,0},{5,1}} | collective-permute-start | bytes 1572872 | tf_op jit(solution)/shard_map/ppermute | solution.py:168
  59.4 35.7 %collective-permute-start.8 = (bf16[1024,256]{1,0:T(8,128)(2,1)}, bf16[1024,256]{1,0:T(8,128)(2,1)}, u32[]{:S(2)}, u32[]{:S(2)}) collective-permute-start(bf16[1024,256]{1,0:T(8,128)(2,1)} %broadcast_select_fusion.1), channel_id=1, source_target_pairs={{2,0},{3,1},{18,16},{19,17}} | collective-permute-start | bytes 1572872 | tf_op jit(solution)/shard_map/ppermute | solution.py:168
  60.9 35.4 %collective-permute-start.15 = (bf16[512,256]{1,0:T(8,128)(2,1)S(1)}, bf16[512,256]{1,0:T(8,128)(2,1)S(1)}, u32[]{:S(2)}, u32[]{:S(2)}) collective-permute-start(bf16[512,256]{1,0:T(8,128)(2,1)S(1)} %get-tuple-element.21), channel_id=1, source_target_pairs={{6,22},{7,23}} | collective-permute-start | bytes 786440 | tf_op jit(solution)/shard_map/ppermute | solution.py:168
  93.7 8.0 %collective-permute-start.14 = (bf16[1024,256]{1,0:T(8,128)(2,1)S(1)}, bf16[1024,256]{1,0:T(8,128)(2,1)S(1)}, u32[]{:S(2)}, u32[]{:S(2)}) collective-permute-start(bf16[1024,256]{1,0:T(8,128)(2,1)S(1)} %select_select_fusion), channel_id=1, source_target_pairs={{0,16},{1,17},{2,18},{3,19},{4,20},{5,21},{6,22},{7,23}} | collective-permute-start | bytes 1572872 | tf_op jit(solution)/shard_map/ppermute | solution.py:168
  101.9 19.4 %collective-permute-start.17 = (bf16[2048,256]{1,0:T(8,128)(2,1)S(1)}, bf16[2048,256]{1,0:T(8,128)(2,1)S(1)}, u32[]{:S(2)}, u32[]{:S(2)}) collective-permute-start(bf16[2048,256]{1,0:T(8,128)(2,1)S(1)} %pad_maximum_fusion.refs_2_), channel_id=1, source_target_pairs={{1,0},{0,1},{3,2},{2,3},{5,4},{4,5},{7,6},{6,7},{17,16},{16,17},{1... | collective-permute-start | bytes 3145736 | tf_op jit(solution)/shard_map/ppermute | solution.py:168
  103.8 2.7 %collective-permute-start.18 = (bf16[512,256]{1,0:T(8,128)(2,1)S(1)}, bf16[512,256]{1,0:T(8,128)(2,1)S(1)}, u32[]{:S(2)}, u32[]{:S(2)}) collective-permute-start(bf16[512,256]{1,0:T(8,128)(2,1)S(1)} %broadcast_select_fusion.2), channel_id=1, source_target_pairs={{6,4},{7,5},{22,20},{23,21}} | collective-permute-start | bytes 786440 | tf_op jit(solution)/shard_map/ppermute | solution.py:168
  105.2 14.7 %collective-permute-start.20 = (bf16[512,256]{1,0:T(8,128)(2,1)S(1)}, bf16[512,256]{1,0:T(8,128)(2,1)S(1)}, u32[]{:S(2)}, u32[]{:S(2)}) collective-permute-start(bf16[512,256]{1,0:T(8,128)(2,1)S(1)} %broadcast_select_fusion.2), channel_id=1, source_target_pairs={{6,0},{7,1},{22,16},{23,17}} | collective-permute-start | bytes 786440 | tf_op jit(solution)/shard_map/ppermute | solution.py:168
  119.9 18.8 %collective-permute-start.16 = (bf16[2048,256]{1,0:T(8,128)(2,1)S(1)}, bf16[2048,256]{1,0:T(8,128)(2,1)S(1)}, u32[]{:S(2)}, u32[]{:S(2)}) collective-permute-start(bf16[2048,256]{1,0:T(8,128)(2,1)S(1)} %pad_maximum_fusion.refs_2_), channel_id=1, source_target_pairs={{0,8},{1,9},{2,10},{3,11},{4,12},{5,13},{6,14},{7,15},{16,24},{17,... | collective-permute-start | bytes 3145736 | tf_op jit(solution)/shard_map/ppermute | solution.py:168
  121.3 17.4 %collective-permute-start.21 = (bf16[2048,256]{1,0:T(8,128)(2,1)S(1)}, bf16[2048,256]{1,0:T(8,128)(2,1)S(1)}, u32[]{:S(2)}, u32[]{:S(2)}) collective-permute-start(bf16[2048,256]{1,0:T(8,128)(2,1)S(1)} %collective-permute-done.17.refs_4_), channel_id=1, source_target_pairs={{0,8},{1,9},{2,10},{3,11},{4,12},{5,13},{6,14},{7,15},{16,24},{17,... | collective-permute-start | bytes 3145736 | tf_op jit(solution)/shard_map/ppermute | solution.py:168
  122.6 8.7 %collective-permute-start.23 = (bf16[512,256]{1,0:T(8,128)(2,1)S(1)}, bf16[512,256]{1,0:T(8,128)(2,1)S(1)}, u32[]{:S(2)}, u32[]{:S(2)}) collective-permute-start(bf16[512,256]{1,0:T(8,128)(2,1)S(1)} %select_select_fusion.2), channel_id=1, source_target_pairs={{16,0},{17,1},{18,2},{19,3},{20,4},{21,5},{22,6},{23,7},{0,16},{1,... | collective-permute-start | bytes 786440 | tf_op jit(solution)/shard_map/ppermute | solution.py:168
  127.0 8.3 %collective-permute-start.22 = (bf16[512,256]{1,0:T(8,128)(2,1)S(1)}, bf16[512,256]{1,0:T(8,128)(2,1)S(1)}, u32[]{:S(2)}, u32[]{:S(2)}) collective-permute-start(bf16[512,256]{1,0:T(8,128)(2,1)S(1)} %select_select_fusion.2), channel_id=1, source_target_pairs={{1,0},{0,1},{3,2},{2,3},{5,4},{4,5},{7,6},{6,7},{17,16},{16,17},{1... | collective-permute-start | bytes 786440 | tf_op jit(solution)/shard_map/ppermute | solution.py:168
  135.4 11.2 %collective-permute-start.24 = (bf16[1536,256]{1,0:T(8,128)(2,1)S(1)}, bf16[1536,256]{1,0:T(8,128)(2,1)S(1)}, u32[]{:S(2)}, u32[]{:S(2)}) collective-permute-start(bf16[1536,256]{1,0:T(8,128)(2,1)S(1)} %pad_maximum_fusion.1.refs_2_), channel_id=1, source_target_pairs={{0,8},{1,9},{2,10},{3,11},{4,12},{5,13},{6,14},{7,15},{16,24},{17,... | collective-permute-start | bytes 2359304 | tf_op jit(solution)/shard_map/ppermute | solution.py:168
  136.7 8.5 %collective-permute-start.25 = (bf16[512,256]{1,0:T(8,128)(2,1)S(1)}, bf16[512,256]{1,0:T(8,128)(2,1)S(1)}, u32[]{:S(2)}, u32[]{:S(2)}) collective-permute-start(bf16[512,256]{1,0:T(8,128)(2,1)S(1)} %collective-permute-done.23), channel_id=1, source_target_pairs={{1,0},{0,1},{3,2},{2,3},{5,4},{4,5},{7,6},{6,7},{17,16},{16,17},{1... | collective-permute-start | bytes 786440 | tf_op jit(solution)/shard_map/ppermute | solution.py:168
  145.2 2.4 %collective-permute-start.26 = (bf16[512,256]{1,0:T(8,128)(2,1)S(1)}, bf16[512,256]{1,0:T(8,128)(2,1)S(1)}, u32[]{:S(2)}, u32[]{:S(2)}) collective-permute-start(bf16[512,256]{1,0:T(8,128)(2,1)S(1)} %collective-permute-done.25.refs_4_), channel_id=1, source_target_pairs={{0,8},{1,9},{2,10},{3,11},{4,12},{5,13},{6,14},{7,15},{16,24},{17,... | collective-permute-start | bytes 786440 | tf_op jit(solution)/shard_map/ppermute | solution.py:168
  (5 other events, 41.2 us)

commit v6 on v5

--- a/solution.py
+++ b/solution.py
@@ -239,13 +239,16 @@
 
         extra = NB // members
         start_places = [
-            functools.partial(lambda dc, q, at: q(at) * CORES + (at.core + dc) % CORES, dc, q)
-            for dc in range(CORES) for q in tree_places
-        ]
-        first = rhs_scen[:, :NB].reshape(-1, lanes, n_y, CORES, extra).transpose(0, 2, 3, 1, 4)
-        first = jnp.broadcast_to(
-            first[:, :, :, None], (first.shape[0], n_y, CORES, planes, lanes, extra)
-        ).reshape(first.shape[0], n_row * n_col, extra)
+            functools.partial(
+                lambda dc, dy, dm, at: ((at.y + dy) % n_y * CORES + (at.core + dc) % CORES) * lanes
+                + (at.lane + dm) % lanes,
+                dc, dy, dm,
+            )
+            for dc in range(CORES) for dy in range(n_y) for dm in range(lanes)
+        ]
+        first = rhs_scen[:, :NB].reshape(-1, n_row, 1, lanes, extra)
+        first = jnp.broadcast_to(first, (first.shape[0], n_row, planes, lanes, extra))
+        first = first.reshape(first.shape[0], n_row * n_col, extra)
         outgoing = jnp.concatenate(
             [rhs_scen.reshape(rhs_scen.shape[0], n_row * n_col, rows_here), first], axis=2
         )
@@ -282,68 +285,69 @@
 
         current, own1 = run(current, [(0, pieces)], [f32_rows, own_rows])
 
-        def to_y(own, k):
-            value = own
-            for t in range(1, n_y):
-                pairs = [(device(0, 0, k, m), device(t, 0, k, m)) for m in range(lanes)]
-                value = jnp.where(y == t, send(own, pairs), value)
-            return value
-
-        def pairs_to(k, z, ys):
-            return [(device(t, 0, k, m), device(t, 0, z, m)) for t in ys for m in range(lanes)]
-
-        every_y = range(n_y)
+        def to_plane(value, k, z):
+            return send(value, [(device(0, 0, k, m), device(0, 0, z, m)) for m in range(lanes)])
+
+        def to_y(value, t, zs):
+            return send(value, [(device(0, 0, z, m), device(t, 0, z, m)) for z in zs for m in range(lanes)])
 
         hop1 = ahead(own1, 1)
-        near1 = after(to_y(own1, 1), hop1[0])
+        own1 = after(own1, hop1[0])
+        got1 = {2: hop1[0], 3: to_plane(own1, 1, 3)}
         crossed = [
-            send(
-                near1,
-                [(device(0, 0, 1, (m + d) % lanes), device(0, 0, 3, m)) for m in range(lanes)]
-                + (pairs_to(1, 2, every_y[1:]) if d == 1 else []),
-            )
+            send(own1, [(device(0, 0, 1, (m + d) % lanes), device(0, 0, 3, m)) for m in range(lanes)])
             for d in range(1, lanes)
         ]
-        got1 = {z: send(near1, pairs_to(1, z, every_y)) for z in range(planes) if z not in (1, 2)}
-        got1[2] = jnp.where(y == 0, hop1[0], crossed[0])
+        for z in range(planes):
+            if z not in (1, 2, 3):
+                got1[z] = to_plane(own1, 1, z)
         (own2,) = run(current, [(1, lane_pieces(hop1))], [own_rows], 2)
         hop2 = ahead(own2, 2)
         (chained,) = run(current, [(1, lane_pieces([got1[3], *crossed]))], [f32_rows], 3)
-        cuts3 = run(chained, [(2, lane_pieces(hop2))], own_cuts, 3)
-        start2 = after(own2, chained)
-        got2 = {z: send(start2, pairs_to(2, z, [0])) for z in range(planes) if z not in (2, 3)}
-        got2[3] = hop2[0]
-
-        piece3 = scatter_y(cuts3, [3])
-        halves = []
-        for value, got in ((near1, got1), (own2, got2)):
-            for z, part in got.items():
-                value = jnp.where(plane == z, part, value)
-            halves.append(value)
-        near2 = after(halves[1], cuts3[0])
-        for t in every_y[1:]:
-            pairs = [(device(0, 0, z, m), device(t, 0, z, m)) for z in range(planes) for m in range(lanes)]
-            near2 = jnp.where(y == t, send(near2, pairs), near2)
-        near12 = after(jnp.concatenate([halves[0], near2], axis=0), piece3)
-        all12 = lane_gather(near12, [0], range(planes))
-        (piece3,) = along_planes(piece3, [3])
-        all12 = [near12] + [after(part, piece3) for part in all12[1:]]
-        other12 = [core_send(part) for part in all12]
-        *most3, last3 = plane_gather(piece3, [0])
-        most3 = jnp.concatenate(most3, axis=0)
-        other3 = core_send(most3)
-
-        def whole_pieces(first):
+        cuts3 = list(run(chained, [(2, lane_pieces(hop2))], own_cuts, 3))
+
+        near1 = own1
+        for z, part in got1.items():
+            near1 = jnp.where(plane == z, part, near1)
+        near1 = after(near1, chained)
+        for t in range(1, n_y):
+            near1 = jnp.where(y == t, to_y(near1, t, range(planes)), near1)
+        own2 = after(own2, chained)
+        cuts2 = [own2[t * cut : (t + 1) * cut] for t in range(n_y)]
+        cuts2 = cuts2[:1] + [to_y(cuts2[t], t, [2]) for t in range(1, n_y)]
+
+        cuts3 = cuts3[:1] + [to_y(cuts3[t], t, [3]) for t in range(1, n_y)]
+        piece = jnp.where(plane == 2, cuts2[0], cuts3[0])
+        for t in range(1, n_y):
+            piece = jnp.where(y == t, jnp.where(plane == 2, cuts2[t], cuts3[t]), piece)
+        near1 = after(near1, piece)
+        all1 = lane_gather(near1, [0], range(planes))
+        piece = jnp.concatenate(along_planes(piece, [2, 3]), axis=0)
+        other1 = [core_send(part) for part in all1]
+        pieces1 = [
+            (mine, other, 0, rows_here, lane_places[d]) for d, (mine, other) in enumerate(zip(all1, other1))
+        ]
+        (current,) = run(current, [(1, pieces1)], [f32_rows])
+        near = lane_gather(piece, [0], range(planes))
+        far = [after(got, current) for got in y_gather(piece, [0])[1:]]
+        most = jnp.concatenate(near + far, axis=0)
+        last = [part for got in far for part in lane_gather(got, [0], range(planes))[1:]]
+        other_most = core_send(most)
+        last = last[0] if len(last) == 1 else jnp.concatenate(last, axis=0)
+        other_last = core_send(last)
+        places_most = tree_places[:lanes] + tree_places[lanes::lanes]
+        places_last = [p for i, p in enumerate(tree_places) if i >= lanes and i % lanes]
+
+        def tree_pieces(first):
             return [
-                (mine, other, first * rows_here, rows_here, lane_places[d])
-                for d, (mine, other) in enumerate(zip(all12, other12))
+                (mine, other, i * 2 * cut + first, cut, place)
+                for mine, other, places in ((most, other_most, places_most), (last, other_last, places_last))
+                for i, place in enumerate(places)
             ]
 
-        (current,) = run(current, [(1, whole_pieces(0)), (2, whole_pieces(1))], [f32_rows])
-        other_last3 = core_send(after(last3, current))
-        pieces3 = [(most3, other3, i * cut, cut, place) for i, place in enumerate(tree_places[:-1])]
-        pieces3.append((last3, other_last3, 0, cut, tree_places[-1]))
-        (out,) = run(current, [(3, pieces3)], [(jnp.float32, 0, rows_here, True)])
+        (out,) = run(
+            current, [(2, tree_pieces(0)), (3, tree_pieces(cut))], [(jnp.float32, 0, rows_here, True)]
+        )
         return out
 
     return on_device

time: 153 us -> 151 us (0.987)
  the two profiles are of different devices: /device:TPU:0 before, /device:TPU:25 now
where the time goes in v6:
time: 151 us
  waiting for transfers between devices  79.8 us (53%)
  starting transfers between devices  24.4 us (16%)
  blocking collectives  22.5 us (15%)
  Pallas kernels  17.9 us (12%)
  other arithmetic  4.5 us (3%)
    ppermute x25, waiting for transfers between devices, send(): return lax.ppermute(value, AXES, pairs)  79.8 us
    ppermute x25, starting transfers between devices, send(): return lax.ppermute(value, AXES, pairs)  24.4 us
    all_to_all x1, blocking collectives, on_device(): lax.all_to_all(outgoing, AXES, split_axis=1, concat_axis=0, tiled=True)  22.5 us
    pallas_call x6, Pallas kernels, steps(): pl.pallas_call(functools.partial(step_kernel, tuple(plan), len(arrays), t...  17.9 us
  transfers between devices with their start and end apart: 25, of which 7 were waited for; matrix products, arithmetic and copies ran while one was open for 2% of the time, Pallas kernels for 3%

profile of v6, /device:TPU:25, one launch (start us, length us, event | category | flops | bytes accessed | tf_op | source)
XLA Modules:
  0.0 150.6 jit_solution(1305678430520676487)
XLA Ops:
  0.8 1.1 pad_maximum_fusion.1
  1.9 22.5 %all_to_all.15 = bf16[8,32,1280]{2,0,1:T(8,128)(2,1)S(1)} all-to-all(bf16[8,32,1280]{2,0,1:T(8,128)(2,1)S(1)} %pad_maximum_fusion.1), channel_id=1, replica_groups=mesh['row'=4,'col'=8] {'row','col'}, dimensions={1} | all-to-all | bytes 1310720 | tf_op jit(solution)/shard_map/all_to_all | solution.py:255
  24.4 1.2 collective-permute-start.1
  25.7 3.4 %collective-permute-done.1 = bf16[256,256]{1,0:T(8,128)(2,1)S(1)} collective-permute-done((bf16[256,256]{1,0:T(8,128)(2,1)S(1)}, bf16[256,256]{1,0:T(8,128)(2,1)S(1)}, u32[]{:S(2)}, u32[]{:S(2)}) %collective-permute-start.1) | collective-permute-done | bytes 131104 | tf_op jit(solution)/shard_map/ppermute | solution.py:168
  30.0 3.0 %collective-permute-done.2 = bf16[256,256]{1,0:T(8,128)(2,1)S(1)} collective-permute-done((bf16[256,256]{1,0:T(8,128)(2,1)S(1)}, bf16[256,256]{1,0:T(8,128)(2,1)S(1)}, u32[]{:S(2)}, u32[]{:S(2)}) %collective-permute-start.2) | collective-permute-done | bytes 131104 | tf_op jit(solution)/shard_map/ppermute | solution.py:168
  33.0 2.5 %collective-permute-start.3 = (bf16[1024,256]{1,0:T(8,128)(2,1)S(1)}, bf16[1024,256]{1,0:T(8,128)(2,1)S(1)}, u32[]{:S(2)}, u32[]{:S(2)}) collective-permute-start(bf16[1024,256]{1,0:T(8,128)(2,1)S(1)} %pad_maximum_fusion.2.refs_2_), channel_id=1, source_target_pairs={{8,0},{9,1},{10,2},{11,3},{12,4},{13,5},{14,6},{15,7},{0,8},{1,9},... | collective-permute-start | bytes 1572872 | tf_op jit(solution)/shard_map/ppermute | solution.py:168
  35.8 1.2 collective-permute-done.3.refs_3_
  37.0 6.2 %shard_map.28 = (f32[1024,256]{1,0:T(8,128)S(1)}, bf16[1024,256]{1,0:T(8,128)(2,1)}) custom-call(f32[1024,256]{1,0:T(8,128)S(1)} %convert_bitcast_fusion.refs_0_, bf16[1024,8192]{1,0:T(8,128)(2,1)} %refs_1_.11, bf16[1024,256]{1,0:T(8,128)(2,1)S(1)} %pad_maximum_fusion.2.refs_2_, bf16[1024,256]{1,0:T(8,128)(2,1)S(1)} %collective-permute-done.3.refs_3_), custom_call_target="tpu_custom_call" | custom-call | flops 1073741824 | bytes 2097152 | tf_op jit(solution)/shard_map/pallas_call | solution.py:121
  44.6 1.5 collective-permute-start.7
  46.8 1.5 collective-permute-start.5
  49.0 1.5 collective-permute-start.11
  50.7 1.4 collective-permute-start.10
  52.0 1.9 %select_select_fusion = bf16[1024,256]{1,0:T(8,128)(2,1)} fusion(bf16[1024,256]{1,0:T(8,128)(2,1)} %collective-permute-done.5, bf16[1024,256]{1,0:T(8,128)(2,1)S(1)} %collective-permute-done.6.refs_2_, bf16[1024,256]{1,0:T(8,128)(2,1)S(1)} %collective-permute-done.4.refs_2_, bf16[1024,256]{1,0:T(8,128)(2,1)} %get-tuple-element.16, pred[]{:T(512)S(6)} %eq.26, ...), kind=kLoop, calls=%fused_computation.5 | loop fusion | flops 786432 | bytes 2621443 | tf_op jit(solution)/shard_map/jit(_where)/select_n | solution.py:311
  54.0 1.5 collective-permute-start.8
  58.4 1.1 broadcast_select_fusion.refs_2_
  60.2 1.3 collective-permute-start.14
  61.6 1.3 collective-permute-start.16
  64.4 41.7 %collective-permute-done.14.refs_3_ = bf16[1024,256]{1,0:T(8,128)(2,1)S(1)} collective-permute-done((bf16[1024,256]{1,0:T(8,128)(2,1)S(1)}, bf16[1024,256]{1,0:T(8,128)(2,1)S(1)}, u32[]{:S(2)}, u32[]{:S(2)}) %collective-permute-start.14) | collective-permute-done | bytes 524320 | tf_op jit(solution)/shard_map/ppermute | solution.py:168
  106.1 7.7 %collective-permute-done.16.refs_5_ = bf16[1024,256]{1,0:T(8,128)(2,1)S(1)} collective-permute-done((bf16[1024,256]{1,0:T(8,128)(2,1)S(1)}, bf16[1024,256]{1,0:T(8,128)(2,1)S(1)}, u32[]{:S(2)}, u32[]{:S(2)}) %collective-permute-start.16) | collective-permute-done | bytes 524320 | tf_op jit(solution)/shard_map/ppermute | solution.py:168
  113.8 4.0 %shard_map.32.refs_0_ = f32[1024,256]{1,0:T(8,128)S(1)} custom-call(f32[1024,256]{1,0:T(8,128)S(1)} %get-tuple-element.14.refs_0_, bf16[1024,8192]{1,0:T(8,128)(2,1)} %refs_1_.11, bf16[1024,256]{1,0:T(8,128)(2,1)S(1)} %broadcast_select_fusion.refs_2_, bf16[1024,256]{1,0:T(8,128)(2,1)S(1)} %collective-permute-done.14.refs_3_, ...), custom_call_target="tpu_custom_call" | custom-call | flops 1073741824 | bytes 2097152 | tf_op jit(solution)/shard_map/pallas_call | solution.py:121
  118.0 1.3 collective-permute-start.22
  120.0 1.3 collective-permute-start.24
  121.3 21.9 %collective-permute-done.24.refs_5_ = bf16[1024,256]{1,0:T(8,128)(2,1)S(1)} collective-permute-done((bf16[1024,256]{1,0:T(8,128)(2,1)S(1)}, bf16[1024,256]{1,0:T(8,128)(2,1)S(1)}, u32[]{:S(2)}, u32[]{:S(2)}) %collective-permute-start.24) | collective-permute-done | bytes 524320 | tf_op jit(solution)/shard_map/ppermute | solution.py:168
  143.2 7.4 %shard_map.33 = f32[1024,256]{1,0:T(8,128)} custom-call(f32[1024,256]{1,0:T(8,128)S(1)} %shard_map.32.refs_0_, bf16[1024,8192]{1,0:T(8,128)(2,1)} %refs_1_.11, bf16[3072,256]{1,0:T(8,128)(2,1)S(1)} %pad_maximum_fusion.refs_2_, bf16[3072,256]{1,0:T(8,128)(2,1)S(1)} %collective-permute-done.22.refs_3_, bf16[1024,256]{1,0:T(8,128)(2,1)S(1)} %collective-permute-done.23.refs_4_, ...), custom_call_target="tpu_custom_call" | custom-call | flops 2147483648 | bytes 2097152 | tf_op jit(solution)/shard_map/pallas_call | solution.py:121
  (49 shorter events, 11.0 us)
Async XLA Ops:
  24.4 4.7 %collective-permute-start.1 = (bf16[256,256]{1,0:T(8,128)(2,1)S(1)}, bf16[256,256]{1,0:T(8,128)(2,1)S(1)}, u32[]{:S(2)}, u32[]{:S(2)}) collective-permute-start(bf16[256,256]{1,0:T(8,128)(2,1)S(1)} %bitcast.15), channel_id=1, source_target_pairs={{16,0},{17,1},{18,2},{19,3},{20,4},{21,5},{22,6},{23,7},{24,8},{25... | collective-permute-start | bytes 393224 | tf_op jit(solution)/shard_map/ppermute | solution.py:168
  25.7 4.3 %collective-permute-start = (bf16[256,256]{1,0:T(8,128)(2,1)S(1)}, bf16[256,256]{1,0:T(8,128)(2,1)S(1)}, u32[]{:S(2)}, u32[]{:S(2)}) collective-permute-start(bf16[256,256]{1,0:T(8,128)(2,1)S(1)} %bitcast.16), channel_id=1, source_target_pairs={{1,0},{0,1},{3,2},{2,3},{5,4},{4,5},{7,6},{6,7},{9,8},{8,9},{11,10... | collective-permute-start | bytes 393224 | tf_op jit(solution)/shard_map/ppermute | solution.py:168
  29.1 3.8 %collective-permute-start.2 = (bf16[256,256]{1,0:T(8,128)(2,1)S(1)}, bf16[256,256]{1,0:T(8,128)(2,1)S(1)}, u32[]{:S(2)}, u32[]{:S(2)}) collective-permute-start(bf16[256,256]{1,0:T(8,128)(2,1)S(1)} %collective-permute-done.1), channel_id=1, source_target_pairs={{1,0},{0,1},{3,2},{2,3},{5,4},{4,5},{7,6},{6,7},{9,8},{8,9},{11,10... | collective-permute-start | bytes 393224 | tf_op jit(solution)/shard_map/ppermute | solution.py:168
  33.0 4.0 %collective-permute-start.3 = (bf16[1024,256]{1,0:T(8,128)(2,1)S(1)}, bf16[1024,256]{1,0:T(8,128)(2,1)S(1)}, u32[]{:S(2)}, u32[]{:S(2)}) collective-permute-start(bf16[1024,256]{1,0:T(8,128)(2,1)S(1)} %pad_maximum_fusion.2.refs_2_), channel_id=1, source_target_pairs={{8,0},{9,1},{10,2},{11,3},{12,4},{13,5},{14,6},{15,7},{0,8},{1,9},... | collective-permute-start | bytes 1572872 | tf_op jit(solution)/shard_map/ppermute | solution.py:168
  43.2 1.4 collective-permute-start.4
  43.9 4.4 %collective-permute-start.9 = (bf16[1024,256]{1,0:T(8,128)(2,1)}, bf16[1024,256]{1,0:T(8,128)(2,1)S(1)}, u32[]{:S(2)}, u32[]{:S(2)}) collective-permute-start(bf16[1024,256]{1,0:T(8,128)(2,1)} %get-tuple-element.16), channel_id=1, source_target_pairs={{3,4},{2,5}} | collective-permute-start | bytes 1572872 | tf_op jit(solution)/shard_map/ppermute | solution.py:168
  44.6 5.9 %collective-permute-start.7 = (bf16[1024,256]{1,0:T(8,128)(2,1)}, bf16[1024,256]{1,0:T(8,128)(2,1)}, u32[]{:S(2)}, u32[]{:S(2)}) collective-permute-start(bf16[1024,256]{1,0:T(8,128)(2,1)} %get-tuple-element.16), channel_id=1, source_target_pairs={{3,6},{2,7}} | collective-permute-start | bytes 1572872 | tf_op jit(solution)/shard_map/ppermute | solution.py:168
  46.1 4.5 %collective-permute-start.6 = (bf16[1024,256]{1,0:T(8,128)(2,1)}, bf16[1024,256]{1,0:T(8,128)(2,1)S(1)}, u32[]{:S(2)}, u32[]{:S(2)}) collective-permute-start(bf16[1024,256]{1,0:T(8,128)(2,1)} %get-tuple-element.16), channel_id=1, source_target_pairs={{2,6},{3,7}} | collective-permute-start | bytes 1572872 | tf_op jit(solution)/shard_map/ppermute | solution.py:168
  46.8 5.3 %collective-permute-start.5 = (bf16[1024,256]{1,0:T(8,128)(2,1)}, bf16[1024,256]{1,0:T(8,128)(2,1)}, u32[]{:S(2)}, u32[]{:S(2)}) collective-permute-start(bf16[1024,256]{1,0:T(8,128)(2,1)} %get-tuple-element.16), channel_id=1, source_target_pairs={{2,0},{3,1}} | collective-permute-start | bytes 1572872 | tf_op jit(solution)/shard_map/ppermute | solution.py:168
  48.3 7.1 %collective-permute-start.12 = (bf16[1024,256]{1,0:T(8,128)(2,1)S(1)}, bf16[1024,256]{1,0:T(8,128)(2,1)S(1)}, u32[]{:S(2)}, u32[]{:S(2)}) collective-permute-start(bf16[1024,256]{1,0:T(8,128)(2,1)S(1)} %shard_map.30), channel_id=1, source_target_pairs={{5,6},{4,7}} | collective-permute-start | bytes 1572872 | tf_op jit(solution)/shard_map/ppermute | solution.py:168
  49.0 6.4 %collective-permute-start.11 = (bf16[1024,256]{1,0:T(8,128)(2,1)S(1)}, bf16[1024,256]{1,0:T(8,128)(2,1)}, u32[]{:S(2)}, u32[]{:S(2)}) collective-permute-start(bf16[1024,256]{1,0:T(8,128)(2,1)S(1)} %shard_map.30), channel_id=1, source_target_pairs={{4,6},{5,7}} | collective-permute-start | bytes 1572872 | tf_op jit(solution)/shard_map/ppermute | solution.py:168
  50.7 5.6 %collective-permute-start.10 = (bf16[512,256]{1,0:T(8,128)(2,1)S(1)}, bf16[512,256]{1,0:T(8,128)(2,1)}, u32[]{:S(2)}, u32[]{:S(2)}) collective-permute-start(bf16[512,256]{1,0:T(8,128)(2,1)S(1)} %slice.18), channel_id=1, source_target_pairs={{4,20},{5,21}} | collective-permute-start | bytes 786440 | tf_op jit(solution)/shard_map/ppermute | solution.py:168
  54.0 4.4 %collective-permute-start.8 = (bf16[1024,256]{1,0:T(8,128)(2,1)}, bf16[1024,256]{1,0:T(8,128)(2,1)}, u32[]{:S(2)}, u32[]{:S(2)}) collective-permute-start(bf16[1024,256]{1,0:T(8,128)(2,1)} %select_select_fusion), channel_id=1, source_target_pairs={{0,16},{1,17},{2,18},{3,19},{4,20},{5,21},{6,22},{7,23}} | collective-permute-start | bytes 1572872 | tf_op jit(solution)/shard_map/ppermute | solution.py:168
  55.5 0.7 collective-permute-start.13
  56.3 5.2 %collective-permute-start.19 = (bf16[512,256]{1,0:T(8,128)(2,1)S(1)}, bf16[512,256]{1,0:T(8,128)(2,1)S(1)}, u32[]{:S(2)}, u32[]{:S(2)}) collective-permute-start(bf16[512,256]{1,0:T(8,128)(2,1)S(1)} %select_select_fusion.3), channel_id=1, source_target_pairs={{4,6},{5,7},{20,22},{21,23},{6,0},{7,1},{22,16},{23,17}} | collective-permute-start | bytes 786440 | tf_op jit(solution)/shard_map/ppermute | solution.py:168
  57.0 4.5 %collective-permute-start.18 = (bf16[512,256]{1,0:T(8,128)(2,1)S(1)}, bf16[512,256]{1,0:T(8,128)(2,1)S(1)}, u32[]{:S(2)}, u32[]{:S(2)}) collective-permute-start(bf16[512,256]{1,0:T(8,128)(2,1)S(1)} %select_select_fusion.3), channel_id=1, source_target_pairs={{4,0},{5,1},{20,16},{21,17},{6,2},{7,3},{22,18},{23,19}} | collective-permute-start | bytes 786440 | tf_op jit(solution)/shard_map/ppermute | solution.py:168
  57.7 3.8 %collective-permute-start.17 = (bf16[512,256]{1,0:T(8,128)(2,1)S(1)}, bf16[512,256]{1,0:T(8,128)(2,1)S(1)}, u32[]{:S(2)}, u32[]{:S(2)}) collective-permute-start(bf16[512,256]{1,0:T(8,128)(2,1)S(1)} %select_select_fusion.3), channel_id=1, source_target_pairs={{4,2},{5,3},{20,18},{21,19},{6,4},{7,5},{22,20},{23,21}} | collective-permute-start | bytes 786440 | tf_op jit(solution)/shard_map/ppermute | solution.py:168
  59.5 2.1 %collective-permute-start.15 = (bf16[1024,256]{1,0:T(8,128)(2,1)S(1)}, bf16[1024,256]{1,0:T(8,128)(2,1)S(1)}, u32[]{:S(2)}, u32[]{:S(2)}) collective-permute-start(bf16[1024,256]{1,0:T(8,128)(2,1)S(1)} %broadcast_select_fusion.refs_2_), channel_id=1, source_target_pairs={{1,0},{0,1},{3,2},{2,3},{5,4},{4,5},{7,6},{6,7},{17,16},{16,17},{1... | collective-permute-start | bytes 1572872 | tf_op jit(solution)/shard_map/ppermute | solution.py:168
  60.2 45.9 %collective-permute-start.14 = (bf16[1024,256]{1,0:T(8,128)(2,1)S(1)}, bf16[1024,256]{1,0:T(8,128)(2,1)S(1)}, u32[]{:S(2)}, u32[]{:S(2)}) collective-permute-start(bf16[1024,256]{1,0:T(8,128)(2,1)S(1)} %broadcast_select_fusion.refs_2_), channel_id=1, source_target_pairs={{0,8},{1,9},{2,10},{3,11},{4,12},{5,13},{6,14},{7,15},{16,24},{17,... | collective-permute-start | bytes 1572872 | tf_op jit(solution)/shard_map/ppermute | solution.py:168
  61.6 52.2 %collective-permute-start.16 = (bf16[1024,256]{1,0:T(8,128)(2,1)S(1)}, bf16[1024,256]{1,0:T(8,128)(2,1)S(1)}, u32[]{:S(2)}, u32[]{:S(2)}) collective-permute-start(bf16[1024,256]{1,0:T(8,128)(2,1)S(1)} %collective-permute-done.15.refs_4_), channel_id=1, source_target_pairs={{0,8},{1,9},{2,10},{3,11},{4,12},{5,13},{6,14},{7,15},{16,24},{17,... | collective-permute-start | bytes 1572872 | tf_op jit(solution)/shard_map/ppermute | solution.py:168
  63.0 54.9 %collective-permute-start.21 = (bf16[1024,256]{1,0:T(8,128)(2,1)S(1)}, bf16[1024,256]{1,0:T(8,128)(2,1)S(1)}, u32[]{:S(2)}, u32[]{:S(2)}) collective-permute-start(bf16[1024,256]{1,0:T(8,128)(2,1)S(1)} %pad_maximum_fusion.3), channel_id=1, source_target_pairs={{16,0},{17,1},{18,2},{19,3},{20,4},{21,5},{22,6},{23,7},{0,16},{1,... | collective-permute-start | bytes 1572872 | tf_op jit(solution)/shard_map/ppermute | solution.py:168
  63.7 54.2 %collective-permute-start.20 = (bf16[1024,256]{1,0:T(8,128)(2,1)S(1)}, bf16[1024,256]{1,0:T(8,128)(2,1)S(1)}, u32[]{:S(2)}, u32[]{:S(2)}) collective-permute-start(bf16[1024,256]{1,0:T(8,128)(2,1)S(1)} %pad_maximum_fusion.3), channel_id=1, source_target_pairs={{1,0},{0,1},{3,2},{2,3},{5,4},{4,5},{7,6},{6,7},{17,16},{16,17},{1... | collective-permute-start | bytes 1572872 | tf_op jit(solution)/shard_map/ppermute | solution.py:168
  118.0 25.2 %collective-permute-start.22 = (bf16[3072,256]{1,0:T(8,128)(2,1)S(1)}, bf16[3072,256]{1,0:T(8,128)(2,1)S(1)}, u32[]{:S(2)}, u32[]{:S(2)}) collective-permute-start(bf16[3072,256]{1,0:T(8,128)(2,1)S(1)} %pad_maximum_fusion.refs_2_), channel_id=1, source_target_pairs={{0,8},{1,9},{2,10},{3,11},{4,12},{5,13},{6,14},{7,15},{16,24},{17,... | collective-permute-start | bytes 4718600 | tf_op jit(solution)/shard_map/ppermute | solution.py:168
  120.0 23.2 %collective-permute-start.24 = (bf16[1024,256]{1,0:T(8,128)(2,1)S(1)}, bf16[1024,256]{1,0:T(8,128)(2,1)S(1)}, u32[]{:S(2)}, u32[]{:S(2)}) collective-permute-start(bf16[1024,256]{1,0:T(8,128)(2,1)S(1)} %collective-permute-done.23.refs_4_), channel_id=1, source_target_pairs={{0,8},{1,9},{2,10},{3,11},{4,12},{5,13},{6,14},{7,15},{16,24},{17,... | collective-permute-start | bytes 1572872 | tf_op jit(solution)/shard_map/ppermute | solution.py:168
  (1 other events, 0.7 us)

commit v7 on v0

v7 whole, which is shorter than its diff:
```python
import functools

import jax
import jax.numpy as jnp
from jax import lax
from jax.experimental import pallas as pl
from jax.experimental.pallas import tpu as pltpu
from jax.sharding import PartitionSpec as P

NB = 2048
STEPS = 4
AXES = ("row", "col")
CORES = 2
DEPTH = 512
KERNEL_VMEM = 40 * 1024 * 1024


def after(value, *others):
    return lax.optimization_barrier((value, *others))[0]


class Place:
    def __init__(self, n_col, lanes):
        row, col = lax.axis_index("row"), lax.axis_index("col")
        self.y, self.core = row // CORES, row % CORES
        self.plane, self.lane = col // lanes, col % lanes
        self.block = (row * n_col + col) // lanes


def step_kernel(terms, handed, n_arrays, outs, where_am_i, only, *refs):
    current, panels = refs[:2]
    arrays = refs[2 : 2 + n_arrays]
    results = refs[2 + n_arrays : 2 + n_arrays + len(outs)]
    current_here, panels_here, held, sems, piece_sems, current_sem, out_sem = refs[2 + n_arrays + len(outs) :]
    rows = current.shape[0]
    depth = min(DEPTH, NB)
    chunks = NB // depth
    here = where_am_i()

    def work():
        copies = []
        for t, (_, pieces) in enumerate(terms):
            for array, first, size, place in pieces:
                start = pl.multiple_of(place(here) * size, size)
                copy = pltpu.make_async_copy(
                    arrays[array].at[pl.ds(first, size), :],
                    held.at[t, pl.ds(start, size), :],
                    piece_sems.at[len(copies)],
                )
                copy.start()
                copies.append(copy)

        def panel_copy(t, i):
            k = terms[t][0]
            return pltpu.make_async_copy(
                panels.at[:, pl.ds(k * NB + i * depth, depth)], panels_here.at[t, i], sems.at[t, i]
            )

        for t in range(len(terms)):
            for i in range(chunks):
                panel_copy(t, i).start()
        current_copy = pltpu.make_async_copy(current, current_here, current_sem)
        current_copy.start()
        for copy in copies:
            copy.wait()
        current_copy.wait()
        for t, (k, _) in enumerate(terms):
            own = here.block == k
            for i in range(chunks):
                panel_copy(t, i).wait()
                part = jnp.dot(
                    panels_here[t, i], held[t, pl.ds(i * depth, depth), :], preferred_element_type=jnp.float32
                )
                now = current_here[...]
                current_here[...] = jnp.where(own, part if i == 0 else now + part, now - part)
        sent = []
        for o, (dtype, first, size, far) in enumerate(outs):
            if far:
                sent.append(pltpu.make_async_copy(current_here.at[pl.ds(first, size), :], results[o], out_sem))
                sent[-1].start()
            else:
                results[o][...] = current_here[pl.ds(first, size), :].astype(dtype)
        for out in sent:
            out.wait()

    if only is None:
        work()
    else:
        pl.when(here.block == only)(work)
    for block, array in handed:

        def hand(array=array):
            copies = [
                pltpu.make_async_copy(arrays[array].at[pl.ds(first, size), :], results[o], piece_sems.at[o])
                for o, (_, first, size, _) in enumerate(outs)
            ]
            for copy in copies:
                copy.start()
            for copy in copies:
                copy.wait()

        pl.when(here.block == block)(hand)


def steps(current, factor_panels, terms, outs, where_am_i, only=None, handed=()):
    rows, scenarios = current.shape
    arrays = []

    def index(array):
        for i, other in enumerate(arrays):
            if other is array:
                return i
        arrays.append(array)
        return len(arrays) - 1

    plan = tuple(
        (k, tuple((index(array), first, size, place) for array, first, size, place in pieces)) for k, pieces in terms
    )
    handed = tuple((block, index(array)) for block, array in handed)
    n_terms = len(terms)
    depth = min(DEPTH, NB)
    n_pieces = max(sum(len(pieces) for _, pieces in terms), len(outs))
    anywhere = pl.BlockSpec(memory_space=pl.ANY)
    return pl.pallas_call(
        functools.partial(step_kernel, plan, handed, len(arrays), tuple(outs), where_am_i, only),
        in_specs=[anywhere] * (2 + len(arrays)),
        out_specs=[anywhere if out[3] else pl.BlockSpec(memory_space=pltpu.VMEM) for out in outs],
        out_shape=[jax.ShapeDtypeStruct((size, scenarios), dtype) for dtype, _, size, _ in outs],
        scratch_shapes=[
            pltpu.VMEM((rows, scenarios), jnp.float32),
            pltpu.VMEM((n_terms, NB // depth, rows, depth), jnp.bfloat16),
            pltpu.VMEM((n_terms, NB, scenarios), jnp.bfloat16),
            pltpu.SemaphoreType.DMA((n_terms, NB // depth)),
            pltpu.SemaphoreType.DMA((n_pieces,)),
            pltpu.SemaphoreType.DMA,
            pltpu.SemaphoreType.DMA,
        ],
        compiler_params=pltpu.CompilerParams(vmem_limit_bytes=KERNEL_VMEM),
        cost_estimate=pl.CostEstimate(
            flops=2 * rows * NB * scenarios * n_terms,
            bytes_accessed=8 * rows * scenarios,
            transcendentals=0,
        ),
    )(current, factor_panels, *arrays)


def make_on_device(n_row, n_col):
    def on_device(rhs_scen, factor_panels):
        rows_here = factor_panels.shape[0]
        lanes = NB // rows_here
        planes = n_col // lanes
        n_y = n_row // CORES
        members = n_row * lanes
        where_am_i = functools.partial(Place, n_col, lanes)
        here = where_am_i()
        core, plane = here.core, here.plane

        def device(y, core, plane, lane):
            return (y * CORES + core) * n_col + plane * lanes + lane

        def send(value, pairs):
            return lax.ppermute(value, AXES, pairs)

        def run(current, terms, outs, only=None, handed=()):
            return steps(current, factor_panels, terms, outs, where_am_i, only, handed)

        def ahead(own, k):
            return [
                send(own, [(device(0, 0, k, (m + d) % lanes), device(0, 0, k + 1, m)) for m in range(lanes)])
                for d in range(lanes)
            ]

        along_x = [(0, d) for d in range(1, lanes)]
        along_y = [(d, 0) for d in range(1, n_y)]
        first_0, first_1 = along_x + along_y, along_y + along_x
        across = [(dy, dm) for dy, _ in along_y for _, dm in along_x]
        offsets = [((0, 0), (0, 0)), *zip(first_0, first_1), *zip(across, across)]

        def plane_gather(value):
            def pairs(c, step):
                return [
                    (device((t + step[0]) % n_y, c, z, (m + step[1]) % lanes), device(t, c, z, m))
                    for t in range(n_y) for z in range(planes) for m in range(lanes)
                ]

            got = [send(value, pairs(0, a) + pairs(1, b)) for a, b in zip(first_0, first_1)]
            last = []
            for dy, dm in across:
                a, b = first_0.index((dy, 0)), first_1.index((0, dm))
                payload = got[a] if a == b else jnp.where(core == 0, got[a], got[b])
                last.append(send(payload, pairs(0, (0, dm)) + pairs(1, (dy, 0))))
            return jnp.concatenate([value, *got, *last], axis=0)

        def core_exchange(value):
            pairs = [
                (device(t, 1 - c, z, m), device(t, c, z, m))
                for t in range(n_y) for c in range(CORES) for z in range(planes) for m in range(lanes)
            ]
            return send(value, pairs)

        def gathered_pieces(mine, other, first, size, stride, number):
            def place(offset, own, at):
                c = at.core if own else 1 - at.core
                a, b = (number((at.y + dy) % n_y, c, (at.lane + dm) % lanes) for dy, dm in offset)
                return a if offset[0] == offset[1] else jnp.where(c == 0, a, b)

            return [
                (array, i * stride + first, size, functools.partial(place, offset, array is mine))
                for array in (mine, other) for i, offset in enumerate(offsets)
            ]

        def lane_pieces(parts):
            return [
                (part, 0, rows_here, functools.partial(lambda d, at: (at.lane + d) % lanes, d))
                for d, part in enumerate(parts)
            ]

        f32_rows = (jnp.float32, 0, rows_here, False)
        own_rows = (jnp.bfloat16, 0, rows_here, False)
        cut = rows_here // n_row
        own_cuts = [(jnp.bfloat16, t * cut, cut, False) for t in range(n_row)]

        extra = NB // members
        first = rhs_scen[:, :NB].reshape(-1, n_row, 1, lanes, extra)
        first = jnp.broadcast_to(first, (first.shape[0], n_row, planes, lanes, extra))
        first = first.reshape(first.shape[0], n_row * n_col, extra)
        outgoing = jnp.concatenate(
            [rhs_scen.reshape(rhs_scen.shape[0], n_row * n_col, rows_here), first], axis=2
        )
        regrouped = lax.all_to_all(outgoing, AXES, split_axis=1, concat_axis=0, tiled=True)
        regrouped = regrouped.reshape(-1, rows_here + extra)
        current = jnp.transpose(regrouped[:, :rows_here]).astype(jnp.float32)
        whole = plane_gather(jnp.transpose(regrouped[:, rows_here:]))
        pieces = gathered_pieces(
            whole, core_exchange(whole), 0, extra, extra, lambda y, c, m: (y * CORES + c) * lanes + m
        )
        current, own1 = run(current, [(0, pieces)], [f32_rows, own_rows])

        hop1 = ahead(own1, 1)
        start1 = after(own1, hop1[0])
        at_3 = [
            send(start1, [(device(0, 0, 1, (m + d) % lanes), device(0, 0, 3, m)) for m in range(lanes)])
            for d in range(lanes)
        ]
        (own2,) = run(current, [(1, lane_pieces(hop1))], [own_rows], 2)
        hop2 = ahead(own2, 2)
        (chained,) = run(current, [(1, lane_pieces(at_3))], [f32_rows], 3)
        cuts = run(chained, [(2, lane_pieces(hop2))], own_cuts, 3, [(1, own1), (2, own2)])

        piece = cuts[0]
        for t in range(1, n_row):
            pairs = [
                (device(0, 0, k, m), device(t // CORES, t % CORES, k, m)) for k in range(1, STEPS) for m in range(lanes)
            ]
            piece = jnp.where(here.y * CORES + core == t, send(cuts[t], pairs), piece)
        got = [
            send(
                piece,
                [
                    (device(t, c, k, m), device(t, c, (k + d) % planes, m))
                    for k in range(1, STEPS) for t in range(n_y) for c in range(CORES) for m in range(lanes)
                ],
            )
            for d in range(1, planes)
        ]
        three = []
        for k in range(1, STEPS):
            value = piece
            for d in range(1, planes):
                value = jnp.where(plane == (k + d) % planes, got[d - 1], value)
            three.append(value)
        whole = plane_gather(jnp.concatenate(three, axis=0))
        other = core_exchange(whole)
        terms = [
            (
                k,
                gathered_pieces(
                    whole, other, (k - 1) * cut, cut, (STEPS - 1) * cut, lambda y, c, m: m * n_row + y * CORES + c
                ),
            )
            for k in range(1, STEPS)
        ]
        (out,) = run(current, terms, [(jnp.float32, 0, rows_here, True)])
        return out

    return on_device


def solution(mesh):
    placed = (P(AXES, None), P(AXES, None))
    on_device = make_on_device(mesh.shape["row"], mesh.shape["col"])
    return jax.shard_map(
        on_device, mesh=mesh, in_specs=placed, out_specs=P(AXES, None), check_vma=False
    )
```

time: 579 us -> 145 us (0.25)
  waiting for transfers between devices: 532 us -> 79 us
  blocking collectives: 0 us -> 26.3 us
  matrix products: 23.5 us -> 0 us
  Pallas kernels: 0 us -> 20.7 us
  between operations: 13.2 us -> 0.52 us
  starting transfers between devices: 7.46 us -> 15.4 us
    psum x4 -> x0, waiting for transfers between devices: 516 us -> none  [broadcast(): return lax.psum(kept, axis)]
    ppermute x0 -> x20, waiting for transfers between devices: none -> 79 us  [send(): return lax.ppermute(value, AXES, pairs)]
    all_to_all x0 -> x1, blocking collectives: none -> 26.3 us  [on_device(): lax.all_to_all(outgoing, AXES, split_axis=1, concat_axis=0, tiled=True)]
    dot_general x8 -> x0, matrix products: 23.5 us -> none  [on_device(): jnp.dot(panel_cols, received, preferred_element_type=jnp.float32)]
    pallas_call x0 -> x5, Pallas kernels: none -> 20.7 us  [steps(): pl.pallas_call(functools.partial(step_kernel, plan, handed, len(arrays),...]
    all_to_all x1 -> x0, waiting for transfers between devices: 16.3 us -> none  [on_device(): lax.all_to_all(rhs_scen, ('row', 'col'), split_axis=1, concat_axis=0, til...]
    ppermute x0 -> x20, starting transfers between devices: none -> 15.4 us  [send(): return lax.ppermute(value, AXES, pairs)]
    all_to_all x1 -> x0, starting transfers between devices: 7.3 us -> none  [on_device(): lax.all_to_all(rhs_scen, ('row', 'col'), split_axis=1, concat_axis=0, til...]
  transfers between devices with their start and end apart: 5 -> 20, of which waited for: 5 -> 9; matrix products, arithmetic and copies ran while one was open for 0% -> 0% of each run, Pallas kernels for 0% -> 0%
where the time goes in v7:
time: 145 us
  waiting for transfers between devices  79 us (54%)
  blocking collectives  26.3 us (18%)
  Pallas kernels  20.7 us (14%)
  starting transfers between devices  15.4 us (11%)
  other arithmetic  1.46 us (1%)
    ppermute x20, waiting for transfers between devices, send(): return lax.ppermute(value, AXES, pairs)  79 us
    all_to_all x1, blocking collectives, on_device(): lax.all_to_all(outgoing, AXES, split_axis=1, concat_axis=0, tiled=True)  26.3 us
    pallas_call x5, Pallas kernels, steps(): pl.pallas_call(functools.partial(step_kernel, plan, handed, len(arrays),...  20.7 us
    ppermute x20, starting transfers between devices, send(): return lax.ppermute(value, AXES, pairs)  15.4 us
  transfers between devices with their start and end apart: 20, of which 9 were waited for; matrix products, arithmetic and copies ran while one was open for 0% of the time, Pallas kernels for 0%

profile of v7, /device:TPU:0, one launch (start us, length us, event | category | flops | bytes accessed | tf_op | source)
XLA Modules:
  0.0 144.6 jit_solution(18278613821239129936)
XLA Ops:
  0.0 0.8 slice.9
  0.8 1.1 pad_maximum_fusion
  1.9 26.3 %all_to_all.15 = bf16[8,32,1280]{2,0,1:T(8,128)(2,1)S(1)} all-to-all(bf16[8,32,1280]{2,0,1:T(8,128)(2,1)S(1)} %pad_maximum_fusion), channel_id=1, replica_groups=mesh['row'=4,'col'=8] {'row','col'}, dimensions={1} | all-to-all | bytes 1310720 | tf_op jit(solution)/shard_map/all_to_all | solution.py:230
  28.9 0.8 collective-permute-start
  29.7 4.8 %collective-permute-done.1 = bf16[256,256]{1,0:T(8,128)(2,1)S(1)} collective-permute-done((bf16[256,256]{1,0:T(8,128)(2,1)S(1)}, bf16[256,256]{1,0:T(8,128)(2,1)S(1)}, u32[]{:S(2)}, u32[]{:S(2)}) %collective-permute-start.1) | collective-permute-done | bytes 131104 | tf_op jit(solution)/shard_map/ppermute | solution.py:162
  34.8 4.6 %collective-permute-done.2 = bf16[256,256]{1,0:T(8,128)(2,1)S(1)} collective-permute-done((bf16[256,256]{1,0:T(8,128)(2,1)S(1)}, bf16[256,256]{1,0:T(8,128)(2,1)S(1)}, u32[]{:S(2)}, u32[]{:S(2)}) %collective-permute-start.2) | collective-permute-done | bytes 131104 | tf_op jit(solution)/shard_map/ppermute | solution.py:162
  39.9 1.5 %collective-permute-done.3.refs_3_ = bf16[1024,256]{1,0:T(8,128)(2,1)S(1)} collective-permute-done((bf16[1024,256]{1,0:T(8,128)(2,1)S(1)}, bf16[1024,256]{1,0:T(8,128)(2,1)S(1)}, u32[]{:S(2)}, u32[]{:S(2)}) %collective-permute-start.3) | collective-permute-done | bytes 524320 | tf_op jit(solution)/shard_map/ppermute | solution.py:162
  41.5 5.5 %shard_map.28 = (f32[1024,256]{1,0:T(8,128)S(1)}, bf16[1024,256]{1,0:T(8,128)(2,1)S(1)}) custom-call(f32[1024,256]{1,0:T(8,128)S(1)} %convert_bitcast_fusion.refs_0_, bf16[1024,8192]{1,0:T(8,128)(2,1)} %refs_1_.9, bf16[1024,256]{1,0:T(8,128)(2,1)S(1)} %pad_maximum_fusion.1.refs_2_, bf16[1024,256]{1,0:T(8,128)(2,1)S(1)} %collective-permute-done.3.refs_3_), custom_call_target="tpu_custom_call" | custom-call | flops 1073741824 | bytes 2097152 | tf_op jit(solution)/shard_map/pallas_call | solution.py:124
  47.0 0.7 collective-permute-start.4
  47.7 0.7 collective-permute-start.7
  49.1 0.7 collective-permute-start.6
  49.9 0.7 collective-permute-start.8
  53.7 1.3 collective-permute-start.13
  55.0 1.3 collective-permute-start.14
  56.3 1.5 %collective-permute-start.15 = (bf16[256,256]{1,0:T(8,128)(2,1)S(1)}, bf16[256,256]{1,0:T(8,128)(2,1)S(1)}, u32[]{:S(2)}, u32[]{:S(2)}) collective-permute-start(bf16[256,256]{1,0:T(8,128)(2,1)S(1)} %select_select_fusion.3), channel_id=1, source_target_pairs={{2,4},{3,5},{10,12},{11,13},{18,20},{19,21},{26,28},{27,29},{4,6},... | collective-permute-start | bytes 393224 | tf_op jit(solution)/shard_map/ppermute | solution.py:162
  57.8 25.8 %collective-permute-done.13 = bf16[256,256]{1,0:T(8,128)(2,1)S(1)} collective-permute-done((bf16[256,256]{1,0:T(8,128)(2,1)S(1)}, bf16[256,256]{1,0:T(8,128)(2,1)S(1)}, u32[]{:S(2)}, u32[]{:S(2)}) %collective-permute-start.13) | collective-permute-done | bytes 131104 | tf_op jit(solution)/shard_map/ppermute | solution.py:162
  83.6 14.7 %collective-permute-done.14 = bf16[256,256]{1,0:T(8,128)(2,1)S(1)} collective-permute-done((bf16[256,256]{1,0:T(8,128)(2,1)S(1)}, bf16[256,256]{1,0:T(8,128)(2,1)S(1)}, u32[]{:S(2)}, u32[]{:S(2)}) %collective-permute-start.14) | collective-permute-done | bytes 131104 | tf_op jit(solution)/shard_map/ppermute | solution.py:162
  98.3 8.4 %collective-permute-done.15 = bf16[256,256]{1,0:T(8,128)(2,1)S(1)} collective-permute-done((bf16[256,256]{1,0:T(8,128)(2,1)S(1)}, bf16[256,256]{1,0:T(8,128)(2,1)S(1)}, u32[]{:S(2)}, u32[]{:S(2)}) %collective-permute-start.15) | collective-permute-done | bytes 131104 | tf_op jit(solution)/shard_map/ppermute | solution.py:162
  107.0 1.4 collective-permute-start.17
  109.0 9.3 %collective-permute-done.17 = bf16[768,256]{1,0:T(8,128)(2,1)S(1)} collective-permute-done((bf16[768,256]{1,0:T(8,128)(2,1)S(1)}, bf16[768,256]{1,0:T(8,128)(2,1)S(1)}, u32[]{:S(2)}, u32[]{:S(2)}) %collective-permute-start.17) | collective-permute-done | bytes 393248 | tf_op jit(solution)/shard_map/ppermute | solution.py:162
  118.3 1.3 collective-permute-start.18
  119.7 6.4 %collective-permute-done.18 = bf16[768,256]{1,0:T(8,128)(2,1)S(1)} collective-permute-done((bf16[768,256]{1,0:T(8,128)(2,1)S(1)}, bf16[768,256]{1,0:T(8,128)(2,1)S(1)}, u32[]{:S(2)}, u32[]{:S(2)}) %collective-permute-start.18) | collective-permute-done | bytes 393248 | tf_op jit(solution)/shard_map/ppermute | solution.py:162
  126.2 3.4 %collective-permute-done.19.refs_3_ = bf16[3072,256]{1,0:T(8,128)(2,1)S(1)} collective-permute-done((bf16[3072,256]{1,0:T(8,128)(2,1)S(1)}, bf16[3072,256]{1,0:T(8,128)(2,1)S(1)}, u32[]{:S(2)}, u32[]{:S(2)}) %collective-permute-start.19) | collective-permute-done | bytes 1572896 | tf_op jit(solution)/shard_map/ppermute | solution.py:162
  129.6 14.9 %shard_map.32 = f32[1024,256]{1,0:T(8,128)} custom-call(f32[1024,256]{1,0:T(8,128)S(1)} %get-tuple-element.12.refs_0_, bf16[1024,8192]{1,0:T(8,128)(2,1)} %refs_1_.9, bf16[3072,256]{1,0:T(8,128)(2,1)S(1)} %constant_dynamic-update-slice_fusion.refs_2_, bf16[3072,256]{1,0:T(8,128)(2,1)S(1)} %collective-permute-done.19.refs_3_), custom_call_target="tpu_custom_call" | custom-call | flops 3221225472 | bytes 2097152 | tf_op jit(solution)/shard_map/pallas_call | solution.py:124
  (39 shorter events, 6.2 us)
Async XLA Ops:
  28.2 6.3 %collective-permute-start.1 = (bf16[256,256]{1,0:T(8,128)(2,1)S(1)}, bf16[256,256]{1,0:T(8,128)(2,1)S(1)}, u32[]{:S(2)}, u32[]{:S(2)}) collective-permute-start(bf16[256,256]{1,0:T(8,128)(2,1)S(1)} %bitcast.15), channel_id=1, source_target_pairs={{16,0},{17,1},{18,2},{19,3},{20,4},{21,5},{22,6},{23,7},{0,16},{1,... | collective-permute-start | bytes 393224 | tf_op jit(solution)/shard_map/ppermute | solution.py:162
  28.9 6.0 %collective-permute-start = (bf16[256,256]{1,0:T(8,128)(2,1)S(1)}, bf16[256,256]{1,0:T(8,128)(2,1)S(1)}, u32[]{:S(2)}, u32[]{:S(2)}) collective-permute-start(bf16[256,256]{1,0:T(8,128)(2,1)S(1)} %bitcast.16), channel_id=1, source_target_pairs={{1,0},{0,1},{3,2},{2,3},{5,4},{4,5},{7,6},{6,7},{17,16},{16,17},{1... | collective-permute-start | bytes 393224 | tf_op jit(solution)/shard_map/ppermute | solution.py:162
  34.5 5.0 %collective-permute-start.2 = (bf16[256,256]{1,0:T(8,128)(2,1)S(1)}, bf16[256,256]{1,0:T(8,128)(2,1)S(1)}, u32[]{:S(2)}, u32[]{:S(2)}) collective-permute-start(bf16[256,256]{1,0:T(8,128)(2,1)S(1)} %collective-permute-done.1), channel_id=1, source_target_pairs={{1,0},{0,1},{3,2},{2,3},{5,4},{4,5},{7,6},{6,7},{17,16},{16,17},{1... | collective-permute-start | bytes 393224 | tf_op jit(solution)/shard_map/ppermute | solution.py:162
  39.5 2.0 %collective-permute-start.3 = (bf16[1024,256]{1,0:T(8,128)(2,1)S(1)}, bf16[1024,256]{1,0:T(8,128)(2,1)S(1)}, u32[]{:S(2)}, u32[]{:S(2)}) collective-permute-start(bf16[1024,256]{1,0:T(8,128)(2,1)S(1)} %pad_maximum_fusion.1.refs_2_), channel_id=1, source_target_pairs={{8,0},{9,1},{10,2},{11,3},{12,4},{13,5},{14,6},{15,7},{0,8},{1,9},... | collective-permute-start | bytes 1572872 | tf_op jit(solution)/shard_map/ppermute | solution.py:162
  47.0 1.4 collective-permute-start.4
  47.7 2.1 %collective-permute-start.7 = (bf16[1024,256]{1,0:T(8,128)(2,1)S(1)}, bf16[1024,256]{1,0:T(8,128)(2,1)S(1)}, u32[]{:S(2)}, u32[]{:S(2)}) collective-permute-start(bf16[1024,256]{1,0:T(8,128)(2,1)S(1)} %get-tuple-element.14.refs_4_), channel_id=1, source_target_pairs={{3,4},{2,5}} | collective-permute-start | bytes 1572872 | tf_op jit(solution)/shard_map/ppermute | solution.py:162
  48.4 2.9 %collective-permute-start.5 = (bf16[1024,256]{1,0:T(8,128)(2,1)S(1)}, bf16[1024,256]{1,0:T(8,128)(2,1)S(1)}, u32[]{:S(2)}, u32[]{:S(2)}) collective-permute-start(bf16[1024,256]{1,0:T(8,128)(2,1)S(1)} %get-tuple-element.14.refs_4_), channel_id=1, source_target_pairs={{2,6},{3,7}} | collective-permute-start | bytes 1572872 | tf_op jit(solution)/shard_map/ppermute | solution.py:162
  49.1 2.2 %collective-permute-start.6 = (bf16[1024,256]{1,0:T(8,128)(2,1)S(1)}, bf16[1024,256]{1,0:T(8,128)(2,1)S(1)}, u32[]{:S(2)}, u32[]{:S(2)}) collective-permute-start(bf16[1024,256]{1,0:T(8,128)(2,1)S(1)} %get-tuple-element.14.refs_4_), channel_id=1, source_target_pairs={{3,6},{2,7}} | collective-permute-start | bytes 1572872 | tf_op jit(solution)/shard_map/ppermute | solution.py:162
  49.9 1.5 %collective-permute-start.8 = (bf16[1024,256]{1,0:T(8,128)(2,1)S(1)}, bf16[1024,256]{1,0:T(8,128)(2,1)S(1)}, u32[]{:S(2)}, u32[]{:S(2)}) collective-permute-start(bf16[1024,256]{1,0:T(8,128)(2,1)S(1)} %shard_map.30.refs_5_), channel_id=1, source_target_pairs={{4,6},{5,7}} | collective-permute-start | bytes 1572872 | tf_op jit(solution)/shard_map/ppermute | solution.py:162
  50.6 0.8 collective-permute-start.9
  51.6 2.1 %collective-permute-start.10 = (bf16[256,256]{1,0:T(8,128)(2,1)S(1)}, bf16[256,256]{1,0:T(8,128)(2,1)S(1)}, u32[]{:S(2)}, u32[]{:S(2)}) collective-permute-start(bf16[256,256]{1,0:T(8,128)(2,1)S(1)} %get-tuple-element.15), channel_id=1, source_target_pairs={{2,26},{3,27},{4,28},{5,29},{6,30},{7,31}} | collective-permute-start | bytes 393224 | tf_op jit(solution)/shard_map/ppermute | solution.py:162
  52.2 1.4 collective-permute-start.11
  52.9 0.7 collective-permute-start.12
  53.7 29.9 %collective-permute-start.13 = (bf16[256,256]{1,0:T(8,128)(2,1)S(1)}, bf16[256,256]{1,0:T(8,128)(2,1)S(1)}, u32[]{:S(2)}, u32[]{:S(2)}) collective-permute-start(bf16[256,256]{1,0:T(8,128)(2,1)S(1)} %select_select_fusion.3), channel_id=1, source_target_pairs={{2,0},{3,1},{10,8},{11,9},{18,16},{19,17},{26,24},{27,25},{4,2},{5... | collective-permute-start | bytes 393224 | tf_op jit(solution)/shard_map/ppermute | solution.py:162
  55.0 43.3 %collective-permute-start.14 = (bf16[256,256]{1,0:T(8,128)(2,1)S(1)}, bf16[256,256]{1,0:T(8,128)(2,1)S(1)}, u32[]{:S(2)}, u32[]{:S(2)}) collective-permute-start(bf16[256,256]{1,0:T(8,128)(2,1)S(1)} %select_select_fusion.3), channel_id=1, source_target_pairs={{2,6},{3,7},{10,14},{11,15},{18,22},{19,23},{26,30},{27,31},{4,0},... | collective-permute-start | bytes 393224 | tf_op jit(solution)/shard_map/ppermute | solution.py:162
  56.3 50.4 %collective-permute-start.15 = (bf16[256,256]{1,0:T(8,128)(2,1)S(1)}, bf16[256,256]{1,0:T(8,128)(2,1)S(1)}, u32[]{:S(2)}, u32[]{:S(2)}) collective-permute-start(bf16[256,256]{1,0:T(8,128)(2,1)S(1)} %select_select_fusion.3), channel_id=1, source_target_pairs={{2,4},{3,5},{10,12},{11,13},{18,20},{19,21},{26,28},{27,29},{4,6},... | collective-permute-start | bytes 393224 | tf_op jit(solution)/shard_map/ppermute | solution.py:162
  107.0 11.3 %collective-permute-start.17 = (bf16[768,256]{1,0:T(8,128)(2,1)S(1)}, bf16[768,256]{1,0:T(8,128)(2,1)S(1)}, u32[]{:S(2)}, u32[]{:S(2)}) collective-permute-start(bf16[768,256]{1,0:T(8,128)(2,1)S(1)} %pad_maximum_fusion.2), channel_id=1, source_target_pairs={{16,0},{17,1},{18,2},{19,3},{20,4},{21,5},{22,6},{23,7},{0,16},{1,... | collective-permute-start | bytes 1179656 | tf_op jit(solution)/shard_map/ppermute | solution.py:162
  108.4 11.2 %collective-permute-start.16 = (bf16[768,256]{1,0:T(8,128)(2,1)S(1)}, bf16[768,256]{1,0:T(8,128)(2,1)S(1)}, u32[]{:S(2)}, u32[]{:S(2)}) collective-permute-start(bf16[768,256]{1,0:T(8,128)(2,1)S(1)} %pad_maximum_fusion.2), channel_id=1, source_target_pairs={{1,0},{0,1},{3,2},{2,3},{5,4},{4,5},{7,6},{6,7},{17,16},{16,17},{1... | collective-permute-start | bytes 1179656 | tf_op jit(solution)/shard_map/ppermute | solution.py:162
  118.3 7.8 %collective-permute-start.18 = (bf16[768,256]{1,0:T(8,128)(2,1)S(1)}, bf16[768,256]{1,0:T(8,128)(2,1)S(1)}, u32[]{:S(2)}, u32[]{:S(2)}) collective-permute-start(bf16[768,256]{1,0:T(8,128)(2,1)S(1)} %collective-permute-done.17), channel_id=1, source_target_pairs={{1,0},{0,1},{3,2},{2,3},{5,4},{4,5},{7,6},{6,7},{17,16},{16,17},{1... | collective-permute-start | bytes 1179656 | tf_op jit(solution)/shard_map/ppermute | solution.py:162
  126.1 3.5 %collective-permute-start.19 = (bf16[3072,256]{1,0:T(8,128)(2,1)S(1)}, bf16[3072,256]{1,0:T(8,128)(2,1)S(1)}, u32[]{:S(2)}, u32[]{:S(2)}) collective-permute-start(bf16[3072,256]{1,0:T(8,128)(2,1)S(1)} %constant_dynamic-update-slice_fusion.refs_2_), channel_id=1, source_target_pairs={{8,0},{9,1},{10,2},{11,3},{12,4},{13,5},{14,6},{15,7},{0,8},{1,9},... | collective-permute-start | bytes 4718600 | tf_op jit(solution)/shard_map/ppermute | solution.py:162

commit v8 on v7

--- a/solution.py
+++ b/solution.py
@@ -12,6 +12,7 @@
 AXES = ("row", "col")
 CORES = 2
 DEPTH = 512
+IN_FLIGHT = 3
 KERNEL_VMEM = 40 * 1024 * 1024
 
 
@@ -38,17 +39,17 @@
     here = where_am_i()
 
     def work():
-        copies = []
+        copies = [[] for _ in terms]
         for t, (_, pieces) in enumerate(terms):
             for array, first, size, place in pieces:
                 start = pl.multiple_of(place(here) * size, size)
-                copy = pltpu.make_async_copy(
-                    arrays[array].at[pl.ds(first, size), :],
-                    held.at[t, pl.ds(start, size), :],
-                    piece_sems.at[len(copies)],
+                copies[t].append(
+                    pltpu.make_async_copy(
+                        arrays[array].at[pl.ds(first, size), :],
+                        held.at[t, pl.ds(start, size), :],
+                        piece_sems.at[sum(len(c) for c in copies)],
+                    )
                 )
-                copy.start()
-                copies.append(copy)
 
         def panel_copy(t, i):
             k = terms[t][0]
@@ -56,23 +57,31 @@
                 panels.at[:, pl.ds(k * NB + i * depth, depth)], panels_here.at[t, i], sems.at[t, i]
             )
 
-        for t in range(len(terms)):
-            for i in range(chunks):
-                panel_copy(t, i).start()
+        def load(t, i):
+            if i == 0:
+                for copy in copies[t]:
+                    copy.start()
+            panel_copy(t, i).start()
+
+        order = [(t, i) for t in range(len(terms)) for i in range(chunks)]
         current_copy = pltpu.make_async_copy(current, current_here, current_sem)
         current_copy.start()
-        for copy in copies:
-            copy.wait()
+        for t, i in order[:IN_FLIGHT]:
+            load(t, i)
         current_copy.wait()
-        for t, (k, _) in enumerate(terms):
-            own = here.block == k
-            for i in range(chunks):
-                panel_copy(t, i).wait()
-                part = jnp.dot(
-                    panels_here[t, i], held[t, pl.ds(i * depth, depth), :], preferred_element_type=jnp.float32
-                )
-                now = current_here[...]
-                current_here[...] = jnp.where(own, part if i == 0 else now + part, now - part)
+        for n, (t, i) in enumerate(order):
+            if i == 0:
+                for copy in copies[t]:
+                    copy.wait()
+            panel_copy(t, i).wait()
+            if n + IN_FLIGHT < len(order):
+                load(*order[n + IN_FLIGHT])
+            part = jnp.dot(
+                panels_here[t, i], held[t, pl.ds(i * depth, depth), :], preferred_element_type=jnp.float32
+            )
+            own = here.block == terms[t][0]
+            now = current_here[...]
+            current_here[...] = jnp.where(own, part if i == 0 else now + part, now - part)
         sent = []
         for o, (dtype, first, size, far) in enumerate(outs):
             if far:

time: 145 us -> 145 us (level)
  no operation moved by 1% of the time
where the time goes in v8:
time: 145 us
  waiting for transfers between devices  79.1 us (55%)
  blocking collectives  26.3 us (18%)
  Pallas kernels  20.9 us (14%)
  starting transfers between devices  15.4 us (11%)
  other arithmetic  1.46 us (1%)
    ppermute x20, waiting for transfers between devices, send(): return lax.ppermute(value, AXES, pairs)  79.1 us
    all_to_all x1, blocking collectives, on_device(): lax.all_to_all(outgoing, AXES, split_axis=1, concat_axis=0, tiled=True)  26.3 us
    pallas_call x5, Pallas kernels, steps(): pl.pallas_call(functools.partial(step_kernel, plan, handed, len(arrays),...  20.9 us
    ppermute x20, starting transfers between devices, send(): return lax.ppermute(value, AXES, pairs)  15.4 us
  transfers between devices with their start and end apart: 20, of which 9 were waited for; matrix products, arithmetic and copies ran while one was open for 0% of the time, Pallas kernels for 0%

profile of v8, /device:TPU:0, one launch (start us, length us, event | category | flops | bytes accessed | tf_op | source)
XLA Modules:
  0.0 144.9 jit_solution(8884935968689312046)
XLA Ops:
  0.0 0.8 slice.9
  0.8 1.1 pad_maximum_fusion
  1.9 26.3 %all_to_all.15 = bf16[8,32,1280]{2,0,1:T(8,128)(2,1)S(1)} all-to-all(bf16[8,32,1280]{2,0,1:T(8,128)(2,1)S(1)} %pad_maximum_fusion), channel_id=1, replica_groups=mesh['row'=4,'col'=8] {'row','col'}, dimensions={1} | all-to-all | bytes 1310720 | tf_op jit(solution)/shard_map/all_to_all | solution.py:239
  28.9 0.8 collective-permute-start
  29.7 4.8 %collective-permute-done.1 = bf16[256,256]{1,0:T(8,128)(2,1)S(1)} collective-permute-done((bf16[256,256]{1,0:T(8,128)(2,1)S(1)}, bf16[256,256]{1,0:T(8,128)(2,1)S(1)}, u32[]{:S(2)}, u32[]{:S(2)}) %collective-permute-start.1) | collective-permute-done | bytes 131104 | tf_op jit(solution)/shard_map/ppermute | solution.py:171
  34.8 4.6 %collective-permute-done.2 = bf16[256,256]{1,0:T(8,128)(2,1)S(1)} collective-permute-done((bf16[256,256]{1,0:T(8,128)(2,1)S(1)}, bf16[256,256]{1,0:T(8,128)(2,1)S(1)}, u32[]{:S(2)}, u32[]{:S(2)}) %collective-permute-start.2) | collective-permute-done | bytes 131104 | tf_op jit(solution)/shard_map/ppermute | solution.py:171
  39.9 1.5 %collective-permute-done.3.refs_3_ = bf16[1024,256]{1,0:T(8,128)(2,1)S(1)} collective-permute-done((bf16[1024,256]{1,0:T(8,128)(2,1)S(1)}, bf16[1024,256]{1,0:T(8,128)(2,1)S(1)}, u32[]{:S(2)}, u32[]{:S(2)}) %collective-permute-start.3) | collective-permute-done | bytes 524320 | tf_op jit(solution)/shard_map/ppermute | solution.py:171
  41.5 5.5 %shard_map.28 = (f32[1024,256]{1,0:T(8,128)S(1)}, bf16[1024,256]{1,0:T(8,128)(2,1)S(1)}) custom-call(f32[1024,256]{1,0:T(8,128)S(1)} %convert_bitcast_fusion.refs_0_, bf16[1024,8192]{1,0:T(8,128)(2,1)} %refs_1_.9, bf16[1024,256]{1,0:T(8,128)(2,1)S(1)} %pad_maximum_fusion.1.refs_2_, bf16[1024,256]{1,0:T(8,128)(2,1)S(1)} %collective-permute-done.3.refs_3_), custom_call_target="tpu_custom_call" | custom-call | flops 1073741824 | bytes 2097152 | tf_op jit(solution)/shard_map/pallas_call | solution.py:133
  47.0 0.7 collective-permute-start.4
  47.7 0.7 collective-permute-start.7
  49.2 0.7 collective-permute-start.6
  50.7 0.7 collective-permute-start.9
  53.8 1.3 collective-permute-start.13
  55.1 1.3 collective-permute-start.14
  56.4 1.5 %collective-permute-start.15 = (bf16[256,256]{1,0:T(8,128)(2,1)S(1)}, bf16[256,256]{1,0:T(8,128)(2,1)S(1)}, u32[]{:S(2)}, u32[]{:S(2)}) collective-permute-start(bf16[256,256]{1,0:T(8,128)(2,1)S(1)} %select_select_fusion.3), channel_id=1, source_target_pairs={{2,4},{3,5},{10,12},{11,13},{18,20},{19,21},{26,28},{27,29},{4,6},... | collective-permute-start | bytes 393224 | tf_op jit(solution)/shard_map/ppermute | solution.py:171
  57.9 25.8 %collective-permute-done.13 = bf16[256,256]{1,0:T(8,128)(2,1)S(1)} collective-permute-done((bf16[256,256]{1,0:T(8,128)(2,1)S(1)}, bf16[256,256]{1,0:T(8,128)(2,1)S(1)}, u32[]{:S(2)}, u32[]{:S(2)}) %collective-permute-start.13) | collective-permute-done | bytes 131104 | tf_op jit(solution)/shard_map/ppermute | solution.py:171
  83.7 14.7 %collective-permute-done.14 = bf16[256,256]{1,0:T(8,128)(2,1)S(1)} collective-permute-done((bf16[256,256]{1,0:T(8,128)(2,1)S(1)}, bf16[256,256]{1,0:T(8,128)(2,1)S(1)}, u32[]{:S(2)}, u32[]{:S(2)}) %collective-permute-start.14) | collective-permute-done | bytes 131104 | tf_op jit(solution)/shard_map/ppermute | solution.py:171
  98.4 8.5 %collective-permute-done.15 = bf16[256,256]{1,0:T(8,128)(2,1)S(1)} collective-permute-done((bf16[256,256]{1,0:T(8,128)(2,1)S(1)}, bf16[256,256]{1,0:T(8,128)(2,1)S(1)}, u32[]{:S(2)}, u32[]{:S(2)}) %collective-permute-start.15) | collective-permute-done | bytes 131104 | tf_op jit(solution)/shard_map/ppermute | solution.py:171
  107.1 1.4 collective-permute-start.17
  109.2 9.3 %collective-permute-done.17 = bf16[768,256]{1,0:T(8,128)(2,1)S(1)} collective-permute-done((bf16[768,256]{1,0:T(8,128)(2,1)S(1)}, bf16[768,256]{1,0:T(8,128)(2,1)S(1)}, u32[]{:S(2)}, u32[]{:S(2)}) %collective-permute-start.17) | collective-permute-done | bytes 393248 | tf_op jit(solution)/shard_map/ppermute | solution.py:171
  118.4 1.3 collective-permute-start.18
  119.8 6.4 %collective-permute-done.18 = bf16[768,256]{1,0:T(8,128)(2,1)S(1)} collective-permute-done((bf16[768,256]{1,0:T(8,128)(2,1)S(1)}, bf16[768,256]{1,0:T(8,128)(2,1)S(1)}, u32[]{:S(2)}, u32[]{:S(2)}) %collective-permute-start.18) | collective-permute-done | bytes 393248 | tf_op jit(solution)/shard_map/ppermute | solution.py:171
  126.3 3.4 %collective-permute-done.19.refs_3_ = bf16[3072,256]{1,0:T(8,128)(2,1)S(1)} collective-permute-done((bf16[3072,256]{1,0:T(8,128)(2,1)S(1)}, bf16[3072,256]{1,0:T(8,128)(2,1)S(1)}, u32[]{:S(2)}, u32[]{:S(2)}) %collective-permute-start.19) | collective-permute-done | bytes 1572896 | tf_op jit(solution)/shard_map/ppermute | solution.py:171
  129.7 15.0 %shard_map.32 = f32[1024,256]{1,0:T(8,128)} custom-call(f32[1024,256]{1,0:T(8,128)S(1)} %get-tuple-element.12.refs_0_, bf16[1024,8192]{1,0:T(8,128)(2,1)} %refs_1_.9, bf16[3072,256]{1,0:T(8,128)(2,1)S(1)} %constant_dynamic-update-slice_fusion.refs_2_, bf16[3072,256]{1,0:T(8,128)(2,1)S(1)} %collective-permute-done.19.refs_3_), custom_call_target="tpu_custom_call" | custom-call | flops 3221225472 | bytes 2097152 | tf_op jit(solution)/shard_map/pallas_call | solution.py:133
  (39 shorter events, 6.2 us)
Async XLA Ops:
  28.2 6.3 %collective-permute-start.1 = (bf16[256,256]{1,0:T(8,128)(2,1)S(1)}, bf16[256,256]{1,0:T(8,128)(2,1)S(1)}, u32[]{:S(2)}, u32[]{:S(2)}) collective-permute-start(bf16[256,256]{1,0:T(8,128)(2,1)S(1)} %bitcast.15), channel_id=1, source_target_pairs={{16,0},{17,1},{18,2},{19,3},{20,4},{21,5},{22,6},{23,7},{0,16},{1,... | collective-permute-start | bytes 393224 | tf_op jit(solution)/shard_map/ppermute | solution.py:171
  28.9 6.0 %collective-permute-start = (bf16[256,256]{1,0:T(8,128)(2,1)S(1)}, bf16[256,256]{1,0:T(8,128)(2,1)S(1)}, u32[]{:S(2)}, u32[]{:S(2)}) collective-permute-start(bf16[256,256]{1,0:T(8,128)(2,1)S(1)} %bitcast.16), channel_id=1, source_target_pairs={{1,0},{0,1},{3,2},{2,3},{5,4},{4,5},{7,6},{6,7},{17,16},{16,17},{1... | collective-permute-start | bytes 393224 | tf_op jit(solution)/shard_map/ppermute | solution.py:171
  34.5 5.0 %collective-permute-start.2 = (bf16[256,256]{1,0:T(8,128)(2,1)S(1)}, bf16[256,256]{1,0:T(8,128)(2,1)S(1)}, u32[]{:S(2)}, u32[]{:S(2)}) collective-permute-start(bf16[256,256]{1,0:T(8,128)(2,1)S(1)} %collective-permute-done.1), channel_id=1, source_target_pairs={{1,0},{0,1},{3,2},{2,3},{5,4},{4,5},{7,6},{6,7},{17,16},{16,17},{1... | collective-permute-start | bytes 393224 | tf_op jit(solution)/shard_map/ppermute | solution.py:171
  39.5 2.0 %collective-permute-start.3 = (bf16[1024,256]{1,0:T(8,128)(2,1)S(1)}, bf16[1024,256]{1,0:T(8,128)(2,1)S(1)}, u32[]{:S(2)}, u32[]{:S(2)}) collective-permute-start(bf16[1024,256]{1,0:T(8,128)(2,1)S(1)} %pad_maximum_fusion.1.refs_2_), channel_id=1, source_target_pairs={{8,0},{9,1},{10,2},{11,3},{12,4},{13,5},{14,6},{15,7},{0,8},{1,9},... | collective-permute-start | bytes 1572872 | tf_op jit(solution)/shard_map/ppermute | solution.py:171
  47.0 1.4 collective-permute-start.4
  47.7 2.1 %collective-permute-start.7 = (bf16[1024,256]{1,0:T(8,128)(2,1)S(1)}, bf16[1024,256]{1,0:T(8,128)(2,1)S(1)}, u32[]{:S(2)}, u32[]{:S(2)}) collective-permute-start(bf16[1024,256]{1,0:T(8,128)(2,1)S(1)} %get-tuple-element.14.refs_4_), channel_id=1, source_target_pairs={{3,4},{2,5}} | collective-permute-start | bytes 1572872 | tf_op jit(solution)/shard_map/ppermute | solution.py:171
  48.5 2.9 %collective-permute-start.5 = (bf16[1024,256]{1,0:T(8,128)(2,1)S(1)}, bf16[1024,256]{1,0:T(8,128)(2,1)S(1)}, u32[]{:S(2)}, u32[]{:S(2)}) collective-permute-start(bf16[1024,256]{1,0:T(8,128)(2,1)S(1)} %get-tuple-element.14.refs_4_), channel_id=1, source_target_pairs={{2,6},{3,7}} | collective-permute-start | bytes 1572872 | tf_op jit(solution)/shard_map/ppermute | solution.py:171
  49.2 2.2 %collective-permute-start.6 = (bf16[1024,256]{1,0:T(8,128)(2,1)S(1)}, bf16[1024,256]{1,0:T(8,128)(2,1)S(1)}, u32[]{:S(2)}, u32[]{:S(2)}) collective-permute-start(bf16[1024,256]{1,0:T(8,128)(2,1)S(1)} %get-tuple-element.14.refs_4_), channel_id=1, source_target_pairs={{3,6},{2,7}} | collective-permute-start | bytes 1572872 | tf_op jit(solution)/shard_map/ppermute | solution.py:171
  50.0 1.5 %collective-permute-start.8 = (bf16[1024,256]{1,0:T(8,128)(2,1)S(1)}, bf16[1024,256]{1,0:T(8,128)(2,1)S(1)}, u32[]{:S(2)}, u32[]{:S(2)}) collective-permute-start(bf16[1024,256]{1,0:T(8,128)(2,1)S(1)} %shard_map.30.refs_5_), channel_id=1, source_target_pairs={{4,6},{5,7}} | collective-permute-start | bytes 1572872 | tf_op jit(solution)/shard_map/ppermute | solution.py:171
  50.7 0.8 collective-permute-start.9
  51.7 2.1 %collective-permute-start.10 = (bf16[256,256]{1,0:T(8,128)(2,1)S(1)}, bf16[256,256]{1,0:T(8,128)(2,1)S(1)}, u32[]{:S(2)}, u32[]{:S(2)}) collective-permute-start(bf16[256,256]{1,0:T(8,128)(2,1)S(1)} %get-tuple-element.15), channel_id=1, source_target_pairs={{2,26},{3,27},{4,28},{5,29},{6,30},{7,31}} | collective-permute-start | bytes 393224 | tf_op jit(solution)/shard_map/ppermute | solution.py:171
  52.3 1.4 collective-permute-start.11
  53.0 0.7 collective-permute-start.12
  53.8 29.9 %collective-permute-start.13 = (bf16[256,256]{1,0:T(8,128)(2,1)S(1)}, bf16[256,256]{1,0:T(8,128)(2,1)S(1)}, u32[]{:S(2)}, u32[]{:S(2)}) collective-permute-start(bf16[256,256]{1,0:T(8,128)(2,1)S(1)} %select_select_fusion.3), channel_id=1, source_target_pairs={{2,0},{3,1},{10,8},{11,9},{18,16},{19,17},{26,24},{27,25},{4,2},{5... | collective-permute-start | bytes 393224 | tf_op jit(solution)/shard_map/ppermute | solution.py:171
  55.1 43.3 %collective-permute-start.14 = (bf16[256,256]{1,0:T(8,128)(2,1)S(1)}, bf16[256,256]{1,0:T(8,128)(2,1)S(1)}, u32[]{:S(2)}, u32[]{:S(2)}) collective-permute-start(bf16[256,256]{1,0:T(8,128)(2,1)S(1)} %select_select_fusion.3), channel_id=1, source_target_pairs={{2,6},{3,7},{10,14},{11,15},{18,22},{19,23},{26,30},{27,31},{4,0},... | collective-permute-start | bytes 393224 | tf_op jit(solution)/shard_map/ppermute | solution.py:171
  56.4 50.5 %collective-permute-start.15 = (bf16[256,256]{1,0:T(8,128)(2,1)S(1)}, bf16[256,256]{1,0:T(8,128)(2,1)S(1)}, u32[]{:S(2)}, u32[]{:S(2)}) collective-permute-start(bf16[256,256]{1,0:T(8,128)(2,1)S(1)} %select_select_fusion.3), channel_id=1, source_target_pairs={{2,4},{3,5},{10,12},{11,13},{18,20},{19,21},{26,28},{27,29},{4,6},... | collective-permute-start | bytes 393224 | tf_op jit(solution)/shard_map/ppermute | solution.py:171
  107.1 11.3 %collective-permute-start.17 = (bf16[768,256]{1,0:T(8,128)(2,1)S(1)}, bf16[768,256]{1,0:T(8,128)(2,1)S(1)}, u32[]{:S(2)}, u32[]{:S(2)}) collective-permute-start(bf16[768,256]{1,0:T(8,128)(2,1)S(1)} %pad_maximum_fusion.2), channel_id=1, source_target_pairs={{16,0},{17,1},{18,2},{19,3},{20,4},{21,5},{22,6},{23,7},{0,16},{1,... | collective-permute-start | bytes 1179656 | tf_op jit(solution)/shard_map/ppermute | solution.py:171
  108.6 11.2 %collective-permute-start.16 = (bf16[768,256]{1,0:T(8,128)(2,1)S(1)}, bf16[768,256]{1,0:T(8,128)(2,1)S(1)}, u32[]{:S(2)}, u32[]{:S(2)}) collective-permute-start(bf16[768,256]{1,0:T(8,128)(2,1)S(1)} %pad_maximum_fusion.2), channel_id=1, source_target_pairs={{1,0},{0,1},{3,2},{2,3},{5,4},{4,5},{7,6},{6,7},{17,16},{16,17},{1... | collective-permute-start | bytes 1179656 | tf_op jit(solution)/shard_map/ppermute | solution.py:171
  118.4 7.8 %collective-permute-start.18 = (bf16[768,256]{1,0:T(8,128)(2,1)S(1)}, bf16[768,256]{1,0:T(8,128)(2,1)S(1)}, u32[]{:S(2)}, u32[]{:S(2)}) collective-permute-start(bf16[768,256]{1,0:T(8,128)(2,1)S(1)} %collective-permute-done.17), channel_id=1, source_target_pairs={{1,0},{0,1},{3,2},{2,3},{5,4},{4,5},{7,6},{6,7},{17,16},{16,17},{1... | collective-permute-start | bytes 1179656 | tf_op jit(solution)/shard_map/ppermute | solution.py:171
  126.3 3.5 %collective-permute-start.19 = (bf16[3072,256]{1,0:T(8,128)(2,1)S(1)}, bf16[3072,256]{1,0:T(8,128)(2,1)S(1)}, u32[]{:S(2)}, u32[]{:S(2)}) collective-permute-start(bf16[3072,256]{1,0:T(8,128)(2,1)S(1)} %constant_dynamic-update-slice_fusion.refs_2_), channel_id=1, source_target_pairs={{8,0},{9,1},{10,2},{11,3},{12,4},{13,5},{14,6},{15,7},{0,8},{1,9},... | collective-permute-start | bytes 4718600 | tf_op jit(solution)/shard_map/ppermute | solution.py:171

commit v9 on v8

--- a/solution.py
+++ b/solution.py
@@ -11,7 +11,7 @@
 STEPS = 4
 AXES = ("row", "col")
 CORES = 2
-DEPTH = 512
+TILE = 256
 IN_FLIGHT = 3
 KERNEL_VMEM = 40 * 1024 * 1024
 
@@ -32,10 +32,9 @@
     current, panels = refs[:2]
     arrays = refs[2 : 2 + n_arrays]
     results = refs[2 + n_arrays : 2 + n_arrays + len(outs)]
-    current_here, panels_here, held, sems, piece_sems, current_sem, out_sem = refs[2 + n_arrays + len(outs) :]
+    current_here, panels_here, held, sems, piece_sems, out_sems = refs[2 + n_arrays + len(outs) :]
     rows = current.shape[0]
-    depth = min(DEPTH, NB)
-    chunks = NB // depth
+    tile = min(TILE, rows)
     here = where_am_i()
 
     def work():
@@ -54,41 +53,51 @@
         def panel_copy(t, i):
             k = terms[t][0]
             return pltpu.make_async_copy(
-                panels.at[:, pl.ds(k * NB + i * depth, depth)], panels_here.at[t, i], sems.at[t, i]
+                panels.at[pl.ds(i * tile, tile), pl.ds(k * NB, NB)], panels_here.at[t, i], sems.at[t, i]
             )
+
+        def current_copy(i):
+            at = pl.ds(i * tile, tile)
+            return pltpu.make_async_copy(current.at[at, :], current_here.at[at, :], sems.at[len(terms), i])
 
         def load(t, i):
             if i == 0:
                 for copy in copies[t]:
                     copy.start()
             panel_copy(t, i).start()
-
-        order = [(t, i) for t in range(len(terms)) for i in range(chunks)]
-        current_copy = pltpu.make_async_copy(current, current_here, current_sem)
-        current_copy.start()
-        for t, i in order[:IN_FLIGHT]:
+            if t == 0:
+                current_copy(i).start()
+
+        order = [(t, i) for i in range(rows // tile) for t in range(len(terms))]
+        in_flight = max(IN_FLIGHT, len(terms))
+        for t, i in order[:in_flight]:
             load(t, i)
-        current_copy.wait()
+        sent = []
         for n, (t, i) in enumerate(order):
+            at = pl.ds(i * tile, tile)
             if i == 0:
                 for copy in copies[t]:
                     copy.wait()
+            if t == 0:
+                current_copy(i).wait()
+                value = current_here[at, :]
             panel_copy(t, i).wait()
-            if n + IN_FLIGHT < len(order):
-                load(*order[n + IN_FLIGHT])
-            part = jnp.dot(
-                panels_here[t, i], held[t, pl.ds(i * depth, depth), :], preferred_element_type=jnp.float32
-            )
-            own = here.block == terms[t][0]
-            now = current_here[...]
-            current_here[...] = jnp.where(own, part if i == 0 else now + part, now - part)
-        sent = []
-        for o, (dtype, first, size, far) in enumerate(outs):
-            if far:
-                sent.append(pltpu.make_async_copy(current_here.at[pl.ds(first, size), :], results[o], out_sem))
-                sent[-1].start()
-            else:
-                results[o][...] = current_here[pl.ds(first, size), :].astype(dtype)
+            if n + in_flight < len(order):
+                load(*order[n + in_flight])
+            product = jnp.dot(panels_here[t, i], held[t], preferred_element_type=jnp.float32)
+            value = jnp.where(here.block == terms[t][0], product, value - product)
+            if t < len(terms) - 1:
+                continue
+            for o, (dtype, first, size, far) in enumerate(outs):
+                low, high = max(first, i * tile), min(first + size, (i + 1) * tile)
+                if low < high:
+                    part = value[low - i * tile : high - i * tile].astype(dtype)
+                    if far:
+                        current_here[at, :] = part
+                        sent.append(pltpu.make_async_copy(current_here.at[at, :], results[o].at[at, :], out_sems.at[i]))
+                        sent[-1].start()
+                    else:
+                        results[o][pl.ds(low - first, high - low), :] = part
         for out in sent:
             out.wait()
 
@@ -127,7 +136,7 @@
     )
     handed = tuple((block, index(array)) for block, array in handed)
     n_terms = len(terms)
-    depth = min(DEPTH, NB)
+    tile = min(TILE, rows)
     n_pieces = max(sum(len(pieces) for _, pieces in terms), len(outs))
     anywhere = pl.BlockSpec(memory_space=pl.ANY)
     return pl.pallas_call(
@@ -137,12 +146,11 @@
         out_shape=[jax.ShapeDtypeStruct((size, scenarios), dtype) for dtype, _, size, _ in outs],
         scratch_shapes=[
             pltpu.VMEM((rows, scenarios), jnp.float32),
-            pltpu.VMEM((n_terms, NB // depth, rows, depth), jnp.bfloat16),
+            pltpu.VMEM((n_terms, rows // tile, tile, NB), jnp.bfloat16),
             pltpu.VMEM((n_terms, NB, scenarios), jnp.bfloat16),
-            pltpu.SemaphoreType.DMA((n_terms, NB // depth)),
+            pltpu.SemaphoreType.DMA((n_terms + 1, rows // tile)),
             pltpu.SemaphoreType.DMA((n_pieces,)),
-            pltpu.SemaphoreType.DMA,
-            pltpu.SemaphoreType.DMA,
+            pltpu.SemaphoreType.DMA((rows // tile,)),
         ],
         compiler_params=pltpu.CompilerParams(vmem_limit_bytes=KERNEL_VMEM),
         cost_estimate=pl.CostEstimate(

time: 145 us -> 144 us (level)
  no operation moved by 1% of the time
where the time goes in v9:
time: 144 us
  waiting for transfers between devices  79 us (55%)
  blocking collectives  26.3 us (18%)
  Pallas kernels  19.6 us (14%)
  starting transfers between devices  15.4 us (11%)
  other arithmetic  1.46 us (1%)
    ppermute x20, waiting for transfers between devices, send(): return lax.ppermute(value, AXES, pairs)  79 us
    all_to_all x1, blocking collectives, on_device(): lax.all_to_all(outgoing, AXES, split_axis=1, concat_axis=0, tiled=True)  26.3 us
    pallas_call x5, Pallas kernels, steps(): pl.pallas_call(functools.partial(step_kernel, plan, handed, len(arrays),...  19.6 us
    ppermute x20, starting transfers between devices, send(): return lax.ppermute(value, AXES, pairs)  15.4 us
  transfers between devices with their start and end apart: 20, of which 9 were waited for; matrix products, arithmetic and copies ran while one was open for 0% of the time, Pallas kernels for 0%

profile of v9, /device:TPU:0, one launch (start us, length us, event | category | flops | bytes accessed | tf_op | source)
XLA Modules:
  0.0 143.5 jit_solution(13219651143917493448)
XLA Ops:
  0.0 0.8 slice.9
  0.8 1.1 pad_maximum_fusion
  1.9 26.3 %all_to_all.15 = bf16[8,32,1280]{2,0,1:T(8,128)(2,1)S(1)} all-to-all(bf16[8,32,1280]{2,0,1:T(8,128)(2,1)S(1)} %pad_maximum_fusion), channel_id=1, replica_groups=mesh['row'=4,'col'=8] {'row','col'}, dimensions={1} | all-to-all | bytes 1310720 | tf_op jit(solution)/shard_map/all_to_all | solution.py:247
  28.9 0.8 collective-permute-start
  29.7 4.8 %collective-permute-done.1 = bf16[256,256]{1,0:T(8,128)(2,1)S(1)} collective-permute-done((bf16[256,256]{1,0:T(8,128)(2,1)S(1)}, bf16[256,256]{1,0:T(8,128)(2,1)S(1)}, u32[]{:S(2)}, u32[]{:S(2)}) %collective-permute-start.1) | collective-permute-done | bytes 131104 | tf_op jit(solution)/shard_map/ppermute | solution.py:179
  34.8 4.6 %collective-permute-done.2 = bf16[256,256]{1,0:T(8,128)(2,1)S(1)} collective-permute-done((bf16[256,256]{1,0:T(8,128)(2,1)S(1)}, bf16[256,256]{1,0:T(8,128)(2,1)S(1)}, u32[]{:S(2)}, u32[]{:S(2)}) %collective-permute-start.2) | collective-permute-done | bytes 131104 | tf_op jit(solution)/shard_map/ppermute | solution.py:179
  39.9 1.5 %collective-permute-done.3.refs_3_ = bf16[1024,256]{1,0:T(8,128)(2,1)S(1)} collective-permute-done((bf16[1024,256]{1,0:T(8,128)(2,1)S(1)}, bf16[1024,256]{1,0:T(8,128)(2,1)S(1)}, u32[]{:S(2)}, u32[]{:S(2)}) %collective-permute-start.3) | collective-permute-done | bytes 524320 | tf_op jit(solution)/shard_map/ppermute | solution.py:179
  41.5 5.6 %shard_map.28 = (f32[1024,256]{1,0:T(8,128)S(1)}, bf16[1024,256]{1,0:T(8,128)(2,1)S(1)}) custom-call(f32[1024,256]{1,0:T(8,128)S(1)} %convert_bitcast_fusion.refs_0_, bf16[1024,8192]{1,0:T(8,128)(2,1)} %refs_1_.9, bf16[1024,256]{1,0:T(8,128)(2,1)S(1)} %pad_maximum_fusion.1.refs_2_, bf16[1024,256]{1,0:T(8,128)(2,1)S(1)} %collective-permute-done.3.refs_3_), custom_call_target="tpu_custom_call" | custom-call | flops 1073741824 | bytes 2097152 | tf_op jit(solution)/shard_map/pallas_call | solution.py:142
  47.1 0.7 collective-permute-start.4
  47.8 0.7 collective-permute-start.7
  49.2 0.7 collective-permute-start.6
  50.7 0.7 collective-permute-start.9
  53.9 1.3 collective-permute-start.13
  55.2 1.3 collective-permute-start.14
  56.5 1.5 %collective-permute-start.15 = (bf16[256,256]{1,0:T(8,128)(2,1)S(1)}, bf16[256,256]{1,0:T(8,128)(2,1)S(1)}, u32[]{:S(2)}, u32[]{:S(2)}) collective-permute-start(bf16[256,256]{1,0:T(8,128)(2,1)S(1)} %select_select_fusion.3), channel_id=1, source_target_pairs={{2,4},{3,5},{10,12},{11,13},{18,20},{19,21},{26,28},{27,29},{4,6},... | collective-permute-start | bytes 393224 | tf_op jit(solution)/shard_map/ppermute | solution.py:179
  58.1 25.7 %collective-permute-done.13 = bf16[256,256]{1,0:T(8,128)(2,1)S(1)} collective-permute-done((bf16[256,256]{1,0:T(8,128)(2,1)S(1)}, bf16[256,256]{1,0:T(8,128)(2,1)S(1)}, u32[]{:S(2)}, u32[]{:S(2)}) %collective-permute-start.13) | collective-permute-done | bytes 131104 | tf_op jit(solution)/shard_map/ppermute | solution.py:179
  83.8 14.7 %collective-permute-done.14 = bf16[256,256]{1,0:T(8,128)(2,1)S(1)} collective-permute-done((bf16[256,256]{1,0:T(8,128)(2,1)S(1)}, bf16[256,256]{1,0:T(8,128)(2,1)S(1)}, u32[]{:S(2)}, u32[]{:S(2)}) %collective-permute-start.14) | collective-permute-done | bytes 131104 | tf_op jit(solution)/shard_map/ppermute | solution.py:179
  98.5 8.5 %collective-permute-done.15 = bf16[256,256]{1,0:T(8,128)(2,1)S(1)} collective-permute-done((bf16[256,256]{1,0:T(8,128)(2,1)S(1)}, bf16[256,256]{1,0:T(8,128)(2,1)S(1)}, u32[]{:S(2)}, u32[]{:S(2)}) %collective-permute-start.15) | collective-permute-done | bytes 131104 | tf_op jit(solution)/shard_map/ppermute | solution.py:179
  107.2 1.4 collective-permute-start.17
  109.2 9.3 %collective-permute-done.17 = bf16[768,256]{1,0:T(8,128)(2,1)S(1)} collective-permute-done((bf16[768,256]{1,0:T(8,128)(2,1)S(1)}, bf16[768,256]{1,0:T(8,128)(2,1)S(1)}, u32[]{:S(2)}, u32[]{:S(2)}) %collective-permute-start.17) | collective-permute-done | bytes 393248 | tf_op jit(solution)/shard_map/ppermute | solution.py:179
  118.5 1.3 collective-permute-start.18
  119.9 6.4 %collective-permute-done.18 = bf16[768,256]{1,0:T(8,128)(2,1)S(1)} collective-permute-done((bf16[768,256]{1,0:T(8,128)(2,1)S(1)}, bf16[768,256]{1,0:T(8,128)(2,1)S(1)}, u32[]{:S(2)}, u32[]{:S(2)}) %collective-permute-start.18) | collective-permute-done | bytes 393248 | tf_op jit(solution)/shard_map/ppermute | solution.py:179
  126.4 3.4 %collective-permute-done.19.refs_3_ = bf16[3072,256]{1,0:T(8,128)(2,1)S(1)} collective-permute-done((bf16[3072,256]{1,0:T(8,128)(2,1)S(1)}, bf16[3072,256]{1,0:T(8,128)(2,1)S(1)}, u32[]{:S(2)}, u32[]{:S(2)}) %collective-permute-start.19) | collective-permute-done | bytes 1572896 | tf_op jit(solution)/shard_map/ppermute | solution.py:179
  129.8 13.6 %shard_map.32 = f32[1024,256]{1,0:T(8,128)} custom-call(f32[1024,256]{1,0:T(8,128)S(1)} %get-tuple-element.12.refs_0_, bf16[1024,8192]{1,0:T(8,128)(2,1)} %refs_1_.9, bf16[3072,256]{1,0:T(8,128)(2,1)S(1)} %constant_dynamic-update-slice_fusion.refs_2_, bf16[3072,256]{1,0:T(8,128)(2,1)S(1)} %collective-permute-done.19.refs_3_), custom_call_target="tpu_custom_call" | custom-call | flops 3221225472 | bytes 2097152 | tf_op jit(solution)/shard_map/pallas_call | solution.py:142
  (39 shorter events, 6.4 us)
Async XLA Ops:
  28.2 6.3 %collective-permute-start.1 = (bf16[256,256]{1,0:T(8,128)(2,1)S(1)}, bf16[256,256]{1,0:T(8,128)(2,1)S(1)}, u32[]{:S(2)}, u32[]{:S(2)}) collective-permute-start(bf16[256,256]{1,0:T(8,128)(2,1)S(1)} %bitcast.15), channel_id=1, source_target_pairs={{16,0},{17,1},{18,2},{19,3},{20,4},{21,5},{22,6},{23,7},{0,16},{1,... | collective-permute-start | bytes 393224 | tf_op jit(solution)/shard_map/ppermute | solution.py:179
  28.9 6.0 %collective-permute-start = (bf16[256,256]{1,0:T(8,128)(2,1)S(1)}, bf16[256,256]{1,0:T(8,128)(2,1)S(1)}, u32[]{:S(2)}, u32[]{:S(2)}) collective-permute-start(bf16[256,256]{1,0:T(8,128)(2,1)S(1)} %bitcast.16), channel_id=1, source_target_pairs={{1,0},{0,1},{3,2},{2,3},{5,4},{4,5},{7,6},{6,7},{17,16},{16,17},{1... | collective-permute-start | bytes 393224 | tf_op jit(solution)/shard_map/ppermute | solution.py:179
  34.5 5.0 %collective-permute-start.2 = (bf16[256,256]{1,0:T(8,128)(2,1)S(1)}, bf16[256,256]{1,0:T(8,128)(2,1)S(1)}, u32[]{:S(2)}, u32[]{:S(2)}) collective-permute-start(bf16[256,256]{1,0:T(8,128)(2,1)S(1)} %collective-permute-done.1), channel_id=1, source_target_pairs={{1,0},{0,1},{3,2},{2,3},{5,4},{4,5},{7,6},{6,7},{17,16},{16,17},{1... | collective-permute-start | bytes 393224 | tf_op jit(solution)/shard_map/ppermute | solution.py:179
  39.5 2.0 %collective-permute-start.3 = (bf16[1024,256]{1,0:T(8,128)(2,1)S(1)}, bf16[1024,256]{1,0:T(8,128)(2,1)S(1)}, u32[]{:S(2)}, u32[]{:S(2)}) collective-permute-start(bf16[1024,256]{1,0:T(8,128)(2,1)S(1)} %pad_maximum_fusion.1.refs_2_), channel_id=1, source_target_pairs={{8,0},{9,1},{10,2},{11,3},{12,4},{13,5},{14,6},{15,7},{0,8},{1,9},... | collective-permute-start | bytes 1572872 | tf_op jit(solution)/shard_map/ppermute | solution.py:179
  47.1 1.4 collective-permute-start.4
  47.8 2.1 %collective-permute-start.7 = (bf16[1024,256]{1,0:T(8,128)(2,1)S(1)}, bf16[1024,256]{1,0:T(8,128)(2,1)S(1)}, u32[]{:S(2)}, u32[]{:S(2)}) collective-permute-start(bf16[1024,256]{1,0:T(8,128)(2,1)S(1)} %get-tuple-element.14.refs_4_), channel_id=1, source_target_pairs={{3,4},{2,5}} | collective-permute-start | bytes 1572872 | tf_op jit(solution)/shard_map/ppermute | solution.py:179
  48.5 3.0 %collective-permute-start.5 = (bf16[1024,256]{1,0:T(8,128)(2,1)S(1)}, bf16[1024,256]{1,0:T(8,128)(2,1)S(1)}, u32[]{:S(2)}, u32[]{:S(2)}) collective-permute-start(bf16[1024,256]{1,0:T(8,128)(2,1)S(1)} %get-tuple-element.14.refs_4_), channel_id=1, source_target_pairs={{2,6},{3,7}} | collective-permute-start | bytes 1572872 | tf_op jit(solution)/shard_map/ppermute | solution.py:179
  49.2 2.3 %collective-permute-start.6 = (bf16[1024,256]{1,0:T(8,128)(2,1)S(1)}, bf16[1024,256]{1,0:T(8,128)(2,1)S(1)}, u32[]{:S(2)}, u32[]{:S(2)}) collective-permute-start(bf16[1024,256]{1,0:T(8,128)(2,1)S(1)} %get-tuple-element.14.refs_4_), channel_id=1, source_target_pairs={{3,6},{2,7}} | collective-permute-start | bytes 1572872 | tf_op jit(solution)/shard_map/ppermute | solution.py:179
  50.0 1.6 %collective-permute-start.8 = (bf16[1024,256]{1,0:T(8,128)(2,1)S(1)}, bf16[1024,256]{1,0:T(8,128)(2,1)S(1)}, u32[]{:S(2)}, u32[]{:S(2)}) collective-permute-start(bf16[1024,256]{1,0:T(8,128)(2,1)S(1)} %shard_map.30.refs_5_), channel_id=1, source_target_pairs={{4,6},{5,7}} | collective-permute-start | bytes 1572872 | tf_op jit(solution)/shard_map/ppermute | solution.py:179
  50.7 0.9 collective-permute-start.9
  51.8 2.1 %collective-permute-start.10 = (bf16[256,256]{1,0:T(8,128)(2,1)S(1)}, bf16[256,256]{1,0:T(8,128)(2,1)S(1)}, u32[]{:S(2)}, u32[]{:S(2)}) collective-permute-start(bf16[256,256]{1,0:T(8,128)(2,1)S(1)} %get-tuple-element.15), channel_id=1, source_target_pairs={{2,26},{3,27},{4,28},{5,29},{6,30},{7,31}} | collective-permute-start | bytes 393224 | tf_op jit(solution)/shard_map/ppermute | solution.py:179
  52.5 1.4 collective-permute-start.11
  53.2 0.7 collective-permute-start.12
  53.9 29.8 %collective-permute-start.13 = (bf16[256,256]{1,0:T(8,128)(2,1)S(1)}, bf16[256,256]{1,0:T(8,128)(2,1)S(1)}, u32[]{:S(2)}, u32[]{:S(2)}) collective-permute-start(bf16[256,256]{1,0:T(8,128)(2,1)S(1)} %select_select_fusion.3), channel_id=1, source_target_pairs={{2,0},{3,1},{10,8},{11,9},{18,16},{19,17},{26,24},{27,25},{4,2},{5... | collective-permute-start | bytes 393224 | tf_op jit(solution)/shard_map/ppermute | solution.py:179
  55.2 43.2 %collective-permute-start.14 = (bf16[256,256]{1,0:T(8,128)(2,1)S(1)}, bf16[256,256]{1,0:T(8,128)(2,1)S(1)}, u32[]{:S(2)}, u32[]{:S(2)}) collective-permute-start(bf16[256,256]{1,0:T(8,128)(2,1)S(1)} %select_select_fusion.3), channel_id=1, source_target_pairs={{2,6},{3,7},{10,14},{11,15},{18,22},{19,23},{26,30},{27,31},{4,0},... | collective-permute-start | bytes 393224 | tf_op jit(solution)/shard_map/ppermute | solution.py:179
  56.5 50.4 %collective-permute-start.15 = (bf16[256,256]{1,0:T(8,128)(2,1)S(1)}, bf16[256,256]{1,0:T(8,128)(2,1)S(1)}, u32[]{:S(2)}, u32[]{:S(2)}) collective-permute-start(bf16[256,256]{1,0:T(8,128)(2,1)S(1)} %select_select_fusion.3), channel_id=1, source_target_pairs={{2,4},{3,5},{10,12},{11,13},{18,20},{19,21},{26,28},{27,29},{4,6},... | collective-permute-start | bytes 393224 | tf_op jit(solution)/shard_map/ppermute | solution.py:179
  107.2 11.3 %collective-permute-start.17 = (bf16[768,256]{1,0:T(8,128)(2,1)S(1)}, bf16[768,256]{1,0:T(8,128)(2,1)S(1)}, u32[]{:S(2)}, u32[]{:S(2)}) collective-permute-start(bf16[768,256]{1,0:T(8,128)(2,1)S(1)} %pad_maximum_fusion.2), channel_id=1, source_target_pairs={{16,0},{17,1},{18,2},{19,3},{20,4},{21,5},{22,6},{23,7},{0,16},{1,... | collective-permute-start | bytes 1179656 | tf_op jit(solution)/shard_map/ppermute | solution.py:179
  108.6 11.2 %collective-permute-start.16 = (bf16[768,256]{1,0:T(8,128)(2,1)S(1)}, bf16[768,256]{1,0:T(8,128)(2,1)S(1)}, u32[]{:S(2)}, u32[]{:S(2)}) collective-permute-start(bf16[768,256]{1,0:T(8,128)(2,1)S(1)} %pad_maximum_fusion.2), channel_id=1, source_target_pairs={{1,0},{0,1},{3,2},{2,3},{5,4},{4,5},{7,6},{6,7},{17,16},{16,17},{1... | collective-permute-start | bytes 1179656 | tf_op jit(solution)/shard_map/ppermute | solution.py:179
  118.5 7.8 %collective-permute-start.18 = (bf16[768,256]{1,0:T(8,128)(2,1)S(1)}, bf16[768,256]{1,0:T(8,128)(2,1)S(1)}, u32[]{:S(2)}, u32[]{:S(2)}) collective-permute-start(bf16[768,256]{1,0:T(8,128)(2,1)S(1)} %collective-permute-done.17), channel_id=1, source_target_pairs={{1,0},{0,1},{3,2},{2,3},{5,4},{4,5},{7,6},{6,7},{17,16},{16,17},{1... | collective-permute-start | bytes 1179656 | tf_op jit(solution)/shard_map/ppermute | solution.py:179
  126.3 3.5 %collective-permute-start.19 = (bf16[3072,256]{1,0:T(8,128)(2,1)S(1)}, bf16[3072,256]{1,0:T(8,128)(2,1)S(1)}, u32[]{:S(2)}, u32[]{:S(2)}) collective-permute-start(bf16[3072,256]{1,0:T(8,128)(2,1)S(1)} %constant_dynamic-update-slice_fusion.refs_2_), channel_id=1, source_target_pairs={{8,0},{9,1},{10,2},{11,3},{12,4},{13,5},{14,6},{15,7},{0,8},{1,9},... | collective-permute-start | bytes 4718600 | tf_op jit(solution)/shard_map/ppermute | solution.py:179

commit v10 on v9

--- a/solution.py
+++ b/solution.py
@@ -13,7 +13,7 @@
 CORES = 2
 TILE = 256
 IN_FLIGHT = 3
-KERNEL_VMEM = 40 * 1024 * 1024
+MIB = 1024 * 1024
 
 
 def after(value, *others):
@@ -29,17 +29,20 @@
 
 
 def step_kernel(terms, handed, n_arrays, outs, where_am_i, only, *refs):
-    current, panels = refs[:2]
-    arrays = refs[2 : 2 + n_arrays]
-    results = refs[2 + n_arrays : 2 + n_arrays + len(outs)]
-    current_here, panels_here, held, sems, piece_sems, out_sems = refs[2 + n_arrays + len(outs) :]
+    refs = list(refs)
+    current = refs.pop(0)
+    panels = refs.pop(0) if any(near is None for _, _, near in terms) else None
+    near_panels = [None if near is None else refs.pop(0) for _, _, near in terms]
+    arrays, refs = refs[:n_arrays], refs[n_arrays:]
+    results, refs = refs[: len(outs)], refs[len(outs) :]
+    current_here, panels_here, held, sems, piece_sems, out_sems = refs
     rows = current.shape[0]
     tile = min(TILE, rows)
     here = where_am_i()
 
     def work():
         copies = [[] for _ in terms]
-        for t, (_, pieces) in enumerate(terms):
+        for t, (_, pieces, _) in enumerate(terms):
             for array, first, size, place in pieces:
                 start = pl.multiple_of(place(here) * size, size)
                 copies[t].append(
@@ -64,7 +67,8 @@
             if i == 0:
                 for copy in copies[t]:
                     copy.start()
-            panel_copy(t, i).start()
+            if near_panels[t] is None:
+                panel_copy(t, i).start()
             if t == 0:
                 current_copy(i).start()
 
@@ -81,10 +85,14 @@
             if t == 0:
                 current_copy(i).wait()
                 value = current_here[at, :]
-            panel_copy(t, i).wait()
+            if near_panels[t] is None:
+                panel_copy(t, i).wait()
+                panel = panels_here[t, i]
+            else:
+                panel = near_panels[t][at, :]
             if n + in_flight < len(order):
                 load(*order[n + in_flight])
-            product = jnp.dot(panels_here[t, i], held[t], preferred_element_type=jnp.float32)
+            product = jnp.dot(panel, held[t], preferred_element_type=jnp.float32)
             value = jnp.where(here.block == terms[t][0], product, value - product)
             if t < len(terms) - 1:
                 continue
@@ -132,33 +140,64 @@
         return len(arrays) - 1
 
     plan = tuple(
-        (k, tuple((index(array), first, size, place) for array, first, size, place in pieces)) for k, pieces in terms
+        (k, tuple((index(array), first, size, place) for array, first, size, place in pieces), None if near is None else 0)
+        for k, pieces, near in terms
     )
+    near_panels = [near for _, _, near in terms if near is not None]
     handed = tuple((block, index(array)) for block, array in handed)
     n_terms = len(terms)
     tile = min(TILE, rows)
-    n_pieces = max(sum(len(pieces) for _, pieces in terms), len(outs))
+    n_pieces = max(sum(len(pieces) for _, pieces, _ in terms), len(outs))
+    n_far = max(n_terms - len(near_panels), 1)
+    assert not near_panels or len(near_panels) == n_terms
     anywhere = pl.BlockSpec(memory_space=pl.ANY)
     return pl.pallas_call(
         functools.partial(step_kernel, plan, handed, len(arrays), tuple(outs), where_am_i, only),
-        in_specs=[anywhere] * (2 + len(arrays)),
+        in_specs=[anywhere] * (1 if near_panels else 2)
+        + [pl.BlockSpec(memory_space=pltpu.VMEM)] * len(near_panels)
+        + [anywhere] * len(arrays),
         out_specs=[anywhere if out[3] else pl.BlockSpec(memory_space=pltpu.VMEM) for out in outs],
         out_shape=[jax.ShapeDtypeStruct((size, scenarios), dtype) for dtype, _, size, _ in outs],
         scratch_shapes=[
             pltpu.VMEM((rows, scenarios), jnp.float32),
-            pltpu.VMEM((n_terms, rows // tile, tile, NB), jnp.bfloat16),
+            pltpu.VMEM((n_far, 1 if near_panels else rows // tile, 16 if near_panels else tile, NB), jnp.bfloat16),
             pltpu.VMEM((n_terms, NB, scenarios), jnp.bfloat16),
             pltpu.SemaphoreType.DMA((n_terms + 1, rows // tile)),
             pltpu.SemaphoreType.DMA((n_pieces,)),
             pltpu.SemaphoreType.DMA((rows // tile,)),
         ],
-        compiler_params=pltpu.CompilerParams(vmem_limit_bytes=KERNEL_VMEM),
+        compiler_params=pltpu.CompilerParams(vmem_limit_bytes=(28 if near_panels else 48) * MIB),
         cost_estimate=pl.CostEstimate(
             flops=2 * rows * NB * scenarios * n_terms,
             bytes_accessed=8 * rows * scenarios,
             transcendentals=0,
         ),
-    )(current, factor_panels, *arrays)
+    )(current, *([] if near_panels else [factor_panels]), *near_panels, *arrays)
+
+
+def near_kernel(k, panels, out, sems):
+    parts = sems.shape[0]
+    rows = out.shape[0] // parts
+    copies = []
+    for i in range(parts):
+        at = pl.ds(i * rows, rows)
+        copies.append(pltpu.make_async_copy(panels.at[at, pl.ds(k * NB, NB)], out.at[at, :], sems.at[i]))
+        copies[-1].start()
+    for copy in copies:
+        copy.wait()
+
+
+def near_panel(factor_panels, k):
+    rows = factor_panels.shape[0]
+    return pl.pallas_call(
+        functools.partial(near_kernel, k),
+        in_specs=[pl.BlockSpec(memory_space=pl.ANY)],
+        out_specs=pl.BlockSpec(memory_space=pl.ANY),
+        out_shape=pltpu.VMEM((rows, NB), jnp.bfloat16),
+        scratch_shapes=[pltpu.SemaphoreType.DMA((4,))],
+        compiler_params=pltpu.CompilerParams(vmem_limit_bytes=44 * MIB),
+        cost_estimate=pl.CostEstimate(flops=0, bytes_accessed=1, transcendentals=0),
+    )(factor_panels)
 
 
 def make_on_device(n_row, n_col):
@@ -251,18 +290,20 @@
         pieces = gathered_pieces(
             whole, core_exchange(whole), 0, extra, extra, lambda y, c, m: (y * CORES + c) * lanes + m
         )
-        current, own1 = run(current, [(0, pieces)], [f32_rows, own_rows])
+        current, own1 = run(current, [(0, pieces, None)], [f32_rows, own_rows])
 
         hop1 = ahead(own1, 1)
-        start1 = after(own1, hop1[0])
+        near1 = near_panel(after(factor_panels, own1), 1)
+        start1 = after(own1, hop1[0], near1)
         at_3 = [
             send(start1, [(device(0, 0, 1, (m + d) % lanes), device(0, 0, 3, m)) for m in range(lanes)])
             for d in range(lanes)
         ]
-        (own2,) = run(current, [(1, lane_pieces(hop1))], [own_rows], 2)
+        (own2,) = run(current, [(1, lane_pieces(hop1), near1)], [own_rows], 2)
         hop2 = ahead(own2, 2)
-        (chained,) = run(current, [(1, lane_pieces(at_3))], [f32_rows], 3)
-        cuts = run(chained, [(2, lane_pieces(hop2))], own_cuts, 3, [(1, own1), (2, own2)])
+        near2 = near_panel(after(factor_panels, own2), 2)
+        (chained,) = run(after(current, near2), [(1, lane_pieces(at_3), near1)], [f32_rows], 3)
+        cuts = run(chained, [(2, lane_pieces(hop2), near2)], own_cuts, 3, [(1, own1), (2, own2)])
 
         piece = cuts[0]
         for t in range(1, n_row):
@@ -286,7 +327,8 @@
             for d in range(1, planes):
                 value = jnp.where(plane == (k + d) % planes, got[d - 1], value)
             three.append(value)
-        whole = plane_gather(jnp.concatenate(three, axis=0))
+        near3 = near_panel(after(factor_panels, cuts[0]), 3)
+        whole = plane_gather(after(jnp.concatenate(three, axis=0), near3))
         other = core_exchange(whole)
         terms = [
             (
@@ -294,8 +336,9 @@
                 gathered_pieces(
                     whole, other, (k - 1) * cut, cut, (STEPS - 1) * cut, lambda y, c, m: m * n_row + y * CORES + c
                 ),
+                near,
             )
-            for k in range(1, STEPS)
+            for k, near in ((1, near1), (2, near2), (3, near3))
         ]
         (out,) = run(current, terms, [(jnp.float32, 0, rows_here, True)])
         return out

time: 144 us -> 140 us (0.972)
  waiting for transfers between devices: 79 us -> 69.2 us
  Pallas kernels: 19.6 us -> 24.2 us
  local copies, waits for them, and re-layouts: 1.22 us -> 3.07 us
    ppermute x20, waiting for transfers between devices: 79 us -> 69.2 us  [send(): return lax.ppermute(value, AXES, pairs)]
    pallas_call x0 -> x3, Pallas kernels: none -> 6.8 us  [near_panel(): pl.pallas_call(functools.partial(near_kernel, k), in_specs=[pl.BlockSpec(...]
    pallas_call x5, Pallas kernels: 19.6 us -> 17.4 us  [steps(): pl.pallas_call(functools.partial(step_kernel, plan, handed, len(arrays),...]
    unnamed x4 -> x13, local copies, waits for them, and re-layouts: 0.36 us -> 2.21 us
  transfers between devices with their start and end apart: 20 -> 20, of which waited for: 9 -> 9; matrix products, arithmetic and copies ran while one was open for 0% -> 0% of each run, Pallas kernels for 0% -> 5%
where the time goes in v10:
time: 140 us
  waiting for transfers between devices  69.2 us (49%)
  blocking collectives  26.3 us (19%)
  Pallas kernels  24.2 us (17%)
  starting transfers between devices  15.4 us (11%)
  local copies, waits for them, and re-layouts  3.07 us (2%)
    ppermute x20, waiting for transfers between devices, send(): return lax.ppermute(value, AXES, pairs)  69.2 us
    all_to_all x1, blocking collectives, on_device(): lax.all_to_all(outgoing, AXES, split_axis=1, concat_axis=0, tiled=True)  26.3 us
    pallas_call x5, Pallas kernels, steps(): pl.pallas_call(functools.partial(step_kernel, plan, handed, len(arrays),...  17.4 us
    ppermute x20, starting transfers between devices, send(): return lax.ppermute(value, AXES, pairs)  15.4 us
    pallas_call x3, Pallas kernels, near_panel(): pl.pallas_call(functools.partial(near_kernel, k), in_specs=[pl.BlockSpec(...  6.8 us
  transfers between devices with their start and end apart: 20, of which 9 were waited for; matrix products, arithmetic and copies ran while one was open for 0% of the time, Pallas kernels for 5%

profile of v10, /device:TPU:0, one launch (start us, length us, event | category | flops | bytes accessed | tf_op | source)
XLA Modules:
  0.0 140.0 jit_solution(15778015164773359269)
XLA Ops:
  0.0 0.8 slice.9
  0.8 1.1 pad_maximum_fusion
  1.9 26.3 %all_to_all.15 = bf16[8,32,1280]{2,0,1:T(8,128)(2,1)S(1)} all-to-all(bf16[8,32,1280]{2,0,1:T(8,128)(2,1)S(1)} %pad_maximum_fusion), channel_id=1, replica_groups=mesh['row'=4,'col'=8] {'row','col'}, dimensions={1} | all-to-all | bytes 1310720 | tf_op jit(solution)/shard_map/all_to_all | solution.py:286
  28.9 0.8 collective-permute-start
  29.7 4.8 %collective-permute-done.1 = bf16[256,256]{1,0:T(8,128)(2,1)S(1)} collective-permute-done((bf16[256,256]{1,0:T(8,128)(2,1)S(1)}, bf16[256,256]{1,0:T(8,128)(2,1)S(1)}, u32[]{:S(2)}, u32[]{:S(2)}) %collective-permute-start.1) | collective-permute-done | bytes 131104 | tf_op jit(solution)/shard_map/ppermute | solution.py:218
  34.8 4.6 %collective-permute-done.2 = bf16[256,256]{1,0:T(8,128)(2,1)S(1)} collective-permute-done((bf16[256,256]{1,0:T(8,128)(2,1)S(1)}, bf16[256,256]{1,0:T(8,128)(2,1)S(1)}, u32[]{:S(2)}, u32[]{:S(2)}) %collective-permute-start.2) | collective-permute-done | bytes 131104 | tf_op jit(solution)/shard_map/ppermute | solution.py:218
  39.9 1.5 %collective-permute-done.3.refs_3_ = bf16[1024,256]{1,0:T(8,128)(2,1)S(1)} collective-permute-done((bf16[1024,256]{1,0:T(8,128)(2,1)S(1)}, bf16[1024,256]{1,0:T(8,128)(2,1)S(1)}, u32[]{:S(2)}, u32[]{:S(2)}) %collective-permute-start.3) | collective-permute-done | bytes 524320 | tf_op jit(solution)/shard_map/ppermute | solution.py:218
  41.5 5.6 %shard_map.28 = (f32[1024,256]{1,0:T(8,128)S(1)}, bf16[1024,256]{1,0:T(8,128)(2,1)S(1)}) custom-call(f32[1024,256]{1,0:T(8,128)S(1)} %convert_bitcast_fusion.refs_0_, bf16[1024,8192]{1,0:T(8,128)(2,1)} %panels.2, bf16[1024,256]{1,0:T(8,128)(2,1)S(1)} %pad_maximum_fusion.1.refs_2_, bf16[1024,256]{1,0:T(8,128)(2,1)S(1)} %collective-permute-done.3.refs_3_), custom_call_target="tpu_custom_call" | custom-call | flops 1073741824 | bytes 2097152 | tf_op jit(solution)/shard_map/pallas_call | solution.py:154
  48.5 2.2 %shard_map.29.refs_1_ = bf16[1024,2048]{1,0:T(8,128)(2,1)S(1)} custom-call(bf16[1024,8192]{1,0:T(8,128)(2,1)} %panels.2), custom_call_target="tpu_custom_call" | custom-call | bytes 1 | tf_op jit(solution)/shard_map/pallas_call | solution.py:192
  53.7 2.2 %shard_map.31.refs_1_.refs_2_ = bf16[1024,2048]{1,0:T(8,128)(2,1)S(1)} custom-call(bf16[1024,8192]{1,0:T(8,128)(2,1)} %panels.2), custom_call_target="tpu_custom_call" | custom-call | bytes 1 | tf_op jit(solution)/shard_map/pallas_call | solution.py:192
  56.2 1.8 %copy-done.2 = bf16[1024,2048]{1,0:T(8,128)(2,1)} copy-done((bf16[1024,2048]{1,0:T(8,128)(2,1)}, bf16[1024,2048]{1,0:T(8,128)(2,1)S(1)}, u32[]{:S(2)}) %copy-start.2) | copy-done | bytes 4194328
  60.3 1.3 collective-permute-start.13
  61.6 1.3 collective-permute-start.14
  62.9 1.5 %collective-permute-start.15 = (bf16[256,256]{1,0:T(8,128)(2,1)S(1)}, bf16[256,256]{1,0:T(8,128)(2,1)S(1)}, u32[]{:S(2)}, u32[]{:S(2)}) collective-permute-start(bf16[256,256]{1,0:T(8,128)(2,1)S(1)} %select_select_fusion.3), channel_id=1, source_target_pairs={{2,4},{3,5},{10,12},{11,13},{18,20},{19,21},{26,28},{27,29},{4,6},... | collective-permute-start | bytes 393224 | tf_op jit(solution)/shard_map/ppermute | solution.py:218
  64.4 2.4 %shard_map.34.refs_3_ = bf16[1024,2048]{1,0:T(8,128)(2,1)S(1)} custom-call(bf16[1024,8192]{1,0:T(8,128)(2,1)} %panels.2), custom_call_target="tpu_custom_call" | custom-call | bytes 1 | tf_op jit(solution)/shard_map/pallas_call | solution.py:192
  66.7 17.1 %collective-permute-done.13 = bf16[256,256]{1,0:T(8,128)(2,1)S(1)} collective-permute-done((bf16[256,256]{1,0:T(8,128)(2,1)S(1)}, bf16[256,256]{1,0:T(8,128)(2,1)S(1)}, u32[]{:S(2)}, u32[]{:S(2)}) %collective-permute-start.13) | collective-permute-done | bytes 131104 | tf_op jit(solution)/shard_map/ppermute | solution.py:218
  83.9 14.7 %collective-permute-done.14 = bf16[256,256]{1,0:T(8,128)(2,1)S(1)} collective-permute-done((bf16[256,256]{1,0:T(8,128)(2,1)S(1)}, bf16[256,256]{1,0:T(8,128)(2,1)S(1)}, u32[]{:S(2)}, u32[]{:S(2)}) %collective-permute-start.14) | collective-permute-done | bytes 131104 | tf_op jit(solution)/shard_map/ppermute | solution.py:218
  98.5 7.3 %collective-permute-done.15 = bf16[256,256]{1,0:T(8,128)(2,1)S(1)} collective-permute-done((bf16[256,256]{1,0:T(8,128)(2,1)S(1)}, bf16[256,256]{1,0:T(8,128)(2,1)S(1)}, u32[]{:S(2)}, u32[]{:S(2)}) %collective-permute-start.15) | collective-permute-done | bytes 131104 | tf_op jit(solution)/shard_map/ppermute | solution.py:218
  106.0 1.4 %collective-permute-start.17 = (bf16[768,256]{1,0:T(8,128)(2,1)S(1)}, bf16[768,256]{1,0:T(8,128)(2,1)S(1)}, u32[]{:S(2)}, u32[]{:S(2)}) collective-permute-start(bf16[768,256]{1,0:T(8,128)(2,1)S(1)} %pad_maximum_fusion.2), channel_id=1, source_target_pairs={{16,0},{17,1},{18,2},{19,3},{20,4},{21,5},{22,6},{23,7},{0,16},{1,... | collective-permute-start | bytes 1179656 | tf_op jit(solution)/shard_map/ppermute | solution.py:218
  108.0 9.3 %collective-permute-done.17 = bf16[768,256]{1,0:T(8,128)(2,1)S(1)} collective-permute-done((bf16[768,256]{1,0:T(8,128)(2,1)S(1)}, bf16[768,256]{1,0:T(8,128)(2,1)S(1)}, u32[]{:S(2)}, u32[]{:S(2)}) %collective-permute-start.17) | collective-permute-done | bytes 393248 | tf_op jit(solution)/shard_map/ppermute | solution.py:218
  117.3 1.3 collective-permute-start.18
  118.7 6.3 %collective-permute-done.18 = bf16[768,256]{1,0:T(8,128)(2,1)S(1)} collective-permute-done((bf16[768,256]{1,0:T(8,128)(2,1)S(1)}, bf16[768,256]{1,0:T(8,128)(2,1)S(1)}, u32[]{:S(2)}, u32[]{:S(2)}) %collective-permute-start.18) | collective-permute-done | bytes 393248 | tf_op jit(solution)/shard_map/ppermute | solution.py:218
  125.1 3.4 %collective-permute-done.19.refs_5_ = bf16[3072,256]{1,0:T(8,128)(2,1)S(1)} collective-permute-done((bf16[3072,256]{1,0:T(8,128)(2,1)S(1)}, bf16[3072,256]{1,0:T(8,128)(2,1)S(1)}, u32[]{:S(2)}, u32[]{:S(2)}) %collective-permute-start.19) | collective-permute-done | bytes 1572896 | tf_op jit(solution)/shard_map/ppermute | solution.py:218
  128.5 11.3 %shard_map.35 = f32[1024,256]{1,0:T(8,128)} custom-call(f32[1024,256]{1,0:T(8,128)S(1)} %get-tuple-element.21.refs_0_, bf16[1024,2048]{1,0:T(8,128)(2,1)S(1)} %copy-done.1, bf16[1024,2048]{1,0:T(8,128)(2,1)S(1)} %copy-done.3, bf16[1024,2048]{1,0:T(8,128)(2,1)S(1)} %shard_map.34.refs_3_, bf16[3072,256]{1,0:T(8,128)(2,1)S(1)} %constant_dynamic-update-slice_fusion.refs_4_, ...), custom_call_target="tpu_custom_call" | custom-call | flops 3221225472 | bytes 2097152 | tf_op jit(solution)/shard_map/pallas_call | solution.py:154
  (49 shorter events, 9.0 us)
Async XLA Ops:
  28.2 6.3 %collective-permute-start.1 = (bf16[256,256]{1,0:T(8,128)(2,1)S(1)}, bf16[256,256]{1,0:T(8,128)(2,1)S(1)}, u32[]{:S(2)}, u32[]{:S(2)}) collective-permute-start(bf16[256,256]{1,0:T(8,128)(2,1)S(1)} %bitcast.15), channel_id=1, source_target_pairs={{16,0},{17,1},{18,2},{19,3},{20,4},{21,5},{22,6},{23,7},{0,16},{1,... | collective-permute-start | bytes 393224 | tf_op jit(solution)/shard_map/ppermute | solution.py:218
  28.9 6.0 %collective-permute-start = (bf16[256,256]{1,0:T(8,128)(2,1)S(1)}, bf16[256,256]{1,0:T(8,128)(2,1)S(1)}, u32[]{:S(2)}, u32[]{:S(2)}) collective-permute-start(bf16[256,256]{1,0:T(8,128)(2,1)S(1)} %bitcast.16), channel_id=1, source_target_pairs={{1,0},{0,1},{3,2},{2,3},{5,4},{4,5},{7,6},{6,7},{17,16},{16,17},{1... | collective-permute-start | bytes 393224 | tf_op jit(solution)/shard_map/ppermute | solution.py:218
  34.5 5.0 %collective-permute-start.2 = (bf16[256,256]{1,0:T(8,128)(2,1)S(1)}, bf16[256,256]{1,0:T(8,128)(2,1)S(1)}, u32[]{:S(2)}, u32[]{:S(2)}) collective-permute-start(bf16[256,256]{1,0:T(8,128)(2,1)S(1)} %collective-permute-done.1), channel_id=1, source_target_pairs={{1,0},{0,1},{3,2},{2,3},{5,4},{4,5},{7,6},{6,7},{17,16},{16,17},{1... | collective-permute-start | bytes 393224 | tf_op jit(solution)/shard_map/ppermute | solution.py:218
  39.5 2.0 %collective-permute-start.3 = (bf16[1024,256]{1,0:T(8,128)(2,1)S(1)}, bf16[1024,256]{1,0:T(8,128)(2,1)S(1)}, u32[]{:S(2)}, u32[]{:S(2)}) collective-permute-start(bf16[1024,256]{1,0:T(8,128)(2,1)S(1)} %pad_maximum_fusion.1.refs_2_), channel_id=1, source_target_pairs={{8,0},{9,1},{10,2},{11,3},{12,4},{13,5},{14,6},{15,7},{0,8},{1,9},... | collective-permute-start | bytes 1572872 | tf_op jit(solution)/shard_map/ppermute | solution.py:218
  47.1 3.6 %collective-permute-start.4 = (bf16[1024,256]{1,0:T(8,128)(2,1)S(1)}, bf16[1024,256]{1,0:T(8,128)(2,1)S(1)}, u32[]{:S(2)}, u32[]{:S(2)}) collective-permute-start(bf16[1024,256]{1,0:T(8,128)(2,1)S(1)} %get-tuple-element.22.refs_4_), channel_id=1, source_target_pairs={{2,4},{3,5}} | collective-permute-start | bytes 1572872 | tf_op jit(solution)/shard_map/ppermute | solution.py:218
  47.8 4.4 %collective-permute-start.5 = (bf16[1024,256]{1,0:T(8,128)(2,1)S(1)}, bf16[1024,256]{1,0:T(8,128)(2,1)S(1)}, u32[]{:S(2)}, u32[]{:S(2)}) collective-permute-start(bf16[1024,256]{1,0:T(8,128)(2,1)S(1)} %get-tuple-element.22.refs_4_), channel_id=1, source_target_pairs={{3,4},{2,5}} | collective-permute-start | bytes 1572872 | tf_op jit(solution)/shard_map/ppermute | solution.py:218
  50.7 5.3 %copy-start = (bf16[1024,2048]{1,0:T(8,128)(2,1)}, bf16[1024,2048]{1,0:T(8,128)(2,1)S(1)}, u32[]{:S(2)}) copy-start(bf16[1024,2048]{1,0:T(8,128)(2,1)S(1)} %shard_map.29.refs_1_) | copy-start | bytes 12582916
  50.8 5.2 %collective-permute-start.6 = (bf16[1024,256]{1,0:T(8,128)(2,1)S(1)}, bf16[1024,256]{1,0:T(8,128)(2,1)S(1)}, u32[]{:S(2)}, u32[]{:S(2)}) collective-permute-start(bf16[1024,256]{1,0:T(8,128)(2,1)S(1)} %get-tuple-element.22.refs_4_), channel_id=1, source_target_pairs={{2,6},{3,7}} | collective-permute-start | bytes 1572872 | tf_op jit(solution)/shard_map/ppermute | solution.py:218
  51.5 4.5 %collective-permute-start.7 = (bf16[1024,256]{1,0:T(8,128)(2,1)S(1)}, bf16[1024,256]{1,0:T(8,128)(2,1)S(1)}, u32[]{:S(2)}, u32[]{:S(2)}) collective-permute-start(bf16[1024,256]{1,0:T(8,128)(2,1)S(1)} %get-tuple-element.22.refs_4_), channel_id=1, source_target_pairs={{3,6},{2,7}} | collective-permute-start | bytes 1572872 | tf_op jit(solution)/shard_map/ppermute | solution.py:218
  52.3 3.8 %collective-permute-start.8 = (bf16[1024,256]{1,0:T(8,128)(2,1)S(1)}, bf16[1024,256]{1,0:T(8,128)(2,1)S(1)}, u32[]{:S(2)}, u32[]{:S(2)}) collective-permute-start(bf16[1024,256]{1,0:T(8,128)(2,1)S(1)} %shard_map.30.refs_5_), channel_id=1, source_target_pairs={{4,6},{5,7}} | collective-permute-start | bytes 1572872 | tf_op jit(solution)/shard_map/ppermute | solution.py:218
  53.0 3.1 %collective-permute-start.9 = (bf16[1024,256]{1,0:T(8,128)(2,1)S(1)}, bf16[1024,256]{1,0:T(8,128)(2,1)S(1)}, u32[]{:S(2)}, u32[]{:S(2)}) collective-permute-start(bf16[1024,256]{1,0:T(8,128)(2,1)S(1)} %shard_map.30.refs_5_), channel_id=1, source_target_pairs={{5,6},{4,7}} | collective-permute-start | bytes 1572872 | tf_op jit(solution)/shard_map/ppermute | solution.py:218
  56.0 2.0 %copy-start.2 = (bf16[1024,2048]{1,0:T(8,128)(2,1)}, bf16[1024,2048]{1,0:T(8,128)(2,1)S(1)}, u32[]{:S(2)}) copy-start(bf16[1024,2048]{1,0:T(8,128)(2,1)S(1)} %shard_map.31.refs_1_.refs_2_) | copy-start | bytes 12582916
  58.1 2.1 %collective-permute-start.10 = (bf16[256,256]{1,0:T(8,128)(2,1)S(1)}, bf16[256,256]{1,0:T(8,128)(2,1)S(1)}, u32[]{:S(2)}, u32[]{:S(2)}) collective-permute-start(bf16[256,256]{1,0:T(8,128)(2,1)S(1)} %get-tuple-element.25), channel_id=1, source_target_pairs={{2,26},{3,27},{4,28},{5,29},{6,30},{7,31}} | collective-permute-start | bytes 393224 | tf_op jit(solution)/shard_map/ppermute | solution.py:218
  58.8 1.4 collective-permute-start.11
  59.5 0.7 collective-permute-start.12
  60.3 23.6 %collective-permute-start.13 = (bf16[256,256]{1,0:T(8,128)(2,1)S(1)}, bf16[256,256]{1,0:T(8,128)(2,1)S(1)}, u32[]{:S(2)}, u32[]{:S(2)}) collective-permute-start(bf16[256,256]{1,0:T(8,128)(2,1)S(1)} %select_select_fusion.3), channel_id=1, source_target_pairs={{2,0},{3,1},{10,8},{11,9},{18,16},{19,17},{26,24},{27,25},{4,2},{5... | collective-permute-start | bytes 393224 | tf_op jit(solution)/shard_map/ppermute | solution.py:218
  61.6 37.0 %collective-permute-start.14 = (bf16[256,256]{1,0:T(8,128)(2,1)S(1)}, bf16[256,256]{1,0:T(8,128)(2,1)S(1)}, u32[]{:S(2)}, u32[]{:S(2)}) collective-permute-start(bf16[256,256]{1,0:T(8,128)(2,1)S(1)} %select_select_fusion.3), channel_id=1, source_target_pairs={{2,6},{3,7},{10,14},{11,15},{18,22},{19,23},{26,30},{27,31},{4,0},... | collective-permute-start | bytes 393224 | tf_op jit(solution)/shard_map/ppermute | solution.py:218
  62.9 43.0 %collective-permute-start.15 = (bf16[256,256]{1,0:T(8,128)(2,1)S(1)}, bf16[256,256]{1,0:T(8,128)(2,1)S(1)}, u32[]{:S(2)}, u32[]{:S(2)}) collective-permute-start(bf16[256,256]{1,0:T(8,128)(2,1)S(1)} %select_select_fusion.3), channel_id=1, source_target_pairs={{2,4},{3,5},{10,12},{11,13},{18,20},{19,21},{26,28},{27,29},{4,6},... | collective-permute-start | bytes 393224 | tf_op jit(solution)/shard_map/ppermute | solution.py:218
  64.4 64.2 %copy-start.3 = (bf16[1024,2048]{1,0:T(8,128)(2,1)S(1)}, bf16[1024,2048]{1,0:T(8,128)(2,1)}, u32[]{:S(2)}) copy-start(bf16[1024,2048]{1,0:T(8,128)(2,1)} %copy-done.2) | copy-start | bytes 12582916
  105.9 22.7 %copy-start.1 = (bf16[1024,2048]{1,0:T(8,128)(2,1)S(1)}, bf16[1024,2048]{1,0:T(8,128)(2,1)}, u32[]{:S(2)}) copy-start(bf16[1024,2048]{1,0:T(8,128)(2,1)} %copy-done) | copy-start | bytes 12582916
  106.0 11.3 %collective-permute-start.17 = (bf16[768,256]{1,0:T(8,128)(2,1)S(1)}, bf16[768,256]{1,0:T(8,128)(2,1)S(1)}, u32[]{:S(2)}, u32[]{:S(2)}) collective-permute-start(bf16[768,256]{1,0:T(8,128)(2,1)S(1)} %pad_maximum_fusion.2), channel_id=1, source_target_pairs={{16,0},{17,1},{18,2},{19,3},{20,4},{21,5},{22,6},{23,7},{0,16},{1,... | collective-permute-start | bytes 1179656 | tf_op jit(solution)/shard_map/ppermute | solution.py:218
  107.4 11.2 %collective-permute-start.16 = (bf16[768,256]{1,0:T(8,128)(2,1)S(1)}, bf16[768,256]{1,0:T(8,128)(2,1)S(1)}, u32[]{:S(2)}, u32[]{:S(2)}) collective-permute-start(bf16[768,256]{1,0:T(8,128)(2,1)S(1)} %pad_maximum_fusion.2), channel_id=1, source_target_pairs={{1,0},{0,1},{3,2},{2,3},{5,4},{4,5},{7,6},{6,7},{17,16},{16,17},{1... | collective-permute-start | bytes 1179656 | tf_op jit(solution)/shard_map/ppermute | solution.py:218
  117.3 7.8 %collective-permute-start.18 = (bf16[768,256]{1,0:T(8,128)(2,1)S(1)}, bf16[768,256]{1,0:T(8,128)(2,1)S(1)}, u32[]{:S(2)}, u32[]{:S(2)}) collective-permute-start(bf16[768,256]{1,0:T(8,128)(2,1)S(1)} %collective-permute-done.17), channel_id=1, source_target_pairs={{1,0},{0,1},{3,2},{2,3},{5,4},{4,5},{7,6},{6,7},{17,16},{16,17},{1... | collective-permute-start | bytes 1179656 | tf_op jit(solution)/shard_map/ppermute | solution.py:218
  125.1 3.5 %collective-permute-start.19 = (bf16[3072,256]{1,0:T(8,128)(2,1)S(1)}, bf16[3072,256]{1,0:T(8,128)(2,1)S(1)}, u32[]{:S(2)}, u32[]{:S(2)}) collective-permute-start(bf16[3072,256]{1,0:T(8,128)(2,1)S(1)} %constant_dynamic-update-slice_fusion.refs_4_), channel_id=1, source_target_pairs={{8,0},{9,1},{10,2},{11,3},{12,4},{13,5},{14,6},{15,7},{0,8},{1,9},... | collective-permute-start | bytes 4718600 | tf_op jit(solution)/shard_map/ppermute | solution.py:218

commit v11 on v10

--- a/solution.py
+++ b/solution.py
@@ -12,6 +12,7 @@
 AXES = ("row", "col")
 CORES = 2
 TILE = 256
+NEAR_TILE = 512
 IN_FLIGHT = 3
 MIB = 1024 * 1024
 
@@ -31,20 +32,23 @@
 def step_kernel(terms, handed, n_arrays, outs, where_am_i, only, *refs):
     refs = list(refs)
     current = refs.pop(0)
-    panels = refs.pop(0) if any(near is None for _, _, near in terms) else None
-    near_panels = [None if near is None else refs.pop(0) for _, _, near in terms]
+    panels = refs.pop(0) if any(near is None for _, _, near, _ in terms) else None
+    near_panels = [None if near is None else refs.pop(0) for _, _, near, _ in terms]
     arrays, refs = refs[:n_arrays], refs[n_arrays:]
     results, refs = refs[: len(outs)], refs[len(outs) :]
     current_here, panels_here, held, sems, piece_sems, out_sems = refs
     rows = current.shape[0]
-    tile = min(TILE, rows)
+    tile = min(NEAR_TILE if near_panels[0] is not None else TILE, rows)
     here = where_am_i()
 
     def work():
         copies = [[] for _ in terms]
-        for t, (_, pieces, _) in enumerate(terms):
-            for array, first, size, place in pieces:
-                start = pl.multiple_of(place(here) * size, size)
+        places, part_of_block = [], []
+        for t, (_, pieces, _, _) in enumerate(terms):
+            places.append([pl.multiple_of(place(here) * size, size) for _, _, size, place in pieces])
+            part_of_block.append(sum(size for _, _, size, _ in pieces) < NB)
+            for j, (array, first, size, _) in enumerate(pieces):
+                start = j * size if part_of_block[t] else places[t][j]
                 copies[t].append(
                     pltpu.make_async_copy(
                         arrays[array].at[pl.ds(first, size), :],
@@ -89,11 +93,21 @@
                 panel_copy(t, i).wait()
                 panel = panels_here[t, i]
             else:
-                panel = near_panels[t][at, :]
+                if part_of_block[t]:
+                    sizes = [size for _, _, size, _ in terms[t][1]]
+                    panel = jnp.concatenate(
+                        [near_panels[t][at, pl.ds(start, size)] for start, size in zip(places[t], sizes)], axis=1
+                    )
+                else:
+                    panel = near_panels[t][at, :]
             if n + in_flight < len(order):
                 load(*order[n + in_flight])
-            product = jnp.dot(panel, held[t], preferred_element_type=jnp.float32)
-            value = jnp.where(here.block == terms[t][0], product, value - product)
+            product = jnp.dot(panel, held[t, : panel.shape[1]], preferred_element_type=jnp.float32)
+            k, fresh = terms[t][0], terms[t][3]
+            less = value - product
+            if not fresh:
+                less = jnp.where((here.block > k) & (here.block < STEPS), value, less)
+            value = jnp.where(here.block == k, product if fresh else value + product, less)
             if t < len(terms) - 1:
                 continue
             for o, (dtype, first, size, far) in enumerate(outs):
@@ -140,14 +154,14 @@
         return len(arrays) - 1
 
     plan = tuple(
-        (k, tuple((index(array), first, size, place) for array, first, size, place in pieces), None if near is None else 0)
-        for k, pieces, near in terms
+        (k, tuple((index(array), first, size, place) for array, first, size, place in pieces), None if near is None else 0, fresh)
+        for k, pieces, near, fresh in terms
     )
-    near_panels = [near for _, _, near in terms if near is not None]
+    near_panels = [near for _, _, near, _ in terms if near is not None]
     handed = tuple((block, index(array)) for block, array in handed)
     n_terms = len(terms)
-    tile = min(TILE, rows)
-    n_pieces = max(sum(len(pieces) for _, pieces, _ in terms), len(outs))
+    tile = min(NEAR_TILE if near_panels else TILE, rows)
+    n_pieces = max(sum(len(pieces) for _, pieces, _, _ in terms), len(outs))
     n_far = max(n_terms - len(near_panels), 1)
     assert not near_panels or len(near_panels) == n_terms
     anywhere = pl.BlockSpec(memory_space=pl.ANY)
@@ -245,7 +259,7 @@
                 a, b = first_0.index((dy, 0)), first_1.index((0, dm))
                 payload = got[a] if a == b else jnp.where(core == 0, got[a], got[b])
                 last.append(send(payload, pairs(0, (0, dm)) + pairs(1, (dy, 0))))
-            return jnp.concatenate([value, *got, *last], axis=0)
+            return jnp.concatenate([value, *got], axis=0), jnp.concatenate(last, axis=0)
 
         def core_exchange(value):
             pairs = [
@@ -254,15 +268,15 @@
             ]
             return send(value, pairs)
 
-        def gathered_pieces(mine, other, first, size, stride, number):
+        def gathered_pieces(array, own, first, size, stride, offsets, number):
             def place(offset, own, at):
                 c = at.core if own else 1 - at.core
                 a, b = (number((at.y + dy) % n_y, c, (at.lane + dm) % lanes) for dy, dm in offset)
                 return a if offset[0] == offset[1] else jnp.where(c == 0, a, b)
 
             return [
-                (array, i * stride + first, size, functools.partial(place, offset, array is mine))
-                for array in (mine, other) for i, offset in enumerate(offsets)
+                (array, i * stride + first, size, functools.partial(place, offset, own))
+                for i, offset in enumerate(offsets)
             ]
 
         def lane_pieces(parts):
@@ -286,24 +300,30 @@
         regrouped = lax.all_to_all(outgoing, AXES, split_axis=1, concat_axis=0, tiled=True)
         regrouped = regrouped.reshape(-1, rows_here + extra)
         current = jnp.transpose(regrouped[:, :rows_here]).astype(jnp.float32)
-        whole = plane_gather(jnp.transpose(regrouped[:, rows_here:]))
-        pieces = gathered_pieces(
-            whole, core_exchange(whole), 0, extra, extra, lambda y, c, m: (y * CORES + c) * lanes + m
-        )
-        current, own1 = run(current, [(0, pieces, None)], [f32_rows, own_rows])
+        whole = jnp.concatenate(plane_gather(jnp.transpose(regrouped[:, rows_here:])), axis=0)
+        pieces = [
+            piece
+            for array, own in ((whole, True), (core_exchange(whole), False))
+            for piece in gathered_pieces(
+                array, own, 0, extra, extra, offsets, lambda y, c, m: (y * CORES + c) * lanes + m
+            )
+        ]
+        current, own1 = run(current, [(0, pieces, None, True)], [f32_rows, own_rows])
 
         hop1 = ahead(own1, 1)
         near1 = near_panel(after(factor_panels, own1), 1)
-        start1 = after(own1, hop1[0], near1)
-        at_3 = [
-            send(start1, [(device(0, 0, 1, (m + d) % lanes), device(0, 0, 3, m)) for m in range(lanes)])
-            for d in range(lanes)
+        near2 = near_panel(after(factor_panels, own1), 2)
+        start1 = after(own1, hop1[0], near1, near2)
+        to_3 = send(start1, [(device(0, 0, 1, m), device(0, 0, 3, m)) for m in range(lanes)])
+        (own2,) = run(current, [(1, lane_pieces(hop1), near1, True)], [own_rows], 2)
+        hop2 = ahead(own2, 2)
+        to_3 = after(to_3, own2)
+        at_3 = [to_3] + [
+            send(to_3, [(device(0, 0, 3, (m + d) % lanes), device(0, 0, 3, m)) for m in range(lanes)])
+            for d in range(1, lanes)
         ]
-        (own2,) = run(current, [(1, lane_pieces(hop1), near1)], [own_rows], 2)
-        hop2 = ahead(own2, 2)
-        near2 = near_panel(after(factor_panels, own2), 2)
-        (chained,) = run(after(current, near2), [(1, lane_pieces(at_3), near1)], [f32_rows], 3)
-        cuts = run(chained, [(2, lane_pieces(hop2), near2)], own_cuts, 3, [(1, own1), (2, own2)])
+        (chained,) = run(current, [(1, lane_pieces(at_3), near1, True)], [f32_rows], 3)
+        cuts = run(chained, [(2, lane_pieces(hop2), near2, True)], own_cuts, 3, [(1, own1), (2, own2)])
 
         piece = cuts[0]
         for t in range(1, n_row):
@@ -328,19 +348,32 @@
                 value = jnp.where(plane == (k + d) % planes, got[d - 1], value)
             three.append(value)
         near3 = near_panel(after(factor_panels, cuts[0]), 3)
-        whole = plane_gather(after(jnp.concatenate(three, axis=0), near3))
+        most, last = plane_gather(after(jnp.concatenate(three, axis=0), near3))
+        n_most = len(offsets) - len(across)
+
+        def terms(fresh, *arrays):
+            return [
+                (
+                    k,
+                    [
+                        piece
+                        for array, own, start, count in arrays
+                        for piece in gathered_pieces(
+                            array, own, (k - 1) * cut, cut, (STEPS - 1) * cut, offsets[start : start + count],
+                            lambda y, c, m: m * n_row + y * CORES + c,
+                        )
+                    ],
+                    near,
+                    fresh,
+                )
+                for k, near in ((1, near1), (2, near2), (3, near3))
+            ]
+
+        (current,) = run(current, terms(True, (most, True, 0, n_most)), [f32_rows])
+        whole = after(jnp.concatenate([most, last], axis=0), current)
         other = core_exchange(whole)
-        terms = [
-            (
-                k,
-                gathered_pieces(
-                    whole, other, (k - 1) * cut, cut, (STEPS - 1) * cut, lambda y, c, m: m * n_row + y * CORES + c
-                ),
-                near,
-            )
-            for k, near in ((1, near1), (2, near2), (3, near3))
-        ]
-        (out,) = run(current, terms, [(jnp.float32, 0, rows_here, True)])
+        rest = [(last, True, n_most, len(across)), (other, False, 0, len(offsets))]
+        (out,) = run(current, terms(False, *rest), [(jnp.float32, 0, rows_here, True)])
         return out
 
     return on_device

time: 140 us -> 140 us (level)
  Pallas kernels: 24.2 us -> 26.7 us
  local copies, waits for them, and re-layouts: 3.07 us -> 1.16 us
  waiting for transfers between devices: 69.2 us -> 67.4 us
    unnamed x13 -> x10, local copies, waits for them, and re-layouts: 2.21 us -> 0.32 us
    ppermute x20, waiting for transfers between devices: 69.2 us -> 67.4 us  [send(): return lax.ppermute(value, AXES, pairs)]
    pallas_call x3, Pallas kernels: 6.8 us -> 8.31 us  [near_panel(): pl.pallas_call(functools.partial(near_kernel, k), in_specs=[pl.BlockSpec(...]
    pallas_call x5 -> x6, Pallas kernels: 17.4 us -> 18.4 us  [steps(): pl.pallas_call(functools.partial(step_kernel, plan, handed, len(arrays),...]
  transfers between devices with their start and end apart: 20 -> 20, of which waited for: 9 -> 9; matrix products, arithmetic and copies ran while one was open for 0% -> 0% of each run, Pallas kernels for 5% -> 9%
where the time goes in v11:
time: 140 us; the launch traced here: 139 us
  waiting for transfers between devices  67.4 us (48%)
  Pallas kernels  26.7 us (19%)
  blocking collectives  26.3 us (19%)
  starting transfers between devices  15.7 us (11%)
  other arithmetic  1.48 us (1%)
    ppermute x20, waiting for transfers between devices, send(): return lax.ppermute(value, AXES, pairs)  67.4 us
    all_to_all x1, blocking collectives, on_device(): lax.all_to_all(outgoing, AXES, split_axis=1, concat_axis=0, tiled=True)  26.3 us
    pallas_call x6, Pallas kernels, steps(): pl.pallas_call(functools.partial(step_kernel, plan, handed, len(arrays),...  18.4 us
    ppermute x20, starting transfers between devices, send(): return lax.ppermute(value, AXES, pairs)  15.7 us
    pallas_call x3, Pallas kernels, near_panel(): pl.pallas_call(functools.partial(near_kernel, k), in_specs=[pl.BlockSpec(...  8.31 us
  transfers between devices with their start and end apart: 20, of which 9 were waited for; matrix products, arithmetic and copies ran while one was open for 0% of the time, Pallas kernels for 9%

profile of v11, /device:TPU:0, one launch (start us, length us, event | category | flops | bytes accessed | tf_op | source)
XLA Modules:
  0.0 139.3 jit_solution(17572183175102782864)
XLA Ops:
  0.0 0.8 slice.9
  0.8 1.1 pad_maximum_fusion.2
  1.9 26.3 %all_to_all.15 = bf16[8,32,1280]{2,0,1:T(8,128)(2,1)S(1)} all-to-all(bf16[8,32,1280]{2,0,1:T(8,128)(2,1)S(1)} %pad_maximum_fusion.2), channel_id=1, replica_groups=mesh['row'=4,'col'=8] {'row','col'}, dimensions={1} | all-to-all | bytes 1310720 | tf_op jit(solution)/shard_map/all_to_all | solution.py:300
  28.9 0.8 collective-permute-start
  29.7 4.8 %collective-permute-done.1 = bf16[256,256]{1,0:T(8,128)(2,1)S(1)} collective-permute-done((bf16[256,256]{1,0:T(8,128)(2,1)S(1)}, bf16[256,256]{1,0:T(8,128)(2,1)S(1)}, u32[]{:S(2)}, u32[]{:S(2)}) %collective-permute-start.1) | collective-permute-done | bytes 131104 | tf_op jit(solution)/shard_map/ppermute | solution.py:232
  34.8 4.6 %collective-permute-done.2 = bf16[256,256]{1,0:T(8,128)(2,1)S(1)} collective-permute-done((bf16[256,256]{1,0:T(8,128)(2,1)S(1)}, bf16[256,256]{1,0:T(8,128)(2,1)S(1)}, u32[]{:S(2)}, u32[]{:S(2)}) %collective-permute-start.2) | collective-permute-done | bytes 131104 | tf_op jit(solution)/shard_map/ppermute | solution.py:232
  39.9 1.5 %collective-permute-done.3.refs_3_ = bf16[1024,256]{1,0:T(8,128)(2,1)S(1)} collective-permute-done((bf16[1024,256]{1,0:T(8,128)(2,1)S(1)}, bf16[1024,256]{1,0:T(8,128)(2,1)S(1)}, u32[]{:S(2)}, u32[]{:S(2)}) %collective-permute-start.3) | collective-permute-done | bytes 524320 | tf_op jit(solution)/shard_map/ppermute | solution.py:232
  41.5 5.6 %shard_map.28 = (f32[1024,256]{1,0:T(8,128)S(1)}, bf16[1024,256]{1,0:T(8,128)(2,1)S(1)}) custom-call(f32[1024,256]{1,0:T(8,128)S(1)} %convert_bitcast_fusion.refs_0_, bf16[1024,8192]{1,0:T(8,128)(2,1)} %panels.2, bf16[1024,256]{1,0:T(8,128)(2,1)S(1)} %pad_maximum_fusion.3.refs_2_, bf16[1024,256]{1,0:T(8,128)(2,1)S(1)} %collective-permute-done.3.refs_3_), custom_call_target="tpu_custom_call" | custom-call | flops 1073741824 | bytes 2097152 | tf_op jit(solution)/shard_map/pallas_call | solution.py:168
  48.5 2.2 %shard_map.29.refs_1_ = bf16[1024,2048]{1,0:T(8,128)(2,1)S(1)} custom-call(bf16[1024,8192]{1,0:T(8,128)(2,1)} %panels.2), custom_call_target="tpu_custom_call" | custom-call | bytes 1 | tf_op jit(solution)/shard_map/pallas_call | solution.py:206
  50.7 3.7 %shard_map.30.refs_1_.refs_2_ = bf16[1024,2048]{1,0:T(8,128)(2,1)S(1)} custom-call(bf16[1024,8192]{1,0:T(8,128)(2,1)} %panels.2), custom_call_target="tpu_custom_call" | custom-call | bytes 1 | tf_op jit(solution)/shard_map/pallas_call | solution.py:206
  59.9 1.3 collective-permute-start.13
  61.2 1.3 collective-permute-start.14
  62.5 1.5 %collective-permute-start.15 = (bf16[256,256]{1,0:T(8,128)(2,1)S(1)}, bf16[256,256]{1,0:T(8,128)(2,1)S(1)}, u32[]{:S(2)}, u32[]{:S(2)}) collective-permute-start(bf16[256,256]{1,0:T(8,128)(2,1)S(1)} %select_select_fusion.3), channel_id=1, source_target_pairs={{2,4},{3,5},{10,12},{11,13},{18,20},{19,21},{26,28},{27,29},{4,6},... | collective-permute-start | bytes 393224 | tf_op jit(solution)/shard_map/ppermute | solution.py:232
  64.0 2.4 %shard_map.34.refs_3_ = bf16[1024,2048]{1,0:T(8,128)(2,1)S(1)} custom-call(bf16[1024,8192]{1,0:T(8,128)(2,1)} %panels.2), custom_call_target="tpu_custom_call" | custom-call | bytes 1 | tf_op jit(solution)/shard_map/pallas_call | solution.py:206
  66.3 13.9 %collective-permute-done.13 = bf16[256,256]{1,0:T(8,128)(2,1)S(1)} collective-permute-done((bf16[256,256]{1,0:T(8,128)(2,1)S(1)}, bf16[256,256]{1,0:T(8,128)(2,1)S(1)}, u32[]{:S(2)}, u32[]{:S(2)}) %collective-permute-start.13) | collective-permute-done | bytes 131104 | tf_op jit(solution)/shard_map/ppermute | solution.py:232
  80.2 21.6 %collective-permute-done.14 = bf16[256,256]{1,0:T(8,128)(2,1)S(1)} collective-permute-done((bf16[256,256]{1,0:T(8,128)(2,1)S(1)}, bf16[256,256]{1,0:T(8,128)(2,1)S(1)}, u32[]{:S(2)}, u32[]{:S(2)}) %collective-permute-start.14) | collective-permute-done | bytes 131104 | tf_op jit(solution)/shard_map/ppermute | solution.py:232
  101.8 6.0 %collective-permute-done.15 = bf16[256,256]{1,0:T(8,128)(2,1)S(1)} collective-permute-done((bf16[256,256]{1,0:T(8,128)(2,1)S(1)}, bf16[256,256]{1,0:T(8,128)(2,1)S(1)}, u32[]{:S(2)}, u32[]{:S(2)}) %collective-permute-start.15) | collective-permute-done | bytes 131104 | tf_op jit(solution)/shard_map/ppermute | solution.py:232
  107.8 1.4 %collective-permute-start.17 = (bf16[768,256]{1,0:T(8,128)(2,1)S(1)}, bf16[768,256]{1,0:T(8,128)(2,1)S(1)}, u32[]{:S(2)}, u32[]{:S(2)}) collective-permute-start(bf16[768,256]{1,0:T(8,128)(2,1)S(1)} %pad_maximum_fusion.4), channel_id=1, source_target_pairs={{16,0},{17,1},{18,2},{19,3},{20,4},{21,5},{22,6},{23,7},{0,16},{1,... | collective-permute-start | bytes 1179656 | tf_op jit(solution)/shard_map/ppermute | solution.py:232
  109.3 1.5 %collective-permute-start.16 = (bf16[768,256]{1,0:T(8,128)(2,1)S(1)}, bf16[768,256]{1,0:T(8,128)(2,1)S(1)}, u32[]{:S(2)}, u32[]{:S(2)}) collective-permute-start(bf16[768,256]{1,0:T(8,128)(2,1)S(1)} %pad_maximum_fusion.4), channel_id=1, source_target_pairs={{1,0},{0,1},{3,2},{2,3},{5,4},{4,5},{7,6},{6,7},{17,16},{16,17},{1... | collective-permute-start | bytes 1179656 | tf_op jit(solution)/shard_map/ppermute | solution.py:232
  110.7 9.2 %collective-permute-done.17 = bf16[768,256]{1,0:T(8,128)(2,1)S(1)} collective-permute-done((bf16[768,256]{1,0:T(8,128)(2,1)S(1)}, bf16[768,256]{1,0:T(8,128)(2,1)S(1)}, u32[]{:S(2)}, u32[]{:S(2)}) %collective-permute-start.17) | collective-permute-done | bytes 393248 | tf_op jit(solution)/shard_map/ppermute | solution.py:232
  120.7 4.6 %shard_map.35.refs_0_ = f32[1024,256]{1,0:T(8,128)S(1)} custom-call(f32[1024,256]{1,0:T(8,128)S(1)} %get-tuple-element.17.refs_0_, bf16[1024,2048]{1,0:T(8,128)(2,1)S(1)} %copy-done.1, bf16[1024,2048]{1,0:T(8,128)(2,1)S(1)} %copy-done.3, bf16[1024,2048]{1,0:T(8,128)(2,1)S(1)} %shard_map.34.refs_3_, bf16[2304,256]{1,0:T(8,128)(2,1)S(1)} %pad_maximum_fusion.1.refs_4_), custom_call_target="tpu_custom_call" | custom-call | flops 3221225472 | bytes 2097152 | tf_op jit(solution)/shard_map/pallas_call | solution.py:168
  125.3 2.4 %collective-permute-done.18.refs_4_ = bf16[768,256]{1,0:T(8,128)(2,1)S(1)} collective-permute-done((bf16[768,256]{1,0:T(8,128)(2,1)S(1)}, bf16[768,256]{1,0:T(8,128)(2,1)S(1)}, u32[]{:S(2)}, u32[]{:S(2)}) %collective-permute-start.18) | collective-permute-done | bytes 393248 | tf_op jit(solution)/shard_map/ppermute | solution.py:232
  127.9 3.4 %collective-permute-done.19.refs_5_ = bf16[3072,256]{1,0:T(8,128)(2,1)S(1)} collective-permute-done((bf16[3072,256]{1,0:T(8,128)(2,1)S(1)}, bf16[3072,256]{1,0:T(8,128)(2,1)S(1)}, u32[]{:S(2)}, u32[]{:S(2)}) %collective-permute-start.19) | collective-permute-done | bytes 1572896 | tf_op jit(solution)/shard_map/ppermute | solution.py:232
  131.2 7.9 %shard_map.36 = f32[1024,256]{1,0:T(8,128)} custom-call(f32[1024,256]{1,0:T(8,128)S(1)} %shard_map.35.refs_0_, bf16[1024,2048]{1,0:T(8,128)(2,1)S(1)} %copy-done.1, bf16[1024,2048]{1,0:T(8,128)(2,1)S(1)} %copy-done.3, bf16[1024,2048]{1,0:T(8,128)(2,1)S(1)} %shard_map.34.refs_3_, bf16[768,256]{1,0:T(8,128)(2,1)S(1)} %collective-permute-done.18.refs_4_, ...), custom_call_target="tpu_custom_call" | custom-call | flops 3221225472 | bytes 2097152 | tf_op jit(solution)/shard_map/pallas_call | solution.py:168
  (48 shorter events, 9.1 us)
Async XLA Ops:
  28.2 6.3 %collective-permute-start.1 = (bf16[256,256]{1,0:T(8,128)(2,1)S(1)}, bf16[256,256]{1,0:T(8,128)(2,1)S(1)}, u32[]{:S(2)}, u32[]{:S(2)}) collective-permute-start(bf16[256,256]{1,0:T(8,128)(2,1)S(1)} %bitcast.15), channel_id=1, source_target_pairs={{16,0},{17,1},{18,2},{19,3},{20,4},{21,5},{22,6},{23,7},{0,16},{1,... | collective-permute-start | bytes 393224 | tf_op jit(solution)/shard_map/ppermute | solution.py:232
  28.9 6.0 %collective-permute-start = (bf16[256,256]{1,0:T(8,128)(2,1)S(1)}, bf16[256,256]{1,0:T(8,128)(2,1)S(1)}, u32[]{:S(2)}, u32[]{:S(2)}) collective-permute-start(bf16[256,256]{1,0:T(8,128)(2,1)S(1)} %bitcast.16), channel_id=1, source_target_pairs={{1,0},{0,1},{3,2},{2,3},{5,4},{4,5},{7,6},{6,7},{17,16},{16,17},{1... | collective-permute-start | bytes 393224 | tf_op jit(solution)/shard_map/ppermute | solution.py:232
  34.5 5.0 %collective-permute-start.2 = (bf16[256,256]{1,0:T(8,128)(2,1)S(1)}, bf16[256,256]{1,0:T(8,128)(2,1)S(1)}, u32[]{:S(2)}, u32[]{:S(2)}) collective-permute-start(bf16[256,256]{1,0:T(8,128)(2,1)S(1)} %collective-permute-done.1), channel_id=1, source_target_pairs={{1,0},{0,1},{3,2},{2,3},{5,4},{4,5},{7,6},{6,7},{17,16},{16,17},{1... | collective-permute-start | bytes 393224 | tf_op jit(solution)/shard_map/ppermute | solution.py:232
  39.5 2.0 %collective-permute-start.3 = (bf16[1024,256]{1,0:T(8,128)(2,1)S(1)}, bf16[1024,256]{1,0:T(8,128)(2,1)S(1)}, u32[]{:S(2)}, u32[]{:S(2)}) collective-permute-start(bf16[1024,256]{1,0:T(8,128)(2,1)S(1)} %pad_maximum_fusion.3.refs_2_), channel_id=1, source_target_pairs={{8,0},{9,1},{10,2},{11,3},{12,4},{13,5},{14,6},{15,7},{0,8},{1,9},... | collective-permute-start | bytes 1572872 | tf_op jit(solution)/shard_map/ppermute | solution.py:232
  47.1 7.4 %collective-permute-start.4 = (bf16[1024,256]{1,0:T(8,128)(2,1)S(1)}, bf16[1024,256]{1,0:T(8,128)(2,1)S(1)}, u32[]{:S(2)}, u32[]{:S(2)}) collective-permute-start(bf16[1024,256]{1,0:T(8,128)(2,1)S(1)} %get-tuple-element.20.refs_4_), channel_id=1, source_target_pairs={{2,4},{3,5}} | collective-permute-start | bytes 1572872 | tf_op jit(solution)/shard_map/ppermute | solution.py:232
  47.8 7.4 %collective-permute-start.6 = (bf16[1024,256]{1,0:T(8,128)(2,1)S(1)}, bf16[1024,256]{1,0:T(8,128)(2,1)S(1)}, u32[]{:S(2)}, u32[]{:S(2)}) collective-permute-start(bf16[1024,256]{1,0:T(8,128)(2,1)S(1)} %get-tuple-element.20.refs_4_), channel_id=1, source_target_pairs={{3,4},{2,5}} | collective-permute-start | bytes 1572872 | tf_op jit(solution)/shard_map/ppermute | solution.py:232
  50.7 6.7 %copy-start = (bf16[1024,2048]{1,0:T(8,128)(2,1)}, bf16[1024,2048]{1,0:T(8,128)(2,1)S(1)}, u32[]{:S(2)}) copy-start(bf16[1024,2048]{1,0:T(8,128)(2,1)S(1)} %shard_map.29.refs_1_) | copy-start | bytes 12582916
  54.5 3.1 %copy-start.2 = (bf16[1024,2048]{1,0:T(8,128)(2,1)}, bf16[1024,2048]{1,0:T(8,128)(2,1)S(1)}, u32[]{:S(2)}) copy-start(bf16[1024,2048]{1,0:T(8,128)(2,1)S(1)} %shard_map.30.refs_1_.refs_2_) | copy-start | bytes 12582916
  54.5 0.8 collective-permute-start.5
  55.3 2.1 %collective-permute-start.7 = (bf16[1024,256]{1,0:T(8,128)(2,1)S(1)}, bf16[1024,256]{1,0:T(8,128)(2,1)S(1)}, u32[]{:S(2)}, u32[]{:S(2)}) collective-permute-start(bf16[1024,256]{1,0:T(8,128)(2,1)S(1)} %collective-permute-done.5.refs_2_), channel_id=1, source_target_pairs={{7,6},{6,7}} | collective-permute-start | bytes 1572872 | tf_op jit(solution)/shard_map/ppermute | solution.py:232
  56.0 1.5 %collective-permute-start.8 = (bf16[1024,256]{1,0:T(8,128)(2,1)S(1)}, bf16[1024,256]{1,0:T(8,128)(2,1)S(1)}, u32[]{:S(2)}, u32[]{:S(2)}) collective-permute-start(bf16[1024,256]{1,0:T(8,128)(2,1)S(1)} %shard_map.31.refs_5_), channel_id=1, source_target_pairs={{4,6},{5,7}} | collective-permute-start | bytes 1572872 | tf_op jit(solution)/shard_map/ppermute | solution.py:232
  56.7 0.8 collective-permute-start.9
  57.7 2.1 %collective-permute-start.10 = (bf16[256,256]{1,0:T(8,128)(2,1)S(1)}, bf16[256,256]{1,0:T(8,128)(2,1)S(1)}, u32[]{:S(2)}, u32[]{:S(2)}) collective-permute-start(bf16[256,256]{1,0:T(8,128)(2,1)S(1)} %get-tuple-element.24), channel_id=1, source_target_pairs={{2,26},{3,27},{4,28},{5,29},{6,30},{7,31}} | collective-permute-start | bytes 393224 | tf_op jit(solution)/shard_map/ppermute | solution.py:232
  58.4 1.4 collective-permute-start.11
  59.1 0.7 collective-permute-start.12
  59.9 20.4 %collective-permute-start.13 = (bf16[256,256]{1,0:T(8,128)(2,1)S(1)}, bf16[256,256]{1,0:T(8,128)(2,1)S(1)}, u32[]{:S(2)}, u32[]{:S(2)}) collective-permute-start(bf16[256,256]{1,0:T(8,128)(2,1)S(1)} %select_select_fusion.3), channel_id=1, source_target_pairs={{2,0},{3,1},{10,8},{11,9},{18,16},{19,17},{26,24},{27,25},{4,2},{5... | collective-permute-start | bytes 393224 | tf_op jit(solution)/shard_map/ppermute | solution.py:232
  61.2 40.6 %collective-permute-start.14 = (bf16[256,256]{1,0:T(8,128)(2,1)S(1)}, bf16[256,256]{1,0:T(8,128)(2,1)S(1)}, u32[]{:S(2)}, u32[]{:S(2)}) collective-permute-start(bf16[256,256]{1,0:T(8,128)(2,1)S(1)} %select_select_fusion.3), channel_id=1, source_target_pairs={{2,6},{3,7},{10,14},{11,15},{18,22},{19,23},{26,30},{27,31},{4,0},... | collective-permute-start | bytes 393224 | tf_op jit(solution)/shard_map/ppermute | solution.py:232
  62.5 45.3 %collective-permute-start.15 = (bf16[256,256]{1,0:T(8,128)(2,1)S(1)}, bf16[256,256]{1,0:T(8,128)(2,1)S(1)}, u32[]{:S(2)}, u32[]{:S(2)}) collective-permute-start(bf16[256,256]{1,0:T(8,128)(2,1)S(1)} %select_select_fusion.3), channel_id=1, source_target_pairs={{2,4},{3,5},{10,12},{11,13},{18,20},{19,21},{26,28},{27,29},{4,6},... | collective-permute-start | bytes 393224 | tf_op jit(solution)/shard_map/ppermute | solution.py:232
  64.0 56.7 %copy-start.1 = (bf16[1024,2048]{1,0:T(8,128)(2,1)S(1)}, bf16[1024,2048]{1,0:T(8,128)(2,1)}, u32[]{:S(2)}) copy-start(bf16[1024,2048]{1,0:T(8,128)(2,1)} %copy-done) | copy-start | bytes 12582916
  64.0 56.7 %copy-start.3 = (bf16[1024,2048]{1,0:T(8,128)(2,1)S(1)}, bf16[1024,2048]{1,0:T(8,128)(2,1)}, u32[]{:S(2)}) copy-start(bf16[1024,2048]{1,0:T(8,128)(2,1)} %copy-done.2) | copy-start | bytes 12582916
  107.8 12.1 %collective-permute-start.17 = (bf16[768,256]{1,0:T(8,128)(2,1)S(1)}, bf16[768,256]{1,0:T(8,128)(2,1)S(1)}, u32[]{:S(2)}, u32[]{:S(2)}) collective-permute-start(bf16[768,256]{1,0:T(8,128)(2,1)S(1)} %pad_maximum_fusion.4), channel_id=1, source_target_pairs={{16,0},{17,1},{18,2},{19,3},{20,4},{21,5},{22,6},{23,7},{0,16},{1,... | collective-permute-start | bytes 1179656 | tf_op jit(solution)/shard_map/ppermute | solution.py:232
  109.3 11.3 %collective-permute-start.16 = (bf16[768,256]{1,0:T(8,128)(2,1)S(1)}, bf16[768,256]{1,0:T(8,128)(2,1)S(1)}, u32[]{:S(2)}, u32[]{:S(2)}) collective-permute-start(bf16[768,256]{1,0:T(8,128)(2,1)S(1)} %pad_maximum_fusion.4), channel_id=1, source_target_pairs={{1,0},{0,1},{3,2},{2,3},{5,4},{4,5},{7,6},{6,7},{17,16},{16,17},{1... | collective-permute-start | bytes 1179656 | tf_op jit(solution)/shard_map/ppermute | solution.py:232
  119.9 7.8 %collective-permute-start.18 = (bf16[768,256]{1,0:T(8,128)(2,1)S(1)}, bf16[768,256]{1,0:T(8,128)(2,1)S(1)}, u32[]{:S(2)}, u32[]{:S(2)}) collective-permute-start(bf16[768,256]{1,0:T(8,128)(2,1)S(1)} %collective-permute-done.17), channel_id=1, source_target_pairs={{1,0},{0,1},{3,2},{2,3},{5,4},{4,5},{7,6},{6,7},{17,16},{16,17},{1... | collective-permute-start | bytes 1179656 | tf_op jit(solution)/shard_map/ppermute | solution.py:232
  127.8 3.5 %collective-permute-start.19 = (bf16[3072,256]{1,0:T(8,128)(2,1)S(1)}, bf16[3072,256]{1,0:T(8,128)(2,1)S(1)}, u32[]{:S(2)}, u32[]{:S(2)}) collective-permute-start(bf16[3072,256]{1,0:T(8,128)(2,1)S(1)} %pad_maximum_fusion), channel_id=1, source_target_pairs={{8,0},{9,1},{10,2},{11,3},{12,4},{13,5},{14,6},{15,7},{0,8},{1,9},... | collective-permute-start | bytes 4718600 | tf_op jit(solution)/shard_map/ppermute | solution.py:232

commit v12 on v11

--- a/solution.py
+++ b/solution.py
@@ -246,7 +246,7 @@
         across = [(dy, dm) for dy, _ in along_y for _, dm in along_x]
         offsets = [((0, 0), (0, 0)), *zip(first_0, first_1), *zip(across, across)]
 
-        def plane_gather(value):
+        def plane_gather(value, beside=None):
             def pairs(c, step):
                 return [
                     (device((t + step[0]) % n_y, c, z, (m + step[1]) % lanes), device(t, c, z, m))
@@ -254,6 +254,8 @@
                 ]
 
             got = [send(value, pairs(0, a) + pairs(1, b)) for a, b in zip(first_0, first_1)]
+            if beside is not None:
+                got = [after(part, beside) for part in got]
             last = []
             for dy, dm in across:
                 a, b = first_0.index((dy, 0)), first_1.index((0, dm))
@@ -291,7 +293,7 @@
         own_cuts = [(jnp.bfloat16, t * cut, cut, False) for t in range(n_row)]
 
         extra = NB // members
-        first = rhs_scen[:, :NB].reshape(-1, n_row, 1, lanes, extra)
+        first = rhs_scen.reshape(rhs_scen.shape[0], -1, extra)[:, :members].reshape(-1, n_row, 1, lanes, extra)
         first = jnp.broadcast_to(first, (first.shape[0], n_row, planes, lanes, extra))
         first = first.reshape(first.shape[0], n_row * n_col, extra)
         outgoing = jnp.concatenate(
@@ -300,7 +302,8 @@
         regrouped = lax.all_to_all(outgoing, AXES, split_axis=1, concat_axis=0, tiled=True)
         regrouped = regrouped.reshape(-1, rows_here + extra)
         current = jnp.transpose(regrouped[:, :rows_here]).astype(jnp.float32)
-        whole = jnp.concatenate(plane_gather(jnp.transpose(regrouped[:, rows_here:])), axis=0)
+        near0 = near_panel(after(factor_panels, regrouped), 0)
+        whole = jnp.concatenate(plane_gather(jnp.transpose(regrouped[:, rows_here:]), near0), axis=0)
         pieces = [
             piece
             for array, own in ((whole, True), (core_exchange(whole), False))
@@ -308,21 +311,19 @@
                 array, own, 0, extra, extra, offsets, lambda y, c, m: (y * CORES + c) * lanes + m
             )
         ]
-        current, own1 = run(current, [(0, pieces, None, True)], [f32_rows, own_rows])
+        current, own1 = run(current, [(0, pieces, near0, True)], [f32_rows, own_rows])
 
         hop1 = ahead(own1, 1)
         near1 = near_panel(after(factor_panels, own1), 1)
-        near2 = near_panel(after(factor_panels, own1), 2)
-        start1 = after(own1, hop1[0], near1, near2)
-        to_3 = send(start1, [(device(0, 0, 1, m), device(0, 0, 3, m)) for m in range(lanes)])
+        start1 = after(own1, hop1[0], near1)
+        at_3 = [
+            send(start1, [(device(0, 0, 1, (m + d) % lanes), device(0, 0, 3, m)) for m in range(lanes)])
+            for d in range(lanes)
+        ]
         (own2,) = run(current, [(1, lane_pieces(hop1), near1, True)], [own_rows], 2)
         hop2 = ahead(own2, 2)
-        to_3 = after(to_3, own2)
-        at_3 = [to_3] + [
-            send(to_3, [(device(0, 0, 3, (m + d) % lanes), device(0, 0, 3, m)) for m in range(lanes)])
-            for d in range(1, lanes)
-        ]
-        (chained,) = run(current, [(1, lane_pieces(at_3), near1, True)], [f32_rows], 3)
+        near2 = near_panel(after(factor_panels, own2), 2)
+        (chained,) = run(after(current, near2), [(1, lane_pieces(at_3), near1, True)], [f32_rows], 3)
         cuts = run(chained, [(2, lane_pieces(hop2), near2, True)], own_cuts, 3, [(1, own1), (2, own2)])
 
         piece = cuts[0]

time: 140 us -> 138 us (0.986)
  waiting for transfers between devices: 67.4 us -> 59.6 us
  local copies, waits for them, and re-layouts: 1.16 us -> 7.15 us
    ppermute x20, waiting for transfers between devices: 67.4 us -> 59.6 us  [send(): return lax.ppermute(value, AXES, pairs)]
    unnamed x10 -> x14, local copies, waits for them, and re-layouts: 0.32 us -> 6.31 us
    pallas_call x6, Pallas kernels: 18.4 us -> 16.7 us  [steps(): pl.pallas_call(functools.partial(step_kernel, plan, handed, len(arrays),...]
    pallas_call x3 -> x4, Pallas kernels: 8.31 us -> 9.01 us  [near_panel(): pl.pallas_call(functools.partial(near_kernel, k), in_specs=[pl.BlockSpec(...]
  transfers between devices with their start and end apart: 20 -> 20, of which waited for: 9 -> 9; matrix products, arithmetic and copies ran while one was open for 0% -> 0% of each run, Pallas kernels for 9% -> 10%
where the time goes in v12:
time: 138 us; the launch traced here: 137 us
  waiting for transfers between devices  59.6 us (43%)
  blocking collectives  26.3 us (19%)
  Pallas kernels  25.7 us (19%)
  starting transfers between devices  16.6 us (12%)
  local copies, waits for them, and re-layouts  7.15 us (5%)
  other arithmetic  1.48 us (1%)
    ppermute x20, waiting for transfers between devices, send(): return lax.ppermute(value, AXES, pairs)  59.6 us
    all_to_all x1, blocking collectives, on_device(): lax.all_to_all(outgoing, AXES, split_axis=1, concat_axis=0, tiled=True)  26.3 us
    pallas_call x6, Pallas kernels, steps(): pl.pallas_call(functools.partial(step_kernel, plan, handed, len(arrays),...  16.7 us
    ppermute x20, starting transfers between devices, send(): return lax.ppermute(value, AXES, pairs)  16.6 us
    pallas_call x4, Pallas kernels, near_panel(): pl.pallas_call(functools.partial(near_kernel, k), in_specs=[pl.BlockSpec(...  9.01 us
    unnamed x14, local copies, waits for them, and re-layouts  6.31 us
  transfers between devices with their start and end apart: 20, of which 9 were waited for; matrix products, arithmetic and copies ran while one was open for 0% of the time, Pallas kernels for 10%

profile of v12, /device:TPU:0, one launch (start us, length us, event | category | flops | bytes accessed | tf_op | source)
XLA Modules:
  0.0 137.4 jit_solution(3494269099144457304)
XLA Ops:
  1.9 26.3 %all_to_all.15 = bf16[8,32,1280]{2,0,1:T(8,128)(2,1)S(1)} all-to-all(bf16[8,32,1280]{2,0,1:T(8,128)(2,1)S(1)} %pad_maximum_fusion.2), channel_id=1, replica_groups=mesh['row'=4,'col'=8] {'row','col'}, dimensions={1} | all-to-all | bytes 1310720 | tf_op jit(solution)/shard_map/all_to_all | solution.py:302
  29.7 2.2 %shard_map.28.refs_1_ = bf16[1024,2048]{1,0:T(8,128)(2,1)S(1)} custom-call(bf16[1024,8192]{1,0:T(8,128)(2,1)} %panels.3), custom_call_target="tpu_custom_call" | custom-call | bytes 1 | tf_op jit(solution)/shard_map/pallas_call | solution.py:206
  31.9 1.9 %copy-done.4 = bf16[1024,2048]{1,0:T(8,128)(2,1)} copy-done((bf16[1024,2048]{1,0:T(8,128)(2,1)}, bf16[1024,2048]{1,0:T(8,128)(2,1)S(1)}, u32[]{:S(2)}) %copy-start.4) | copy-done | bytes 4194328
  35.0 4.3 %collective-permute-done.2 = bf16[256,256]{1,0:T(8,128)(2,1)S(1)} collective-permute-done((bf16[256,256]{1,0:T(8,128)(2,1)S(1)}, bf16[256,256]{1,0:T(8,128)(2,1)S(1)}, u32[]{:S(2)}, u32[]{:S(2)}) %collective-permute-start.2) | collective-permute-done | bytes 131104 | tf_op jit(solution)/shard_map/ppermute | solution.py:232
  39.8 1.5 %collective-permute-done.3.refs_3_ = bf16[1024,256]{1,0:T(8,128)(2,1)S(1)} collective-permute-done((bf16[1024,256]{1,0:T(8,128)(2,1)S(1)}, bf16[1024,256]{1,0:T(8,128)(2,1)S(1)}, u32[]{:S(2)}, u32[]{:S(2)}) %collective-permute-start.3) | collective-permute-done | bytes 524320 | tf_op jit(solution)/shard_map/ppermute | solution.py:232
  41.3 2.2 %copy-done.5 = bf16[1024,2048]{1,0:T(8,128)(2,1)S(1)} copy-done((bf16[1024,2048]{1,0:T(8,128)(2,1)S(1)}, bf16[1024,2048]{1,0:T(8,128)(2,1)}, u32[]{:S(2)}) %copy-start.5) | copy-done | bytes 4194328
  43.5 4.0 %shard_map.29 = (f32[1024,256]{1,0:T(8,128)S(1)}, bf16[1024,256]{1,0:T(8,128)(2,1)S(1)}) custom-call(f32[1024,256]{1,0:T(8,128)S(1)} %convert_bitcast_fusion.refs_0_, bf16[1024,2048]{1,0:T(8,128)(2,1)S(1)} %copy-done.5, bf16[1024,256]{1,0:T(8,128)(2,1)S(1)} %pad_maximum_fusion.3.refs_2_, bf16[1024,256]{1,0:T(8,128)(2,1)S(1)} %collective-permute-done.3.refs_3_), custom_call_target="tpu_custom_call" | custom-call | flops 1073741824 | bytes 2097152 | tf_op jit(solution)/shard_map/pallas_call | solution.py:168
  48.9 2.2 %shard_map.30.refs_1_ = bf16[1024,2048]{1,0:T(8,128)(2,1)S(1)} custom-call(bf16[1024,8192]{1,0:T(8,128)(2,1)} %panels.3), custom_call_target="tpu_custom_call" | custom-call | bytes 1 | tf_op jit(solution)/shard_map/pallas_call | solution.py:206
  54.1 2.2 %shard_map.32.refs_1_.refs_2_ = bf16[1024,2048]{1,0:T(8,128)(2,1)S(1)} custom-call(bf16[1024,8192]{1,0:T(8,128)(2,1)} %panels.3), custom_call_target="tpu_custom_call" | custom-call | bytes 1 | tf_op jit(solution)/shard_map/pallas_call | solution.py:206
  56.5 1.9 %copy-done.2 = bf16[1024,2048]{1,0:T(8,128)(2,1)} copy-done((bf16[1024,2048]{1,0:T(8,128)(2,1)}, bf16[1024,2048]{1,0:T(8,128)(2,1)S(1)}, u32[]{:S(2)}) %copy-start.2) | copy-done | bytes 4194328
  60.6 1.3 collective-permute-start.13
  61.9 1.3 collective-permute-start.14
  63.2 1.5 %collective-permute-start.15 = (bf16[256,256]{1,0:T(8,128)(2,1)S(1)}, bf16[256,256]{1,0:T(8,128)(2,1)S(1)}, u32[]{:S(2)}, u32[]{:S(2)}) collective-permute-start(bf16[256,256]{1,0:T(8,128)(2,1)S(1)} %select_select_fusion.3), channel_id=1, source_target_pairs={{2,4},{3,5},{10,12},{11,13},{18,20},{19,21},{26,28},{27,29},{4,6},... | collective-permute-start | bytes 393224 | tf_op jit(solution)/shard_map/ppermute | solution.py:232
  64.7 2.4 %shard_map.35.refs_3_ = bf16[1024,2048]{1,0:T(8,128)(2,1)S(1)} custom-call(bf16[1024,8192]{1,0:T(8,128)(2,1)} %panels.3), custom_call_target="tpu_custom_call" | custom-call | bytes 1 | tf_op jit(solution)/shard_map/pallas_call | solution.py:206
  67.1 18.5 %collective-permute-done.13 = bf16[256,256]{1,0:T(8,128)(2,1)S(1)} collective-permute-done((bf16[256,256]{1,0:T(8,128)(2,1)S(1)}, bf16[256,256]{1,0:T(8,128)(2,1)S(1)}, u32[]{:S(2)}, u32[]{:S(2)}) %collective-permute-start.13) | collective-permute-done | bytes 131104 | tf_op jit(solution)/shard_map/ppermute | solution.py:232
  85.6 15.2 %collective-permute-done.14 = bf16[256,256]{1,0:T(8,128)(2,1)S(1)} collective-permute-done((bf16[256,256]{1,0:T(8,128)(2,1)S(1)}, bf16[256,256]{1,0:T(8,128)(2,1)S(1)}, u32[]{:S(2)}, u32[]{:S(2)}) %collective-permute-start.14) | collective-permute-done | bytes 131104 | tf_op jit(solution)/shard_map/ppermute | solution.py:232
  100.8 5.2 %collective-permute-done.15 = bf16[256,256]{1,0:T(8,128)(2,1)S(1)} collective-permute-done((bf16[256,256]{1,0:T(8,128)(2,1)S(1)}, bf16[256,256]{1,0:T(8,128)(2,1)S(1)}, u32[]{:S(2)}, u32[]{:S(2)}) %collective-permute-start.15) | collective-permute-done | bytes 131104 | tf_op jit(solution)/shard_map/ppermute | solution.py:232
  106.1 1.4 %collective-permute-start.17 = (bf16[768,256]{1,0:T(8,128)(2,1)S(1)}, bf16[768,256]{1,0:T(8,128)(2,1)S(1)}, u32[]{:S(2)}, u32[]{:S(2)}) collective-permute-start(bf16[768,256]{1,0:T(8,128)(2,1)S(1)} %pad_maximum_fusion.4), channel_id=1, source_target_pairs={{16,0},{17,1},{18,2},{19,3},{20,4},{21,5},{22,6},{23,7},{0,16},{1,... | collective-permute-start | bytes 1179656 | tf_op jit(solution)/shard_map/ppermute | solution.py:232
  107.5 1.9 %collective-permute-start.16 = (bf16[768,256]{1,0:T(8,128)(2,1)S(1)}, bf16[768,256]{1,0:T(8,128)(2,1)S(1)}, u32[]{:S(2)}, u32[]{:S(2)}) collective-permute-start(bf16[768,256]{1,0:T(8,128)(2,1)S(1)} %pad_maximum_fusion.4), channel_id=1, source_target_pairs={{1,0},{0,1},{3,2},{2,3},{5,4},{4,5},{7,6},{6,7},{17,16},{16,17},{1... | collective-permute-start | bytes 1179656 | tf_op jit(solution)/shard_map/ppermute | solution.py:232
  109.4 8.6 %collective-permute-done.17 = bf16[768,256]{1,0:T(8,128)(2,1)S(1)} collective-permute-done((bf16[768,256]{1,0:T(8,128)(2,1)S(1)}, bf16[768,256]{1,0:T(8,128)(2,1)S(1)}, u32[]{:S(2)}, u32[]{:S(2)}) %collective-permute-start.17) | collective-permute-done | bytes 393248 | tf_op jit(solution)/shard_map/ppermute | solution.py:232
  118.9 4.6 %shard_map.36.refs_0_ = f32[1024,256]{1,0:T(8,128)S(1)} custom-call(f32[1024,256]{1,0:T(8,128)S(1)} %get-tuple-element.28.refs_0_, bf16[1024,2048]{1,0:T(8,128)(2,1)S(1)} %copy-done.1, bf16[1024,2048]{1,0:T(8,128)(2,1)S(1)} %copy-done.3, bf16[1024,2048]{1,0:T(8,128)(2,1)S(1)} %shard_map.35.refs_3_, bf16[2304,256]{1,0:T(8,128)(2,1)S(1)} %pad_maximum_fusion.1.refs_4_), custom_call_target="tpu_custom_call" | custom-call | flops 3221225472 | bytes 2097152 | tf_op jit(solution)/shard_map/pallas_call | solution.py:168
  123.5 2.2 %collective-permute-done.18.refs_4_ = bf16[768,256]{1,0:T(8,128)(2,1)S(1)} collective-permute-done((bf16[768,256]{1,0:T(8,128)(2,1)S(1)}, bf16[768,256]{1,0:T(8,128)(2,1)S(1)}, u32[]{:S(2)}, u32[]{:S(2)}) %collective-permute-start.18) | collective-permute-done | bytes 393248 | tf_op jit(solution)/shard_map/ppermute | solution.py:232
  126.0 3.4 %collective-permute-done.19.refs_5_ = bf16[3072,256]{1,0:T(8,128)(2,1)S(1)} collective-permute-done((bf16[3072,256]{1,0:T(8,128)(2,1)S(1)}, bf16[3072,256]{1,0:T(8,128)(2,1)S(1)}, u32[]{:S(2)}, u32[]{:S(2)}) %collective-permute-start.19) | collective-permute-done | bytes 1572896 | tf_op jit(solution)/shard_map/ppermute | solution.py:232
  129.4 7.9 %shard_map.37 = f32[1024,256]{1,0:T(8,128)} custom-call(f32[1024,256]{1,0:T(8,128)S(1)} %shard_map.36.refs_0_, bf16[1024,2048]{1,0:T(8,128)(2,1)S(1)} %copy-done.1, bf16[1024,2048]{1,0:T(8,128)(2,1)S(1)} %copy-done.3, bf16[1024,2048]{1,0:T(8,128)(2,1)S(1)} %shard_map.35.refs_3_, bf16[768,256]{1,0:T(8,128)(2,1)S(1)} %collective-permute-done.18.refs_4_, ...), custom_call_target="tpu_custom_call" | custom-call | flops 3221225472 | bytes 2097152 | tf_op jit(solution)/shard_map/pallas_call | solution.py:168
  (53 shorter events, 12.7 us)
Async XLA Ops:
  28.2 6.1 %collective-permute-start.1 = (bf16[256,256]{1,0:T(8,128)(2,1)S(1)}, bf16[256,256]{1,0:T(8,128)(2,1)S(1)}, u32[]{:S(2)}, u32[]{:S(2)}) collective-permute-start(bf16[256,256]{1,0:T(8,128)(2,1)S(1)} %bitcast.17), channel_id=1, source_target_pairs={{16,0},{17,1},{18,2},{19,3},{20,4},{21,5},{22,6},{23,7},{0,16},{1,... | collective-permute-start | bytes 393224 | tf_op jit(solution)/shard_map/ppermute | solution.py:232
  28.9 6.2 %collective-permute-start = (bf16[256,256]{1,0:T(8,128)(2,1)S(1)}, bf16[256,256]{1,0:T(8,128)(2,1)S(1)}, u32[]{:S(2)}, u32[]{:S(2)}) collective-permute-start(bf16[256,256]{1,0:T(8,128)(2,1)S(1)} %bitcast.18), channel_id=1, source_target_pairs={{1,0},{0,1},{3,2},{2,3},{5,4},{4,5},{7,6},{6,7},{17,16},{16,17},{1... | collective-permute-start | bytes 393224 | tf_op jit(solution)/shard_map/ppermute | solution.py:232
  34.4 5.0 %collective-permute-start.2 = (bf16[256,256]{1,0:T(8,128)(2,1)S(1)}, bf16[256,256]{1,0:T(8,128)(2,1)S(1)}, u32[]{:S(2)}, u32[]{:S(2)}) collective-permute-start(bf16[256,256]{1,0:T(8,128)(2,1)S(1)} %collective-permute-done.1), channel_id=1, source_target_pairs={{1,0},{0,1},{3,2},{2,3},{5,4},{4,5},{7,6},{6,7},{17,16},{16,17},{1... | collective-permute-start | bytes 393224 | tf_op jit(solution)/shard_map/ppermute | solution.py:232
  39.4 2.0 %collective-permute-start.3 = (bf16[1024,256]{1,0:T(8,128)(2,1)S(1)}, bf16[1024,256]{1,0:T(8,128)(2,1)S(1)}, u32[]{:S(2)}, u32[]{:S(2)}) collective-permute-start(bf16[1024,256]{1,0:T(8,128)(2,1)S(1)} %pad_maximum_fusion.3.refs_2_), channel_id=1, source_target_pairs={{8,0},{9,1},{10,2},{11,3},{12,4},{13,5},{14,6},{15,7},{0,8},{1,9},... | collective-permute-start | bytes 1572872 | tf_op jit(solution)/shard_map/ppermute | solution.py:232
  41.3 2.2 %copy-start.5 = (bf16[1024,2048]{1,0:T(8,128)(2,1)S(1)}, bf16[1024,2048]{1,0:T(8,128)(2,1)}, u32[]{:S(2)}) copy-start(bf16[1024,2048]{1,0:T(8,128)(2,1)} %copy-done.4) | copy-start | bytes 12582916
  47.5 3.6 %collective-permute-start.4 = (bf16[1024,256]{1,0:T(8,128)(2,1)S(1)}, bf16[1024,256]{1,0:T(8,128)(2,1)S(1)}, u32[]{:S(2)}, u32[]{:S(2)}) collective-permute-start(bf16[1024,256]{1,0:T(8,128)(2,1)S(1)} %get-tuple-element.29.refs_4_), channel_id=1, source_target_pairs={{2,4},{3,5}} | collective-permute-start | bytes 1572872 | tf_op jit(solution)/shard_map/ppermute | solution.py:232
  48.2 4.4 %collective-permute-start.5 = (bf16[1024,256]{1,0:T(8,128)(2,1)S(1)}, bf16[1024,256]{1,0:T(8,128)(2,1)S(1)}, u32[]{:S(2)}, u32[]{:S(2)}) collective-permute-start(bf16[1024,256]{1,0:T(8,128)(2,1)S(1)} %get-tuple-element.29.refs_4_), channel_id=1, source_target_pairs={{3,4},{2,5}} | collective-permute-start | bytes 1572872 | tf_op jit(solution)/shard_map/ppermute | solution.py:232
  51.2 5.2 %copy-start = (bf16[1024,2048]{1,0:T(8,128)(2,1)}, bf16[1024,2048]{1,0:T(8,128)(2,1)S(1)}, u32[]{:S(2)}) copy-start(bf16[1024,2048]{1,0:T(8,128)(2,1)S(1)} %shard_map.30.refs_1_) | copy-start | bytes 12582916
  51.2 5.2 %collective-permute-start.6 = (bf16[1024,256]{1,0:T(8,128)(2,1)S(1)}, bf16[1024,256]{1,0:T(8,128)(2,1)S(1)}, u32[]{:S(2)}, u32[]{:S(2)}) collective-permute-start(bf16[1024,256]{1,0:T(8,128)(2,1)S(1)} %get-tuple-element.29.refs_4_), channel_id=1, source_target_pairs={{2,6},{3,7}} | collective-permute-start | bytes 1572872 | tf_op jit(solution)/shard_map/ppermute | solution.py:232
  51.9 4.5 %collective-permute-start.7 = (bf16[1024,256]{1,0:T(8,128)(2,1)S(1)}, bf16[1024,256]{1,0:T(8,128)(2,1)S(1)}, u32[]{:S(2)}, u32[]{:S(2)}) collective-permute-start(bf16[1024,256]{1,0:T(8,128)(2,1)S(1)} %get-tuple-element.29.refs_4_), channel_id=1, source_target_pairs={{3,6},{2,7}} | collective-permute-start | bytes 1572872 | tf_op jit(solution)/shard_map/ppermute | solution.py:232
  52.7 3.8 %collective-permute-start.8 = (bf16[1024,256]{1,0:T(8,128)(2,1)S(1)}, bf16[1024,256]{1,0:T(8,128)(2,1)S(1)}, u32[]{:S(2)}, u32[]{:S(2)}) collective-permute-start(bf16[1024,256]{1,0:T(8,128)(2,1)S(1)} %shard_map.31.refs_5_), channel_id=1, source_target_pairs={{4,6},{5,7}} | collective-permute-start | bytes 1572872 | tf_op jit(solution)/shard_map/ppermute | solution.py:232
  53.4 3.1 %collective-permute-start.9 = (bf16[1024,256]{1,0:T(8,128)(2,1)S(1)}, bf16[1024,256]{1,0:T(8,128)(2,1)S(1)}, u32[]{:S(2)}, u32[]{:S(2)}) collective-permute-start(bf16[1024,256]{1,0:T(8,128)(2,1)S(1)} %shard_map.31.refs_5_), channel_id=1, source_target_pairs={{5,6},{4,7}} | collective-permute-start | bytes 1572872 | tf_op jit(solution)/shard_map/ppermute | solution.py:232
  58.5 2.1 %collective-permute-start.10 = (bf16[256,256]{1,0:T(8,128)(2,1)S(1)}, bf16[256,256]{1,0:T(8,128)(2,1)S(1)}, u32[]{:S(2)}, u32[]{:S(2)}) collective-permute-start(bf16[256,256]{1,0:T(8,128)(2,1)S(1)} %get-tuple-element.32), channel_id=1, source_target_pairs={{2,26},{3,27},{4,28},{5,29},{6,30},{7,31}} | collective-permute-start | bytes 393224 | tf_op jit(solution)/shard_map/ppermute | solution.py:232
  59.1 1.4 %collective-permute-start.11 = (bf16[256,256]{1,0:T(8,128)(2,1)S(1)}, bf16[256,256]{1,0:T(8,128)(2,1)S(1)}, u32[]{:S(2)}, u32[]{:S(2)}) collective-permute-start(bf16[256,256]{1,0:T(8,128)(2,1)S(1)} %get-tuple-element.33), channel_id=1, source_target_pairs={{2,18},{3,19},{4,20},{5,21},{6,22},{7,23}} | collective-permute-start | bytes 393224 | tf_op jit(solution)/shard_map/ppermute | solution.py:232
  59.8 0.7 collective-permute-start.12
  60.6 25.0 %collective-permute-start.13 = (bf16[256,256]{1,0:T(8,128)(2,1)S(1)}, bf16[256,256]{1,0:T(8,128)(2,1)S(1)}, u32[]{:S(2)}, u32[]{:S(2)}) collective-permute-start(bf16[256,256]{1,0:T(8,128)(2,1)S(1)} %select_select_fusion.3), channel_id=1, source_target_pairs={{2,0},{3,1},{10,8},{11,9},{18,16},{19,17},{26,24},{27,25},{4,2},{5... | collective-permute-start | bytes 393224 | tf_op jit(solution)/shard_map/ppermute | solution.py:232
  61.9 39.0 %collective-permute-start.14 = (bf16[256,256]{1,0:T(8,128)(2,1)S(1)}, bf16[256,256]{1,0:T(8,128)(2,1)S(1)}, u32[]{:S(2)}, u32[]{:S(2)}) collective-permute-start(bf16[256,256]{1,0:T(8,128)(2,1)S(1)} %select_select_fusion.3), channel_id=1, source_target_pairs={{2,6},{3,7},{10,14},{11,15},{18,22},{19,23},{26,30},{27,31},{4,0},... | collective-permute-start | bytes 393224 | tf_op jit(solution)/shard_map/ppermute | solution.py:232
  63.2 42.8 %collective-permute-start.15 = (bf16[256,256]{1,0:T(8,128)(2,1)S(1)}, bf16[256,256]{1,0:T(8,128)(2,1)S(1)}, u32[]{:S(2)}, u32[]{:S(2)}) collective-permute-start(bf16[256,256]{1,0:T(8,128)(2,1)S(1)} %select_select_fusion.3), channel_id=1, source_target_pairs={{2,4},{3,5},{10,12},{11,13},{18,20},{19,21},{26,28},{27,29},{4,6},... | collective-permute-start | bytes 393224 | tf_op jit(solution)/shard_map/ppermute | solution.py:232
  64.7 54.2 %copy-start.1 = (bf16[1024,2048]{1,0:T(8,128)(2,1)S(1)}, bf16[1024,2048]{1,0:T(8,128)(2,1)}, u32[]{:S(2)}) copy-start(bf16[1024,2048]{1,0:T(8,128)(2,1)} %copy-done) | copy-start | bytes 12582916
  64.7 54.2 %copy-start.3 = (bf16[1024,2048]{1,0:T(8,128)(2,1)S(1)}, bf16[1024,2048]{1,0:T(8,128)(2,1)}, u32[]{:S(2)}) copy-start(bf16[1024,2048]{1,0:T(8,128)(2,1)} %copy-done.2) | copy-start | bytes 12582916
  106.1 11.9 %collective-permute-start.17 = (bf16[768,256]{1,0:T(8,128)(2,1)S(1)}, bf16[768,256]{1,0:T(8,128)(2,1)S(1)}, u32[]{:S(2)}, u32[]{:S(2)}) collective-permute-start(bf16[768,256]{1,0:T(8,128)(2,1)S(1)} %pad_maximum_fusion.4), channel_id=1, source_target_pairs={{16,0},{17,1},{18,2},{19,3},{20,4},{21,5},{22,6},{23,7},{0,16},{1,... | collective-permute-start | bytes 1179656 | tf_op jit(solution)/shard_map/ppermute | solution.py:232
  107.5 11.3 %collective-permute-start.16 = (bf16[768,256]{1,0:T(8,128)(2,1)S(1)}, bf16[768,256]{1,0:T(8,128)(2,1)S(1)}, u32[]{:S(2)}, u32[]{:S(2)}) collective-permute-start(bf16[768,256]{1,0:T(8,128)(2,1)S(1)} %pad_maximum_fusion.4), channel_id=1, source_target_pairs={{1,0},{0,1},{3,2},{2,3},{5,4},{4,5},{7,6},{6,7},{17,16},{16,17},{1... | collective-permute-start | bytes 1179656 | tf_op jit(solution)/shard_map/ppermute | solution.py:232
  118.0 7.8 %collective-permute-start.18 = (bf16[768,256]{1,0:T(8,128)(2,1)S(1)}, bf16[768,256]{1,0:T(8,128)(2,1)S(1)}, u32[]{:S(2)}, u32[]{:S(2)}) collective-permute-start(bf16[768,256]{1,0:T(8,128)(2,1)S(1)} %collective-permute-done.17), channel_id=1, source_target_pairs={{1,0},{0,1},{3,2},{2,3},{5,4},{4,5},{7,6},{6,7},{17,16},{16,17},{1... | collective-permute-start | bytes 1179656 | tf_op jit(solution)/shard_map/ppermute | solution.py:232
  125.9 3.5 %collective-permute-start.19 = (bf16[3072,256]{1,0:T(8,128)(2,1)S(1)}, bf16[3072,256]{1,0:T(8,128)(2,1)S(1)}, u32[]{:S(2)}, u32[]{:S(2)}) collective-permute-start(bf16[3072,256]{1,0:T(8,128)(2,1)S(1)} %pad_maximum_fusion), channel_id=1, source_target_pairs={{8,0},{9,1},{10,2},{11,3},{12,4},{13,5},{14,6},{15,7},{0,8},{1,9},... | collective-permute-start | bytes 4718600 | tf_op jit(solution)/shard_map/ppermute | solution.py:232
  (2 other events, 4.0 us)

commit v13 on v12

--- a/solution.py
+++ b/solution.py
@@ -246,7 +246,7 @@
         across = [(dy, dm) for dy, _ in along_y for _, dm in along_x]
         offsets = [((0, 0), (0, 0)), *zip(first_0, first_1), *zip(across, across)]
 
-        def plane_gather(value, beside=None):
+        def plane_gather(value):
             def pairs(c, step):
                 return [
                     (device((t + step[0]) % n_y, c, z, (m + step[1]) % lanes), device(t, c, z, m))
@@ -254,8 +254,6 @@
                 ]
 
             got = [send(value, pairs(0, a) + pairs(1, b)) for a, b in zip(first_0, first_1)]
-            if beside is not None:
-                got = [after(part, beside) for part in got]
             last = []
             for dy, dm in across:
                 a, b = first_0.index((dy, 0)), first_1.index((0, dm))
@@ -302,8 +300,8 @@
         regrouped = lax.all_to_all(outgoing, AXES, split_axis=1, concat_axis=0, tiled=True)
         regrouped = regrouped.reshape(-1, rows_here + extra)
         current = jnp.transpose(regrouped[:, :rows_here]).astype(jnp.float32)
-        near0 = near_panel(after(factor_panels, regrouped), 0)
-        whole = jnp.concatenate(plane_gather(jnp.transpose(regrouped[:, rows_here:]), near0), axis=0)
+        whole = jnp.concatenate(plane_gather(jnp.transpose(regrouped[:, rows_here:])), axis=0)
+        near0 = near_panel(after(factor_panels, whole), 0)
         pieces = [
             piece
             for array, own in ((whole, True), (core_exchange(whole), False))
@@ -373,8 +371,8 @@
         (current,) = run(current, terms(True, (most, True, 0, n_most)), [f32_rows])
         whole = after(jnp.concatenate([most, last], axis=0), current)
         other = core_exchange(whole)
-        rest = [(last, True, n_most, len(across)), (other, False, 0, len(offsets))]
-        (out,) = run(current, terms(False, *rest), [(jnp.float32, 0, rows_here, True)])
+        (current,) = run(current, terms(False, (last, True, n_most, len(across))), [f32_rows])
+        (out,) = run(current, terms(False, (other, False, 0, len(offsets))), [(jnp.float32, 0, rows_here, True)])
         return out
 
     return on_device

time: 138 us -> 136 us (0.986)
  local copies, waits for them, and re-layouts: 7.15 us -> 3.01 us
  waiting for transfers between devices: 59.6 us -> 62.6 us
  starting transfers between devices: 16.6 us -> 15.1 us
    unnamed x14 -> x10, local copies, waits for them, and re-layouts: 6.31 us -> 2.18 us
    ppermute x20, waiting for transfers between devices: 59.6 us -> 62.6 us  [send(): return lax.ppermute(value, AXES, pairs)]
    ppermute x20, starting transfers between devices: 16.6 us -> 15.1 us  [send(): return lax.ppermute(value, AXES, pairs)]
    pallas_call x6 -> x7, Pallas kernels: 16.7 us -> 17.7 us  [steps(): pl.pallas_call(functools.partial(step_kernel, plan, handed, len(arrays),...]
  transfers between devices with their start and end apart: 20 -> 20, of which waited for: 9 -> 8; matrix products, arithmetic and copies ran while one was open for 0% -> 0% of each run, Pallas kernels for 10% -> 12%
where the time goes in v13:
time: 136 us
  waiting for transfers between devices  62.6 us (46%)
  Pallas kernels  26.7 us (20%)
  blocking collectives  26.3 us (19%)
  starting transfers between devices  15.1 us (11%)
  local copies, waits for them, and re-layouts  3.01 us (2%)
  other arithmetic  1.48 us (1%)
    ppermute x20, waiting for transfers between devices, send(): return lax.ppermute(value, AXES, pairs)  62.6 us
    all_to_all x1, blocking collectives, on_device(): lax.all_to_all(outgoing, AXES, split_axis=1, concat_axis=0, tiled=True)  26.3 us
    pallas_call x7, Pallas kernels, steps(): pl.pallas_call(functools.partial(step_kernel, plan, handed, len(arrays),...  17.7 us
    ppermute x20, starting transfers between devices, send(): return lax.ppermute(value, AXES, pairs)  15.1 us
    pallas_call x4, Pallas kernels, near_panel(): pl.pallas_call(functools.partial(near_kernel, k), in_specs=[pl.BlockSpec(...  9.01 us
  transfers between devices with their start and end apart: 20, of which 8 were waited for; matrix products, arithmetic and copies ran while one was open for 0% of the time, Pallas kernels for 12%

profile of v13, /device:TPU:0, one launch (start us, length us, event | category | flops | bytes accessed | tf_op | source)
XLA Modules:
  0.0 135.7 jit_solution(4121296508593471609)
XLA Ops:
  0.8 1.1 pad_maximum_fusion.2
  1.9 26.3 %all_to_all.15 = bf16[8,32,1280]{2,0,1:T(8,128)(2,1)S(1)} all-to-all(bf16[8,32,1280]{2,0,1:T(8,128)(2,1)S(1)} %pad_maximum_fusion.2), channel_id=1, replica_groups=mesh['row'=4,'col'=8] {'row','col'}, dimensions={1} | all-to-all | bytes 1310720 | tf_op jit(solution)/shard_map/all_to_all | solution.py:300
  29.7 4.8 %collective-permute-done.1 = bf16[256,256]{1,0:T(8,128)(2,1)S(1)} collective-permute-done((bf16[256,256]{1,0:T(8,128)(2,1)S(1)}, bf16[256,256]{1,0:T(8,128)(2,1)S(1)}, u32[]{:S(2)}, u32[]{:S(2)}) %collective-permute-start.1) | collective-permute-done | bytes 131104 | tf_op jit(solution)/shard_map/ppermute | solution.py:232
  34.8 4.6 %collective-permute-done.2 = bf16[256,256]{1,0:T(8,128)(2,1)S(1)} collective-permute-done((bf16[256,256]{1,0:T(8,128)(2,1)S(1)}, bf16[256,256]{1,0:T(8,128)(2,1)S(1)}, u32[]{:S(2)}, u32[]{:S(2)}) %collective-permute-start.2) | collective-permute-done | bytes 131104 | tf_op jit(solution)/shard_map/ppermute | solution.py:232
  39.9 2.2 %shard_map.28.refs_1_ = bf16[1024,2048]{1,0:T(8,128)(2,1)S(1)} custom-call(bf16[1024,8192]{1,0:T(8,128)(2,1)} %panels.3), custom_call_target="tpu_custom_call" | custom-call | bytes 1 | tf_op jit(solution)/shard_map/pallas_call | solution.py:206
  42.2 4.1 %shard_map.29 = (f32[1024,256]{1,0:T(8,128)S(1)}, bf16[1024,256]{1,0:T(8,128)(2,1)S(1)}) custom-call(f32[1024,256]{1,0:T(8,128)S(1)} %convert_bitcast_fusion.refs_0_, bf16[1024,2048]{1,0:T(8,128)(2,1)S(1)} %shard_map.28.refs_1_, bf16[1024,256]{1,0:T(8,128)(2,1)S(1)} %pad_maximum_fusion.3.refs_2_, bf16[1024,256]{1,0:T(8,128)(2,1)S(1)} %collective-permute-done.3.refs_3_), custom_call_target="tpu_custom_call" | custom-call | flops 1073741824 | bytes 2097152 | tf_op jit(solution)/shard_map/pallas_call | solution.py:168
  47.7 2.2 %shard_map.30.refs_1_ = bf16[1024,2048]{1,0:T(8,128)(2,1)S(1)} custom-call(bf16[1024,8192]{1,0:T(8,128)(2,1)} %panels.3), custom_call_target="tpu_custom_call" | custom-call | bytes 1 | tf_op jit(solution)/shard_map/pallas_call | solution.py:206
  52.8 2.2 %shard_map.32.refs_1_.refs_2_ = bf16[1024,2048]{1,0:T(8,128)(2,1)S(1)} custom-call(bf16[1024,8192]{1,0:T(8,128)(2,1)} %panels.3), custom_call_target="tpu_custom_call" | custom-call | bytes 1 | tf_op jit(solution)/shard_map/pallas_call | solution.py:206
  55.2 1.9 %copy-done.2 = bf16[1024,2048]{1,0:T(8,128)(2,1)} copy-done((bf16[1024,2048]{1,0:T(8,128)(2,1)}, bf16[1024,2048]{1,0:T(8,128)(2,1)S(1)}, u32[]{:S(2)}) %copy-start.2) | copy-done | bytes 4194328
  59.3 1.3 collective-permute-start.15
  60.6 1.3 collective-permute-start.14
  61.9 1.5 %collective-permute-start.13 = (bf16[256,256]{1,0:T(8,128)(2,1)S(1)}, bf16[256,256]{1,0:T(8,128)(2,1)S(1)}, u32[]{:S(2)}, u32[]{:S(2)}) collective-permute-start(bf16[256,256]{1,0:T(8,128)(2,1)S(1)} %select_select_fusion.3), channel_id=1, source_target_pairs={{2,0},{3,1},{10,8},{11,9},{18,16},{19,17},{26,24},{27,25},{4,2},{5... | collective-permute-start | bytes 393224 | tf_op jit(solution)/shard_map/ppermute | solution.py:232
  63.4 2.4 %shard_map.35.refs_3_ = bf16[1024,2048]{1,0:T(8,128)(2,1)S(1)} custom-call(bf16[1024,8192]{1,0:T(8,128)(2,1)} %panels.3), custom_call_target="tpu_custom_call" | custom-call | bytes 1 | tf_op jit(solution)/shard_map/pallas_call | solution.py:206
  65.8 33.6 %collective-permute-done.15 = bf16[256,256]{1,0:T(8,128)(2,1)S(1)} collective-permute-done((bf16[256,256]{1,0:T(8,128)(2,1)S(1)}, bf16[256,256]{1,0:T(8,128)(2,1)S(1)}, u32[]{:S(2)}, u32[]{:S(2)}) %collective-permute-start.15) | collective-permute-done | bytes 131104 | tf_op jit(solution)/shard_map/ppermute | solution.py:232
  99.4 5.1 %collective-permute-done.14 = bf16[256,256]{1,0:T(8,128)(2,1)S(1)} collective-permute-done((bf16[256,256]{1,0:T(8,128)(2,1)S(1)}, bf16[256,256]{1,0:T(8,128)(2,1)S(1)}, u32[]{:S(2)}, u32[]{:S(2)}) %collective-permute-start.14) | collective-permute-done | bytes 131104 | tf_op jit(solution)/shard_map/ppermute | solution.py:232
  104.4 1.1 collective-permute-done.13
  105.6 1.1 collective-permute-start.17
  106.7 1.5 %collective-permute-start.16 = (bf16[768,256]{1,0:T(8,128)(2,1)S(1)}, bf16[768,256]{1,0:T(8,128)(2,1)S(1)}, u32[]{:S(2)}, u32[]{:S(2)}) collective-permute-start(bf16[768,256]{1,0:T(8,128)(2,1)S(1)} %pad_maximum_fusion.4), channel_id=1, source_target_pairs={{1,0},{0,1},{3,2},{2,3},{5,4},{4,5},{7,6},{6,7},{17,16},{16,17},{1... | collective-permute-start | bytes 1179656 | tf_op jit(solution)/shard_map/ppermute | solution.py:232
  108.1 9.5 %collective-permute-done.17 = bf16[768,256]{1,0:T(8,128)(2,1)S(1)} collective-permute-done((bf16[768,256]{1,0:T(8,128)(2,1)S(1)}, bf16[768,256]{1,0:T(8,128)(2,1)S(1)}, u32[]{:S(2)}, u32[]{:S(2)}) %collective-permute-start.17) | collective-permute-done | bytes 393248 | tf_op jit(solution)/shard_map/ppermute | solution.py:232
  118.1 4.6 %shard_map.36.refs_0_ = f32[1024,256]{1,0:T(8,128)S(1)} custom-call(f32[1024,256]{1,0:T(8,128)S(1)} %get-tuple-element.24.refs_0_, bf16[1024,2048]{1,0:T(8,128)(2,1)S(1)} %copy-done.1, bf16[1024,2048]{1,0:T(8,128)(2,1)S(1)} %copy-done.3, bf16[1024,2048]{1,0:T(8,128)(2,1)S(1)} %shard_map.35.refs_3_, bf16[2304,256]{1,0:T(8,128)(2,1)S(1)} %pad_maximum_fusion.1.refs_4_), custom_call_target="tpu_custom_call" | custom-call | flops 3221225472 | bytes 2097152 | tf_op jit(solution)/shard_map/pallas_call | solution.py:168
  122.7 2.6 %collective-permute-done.18.refs_4_ = bf16[768,256]{1,0:T(8,128)(2,1)S(1)} collective-permute-done((bf16[768,256]{1,0:T(8,128)(2,1)S(1)}, bf16[768,256]{1,0:T(8,128)(2,1)S(1)}, u32[]{:S(2)}, u32[]{:S(2)}) %collective-permute-start.18) | collective-permute-done | bytes 393248 | tf_op jit(solution)/shard_map/ppermute | solution.py:232
  125.6 2.1 %shard_map.37.refs_0_ = f32[1024,256]{1,0:T(8,128)S(1)} custom-call(f32[1024,256]{1,0:T(8,128)S(1)} %shard_map.36.refs_0_, bf16[1024,2048]{1,0:T(8,128)(2,1)S(1)} %copy-done.1, bf16[1024,2048]{1,0:T(8,128)(2,1)S(1)} %copy-done.3, bf16[1024,2048]{1,0:T(8,128)(2,1)S(1)} %shard_map.35.refs_3_, bf16[768,256]{1,0:T(8,128)(2,1)S(1)} %collective-permute-done.18.refs_4_), custom_call_target="tpu_custom_call" | custom-call | flops 3221225472 | bytes 2097152 | tf_op jit(solution)/shard_map/pallas_call | solution.py:168
  127.7 1.3 collective-permute-done.19.refs_4_
  129.0 6.6 %shard_map.38 = f32[1024,256]{1,0:T(8,128)} custom-call(f32[1024,256]{1,0:T(8,128)S(1)} %shard_map.37.refs_0_, bf16[1024,2048]{1,0:T(8,128)(2,1)S(1)} %copy-done.1, bf16[1024,2048]{1,0:T(8,128)(2,1)S(1)} %copy-done.3, bf16[1024,2048]{1,0:T(8,128)(2,1)S(1)} %shard_map.35.refs_3_, bf16[3072,256]{1,0:T(8,128)(2,1)S(1)} %collective-permute-done.19.refs_4_), custom_call_target="tpu_custom_call" | custom-call | flops 3221225472 | bytes 2097152 | tf_op jit(solution)/shard_map/pallas_call | solution.py:168
  (50 shorter events, 10.3 us)
Async XLA Ops:
  28.2 6.3 %collective-permute-start.1 = (bf16[256,256]{1,0:T(8,128)(2,1)S(1)}, bf16[256,256]{1,0:T(8,128)(2,1)S(1)}, u32[]{:S(2)}, u32[]{:S(2)}) collective-permute-start(bf16[256,256]{1,0:T(8,128)(2,1)S(1)} %bitcast.17), channel_id=1, source_target_pairs={{16,0},{17,1},{18,2},{19,3},{20,4},{21,5},{22,6},{23,7},{0,16},{1,... | collective-permute-start | bytes 393224 | tf_op jit(solution)/shard_map/ppermute | solution.py:232
  28.9 6.0 %collective-permute-start = (bf16[256,256]{1,0:T(8,128)(2,1)S(1)}, bf16[256,256]{1,0:T(8,128)(2,1)S(1)}, u32[]{:S(2)}, u32[]{:S(2)}) collective-permute-start(bf16[256,256]{1,0:T(8,128)(2,1)S(1)} %bitcast.18), channel_id=1, source_target_pairs={{1,0},{0,1},{3,2},{2,3},{5,4},{4,5},{7,6},{6,7},{17,16},{16,17},{1... | collective-permute-start | bytes 393224 | tf_op jit(solution)/shard_map/ppermute | solution.py:232
  34.5 5.0 %collective-permute-start.2 = (bf16[256,256]{1,0:T(8,128)(2,1)S(1)}, bf16[256,256]{1,0:T(8,128)(2,1)S(1)}, u32[]{:S(2)}, u32[]{:S(2)}) collective-permute-start(bf16[256,256]{1,0:T(8,128)(2,1)S(1)} %collective-permute-done.1), channel_id=1, source_target_pairs={{1,0},{0,1},{3,2},{2,3},{5,4},{4,5},{7,6},{6,7},{17,16},{16,17},{1... | collective-permute-start | bytes 393224 | tf_op jit(solution)/shard_map/ppermute | solution.py:232
  39.5 2.7 %collective-permute-start.3 = (bf16[1024,256]{1,0:T(8,128)(2,1)S(1)}, bf16[1024,256]{1,0:T(8,128)(2,1)S(1)}, u32[]{:S(2)}, u32[]{:S(2)}) collective-permute-start(bf16[1024,256]{1,0:T(8,128)(2,1)S(1)} %pad_maximum_fusion.3.refs_2_), channel_id=1, source_target_pairs={{8,0},{9,1},{10,2},{11,3},{12,4},{13,5},{14,6},{15,7},{0,8},{1,9},... | collective-permute-start | bytes 1572872 | tf_op jit(solution)/shard_map/ppermute | solution.py:232
  46.3 3.6 %collective-permute-start.4 = (bf16[1024,256]{1,0:T(8,128)(2,1)S(1)}, bf16[1024,256]{1,0:T(8,128)(2,1)S(1)}, u32[]{:S(2)}, u32[]{:S(2)}) collective-permute-start(bf16[1024,256]{1,0:T(8,128)(2,1)S(1)} %get-tuple-element.25.refs_4_), channel_id=1, source_target_pairs={{2,4},{3,5}} | collective-permute-start | bytes 1572872 | tf_op jit(solution)/shard_map/ppermute | solution.py:232
  47.0 4.4 %collective-permute-start.5 = (bf16[1024,256]{1,0:T(8,128)(2,1)S(1)}, bf16[1024,256]{1,0:T(8,128)(2,1)S(1)}, u32[]{:S(2)}, u32[]{:S(2)}) collective-permute-start(bf16[1024,256]{1,0:T(8,128)(2,1)S(1)} %get-tuple-element.25.refs_4_), channel_id=1, source_target_pairs={{3,4},{2,5}} | collective-permute-start | bytes 1572872 | tf_op jit(solution)/shard_map/ppermute | solution.py:232
  49.9 5.2 %copy-start = (bf16[1024,2048]{1,0:T(8,128)(2,1)}, bf16[1024,2048]{1,0:T(8,128)(2,1)S(1)}, u32[]{:S(2)}) copy-start(bf16[1024,2048]{1,0:T(8,128)(2,1)S(1)} %shard_map.30.refs_1_) | copy-start | bytes 12582916
  49.9 5.2 %collective-permute-start.7 = (bf16[1024,256]{1,0:T(8,128)(2,1)S(1)}, bf16[1024,256]{1,0:T(8,128)(2,1)S(1)}, u32[]{:S(2)}, u32[]{:S(2)}) collective-permute-start(bf16[1024,256]{1,0:T(8,128)(2,1)S(1)} %get-tuple-element.25.refs_4_), channel_id=1, source_target_pairs={{3,6},{2,7}} | collective-permute-start | bytes 1572872 | tf_op jit(solution)/shard_map/ppermute | solution.py:232
  50.6 4.5 %collective-permute-start.6 = (bf16[1024,256]{1,0:T(8,128)(2,1)S(1)}, bf16[1024,256]{1,0:T(8,128)(2,1)S(1)}, u32[]{:S(2)}, u32[]{:S(2)}) collective-permute-start(bf16[1024,256]{1,0:T(8,128)(2,1)S(1)} %get-tuple-element.25.refs_4_), channel_id=1, source_target_pairs={{2,6},{3,7}} | collective-permute-start | bytes 1572872 | tf_op jit(solution)/shard_map/ppermute | solution.py:232
  51.4 3.8 %collective-permute-start.9 = (bf16[1024,256]{1,0:T(8,128)(2,1)S(1)}, bf16[1024,256]{1,0:T(8,128)(2,1)S(1)}, u32[]{:S(2)}, u32[]{:S(2)}) collective-permute-start(bf16[1024,256]{1,0:T(8,128)(2,1)S(1)} %shard_map.31.refs_5_), channel_id=1, source_target_pairs={{5,6},{4,7}} | collective-permute-start | bytes 1572872 | tf_op jit(solution)/shard_map/ppermute | solution.py:232
  52.1 3.1 %collective-permute-start.8 = (bf16[1024,256]{1,0:T(8,128)(2,1)S(1)}, bf16[1024,256]{1,0:T(8,128)(2,1)S(1)}, u32[]{:S(2)}, u32[]{:S(2)}) collective-permute-start(bf16[1024,256]{1,0:T(8,128)(2,1)S(1)} %shard_map.31.refs_5_), channel_id=1, source_target_pairs={{4,6},{5,7}} | collective-permute-start | bytes 1572872 | tf_op jit(solution)/shard_map/ppermute | solution.py:232
  55.0 2.0 %copy-start.2 = (bf16[1024,2048]{1,0:T(8,128)(2,1)}, bf16[1024,2048]{1,0:T(8,128)(2,1)S(1)}, u32[]{:S(2)}) copy-start(bf16[1024,2048]{1,0:T(8,128)(2,1)S(1)} %shard_map.32.refs_1_.refs_2_) | copy-start | bytes 12582916
  57.2 2.1 %collective-permute-start.10 = (bf16[256,256]{1,0:T(8,128)(2,1)S(1)}, bf16[256,256]{1,0:T(8,128)(2,1)S(1)}, u32[]{:S(2)}, u32[]{:S(2)}) collective-permute-start(bf16[256,256]{1,0:T(8,128)(2,1)S(1)} %get-tuple-element.28), channel_id=1, source_target_pairs={{2,26},{3,27},{4,28},{5,29},{6,30},{7,31}} | collective-permute-start | bytes 393224 | tf_op jit(solution)/shard_map/ppermute | solution.py:232
  57.8 1.4 %collective-permute-start.11 = (bf16[256,256]{1,0:T(8,128)(2,1)S(1)}, bf16[256,256]{1,0:T(8,128)(2,1)S(1)}, u32[]{:S(2)}, u32[]{:S(2)}) collective-permute-start(bf16[256,256]{1,0:T(8,128)(2,1)S(1)} %get-tuple-element.29), channel_id=1, source_target_pairs={{2,18},{3,19},{4,20},{5,21},{6,22},{7,23}} | collective-permute-start | bytes 393224 | tf_op jit(solution)/shard_map/ppermute | solution.py:232
  58.5 0.7 collective-permute-start.12
  59.3 40.1 %collective-permute-start.15 = (bf16[256,256]{1,0:T(8,128)(2,1)S(1)}, bf16[256,256]{1,0:T(8,128)(2,1)S(1)}, u32[]{:S(2)}, u32[]{:S(2)}) collective-permute-start(bf16[256,256]{1,0:T(8,128)(2,1)S(1)} %select_select_fusion.3), channel_id=1, source_target_pairs={{2,4},{3,5},{10,12},{11,13},{18,20},{19,21},{26,28},{27,29},{4,6},... | collective-permute-start | bytes 393224 | tf_op jit(solution)/shard_map/ppermute | solution.py:232
  60.6 43.8 %collective-permute-start.14 = (bf16[256,256]{1,0:T(8,128)(2,1)S(1)}, bf16[256,256]{1,0:T(8,128)(2,1)S(1)}, u32[]{:S(2)}, u32[]{:S(2)}) collective-permute-start(bf16[256,256]{1,0:T(8,128)(2,1)S(1)} %select_select_fusion.3), channel_id=1, source_target_pairs={{2,6},{3,7},{10,14},{11,15},{18,22},{19,23},{26,30},{27,31},{4,0},... | collective-permute-start | bytes 393224 | tf_op jit(solution)/shard_map/ppermute | solution.py:232
  61.9 43.6 %collective-permute-start.13 = (bf16[256,256]{1,0:T(8,128)(2,1)S(1)}, bf16[256,256]{1,0:T(8,128)(2,1)S(1)}, u32[]{:S(2)}, u32[]{:S(2)}) collective-permute-start(bf16[256,256]{1,0:T(8,128)(2,1)S(1)} %select_select_fusion.3), channel_id=1, source_target_pairs={{2,0},{3,1},{10,8},{11,9},{18,16},{19,17},{26,24},{27,25},{4,2},{5... | collective-permute-start | bytes 393224 | tf_op jit(solution)/shard_map/ppermute | solution.py:232
  63.4 54.7 %copy-start.1 = (bf16[1024,2048]{1,0:T(8,128)(2,1)S(1)}, bf16[1024,2048]{1,0:T(8,128)(2,1)}, u32[]{:S(2)}) copy-start(bf16[1024,2048]{1,0:T(8,128)(2,1)} %copy-done) | copy-start | bytes 12582916
  63.4 54.7 %copy-start.3 = (bf16[1024,2048]{1,0:T(8,128)(2,1)S(1)}, bf16[1024,2048]{1,0:T(8,128)(2,1)}, u32[]{:S(2)}) copy-start(bf16[1024,2048]{1,0:T(8,128)(2,1)} %copy-done.2) | copy-start | bytes 12582916
  105.6 12.0 %collective-permute-start.17 = (bf16[768,256]{1,0:T(8,128)(2,1)S(1)}, bf16[768,256]{1,0:T(8,128)(2,1)S(1)}, u32[]{:S(2)}, u32[]{:S(2)}) collective-permute-start(bf16[768,256]{1,0:T(8,128)(2,1)S(1)} %pad_maximum_fusion.4), channel_id=1, source_target_pairs={{16,0},{17,1},{18,2},{19,3},{20,4},{21,5},{22,6},{23,7},{0,16},{1,... | collective-permute-start | bytes 1179656 | tf_op jit(solution)/shard_map/ppermute | solution.py:232
  106.7 11.3 %collective-permute-start.16 = (bf16[768,256]{1,0:T(8,128)(2,1)S(1)}, bf16[768,256]{1,0:T(8,128)(2,1)S(1)}, u32[]{:S(2)}, u32[]{:S(2)}) collective-permute-start(bf16[768,256]{1,0:T(8,128)(2,1)S(1)} %pad_maximum_fusion.4), channel_id=1, source_target_pairs={{1,0},{0,1},{3,2},{2,3},{5,4},{4,5},{7,6},{6,7},{17,16},{16,17},{1... | collective-permute-start | bytes 1179656 | tf_op jit(solution)/shard_map/ppermute | solution.py:232
  117.6 7.8 %collective-permute-start.18 = (bf16[768,256]{1,0:T(8,128)(2,1)S(1)}, bf16[768,256]{1,0:T(8,128)(2,1)S(1)}, u32[]{:S(2)}, u32[]{:S(2)}) collective-permute-start(bf16[768,256]{1,0:T(8,128)(2,1)S(1)} %collective-permute-done.17), channel_id=1, source_target_pairs={{1,0},{0,1},{3,2},{2,3},{5,4},{4,5},{7,6},{6,7},{17,16},{16,17},{1... | collective-permute-start | bytes 1179656 | tf_op jit(solution)/shard_map/ppermute | solution.py:232
  125.5 3.5 %collective-permute-start.19 = (bf16[3072,256]{1,0:T(8,128)(2,1)S(1)}, bf16[3072,256]{1,0:T(8,128)(2,1)S(1)}, u32[]{:S(2)}, u32[]{:S(2)}) collective-permute-start(bf16[3072,256]{1,0:T(8,128)(2,1)S(1)} %pad_maximum_fusion), channel_id=1, source_target_pairs={{8,0},{9,1},{10,2},{11,3},{12,4},{13,5},{14,6},{15,7},{0,8},{1,9},... | collective-permute-start | bytes 4718600 | tf_op jit(solution)/shard_map/ppermute | solution.py:232

commit v14 on v13

--- a/solution.py
+++ b/solution.py
@@ -12,7 +12,7 @@
 AXES = ("row", "col")
 CORES = 2
 TILE = 256
-NEAR_TILE = 512
+NEAR_TILE = 1024
 IN_FLIGHT = 3
 MIB = 1024 * 1024
 

time: 136 us -> 133 us (0.978)
  Pallas kernels: 26.7 us -> 24.5 us
    pallas_call x7, Pallas kernels: 17.7 us -> 15.5 us  [steps(): pl.pallas_call(functools.partial(step_kernel, plan, handed, len(arrays),...]
  transfers between devices with their start and end apart: 20 -> 20, of which waited for: 8 -> 8; matrix products, arithmetic and copies ran while one was open for 0% -> 0% of each run, Pallas kernels for 12% -> 11%
where the time goes in v14:
time: 133 us
  waiting for transfers between devices  62 us (47%)
  blocking collectives  26.3 us (20%)
  Pallas kernels  24.5 us (18%)
  starting transfers between devices  15.1 us (11%)
  local copies, waits for them, and re-layouts  3.04 us (2%)
  other arithmetic  1.48 us (1%)
    ppermute x20, waiting for transfers between devices, send(): return lax.ppermute(value, AXES, pairs)  62 us
    all_to_all x1, blocking collectives, on_device(): lax.all_to_all(outgoing, AXES, split_axis=1, concat_axis=0, tiled=True)  26.3 us
    pallas_call x7, Pallas kernels, steps(): pl.pallas_call(functools.partial(step_kernel, plan, handed, len(arrays),...  15.5 us
    ppermute x20, starting transfers between devices, send(): return lax.ppermute(value, AXES, pairs)  15.1 us
    pallas_call x4, Pallas kernels, near_panel(): pl.pallas_call(functools.partial(near_kernel, k), in_specs=[pl.BlockSpec(...  9.01 us
  transfers between devices with their start and end apart: 20, of which 8 were waited for; matrix products, arithmetic and copies ran while one was open for 0% of the time, Pallas kernels for 11%

profile of v14, /device:TPU:0, one launch (start us, length us, event | category | flops | bytes accessed | tf_op | source)
XLA Modules:
  0.0 133.0 jit_solution(1637712728467451058)
XLA Ops:
  0.8 1.1 pad_maximum_fusion.2
  1.9 26.3 %all_to_all.15 = bf16[8,32,1280]{2,0,1:T(8,128)(2,1)S(1)} all-to-all(bf16[8,32,1280]{2,0,1:T(8,128)(2,1)S(1)} %pad_maximum_fusion.2), channel_id=1, replica_groups=mesh['row'=4,'col'=8] {'row','col'}, dimensions={1} | all-to-all | bytes 1310720 | tf_op jit(solution)/shard_map/all_to_all | solution.py:300
  29.7 4.8 %collective-permute-done.1 = bf16[256,256]{1,0:T(8,128)(2,1)S(1)} collective-permute-done((bf16[256,256]{1,0:T(8,128)(2,1)S(1)}, bf16[256,256]{1,0:T(8,128)(2,1)S(1)}, u32[]{:S(2)}, u32[]{:S(2)}) %collective-permute-start.1) | collective-permute-done | bytes 131104 | tf_op jit(solution)/shard_map/ppermute | solution.py:232
  34.8 4.6 %collective-permute-done.2 = bf16[256,256]{1,0:T(8,128)(2,1)S(1)} collective-permute-done((bf16[256,256]{1,0:T(8,128)(2,1)S(1)}, bf16[256,256]{1,0:T(8,128)(2,1)S(1)}, u32[]{:S(2)}, u32[]{:S(2)}) %collective-permute-start.2) | collective-permute-done | bytes 131104 | tf_op jit(solution)/shard_map/ppermute | solution.py:232
  39.9 2.2 %shard_map.28.refs_1_ = bf16[1024,2048]{1,0:T(8,128)(2,1)S(1)} custom-call(bf16[1024,8192]{1,0:T(8,128)(2,1)} %panels.3), custom_call_target="tpu_custom_call" | custom-call | bytes 1 | tf_op jit(solution)/shard_map/pallas_call | solution.py:206
  42.2 2.8 %shard_map.29 = (f32[1024,256]{1,0:T(8,128)S(1)}, bf16[1024,256]{1,0:T(8,128)(2,1)S(1)}) custom-call(f32[1024,256]{1,0:T(8,128)S(1)} %convert_bitcast_fusion.refs_0_, bf16[1024,2048]{1,0:T(8,128)(2,1)S(1)} %shard_map.28.refs_1_, bf16[1024,256]{1,0:T(8,128)(2,1)S(1)} %pad_maximum_fusion.3.refs_2_, bf16[1024,256]{1,0:T(8,128)(2,1)S(1)} %collective-permute-done.3.refs_3_), custom_call_target="tpu_custom_call" | custom-call | flops 1073741824 | bytes 2097152 | tf_op jit(solution)/shard_map/pallas_call | solution.py:168
  46.4 2.2 %shard_map.30.refs_1_ = bf16[1024,2048]{1,0:T(8,128)(2,1)S(1)} custom-call(bf16[1024,8192]{1,0:T(8,128)(2,1)} %panels.3), custom_call_target="tpu_custom_call" | custom-call | bytes 1 | tf_op jit(solution)/shard_map/pallas_call | solution.py:206
  51.6 2.2 %shard_map.32.refs_1_.refs_2_ = bf16[1024,2048]{1,0:T(8,128)(2,1)S(1)} custom-call(bf16[1024,8192]{1,0:T(8,128)(2,1)} %panels.3), custom_call_target="tpu_custom_call" | custom-call | bytes 1 | tf_op jit(solution)/shard_map/pallas_call | solution.py:206
  53.9 1.9 %copy-done.2 = bf16[1024,2048]{1,0:T(8,128)(2,1)} copy-done((bf16[1024,2048]{1,0:T(8,128)(2,1)}, bf16[1024,2048]{1,0:T(8,128)(2,1)S(1)}, u32[]{:S(2)}) %copy-start.2) | copy-done | bytes 4194328
  58.0 1.3 collective-permute-start.15
  59.3 1.3 collective-permute-start.14
  60.6 1.5 %collective-permute-start.13 = (bf16[256,256]{1,0:T(8,128)(2,1)S(1)}, bf16[256,256]{1,0:T(8,128)(2,1)S(1)}, u32[]{:S(2)}, u32[]{:S(2)}) collective-permute-start(bf16[256,256]{1,0:T(8,128)(2,1)S(1)} %select_select_fusion.3), channel_id=1, source_target_pairs={{2,0},{3,1},{10,8},{11,9},{18,16},{19,17},{26,24},{27,25},{4,2},{5... | collective-permute-start | bytes 393224 | tf_op jit(solution)/shard_map/ppermute | solution.py:232
  62.1 2.4 %shard_map.35.refs_3_ = bf16[1024,2048]{1,0:T(8,128)(2,1)S(1)} custom-call(bf16[1024,8192]{1,0:T(8,128)(2,1)} %panels.3), custom_call_target="tpu_custom_call" | custom-call | bytes 1 | tf_op jit(solution)/shard_map/pallas_call | solution.py:206
  64.5 32.4 %collective-permute-done.15 = bf16[256,256]{1,0:T(8,128)(2,1)S(1)} collective-permute-done((bf16[256,256]{1,0:T(8,128)(2,1)S(1)}, bf16[256,256]{1,0:T(8,128)(2,1)S(1)}, u32[]{:S(2)}, u32[]{:S(2)}) %collective-permute-start.15) | collective-permute-done | bytes 131104 | tf_op jit(solution)/shard_map/ppermute | solution.py:232
  96.9 5.1 %collective-permute-done.14 = bf16[256,256]{1,0:T(8,128)(2,1)S(1)} collective-permute-done((bf16[256,256]{1,0:T(8,128)(2,1)S(1)}, bf16[256,256]{1,0:T(8,128)(2,1)S(1)}, u32[]{:S(2)}, u32[]{:S(2)}) %collective-permute-start.14) | collective-permute-done | bytes 131104 | tf_op jit(solution)/shard_map/ppermute | solution.py:232
  102.0 1.1 collective-permute-done.13
  103.1 1.1 collective-permute-start.17
  104.2 1.5 %collective-permute-start.16 = (bf16[768,256]{1,0:T(8,128)(2,1)S(1)}, bf16[768,256]{1,0:T(8,128)(2,1)S(1)}, u32[]{:S(2)}, u32[]{:S(2)}) collective-permute-start(bf16[768,256]{1,0:T(8,128)(2,1)S(1)} %pad_maximum_fusion.4), channel_id=1, source_target_pairs={{1,0},{0,1},{3,2},{2,3},{5,4},{4,5},{7,6},{6,7},{17,16},{16,17},{1... | collective-permute-start | bytes 1179656 | tf_op jit(solution)/shard_map/ppermute | solution.py:232
  105.7 9.5 %collective-permute-done.17 = bf16[768,256]{1,0:T(8,128)(2,1)S(1)} collective-permute-done((bf16[768,256]{1,0:T(8,128)(2,1)S(1)}, bf16[768,256]{1,0:T(8,128)(2,1)S(1)}, u32[]{:S(2)}, u32[]{:S(2)}) %collective-permute-start.17) | collective-permute-done | bytes 393248 | tf_op jit(solution)/shard_map/ppermute | solution.py:232
  115.6 4.3 %shard_map.36.refs_0_ = f32[1024,256]{1,0:T(8,128)S(1)} custom-call(f32[1024,256]{1,0:T(8,128)S(1)} %get-tuple-element.24.refs_0_, bf16[1024,2048]{1,0:T(8,128)(2,1)S(1)} %copy-done.1, bf16[1024,2048]{1,0:T(8,128)(2,1)S(1)} %copy-done.3, bf16[1024,2048]{1,0:T(8,128)(2,1)S(1)} %shard_map.35.refs_3_, bf16[2304,256]{1,0:T(8,128)(2,1)S(1)} %pad_maximum_fusion.1.refs_4_), custom_call_target="tpu_custom_call" | custom-call | flops 3221225472 | bytes 2097152 | tf_op jit(solution)/shard_map/pallas_call | solution.py:168
  119.9 3.0 %collective-permute-done.18.refs_4_ = bf16[768,256]{1,0:T(8,128)(2,1)S(1)} collective-permute-done((bf16[768,256]{1,0:T(8,128)(2,1)S(1)}, bf16[768,256]{1,0:T(8,128)(2,1)S(1)}, u32[]{:S(2)}, u32[]{:S(2)}) %collective-permute-start.18) | collective-permute-done | bytes 393248 | tf_op jit(solution)/shard_map/ppermute | solution.py:232
  123.1 1.8 %shard_map.37.refs_0_ = f32[1024,256]{1,0:T(8,128)S(1)} custom-call(f32[1024,256]{1,0:T(8,128)S(1)} %shard_map.36.refs_0_, bf16[1024,2048]{1,0:T(8,128)(2,1)S(1)} %copy-done.1, bf16[1024,2048]{1,0:T(8,128)(2,1)S(1)} %copy-done.3, bf16[1024,2048]{1,0:T(8,128)(2,1)S(1)} %shard_map.35.refs_3_, bf16[768,256]{1,0:T(8,128)(2,1)S(1)} %collective-permute-done.18.refs_4_), custom_call_target="tpu_custom_call" | custom-call | flops 3221225472 | bytes 2097152 | tf_op jit(solution)/shard_map/pallas_call | solution.py:168
  124.9 1.6 %collective-permute-done.19.refs_4_ = bf16[3072,256]{1,0:T(8,128)(2,1)S(1)} collective-permute-done((bf16[3072,256]{1,0:T(8,128)(2,1)S(1)}, bf16[3072,256]{1,0:T(8,128)(2,1)S(1)}, u32[]{:S(2)}, u32[]{:S(2)}) %collective-permute-start.19) | collective-permute-done | bytes 1572896 | tf_op jit(solution)/shard_map/ppermute | solution.py:232
  126.5 6.4 %shard_map.38 = f32[1024,256]{1,0:T(8,128)} custom-call(f32[1024,256]{1,0:T(8,128)S(1)} %shard_map.37.refs_0_, bf16[1024,2048]{1,0:T(8,128)(2,1)S(1)} %copy-done.1, bf16[1024,2048]{1,0:T(8,128)(2,1)S(1)} %copy-done.3, bf16[1024,2048]{1,0:T(8,128)(2,1)S(1)} %shard_map.35.refs_3_, bf16[3072,256]{1,0:T(8,128)(2,1)S(1)} %collective-permute-done.19.refs_4_), custom_call_target="tpu_custom_call" | custom-call | flops 3221225472 | bytes 2097152 | tf_op jit(solution)/shard_map/pallas_call | solution.py:168
  (50 shorter events, 10.2 us)
Async XLA Ops:
  28.2 6.3 %collective-permute-start.1 = (bf16[256,256]{1,0:T(8,128)(2,1)S(1)}, bf16[256,256]{1,0:T(8,128)(2,1)S(1)}, u32[]{:S(2)}, u32[]{:S(2)}) collective-permute-start(bf16[256,256]{1,0:T(8,128)(2,1)S(1)} %bitcast.17), channel_id=1, source_target_pairs={{16,0},{17,1},{18,2},{19,3},{20,4},{21,5},{22,6},{23,7},{0,16},{1,... | collective-permute-start | bytes 393224 | tf_op jit(solution)/shard_map/ppermute | solution.py:232
  28.9 6.0 %collective-permute-start = (bf16[256,256]{1,0:T(8,128)(2,1)S(1)}, bf16[256,256]{1,0:T(8,128)(2,1)S(1)}, u32[]{:S(2)}, u32[]{:S(2)}) collective-permute-start(bf16[256,256]{1,0:T(8,128)(2,1)S(1)} %bitcast.18), channel_id=1, source_target_pairs={{1,0},{0,1},{3,2},{2,3},{5,4},{4,5},{7,6},{6,7},{17,16},{16,17},{1... | collective-permute-start | bytes 393224 | tf_op jit(solution)/shard_map/ppermute | solution.py:232
  34.5 5.0 %collective-permute-start.2 = (bf16[256,256]{1,0:T(8,128)(2,1)S(1)}, bf16[256,256]{1,0:T(8,128)(2,1)S(1)}, u32[]{:S(2)}, u32[]{:S(2)}) collective-permute-start(bf16[256,256]{1,0:T(8,128)(2,1)S(1)} %collective-permute-done.1), channel_id=1, source_target_pairs={{1,0},{0,1},{3,2},{2,3},{5,4},{4,5},{7,6},{6,7},{17,16},{16,17},{1... | collective-permute-start | bytes 393224 | tf_op jit(solution)/shard_map/ppermute | solution.py:232
  39.5 2.7 %collective-permute-start.3 = (bf16[1024,256]{1,0:T(8,128)(2,1)S(1)}, bf16[1024,256]{1,0:T(8,128)(2,1)S(1)}, u32[]{:S(2)}, u32[]{:S(2)}) collective-permute-start(bf16[1024,256]{1,0:T(8,128)(2,1)S(1)} %pad_maximum_fusion.3.refs_2_), channel_id=1, source_target_pairs={{8,0},{9,1},{10,2},{11,3},{12,4},{13,5},{14,6},{15,7},{0,8},{1,9},... | collective-permute-start | bytes 1572872 | tf_op jit(solution)/shard_map/ppermute | solution.py:232
  45.0 3.6 %collective-permute-start.4 = (bf16[1024,256]{1,0:T(8,128)(2,1)S(1)}, bf16[1024,256]{1,0:T(8,128)(2,1)S(1)}, u32[]{:S(2)}, u32[]{:S(2)}) collective-permute-start(bf16[1024,256]{1,0:T(8,128)(2,1)S(1)} %get-tuple-element.25.refs_4_), channel_id=1, source_target_pairs={{2,4},{3,5}} | collective-permute-start | bytes 1572872 | tf_op jit(solution)/shard_map/ppermute | solution.py:232
  45.7 4.4 %collective-permute-start.5 = (bf16[1024,256]{1,0:T(8,128)(2,1)S(1)}, bf16[1024,256]{1,0:T(8,128)(2,1)S(1)}, u32[]{:S(2)}, u32[]{:S(2)}) collective-permute-start(bf16[1024,256]{1,0:T(8,128)(2,1)S(1)} %get-tuple-element.25.refs_4_), channel_id=1, source_target_pairs={{3,4},{2,5}} | collective-permute-start | bytes 1572872 | tf_op jit(solution)/shard_map/ppermute | solution.py:232
  48.6 5.2 %copy-start = (bf16[1024,2048]{1,0:T(8,128)(2,1)}, bf16[1024,2048]{1,0:T(8,128)(2,1)S(1)}, u32[]{:S(2)}) copy-start(bf16[1024,2048]{1,0:T(8,128)(2,1)S(1)} %shard_map.30.refs_1_) | copy-start | bytes 12582916
  48.7 5.1 %collective-permute-start.7 = (bf16[1024,256]{1,0:T(8,128)(2,1)S(1)}, bf16[1024,256]{1,0:T(8,128)(2,1)S(1)}, u32[]{:S(2)}, u32[]{:S(2)}) collective-permute-start(bf16[1024,256]{1,0:T(8,128)(2,1)S(1)} %get-tuple-element.25.refs_4_), channel_id=1, source_target_pairs={{3,6},{2,7}} | collective-permute-start | bytes 1572872 | tf_op jit(solution)/shard_map/ppermute | solution.py:232
  49.4 4.4 %collective-permute-start.6 = (bf16[1024,256]{1,0:T(8,128)(2,1)S(1)}, bf16[1024,256]{1,0:T(8,128)(2,1)S(1)}, u32[]{:S(2)}, u32[]{:S(2)}) collective-permute-start(bf16[1024,256]{1,0:T(8,128)(2,1)S(1)} %get-tuple-element.25.refs_4_), channel_id=1, source_target_pairs={{2,6},{3,7}} | collective-permute-start | bytes 1572872 | tf_op jit(solution)/shard_map/ppermute | solution.py:232
  50.2 3.7 %collective-permute-start.9 = (bf16[1024,256]{1,0:T(8,128)(2,1)S(1)}, bf16[1024,256]{1,0:T(8,128)(2,1)S(1)}, u32[]{:S(2)}, u32[]{:S(2)}) collective-permute-start(bf16[1024,256]{1,0:T(8,128)(2,1)S(1)} %shard_map.31.refs_5_), channel_id=1, source_target_pairs={{5,6},{4,7}} | collective-permute-start | bytes 1572872 | tf_op jit(solution)/shard_map/ppermute | solution.py:232
  50.9 3.1 %collective-permute-start.8 = (bf16[1024,256]{1,0:T(8,128)(2,1)S(1)}, bf16[1024,256]{1,0:T(8,128)(2,1)S(1)}, u32[]{:S(2)}, u32[]{:S(2)}) collective-permute-start(bf16[1024,256]{1,0:T(8,128)(2,1)S(1)} %shard_map.31.refs_5_), channel_id=1, source_target_pairs={{4,6},{5,7}} | collective-permute-start | bytes 1572872 | tf_op jit(solution)/shard_map/ppermute | solution.py:232
  53.8 2.0 %copy-start.2 = (bf16[1024,2048]{1,0:T(8,128)(2,1)}, bf16[1024,2048]{1,0:T(8,128)(2,1)S(1)}, u32[]{:S(2)}) copy-start(bf16[1024,2048]{1,0:T(8,128)(2,1)S(1)} %shard_map.32.refs_1_.refs_2_) | copy-start | bytes 12582916
  55.9 2.1 %collective-permute-start.10 = (bf16[256,256]{1,0:T(8,128)(2,1)S(1)}, bf16[256,256]{1,0:T(8,128)(2,1)S(1)}, u32[]{:S(2)}, u32[]{:S(2)}) collective-permute-start(bf16[256,256]{1,0:T(8,128)(2,1)S(1)} %get-tuple-element.28), channel_id=1, source_target_pairs={{2,26},{3,27},{4,28},{5,29},{6,30},{7,31}} | collective-permute-start | bytes 393224 | tf_op jit(solution)/shard_map/ppermute | solution.py:232
  56.6 1.4 %collective-permute-start.11 = (bf16[256,256]{1,0:T(8,128)(2,1)S(1)}, bf16[256,256]{1,0:T(8,128)(2,1)S(1)}, u32[]{:S(2)}, u32[]{:S(2)}) collective-permute-start(bf16[256,256]{1,0:T(8,128)(2,1)S(1)} %get-tuple-element.29), channel_id=1, source_target_pairs={{2,18},{3,19},{4,20},{5,21},{6,22},{7,23}} | collective-permute-start | bytes 393224 | tf_op jit(solution)/shard_map/ppermute | solution.py:232
  57.2 0.7 collective-permute-start.12
  58.0 38.9 %collective-permute-start.15 = (bf16[256,256]{1,0:T(8,128)(2,1)S(1)}, bf16[256,256]{1,0:T(8,128)(2,1)S(1)}, u32[]{:S(2)}, u32[]{:S(2)}) collective-permute-start(bf16[256,256]{1,0:T(8,128)(2,1)S(1)} %select_select_fusion.3), channel_id=1, source_target_pairs={{2,4},{3,5},{10,12},{11,13},{18,20},{19,21},{26,28},{27,29},{4,6},... | collective-permute-start | bytes 393224 | tf_op jit(solution)/shard_map/ppermute | solution.py:232
  59.3 42.7 %collective-permute-start.14 = (bf16[256,256]{1,0:T(8,128)(2,1)S(1)}, bf16[256,256]{1,0:T(8,128)(2,1)S(1)}, u32[]{:S(2)}, u32[]{:S(2)}) collective-permute-start(bf16[256,256]{1,0:T(8,128)(2,1)S(1)} %select_select_fusion.3), channel_id=1, source_target_pairs={{2,6},{3,7},{10,14},{11,15},{18,22},{19,23},{26,30},{27,31},{4,0},... | collective-permute-start | bytes 393224 | tf_op jit(solution)/shard_map/ppermute | solution.py:232
  60.6 42.5 %collective-permute-start.13 = (bf16[256,256]{1,0:T(8,128)(2,1)S(1)}, bf16[256,256]{1,0:T(8,128)(2,1)S(1)}, u32[]{:S(2)}, u32[]{:S(2)}) collective-permute-start(bf16[256,256]{1,0:T(8,128)(2,1)S(1)} %select_select_fusion.3), channel_id=1, source_target_pairs={{2,0},{3,1},{10,8},{11,9},{18,16},{19,17},{26,24},{27,25},{4,2},{5... | collective-permute-start | bytes 393224 | tf_op jit(solution)/shard_map/ppermute | solution.py:232
  62.1 53.5 %copy-start.1 = (bf16[1024,2048]{1,0:T(8,128)(2,1)S(1)}, bf16[1024,2048]{1,0:T(8,128)(2,1)}, u32[]{:S(2)}) copy-start(bf16[1024,2048]{1,0:T(8,128)(2,1)} %copy-done) | copy-start | bytes 12582916
  62.1 53.5 %copy-start.3 = (bf16[1024,2048]{1,0:T(8,128)(2,1)S(1)}, bf16[1024,2048]{1,0:T(8,128)(2,1)}, u32[]{:S(2)}) copy-start(bf16[1024,2048]{1,0:T(8,128)(2,1)} %copy-done.2) | copy-start | bytes 12582916
  103.1 12.0 %collective-permute-start.17 = (bf16[768,256]{1,0:T(8,128)(2,1)S(1)}, bf16[768,256]{1,0:T(8,128)(2,1)S(1)}, u32[]{:S(2)}, u32[]{:S(2)}) collective-permute-start(bf16[768,256]{1,0:T(8,128)(2,1)S(1)} %pad_maximum_fusion.4), channel_id=1, source_target_pairs={{16,0},{17,1},{18,2},{19,3},{20,4},{21,5},{22,6},{23,7},{0,16},{1,... | collective-permute-start | bytes 1179656 | tf_op jit(solution)/shard_map/ppermute | solution.py:232
  104.2 11.3 %collective-permute-start.16 = (bf16[768,256]{1,0:T(8,128)(2,1)S(1)}, bf16[768,256]{1,0:T(8,128)(2,1)S(1)}, u32[]{:S(2)}, u32[]{:S(2)}) collective-permute-start(bf16[768,256]{1,0:T(8,128)(2,1)S(1)} %pad_maximum_fusion.4), channel_id=1, source_target_pairs={{1,0},{0,1},{3,2},{2,3},{5,4},{4,5},{7,6},{6,7},{17,16},{16,17},{1... | collective-permute-start | bytes 1179656 | tf_op jit(solution)/shard_map/ppermute | solution.py:232
  115.1 7.8 %collective-permute-start.18 = (bf16[768,256]{1,0:T(8,128)(2,1)S(1)}, bf16[768,256]{1,0:T(8,128)(2,1)S(1)}, u32[]{:S(2)}, u32[]{:S(2)}) collective-permute-start(bf16[768,256]{1,0:T(8,128)(2,1)S(1)} %collective-permute-done.17), channel_id=1, source_target_pairs={{1,0},{0,1},{3,2},{2,3},{5,4},{4,5},{7,6},{6,7},{17,16},{16,17},{1... | collective-permute-start | bytes 1179656 | tf_op jit(solution)/shard_map/ppermute | solution.py:232
  123.0 3.5 %collective-permute-start.19 = (bf16[3072,256]{1,0:T(8,128)(2,1)S(1)}, bf16[3072,256]{1,0:T(8,128)(2,1)S(1)}, u32[]{:S(2)}, u32[]{:S(2)}) collective-permute-start(bf16[3072,256]{1,0:T(8,128)(2,1)S(1)} %pad_maximum_fusion), channel_id=1, source_target_pairs={{8,0},{9,1},{10,2},{11,3},{12,4},{13,5},{14,6},{15,7},{0,8},{1,9},... | collective-permute-start | bytes 4718600 | tf_op jit(solution)/shard_map/ppermute | solution.py:232

commit v15 on v14

--- a/solution.py
+++ b/solution.py
@@ -368,11 +368,9 @@
                 for k, near in ((1, near1), (2, near2), (3, near3))
             ]
 
-        (current,) = run(current, terms(True, (most, True, 0, n_most)), [f32_rows])
-        whole = after(jnp.concatenate([most, last], axis=0), current)
-        other = core_exchange(whole)
-        (current,) = run(current, terms(False, (last, True, n_most, len(across))), [f32_rows])
-        (out,) = run(current, terms(False, (other, False, 0, len(offsets))), [(jnp.float32, 0, rows_here, True)])
+        other = core_exchange(jnp.concatenate([most, last], axis=0))
+        parts = [(most, True, 0, n_most), (last, True, n_most, len(across)), (other, False, 0, len(offsets))]
+        (out,) = run(current, terms(True, *parts), [(jnp.float32, 0, rows_here, True)])
         return out
 
     return on_device

time: 133 us -> 138 us (1.038)
  waiting for transfers between devices: 62 us -> 68.4 us
    ppermute x20, waiting for transfers between devices: 62 us -> 68.4 us  [send(): return lax.ppermute(value, AXES, pairs)]
    pallas_call x7 -> x5, Pallas kernels: 15.5 us -> 14.3 us  [steps(): pl.pallas_call(functools.partial(step_kernel, plan, handed, len(arrays),...]
  transfers between devices with their start and end apart: 20 -> 20, of which waited for: 8 -> 8; matrix products, arithmetic and copies ran while one was open for 0% -> 0% of each run, Pallas kernels for 11% -> 7%
where the time goes in v15:
time: 138 us
  waiting for transfers between devices  68.4 us (50%)
  blocking collectives  26.3 us (19%)
  Pallas kernels  23.3 us (17%)
  starting transfers between devices  14.9 us (11%)
  local copies, waits for them, and re-layouts  3.04 us (2%)
  other arithmetic  1.48 us (1%)
    ppermute x20, waiting for transfers between devices, send(): return lax.ppermute(value, AXES, pairs)  68.4 us
    all_to_all x1, blocking collectives, on_device(): lax.all_to_all(outgoing, AXES, split_axis=1, concat_axis=0, tiled=True)  26.3 us
    ppermute x20, starting transfers between devices, send(): return lax.ppermute(value, AXES, pairs)  14.9 us
    pallas_call x5, Pallas kernels, steps(): pl.pallas_call(functools.partial(step_kernel, plan, handed, len(arrays),...  14.3 us
    pallas_call x4, Pallas kernels, near_panel(): pl.pallas_call(functools.partial(near_kernel, k), in_specs=[pl.BlockSpec(...  9.01 us
  transfers between devices with their start and end apart: 20, of which 8 were waited for; matrix products, arithmetic and copies ran while one was open for 0% of the time, Pallas kernels for 7%

profile of v15, /device:TPU:0, one launch (start us, length us, event | category | flops | bytes accessed | tf_op | source)
XLA Modules:
  0.0 137.7 jit_solution(6474263875875591344)
XLA Ops:
  0.0 0.8 slice.12
  0.8 1.1 pad_maximum_fusion.2
  1.9 26.3 %all_to_all.15 = bf16[8,32,1280]{2,0,1:T(8,128)(2,1)S(1)} all-to-all(bf16[8,32,1280]{2,0,1:T(8,128)(2,1)S(1)} %pad_maximum_fusion.2), channel_id=1, replica_groups=mesh['row'=4,'col'=8] {'row','col'}, dimensions={1} | all-to-all | bytes 1310720 | tf_op jit(solution)/shard_map/all_to_all | solution.py:300
  28.9 0.8 collective-permute-start
  29.7 4.8 %collective-permute-done.1 = bf16[256,256]{1,0:T(8,128)(2,1)S(1)} collective-permute-done((bf16[256,256]{1,0:T(8,128)(2,1)S(1)}, bf16[256,256]{1,0:T(8,128)(2,1)S(1)}, u32[]{:S(2)}, u32[]{:S(2)}) %collective-permute-start.1) | collective-permute-done | bytes 131104 | tf_op jit(solution)/shard_map/ppermute | solution.py:232
  34.8 4.6 %collective-permute-done.2 = bf16[256,256]{1,0:T(8,128)(2,1)S(1)} collective-permute-done((bf16[256,256]{1,0:T(8,128)(2,1)S(1)}, bf16[256,256]{1,0:T(8,128)(2,1)S(1)}, u32[]{:S(2)}, u32[]{:S(2)}) %collective-permute-start.2) | collective-permute-done | bytes 131104 | tf_op jit(solution)/shard_map/ppermute | solution.py:232
  39.9 2.2 %shard_map.28.refs_1_ = bf16[1024,2048]{1,0:T(8,128)(2,1)S(1)} custom-call(bf16[1024,8192]{1,0:T(8,128)(2,1)} %panels.3), custom_call_target="tpu_custom_call" | custom-call | bytes 1 | tf_op jit(solution)/shard_map/pallas_call | solution.py:206
  42.2 2.8 %shard_map.29 = (f32[1024,256]{1,0:T(8,128)S(1)}, bf16[1024,256]{1,0:T(8,128)(2,1)S(1)}) custom-call(f32[1024,256]{1,0:T(8,128)S(1)} %convert_bitcast_fusion.refs_0_, bf16[1024,2048]{1,0:T(8,128)(2,1)S(1)} %shard_map.28.refs_1_, bf16[1024,256]{1,0:T(8,128)(2,1)S(1)} %pad_maximum_fusion.3.refs_2_, bf16[1024,256]{1,0:T(8,128)(2,1)S(1)} %collective-permute-done.3.refs_3_), custom_call_target="tpu_custom_call" | custom-call | flops 1073741824 | bytes 2097152 | tf_op jit(solution)/shard_map/pallas_call | solution.py:168
  46.4 2.2 %shard_map.30.refs_1_ = bf16[1024,2048]{1,0:T(8,128)(2,1)S(1)} custom-call(bf16[1024,8192]{1,0:T(8,128)(2,1)} %panels.3), custom_call_target="tpu_custom_call" | custom-call | bytes 1 | tf_op jit(solution)/shard_map/pallas_call | solution.py:206
  51.6 2.2 %shard_map.32.refs_1_.refs_2_ = bf16[1024,2048]{1,0:T(8,128)(2,1)S(1)} custom-call(bf16[1024,8192]{1,0:T(8,128)(2,1)} %panels.3), custom_call_target="tpu_custom_call" | custom-call | bytes 1 | tf_op jit(solution)/shard_map/pallas_call | solution.py:206
  53.9 1.9 %copy-done.2 = bf16[1024,2048]{1,0:T(8,128)(2,1)} copy-done((bf16[1024,2048]{1,0:T(8,128)(2,1)}, bf16[1024,2048]{1,0:T(8,128)(2,1)S(1)}, u32[]{:S(2)}) %copy-start.2) | copy-done | bytes 4194328
  58.0 1.3 collective-permute-start.15
  59.3 1.3 collective-permute-start.14
  60.6 1.3 collective-permute-start.13
  61.9 2.4 %shard_map.35.refs_3_ = bf16[1024,2048]{1,0:T(8,128)(2,1)S(1)} custom-call(bf16[1024,8192]{1,0:T(8,128)(2,1)} %panels.3), custom_call_target="tpu_custom_call" | custom-call | bytes 1 | tf_op jit(solution)/shard_map/pallas_call | solution.py:206
  64.3 32.6 %collective-permute-done.15 = bf16[256,256]{1,0:T(8,128)(2,1)S(1)} collective-permute-done((bf16[256,256]{1,0:T(8,128)(2,1)S(1)}, bf16[256,256]{1,0:T(8,128)(2,1)S(1)}, u32[]{:S(2)}, u32[]{:S(2)}) %collective-permute-start.15) | collective-permute-done | bytes 131104 | tf_op jit(solution)/shard_map/ppermute | solution.py:232
  96.9 5.1 %collective-permute-done.14 = bf16[256,256]{1,0:T(8,128)(2,1)S(1)} collective-permute-done((bf16[256,256]{1,0:T(8,128)(2,1)S(1)}, bf16[256,256]{1,0:T(8,128)(2,1)S(1)}, u32[]{:S(2)}, u32[]{:S(2)}) %collective-permute-start.14) | collective-permute-done | bytes 131104 | tf_op jit(solution)/shard_map/ppermute | solution.py:232
  102.0 1.1 collective-permute-done.13
  103.1 1.1 collective-permute-start.17
  104.2 1.5 %collective-permute-start.16 = (bf16[768,256]{1,0:T(8,128)(2,1)S(1)}, bf16[768,256]{1,0:T(8,128)(2,1)S(1)}, u32[]{:S(2)}, u32[]{:S(2)}) collective-permute-start(bf16[768,256]{1,0:T(8,128)(2,1)S(1)} %pad_maximum_fusion.4), channel_id=1, source_target_pairs={{1,0},{0,1},{3,2},{2,3},{5,4},{4,5},{7,6},{6,7},{17,16},{16,17},{1... | collective-permute-start | bytes 1179656 | tf_op jit(solution)/shard_map/ppermute | solution.py:232
  105.7 9.5 %collective-permute-done.17 = bf16[768,256]{1,0:T(8,128)(2,1)S(1)} collective-permute-done((bf16[768,256]{1,0:T(8,128)(2,1)S(1)}, bf16[768,256]{1,0:T(8,128)(2,1)S(1)}, u32[]{:S(2)}, u32[]{:S(2)}) %collective-permute-start.17) | collective-permute-done | bytes 393248 | tf_op jit(solution)/shard_map/ppermute | solution.py:232
  115.5 7.4 %collective-permute-done.18.refs_5_ = bf16[768,256]{1,0:T(8,128)(2,1)S(1)} collective-permute-done((bf16[768,256]{1,0:T(8,128)(2,1)S(1)}, bf16[768,256]{1,0:T(8,128)(2,1)S(1)}, u32[]{:S(2)}, u32[]{:S(2)}) %collective-permute-start.18) | collective-permute-done | bytes 393248 | tf_op jit(solution)/shard_map/ppermute | solution.py:232
  123.2 3.3 %collective-permute-done.19.refs_6_ = bf16[3072,256]{1,0:T(8,128)(2,1)S(1)} collective-permute-done((bf16[3072,256]{1,0:T(8,128)(2,1)S(1)}, bf16[3072,256]{1,0:T(8,128)(2,1)S(1)}, u32[]{:S(2)}, u32[]{:S(2)}) %collective-permute-start.19) | collective-permute-done | bytes 1572896 | tf_op jit(solution)/shard_map/ppermute | solution.py:232
  126.5 11.2 %shard_map.36 = f32[1024,256]{1,0:T(8,128)} custom-call(f32[1024,256]{1,0:T(8,128)S(1)} %get-tuple-element.23.refs_0_, bf16[1024,2048]{1,0:T(8,128)(2,1)S(1)} %copy-done.1, bf16[1024,2048]{1,0:T(8,128)(2,1)S(1)} %copy-done.3, bf16[1024,2048]{1,0:T(8,128)(2,1)S(1)} %shard_map.35.refs_3_, bf16[2304,256]{1,0:T(8,128)(2,1)S(1)} %pad_maximum_fusion.1.refs_4_, ...), custom_call_target="tpu_custom_call" | custom-call | flops 3221225472 | bytes 2097152 | tf_op jit(solution)/shard_map/pallas_call | solution.py:168
  (48 shorter events, 8.7 us)
Async XLA Ops:
  28.2 6.3 %collective-permute-start.1 = (bf16[256,256]{1,0:T(8,128)(2,1)S(1)}, bf16[256,256]{1,0:T(8,128)(2,1)S(1)}, u32[]{:S(2)}, u32[]{:S(2)}) collective-permute-start(bf16[256,256]{1,0:T(8,128)(2,1)S(1)} %bitcast.17), channel_id=1, source_target_pairs={{16,0},{17,1},{18,2},{19,3},{20,4},{21,5},{22,6},{23,7},{0,16},{1,... | collective-permute-start | bytes 393224 | tf_op jit(solution)/shard_map/ppermute | solution.py:232
  28.9 6.0 %collective-permute-start = (bf16[256,256]{1,0:T(8,128)(2,1)S(1)}, bf16[256,256]{1,0:T(8,128)(2,1)S(1)}, u32[]{:S(2)}, u32[]{:S(2)}) collective-permute-start(bf16[256,256]{1,0:T(8,128)(2,1)S(1)} %bitcast.18), channel_id=1, source_target_pairs={{1,0},{0,1},{3,2},{2,3},{5,4},{4,5},{7,6},{6,7},{17,16},{16,17},{1... | collective-permute-start | bytes 393224 | tf_op jit(solution)/shard_map/ppermute | solution.py:232
  34.5 5.0 %collective-permute-start.2 = (bf16[256,256]{1,0:T(8,128)(2,1)S(1)}, bf16[256,256]{1,0:T(8,128)(2,1)S(1)}, u32[]{:S(2)}, u32[]{:S(2)}) collective-permute-start(bf16[256,256]{1,0:T(8,128)(2,1)S(1)} %collective-permute-done.1), channel_id=1, source_target_pairs={{1,0},{0,1},{3,2},{2,3},{5,4},{4,5},{7,6},{6,7},{17,16},{16,17},{1... | collective-permute-start | bytes 393224 | tf_op jit(solution)/shard_map/ppermute | solution.py:232
  39.5 2.7 %collective-permute-start.3 = (bf16[1024,256]{1,0:T(8,128)(2,1)S(1)}, bf16[1024,256]{1,0:T(8,128)(2,1)S(1)}, u32[]{:S(2)}, u32[]{:S(2)}) collective-permute-start(bf16[1024,256]{1,0:T(8,128)(2,1)S(1)} %pad_maximum_fusion.3.refs_2_), channel_id=1, source_target_pairs={{8,0},{9,1},{10,2},{11,3},{12,4},{13,5},{14,6},{15,7},{0,8},{1,9},... | collective-permute-start | bytes 1572872 | tf_op jit(solution)/shard_map/ppermute | solution.py:232
  45.0 3.6 %collective-permute-start.4 = (bf16[1024,256]{1,0:T(8,128)(2,1)S(1)}, bf16[1024,256]{1,0:T(8,128)(2,1)S(1)}, u32[]{:S(2)}, u32[]{:S(2)}) collective-permute-start(bf16[1024,256]{1,0:T(8,128)(2,1)S(1)} %get-tuple-element.24.refs_4_), channel_id=1, source_target_pairs={{2,4},{3,5}} | collective-permute-start | bytes 1572872 | tf_op jit(solution)/shard_map/ppermute | solution.py:232
  45.7 4.4 %collective-permute-start.5 = (bf16[1024,256]{1,0:T(8,128)(2,1)S(1)}, bf16[1024,256]{1,0:T(8,128)(2,1)S(1)}, u32[]{:S(2)}, u32[]{:S(2)}) collective-permute-start(bf16[1024,256]{1,0:T(8,128)(2,1)S(1)} %get-tuple-element.24.refs_4_), channel_id=1, source_target_pairs={{3,4},{2,5}} | collective-permute-start | bytes 1572872 | tf_op jit(solution)/shard_map/ppermute | solution.py:232
  48.6 5.2 %copy-start = (bf16[1024,2048]{1,0:T(8,128)(2,1)}, bf16[1024,2048]{1,0:T(8,128)(2,1)S(1)}, u32[]{:S(2)}) copy-start(bf16[1024,2048]{1,0:T(8,128)(2,1)S(1)} %shard_map.30.refs_1_) | copy-start | bytes 12582916
  48.7 5.1 %collective-permute-start.7 = (bf16[1024,256]{1,0:T(8,128)(2,1)S(1)}, bf16[1024,256]{1,0:T(8,128)(2,1)S(1)}, u32[]{:S(2)}, u32[]{:S(2)}) collective-permute-start(bf16[1024,256]{1,0:T(8,128)(2,1)S(1)} %get-tuple-element.24.refs_4_), channel_id=1, source_target_pairs={{3,6},{2,7}} | collective-permute-start | bytes 1572872 | tf_op jit(solution)/shard_map/ppermute | solution.py:232
  49.4 4.4 %collective-permute-start.6 = (bf16[1024,256]{1,0:T(8,128)(2,1)S(1)}, bf16[1024,256]{1,0:T(8,128)(2,1)S(1)}, u32[]{:S(2)}, u32[]{:S(2)}) collective-permute-start(bf16[1024,256]{1,0:T(8,128)(2,1)S(1)} %get-tuple-element.24.refs_4_), channel_id=1, source_target_pairs={{2,6},{3,7}} | collective-permute-start | bytes 1572872 | tf_op jit(solution)/shard_map/ppermute | solution.py:232
  50.2 3.7 %collective-permute-start.9 = (bf16[1024,256]{1,0:T(8,128)(2,1)S(1)}, bf16[1024,256]{1,0:T(8,128)(2,1)S(1)}, u32[]{:S(2)}, u32[]{:S(2)}) collective-permute-start(bf16[1024,256]{1,0:T(8,128)(2,1)S(1)} %shard_map.31.refs_5_), channel_id=1, source_target_pairs={{5,6},{4,7}} | collective-permute-start | bytes 1572872 | tf_op jit(solution)/shard_map/ppermute | solution.py:232
  50.9 3.1 %collective-permute-start.8 = (bf16[1024,256]{1,0:T(8,128)(2,1)S(1)}, bf16[1024,256]{1,0:T(8,128)(2,1)S(1)}, u32[]{:S(2)}, u32[]{:S(2)}) collective-permute-start(bf16[1024,256]{1,0:T(8,128)(2,1)S(1)} %shard_map.31.refs_5_), channel_id=1, source_target_pairs={{4,6},{5,7}} | collective-permute-start | bytes 1572872 | tf_op jit(solution)/shard_map/ppermute | solution.py:232
  53.8 2.0 %copy-start.2 = (bf16[1024,2048]{1,0:T(8,128)(2,1)}, bf16[1024,2048]{1,0:T(8,128)(2,1)S(1)}, u32[]{:S(2)}) copy-start(bf16[1024,2048]{1,0:T(8,128)(2,1)S(1)} %shard_map.32.refs_1_.refs_2_) | copy-start | bytes 12582916
  55.9 2.1 %collective-permute-start.10 = (bf16[256,256]{1,0:T(8,128)(2,1)S(1)}, bf16[256,256]{1,0:T(8,128)(2,1)S(1)}, u32[]{:S(2)}, u32[]{:S(2)}) collective-permute-start(bf16[256,256]{1,0:T(8,128)(2,1)S(1)} %get-tuple-element.27), channel_id=1, source_target_pairs={{2,26},{3,27},{4,28},{5,29},{6,30},{7,31}} | collective-permute-start | bytes 393224 | tf_op jit(solution)/shard_map/ppermute | solution.py:232
  56.6 1.4 %collective-permute-start.11 = (bf16[256,256]{1,0:T(8,128)(2,1)S(1)}, bf16[256,256]{1,0:T(8,128)(2,1)S(1)}, u32[]{:S(2)}, u32[]{:S(2)}) collective-permute-start(bf16[256,256]{1,0:T(8,128)(2,1)S(1)} %get-tuple-element.28), channel_id=1, source_target_pairs={{2,18},{3,19},{4,20},{5,21},{6,22},{7,23}} | collective-permute-start | bytes 393224 | tf_op jit(solution)/shard_map/ppermute | solution.py:232
  57.2 0.7 collective-permute-start.12
  58.0 38.9 %collective-permute-start.15 = (bf16[256,256]{1,0:T(8,128)(2,1)S(1)}, bf16[256,256]{1,0:T(8,128)(2,1)S(1)}, u32[]{:S(2)}, u32[]{:S(2)}) collective-permute-start(bf16[256,256]{1,0:T(8,128)(2,1)S(1)} %select_select_fusion.3), channel_id=1, source_target_pairs={{2,4},{3,5},{10,12},{11,13},{18,20},{19,21},{26,28},{27,29},{4,6},... | collective-permute-start | bytes 393224 | tf_op jit(solution)/shard_map/ppermute | solution.py:232
  59.3 42.7 %collective-permute-start.14 = (bf16[256,256]{1,0:T(8,128)(2,1)S(1)}, bf16[256,256]{1,0:T(8,128)(2,1)S(1)}, u32[]{:S(2)}, u32[]{:S(2)}) collective-permute-start(bf16[256,256]{1,0:T(8,128)(2,1)S(1)} %select_select_fusion.3), channel_id=1, source_target_pairs={{2,6},{3,7},{10,14},{11,15},{18,22},{19,23},{26,30},{27,31},{4,0},... | collective-permute-start | bytes 393224 | tf_op jit(solution)/shard_map/ppermute | solution.py:232
  60.6 42.5 %collective-permute-start.13 = (bf16[256,256]{1,0:T(8,128)(2,1)S(1)}, bf16[256,256]{1,0:T(8,128)(2,1)S(1)}, u32[]{:S(2)}, u32[]{:S(2)}) collective-permute-start(bf16[256,256]{1,0:T(8,128)(2,1)S(1)} %select_select_fusion.3), channel_id=1, source_target_pairs={{2,0},{3,1},{10,8},{11,9},{18,16},{19,17},{26,24},{27,25},{4,2},{5... | collective-permute-start | bytes 393224 | tf_op jit(solution)/shard_map/ppermute | solution.py:232
  61.9 64.6 %copy-start.3 = (bf16[1024,2048]{1,0:T(8,128)(2,1)S(1)}, bf16[1024,2048]{1,0:T(8,128)(2,1)}, u32[]{:S(2)}) copy-start(bf16[1024,2048]{1,0:T(8,128)(2,1)} %copy-done.2) | copy-start | bytes 12582916
  103.1 23.4 %copy-start.1 = (bf16[1024,2048]{1,0:T(8,128)(2,1)S(1)}, bf16[1024,2048]{1,0:T(8,128)(2,1)}, u32[]{:S(2)}) copy-start(bf16[1024,2048]{1,0:T(8,128)(2,1)} %copy-done) | copy-start | bytes 12582916
  103.1 12.0 %collective-permute-start.17 = (bf16[768,256]{1,0:T(8,128)(2,1)S(1)}, bf16[768,256]{1,0:T(8,128)(2,1)S(1)}, u32[]{:S(2)}, u32[]{:S(2)}) collective-permute-start(bf16[768,256]{1,0:T(8,128)(2,1)S(1)} %pad_maximum_fusion.4), channel_id=1, source_target_pairs={{16,0},{17,1},{18,2},{19,3},{20,4},{21,5},{22,6},{23,7},{0,16},{1,... | collective-permute-start | bytes 1179656 | tf_op jit(solution)/shard_map/ppermute | solution.py:232
  104.2 11.3 %collective-permute-start.16 = (bf16[768,256]{1,0:T(8,128)(2,1)S(1)}, bf16[768,256]{1,0:T(8,128)(2,1)S(1)}, u32[]{:S(2)}, u32[]{:S(2)}) collective-permute-start(bf16[768,256]{1,0:T(8,128)(2,1)S(1)} %pad_maximum_fusion.4), channel_id=1, source_target_pairs={{1,0},{0,1},{3,2},{2,3},{5,4},{4,5},{7,6},{6,7},{17,16},{16,17},{1... | collective-permute-start | bytes 1179656 | tf_op jit(solution)/shard_map/ppermute | solution.py:232
  115.1 7.8 %collective-permute-start.18 = (bf16[768,256]{1,0:T(8,128)(2,1)S(1)}, bf16[768,256]{1,0:T(8,128)(2,1)S(1)}, u32[]{:S(2)}, u32[]{:S(2)}) collective-permute-start(bf16[768,256]{1,0:T(8,128)(2,1)S(1)} %collective-permute-done.17), channel_id=1, source_target_pairs={{1,0},{0,1},{3,2},{2,3},{5,4},{4,5},{7,6},{6,7},{17,16},{16,17},{1... | collective-permute-start | bytes 1179656 | tf_op jit(solution)/shard_map/ppermute | solution.py:232
  123.0 3.5 %collective-permute-start.19 = (bf16[3072,256]{1,0:T(8,128)(2,1)S(1)}, bf16[3072,256]{1,0:T(8,128)(2,1)S(1)}, u32[]{:S(2)}, u32[]{:S(2)}) collective-permute-start(bf16[3072,256]{1,0:T(8,128)(2,1)S(1)} %pad_maximum_fusion), channel_id=1, source_target_pairs={{8,0},{9,1},{10,2},{11,3},{12,4},{13,5},{14,6},{15,7},{0,8},{1,9},... | collective-permute-start | bytes 4718600 | tf_op jit(solution)/shard_map/ppermute | solution.py:232
